TPU v7x, 256 devices: a whole 4x4x8 slice. The times are simulated.
256 devices in a mesh: env: 8 (over y_hi, x), sp: 32 (over z, y_lo, core).
Axes of the slice: x: 4, y: 4 (y_hi: 2, y_lo: 2; y = y_hi * 2 + y_lo), z: 8, core: 2. Of those that a mesh axis runs over, the one named last changes fastest.
Arguments:
- descriptors: bfloat16 [16384, 512], P('env'), may hold values from -6 to 6
- sparse_points: bfloat16 [8192, 512], P('sp'), may hold values from -6 to 6
Outputs:
- gram_bands: float32 [32, 17, 256, 256], P('sp', None, 'env')
All inputs are finite; a program needn't handle non-finite values.
Results may differ from a plain program's by a relative error of at most 0.002.
Values may be sent and summed in bfloat16 or wider, within the bound.
No kernel may reach another device: no remote copies, remote signals or barrier semaphores. Data moves between devices by JAX's collectives and lax.ppermute only.
A program may use at most 64 MiB of HBM per device.

v0:
```python
import jax
import jax.numpy as jnp
from jax import lax
from jax.sharding import PartitionSpec as P

ZETA = 4


def from_behind(x, axis, by):
    peers = lax.axis_size(axis)
    return lax.ppermute(x, axis, [(i, (i + by) % peers) for i in range(peers)])


def unit_rows(values):
    values = values.astype(jnp.float32)
    scale = lax.rsqrt(jnp.sum(values * values, axis=1, keepdims=True) + 1e-06)
    return (values * scale).astype(jnp.bfloat16)


def pass_along(moving, offset):
    return from_behind(moving, "sp", offset)


def on_device(descriptors, sparse_points):
    env_hat = unit_rows(descriptors)
    own_points = unit_rows(sparse_points)
    products = lax.dot_general(
        own_points, env_hat, (((1,), (1,)), ((), ())), preferred_element_type=jnp.float32
    )
    own_kernel = (4.0 * products**ZETA).astype(jnp.bfloat16)
    sp_devices = lax.axis_size("sp")
    half_way = sp_devices // 2

    def gram_tile(moving):
        return lax.dot_general(
            own_kernel, moving, (((1,), (1,)), ((), ())), preferred_element_type=jnp.float32
        )

    def store_tile(partial_value, where, tile_value):
        return lax.dynamic_update_index_in_dim(partial_value, tile_value, where, 0)

    width = own_kernel.shape[0]
    partial_value = jnp.zeros((half_way + 1, width, width), jnp.float32)
    partial_value = store_tile(partial_value, 0, gram_tile(own_kernel))

    def advance(turn, loop_state):
        moving, partial_value = loop_state
        moving = pass_along(moving, -1)
        return (moving, store_tile(partial_value, turn, gram_tile(moving)))

    moving, partial_value = lax.fori_loop(1, half_way + 1, advance, (own_kernel, partial_value))
    summed = lax.psum_scatter(partial_value, "env", scatter_dimension=1, tiled=True)
    total_envs = descriptors.shape[0] * lax.axis_size("env")
    return (summed / jnp.float32(total_envs))[None]


def solution(mesh):
    placed = (P("env", None), P("sp", None))
    return jax.shard_map(
        on_device, mesh=mesh, in_specs=placed, out_specs=P("sp", None, "env", None), check_vma=False
    )
```

profile of v0, /device:TPU:1, one launch (start us, length us, event | category | flops | bytes accessed | tf_op | source)
XLA Modules:
  0.0 398.8 jit_solution(13555928716882983152)
XLA Ops:
  6.5 1.1 fusion.8
  7.6 2.1 fusion.1
  9.7 2.6 fusion.5
  12.3 0.5 convolution_bitcast_fusion.1
  12.8 0.1 copy.5
  12.9 2.5 dynamic_update_slice.14
  15.4 271.9 %while.17 = (s32[]{:T(128)}, bf16[256,2048]{1,0:T(8,128)(2,1)S(1)}, f32[17,256,256]{2,1,0:T(8,128)}, bf16[256,2048]{1,0:T(8,128)(2,1)S(1)}, s32[]{:T(128)}, /*index=5*/s32[]{:T(128)}, s32[]{:T(128)}) while((s32[]{:T(128)}, bf16[256,2048]{1,0:T(8,128)(2,1)S(1)}, f32[17,256,256]{2,1,0:T(8,128)}, bf16[256,2048]{1,0:T(8,128)(2,1)S(1)}, s32[]{:T(128)}, ...), condition=%wide.region_3.4_spmd, body=%wide.region_2.3_spmd.sunk | while | flops 268435456 | bytes 8650907 | solution.py:51
  15.4 3.2 collective-permute-start
  18.7 11.9 %collective-permute-done = bf16[256,2048]{1,0:T(8,128)(2,1)S(1)} collective-permute-done((bf16[256,2048]{1,0:T(8,128)(2,1)S(1)}, bf16[256,2048]{1,0:T(8,128)(2,1)S(1)}, u32[]{:S(2)}, u32[]{:S(2)}) %collective-permute-start) | collective-permute-done | bytes 1048608 | tf_op jit(solution)/shard_map/while/body/eval_jaxpr/ppermute | solution.py:11
  30.6 0.1 copy.11
  30.7 1.2 fusion.21
  31.9 5.0 %collective-permute-start = (bf16[256,2048]{1,0:T(8,128)(2,1)S(1)}, bf16[256,2048]{1,0:T(8,128)(2,1)S(1)}, u32[]{:S(2)}, u32[]{:S(2)}) collective-permute-start(bf16[256,2048]{1,0:T(8,128)(2,1)S(1)} %get-tuple-element.157), channel_id=1, source_target_pairs={{0,31},{1,0},{2,1},{3,2},{4,3},{5,4},{6,5},{7,6},{8,7},{9,8},{10,9... | collective-permute-start | bytes 3145736 | tf_op jit(solution)/shard_map/while/body/eval_jaxpr/ppermute | solution.py:11
  36.8 9.3 %collective-permute-done = bf16[256,2048]{1,0:T(8,128)(2,1)S(1)} collective-permute-done((bf16[256,2048]{1,0:T(8,128)(2,1)S(1)}, bf16[256,2048]{1,0:T(8,128)(2,1)S(1)}, u32[]{:S(2)}, u32[]{:S(2)}) %collective-permute-start) | collective-permute-done | bytes 1048608 | tf_op jit(solution)/shard_map/while/body/eval_jaxpr/ppermute | solution.py:11
  46.1 0.1 copy.11
  46.2 1.2 fusion.21
  47.4 7.1 %collective-permute-start = (bf16[256,2048]{1,0:T(8,128)(2,1)S(1)}, bf16[256,2048]{1,0:T(8,128)(2,1)S(1)}, u32[]{:S(2)}, u32[]{:S(2)}) collective-permute-start(bf16[256,2048]{1,0:T(8,128)(2,1)S(1)} %get-tuple-element.157), channel_id=1, source_target_pairs={{0,31},{1,0},{2,1},{3,2},{4,3},{5,4},{6,5},{7,6},{8,7},{9,8},{10,9... | collective-permute-start | bytes 3145736 | tf_op jit(solution)/shard_map/while/body/eval_jaxpr/ppermute | solution.py:11
  54.5 7.1 %collective-permute-done = bf16[256,2048]{1,0:T(8,128)(2,1)S(1)} collective-permute-done((bf16[256,2048]{1,0:T(8,128)(2,1)S(1)}, bf16[256,2048]{1,0:T(8,128)(2,1)S(1)}, u32[]{:S(2)}, u32[]{:S(2)}) %collective-permute-start) | collective-permute-done | bytes 1048608 | tf_op jit(solution)/shard_map/while/body/eval_jaxpr/ppermute | solution.py:11
  61.6 0.1 copy.11
  61.7 1.2 fusion.21
  62.9 9.2 %collective-permute-start = (bf16[256,2048]{1,0:T(8,128)(2,1)S(1)}, bf16[256,2048]{1,0:T(8,128)(2,1)S(1)}, u32[]{:S(2)}, u32[]{:S(2)}) collective-permute-start(bf16[256,2048]{1,0:T(8,128)(2,1)S(1)} %get-tuple-element.157), channel_id=1, source_target_pairs={{0,31},{1,0},{2,1},{3,2},{4,3},{5,4},{6,5},{7,6},{8,7},{9,8},{10,9... | collective-permute-start | bytes 3145736 | tf_op jit(solution)/shard_map/while/body/eval_jaxpr/ppermute | solution.py:11
  72.1 5.0 %collective-permute-done = bf16[256,2048]{1,0:T(8,128)(2,1)S(1)} collective-permute-done((bf16[256,2048]{1,0:T(8,128)(2,1)S(1)}, bf16[256,2048]{1,0:T(8,128)(2,1)S(1)}, u32[]{:S(2)}, u32[]{:S(2)}) %collective-permute-start) | collective-permute-done | bytes 1048608 | tf_op jit(solution)/shard_map/while/body/eval_jaxpr/ppermute | solution.py:11
  77.1 0.1 copy.11
  77.3 1.2 fusion.21
  78.5 11.3 %collective-permute-start = (bf16[256,2048]{1,0:T(8,128)(2,1)S(1)}, bf16[256,2048]{1,0:T(8,128)(2,1)S(1)}, u32[]{:S(2)}, u32[]{:S(2)}) collective-permute-start(bf16[256,2048]{1,0:T(8,128)(2,1)S(1)} %get-tuple-element.157), channel_id=1, source_target_pairs={{0,31},{1,0},{2,1},{3,2},{4,3},{5,4},{6,5},{7,6},{8,7},{9,8},{10,9... | collective-permute-start | bytes 3145736 | tf_op jit(solution)/shard_map/while/body/eval_jaxpr/ppermute | solution.py:11
  89.7 2.9 collective-permute-done
  92.7 0.1 copy.11
  92.8 1.2 fusion.21
  94.0 13.4 %collective-permute-start = (bf16[256,2048]{1,0:T(8,128)(2,1)S(1)}, bf16[256,2048]{1,0:T(8,128)(2,1)S(1)}, u32[]{:S(2)}, u32[]{:S(2)}) collective-permute-start(bf16[256,2048]{1,0:T(8,128)(2,1)S(1)} %get-tuple-element.157), channel_id=1, source_target_pairs={{0,31},{1,0},{2,1},{3,2},{4,3},{5,4},{6,5},{7,6},{8,7},{9,8},{10,9... | collective-permute-start | bytes 3145736 | tf_op jit(solution)/shard_map/while/body/eval_jaxpr/ppermute | solution.py:11
  107.4 2.3 collective-permute-done
  109.7 0.1 copy.11
  109.8 1.2 fusion.21
  111.0 14.0 %collective-permute-start = (bf16[256,2048]{1,0:T(8,128)(2,1)S(1)}, bf16[256,2048]{1,0:T(8,128)(2,1)S(1)}, u32[]{:S(2)}, u32[]{:S(2)}) collective-permute-start(bf16[256,2048]{1,0:T(8,128)(2,1)S(1)} %get-tuple-element.157), channel_id=1, source_target_pairs={{0,31},{1,0},{2,1},{3,2},{4,3},{5,4},{6,5},{7,6},{8,7},{9,8},{10,9... | collective-permute-start | bytes 3145736 | tf_op jit(solution)/shard_map/while/body/eval_jaxpr/ppermute | solution.py:11
  125.0 2.3 collective-permute-done
  127.3 0.1 copy.11
  127.4 1.2 fusion.21
  128.6 14.0 %collective-permute-start = (bf16[256,2048]{1,0:T(8,128)(2,1)S(1)}, bf16[256,2048]{1,0:T(8,128)(2,1)S(1)}, u32[]{:S(2)}, u32[]{:S(2)}) collective-permute-start(bf16[256,2048]{1,0:T(8,128)(2,1)S(1)} %get-tuple-element.157), channel_id=1, source_target_pairs={{0,31},{1,0},{2,1},{3,2},{4,3},{5,4},{6,5},{7,6},{8,7},{9,8},{10,9... | collective-permute-start | bytes 3145736 | tf_op jit(solution)/shard_map/while/body/eval_jaxpr/ppermute | solution.py:11
  142.6 2.3 collective-permute-done
  145.0 1.2 fusion.21
  146.2 14.0 %collective-permute-start = (bf16[256,2048]{1,0:T(8,128)(2,1)S(1)}, bf16[256,2048]{1,0:T(8,128)(2,1)S(1)}, u32[]{:S(2)}, u32[]{:S(2)}) collective-permute-start(bf16[256,2048]{1,0:T(8,128)(2,1)S(1)} %get-tuple-element.157), channel_id=1, source_target_pairs={{0,31},{1,0},{2,1},{3,2},{4,3},{5,4},{6,5},{7,6},{8,7},{9,8},{10,9... | collective-permute-start | bytes 3145736 | tf_op jit(solution)/shard_map/while/body/eval_jaxpr/ppermute | solution.py:11
  160.3 2.3 collective-permute-done
  162.7 1.2 fusion.21
  163.9 14.0 %collective-permute-start = (bf16[256,2048]{1,0:T(8,128)(2,1)S(1)}, bf16[256,2048]{1,0:T(8,128)(2,1)S(1)}, u32[]{:S(2)}, u32[]{:S(2)}) collective-permute-start(bf16[256,2048]{1,0:T(8,128)(2,1)S(1)} %get-tuple-element.157), channel_id=1, source_target_pairs={{0,31},{1,0},{2,1},{3,2},{4,3},{5,4},{6,5},{7,6},{8,7},{9,8},{10,9... | collective-permute-start | bytes 3145736 | tf_op jit(solution)/shard_map/while/body/eval_jaxpr/ppermute | solution.py:11
  177.9 2.3 collective-permute-done
  180.3 1.2 fusion.21
  181.5 14.1 %collective-permute-start = (bf16[256,2048]{1,0:T(8,128)(2,1)S(1)}, bf16[256,2048]{1,0:T(8,128)(2,1)S(1)}, u32[]{:S(2)}, u32[]{:S(2)}) collective-permute-start(bf16[256,2048]{1,0:T(8,128)(2,1)S(1)} %get-tuple-element.157), channel_id=1, source_target_pairs={{0,31},{1,0},{2,1},{3,2},{4,3},{5,4},{6,5},{7,6},{8,7},{9,8},{10,9... | collective-permute-start | bytes 3145736 | tf_op jit(solution)/shard_map/while/body/eval_jaxpr/ppermute | solution.py:11
  195.5 2.3 collective-permute-done
  197.9 1.2 fusion.21
  199.1 14.0 %collective-permute-start = (bf16[256,2048]{1,0:T(8,128)(2,1)S(1)}, bf16[256,2048]{1,0:T(8,128)(2,1)S(1)}, u32[]{:S(2)}, u32[]{:S(2)}) collective-permute-start(bf16[256,2048]{1,0:T(8,128)(2,1)S(1)} %get-tuple-element.157), channel_id=1, source_target_pairs={{0,31},{1,0},{2,1},{3,2},{4,3},{5,4},{6,5},{7,6},{8,7},{9,8},{10,9... | collective-permute-start | bytes 3145736 | tf_op jit(solution)/shard_map/while/body/eval_jaxpr/ppermute | solution.py:11
  213.2 2.3 collective-permute-done
  215.6 1.2 fusion.21
  216.8 14.0 %collective-permute-start = (bf16[256,2048]{1,0:T(8,128)(2,1)S(1)}, bf16[256,2048]{1,0:T(8,128)(2,1)S(1)}, u32[]{:S(2)}, u32[]{:S(2)}) collective-permute-start(bf16[256,2048]{1,0:T(8,128)(2,1)S(1)} %get-tuple-element.157), channel_id=1, source_target_pairs={{0,31},{1,0},{2,1},{3,2},{4,3},{5,4},{6,5},{7,6},{8,7},{9,8},{10,9... | collective-permute-start | bytes 3145736 | tf_op jit(solution)/shard_map/while/body/eval_jaxpr/ppermute | solution.py:11
  230.8 2.3 collective-permute-done
  233.2 1.2 fusion.21
  234.4 14.0 %collective-permute-start = (bf16[256,2048]{1,0:T(8,128)(2,1)S(1)}, bf16[256,2048]{1,0:T(8,128)(2,1)S(1)}, u32[]{:S(2)}, u32[]{:S(2)}) collective-permute-start(bf16[256,2048]{1,0:T(8,128)(2,1)S(1)} %get-tuple-element.157), channel_id=1, source_target_pairs={{0,31},{1,0},{2,1},{3,2},{4,3},{5,4},{6,5},{7,6},{8,7},{9,8},{10,9... | collective-permute-start | bytes 3145736 | tf_op jit(solution)/shard_map/while/body/eval_jaxpr/ppermute | solution.py:11
  248.5 2.3 collective-permute-done
  250.9 1.2 fusion.21
  252.0 14.0 %collective-permute-start = (bf16[256,2048]{1,0:T(8,128)(2,1)S(1)}, bf16[256,2048]{1,0:T(8,128)(2,1)S(1)}, u32[]{:S(2)}, u32[]{:S(2)}) collective-permute-start(bf16[256,2048]{1,0:T(8,128)(2,1)S(1)} %get-tuple-element.157), channel_id=1, source_target_pairs={{0,31},{1,0},{2,1},{3,2},{4,3},{5,4},{6,5},{7,6},{8,7},{9,8},{10,9... | collective-permute-start | bytes 3145736 | tf_op jit(solution)/shard_map/while/body/eval_jaxpr/ppermute | solution.py:11
  266.1 2.3 collective-permute-done
  268.5 1.2 fusion.21
  269.7 14.0 %collective-permute-start = (bf16[256,2048]{1,0:T(8,128)(2,1)S(1)}, bf16[256,2048]{1,0:T(8,128)(2,1)S(1)}, u32[]{:S(2)}, u32[]{:S(2)}) collective-permute-start(bf16[256,2048]{1,0:T(8,128)(2,1)S(1)} %get-tuple-element.157), channel_id=1, source_target_pairs={{0,31},{1,0},{2,1},{3,2},{4,3},{5,4},{6,5},{7,6},{8,7},{9,8},{10,9... | collective-permute-start | bytes 3145736 | tf_op jit(solution)/shard_map/while/body/eval_jaxpr/ppermute | solution.py:11
  283.7 2.3 collective-permute-done
  286.1 1.2 fusion.21
  287.3 102.8 %reduce-scatter.2.cloned.1.call-done = f32[17,32,256]{2,1,0:T(8,128)} async-done(((f32[17,256,256]{2,1,0:T(8,128)}), f32[17,32,256]{2,1,0:T(8,128)}) %reduce-scatter.2.cloned.1.call-update) | async-done | bytes 557072 | tf_op jit(solution)/shard_map/reduce_scatter | solution.py:52
  390.1 1.9 multiply_bitcast_fusion
  (13 shorter events, 0.9 us)
Async XLA Ops:
  6.5 383.6 %reduce-scatter.2.cloned.1.call-start = ((), (), s32[]{:S(2)}) async-start(), calls=%async_computation.1 | async-start | bytes 5013504 | tf_op jit(solution)/shard_map/reduce_scatter | solution.py:52
  15.4 15.2 %collective-permute-start = (bf16[256,2048]{1,0:T(8,128)(2,1)S(1)}, bf16[256,2048]{1,0:T(8,128)(2,1)S(1)}, u32[]{:S(2)}, u32[]{:S(2)}) collective-permute-start(bf16[256,2048]{1,0:T(8,128)(2,1)S(1)} %get-tuple-element.157), channel_id=1, source_target_pairs={{0,31},{1,0},{2,1},{3,2},{4,3},{5,4},{6,5},{7,6},{8,7},{9,8},{10,9... | collective-permute-start | bytes 3145736 | tf_op jit(solution)/shard_map/while/body/eval_jaxpr/ppermute | solution.py:11
  31.9 14.2 %collective-permute-start = (bf16[256,2048]{1,0:T(8,128)(2,1)S(1)}, bf16[256,2048]{1,0:T(8,128)(2,1)S(1)}, u32[]{:S(2)}, u32[]{:S(2)}) collective-permute-start(bf16[256,2048]{1,0:T(8,128)(2,1)S(1)} %get-tuple-element.157), channel_id=1, source_target_pairs={{0,31},{1,0},{2,1},{3,2},{4,3},{5,4},{6,5},{7,6},{8,7},{9,8},{10,9... | collective-permute-start | bytes 3145736 | tf_op jit(solution)/shard_map/while/body/eval_jaxpr/ppermute | solution.py:11
  47.4 14.2 %collective-permute-start = (bf16[256,2048]{1,0:T(8,128)(2,1)S(1)}, bf16[256,2048]{1,0:T(8,128)(2,1)S(1)}, u32[]{:S(2)}, u32[]{:S(2)}) collective-permute-start(bf16[256,2048]{1,0:T(8,128)(2,1)S(1)} %get-tuple-element.157), channel_id=1, source_target_pairs={{0,31},{1,0},{2,1},{3,2},{4,3},{5,4},{6,5},{7,6},{8,7},{9,8},{10,9... | collective-permute-start | bytes 3145736 | tf_op jit(solution)/shard_map/while/body/eval_jaxpr/ppermute | solution.py:11
  62.9 14.2 %collective-permute-start = (bf16[256,2048]{1,0:T(8,128)(2,1)S(1)}, bf16[256,2048]{1,0:T(8,128)(2,1)S(1)}, u32[]{:S(2)}, u32[]{:S(2)}) collective-permute-start(bf16[256,2048]{1,0:T(8,128)(2,1)S(1)} %get-tuple-element.157), channel_id=1, source_target_pairs={{0,31},{1,0},{2,1},{3,2},{4,3},{5,4},{6,5},{7,6},{8,7},{9,8},{10,9... | collective-permute-start | bytes 3145736 | tf_op jit(solution)/shard_map/while/body/eval_jaxpr/ppermute | solution.py:11
  78.5 14.2 %collective-permute-start = (bf16[256,2048]{1,0:T(8,128)(2,1)S(1)}, bf16[256,2048]{1,0:T(8,128)(2,1)S(1)}, u32[]{:S(2)}, u32[]{:S(2)}) collective-permute-start(bf16[256,2048]{1,0:T(8,128)(2,1)S(1)} %get-tuple-element.157), channel_id=1, source_target_pairs={{0,31},{1,0},{2,1},{3,2},{4,3},{5,4},{6,5},{7,6},{8,7},{9,8},{10,9... | collective-permute-start | bytes 3145736 | tf_op jit(solution)/shard_map/while/body/eval_jaxpr/ppermute | solution.py:11
  94.0 15.7 %collective-permute-start = (bf16[256,2048]{1,0:T(8,128)(2,1)S(1)}, bf16[256,2048]{1,0:T(8,128)(2,1)S(1)}, u32[]{:S(2)}, u32[]{:S(2)}) collective-permute-start(bf16[256,2048]{1,0:T(8,128)(2,1)S(1)} %get-tuple-element.157), channel_id=1, source_target_pairs={{0,31},{1,0},{2,1},{3,2},{4,3},{5,4},{6,5},{7,6},{8,7},{9,8},{10,9... | collective-permute-start | bytes 3145736 | tf_op jit(solution)/shard_map/while/body/eval_jaxpr/ppermute | solution.py:11
  111.0 16.3 %collective-permute-start = (bf16[256,2048]{1,0:T(8,128)(2,1)S(1)}, bf16[256,2048]{1,0:T(8,128)(2,1)S(1)}, u32[]{:S(2)}, u32[]{:S(2)}) collective-permute-start(bf16[256,2048]{1,0:T(8,128)(2,1)S(1)} %get-tuple-element.157), channel_id=1, source_target_pairs={{0,31},{1,0},{2,1},{3,2},{4,3},{5,4},{6,5},{7,6},{8,7},{9,8},{10,9... | collective-permute-start | bytes 3145736 | tf_op jit(solution)/shard_map/while/body/eval_jaxpr/ppermute | solution.py:11
  128.6 16.3 %collective-permute-start = (bf16[256,2048]{1,0:T(8,128)(2,1)S(1)}, bf16[256,2048]{1,0:T(8,128)(2,1)S(1)}, u32[]{:S(2)}, u32[]{:S(2)}) collective-permute-start(bf16[256,2048]{1,0:T(8,128)(2,1)S(1)} %get-tuple-element.157), channel_id=1, source_target_pairs={{0,31},{1,0},{2,1},{3,2},{4,3},{5,4},{6,5},{7,6},{8,7},{9,8},{10,9... | collective-permute-start | bytes 3145736 | tf_op jit(solution)/shard_map/while/body/eval_jaxpr/ppermute | solution.py:11
  146.2 16.3 %collective-permute-start = (bf16[256,2048]{1,0:T(8,128)(2,1)S(1)}, bf16[256,2048]{1,0:T(8,128)(2,1)S(1)}, u32[]{:S(2)}, u32[]{:S(2)}) collective-permute-start(bf16[256,2048]{1,0:T(8,128)(2,1)S(1)} %get-tuple-element.157), channel_id=1, source_target_pairs={{0,31},{1,0},{2,1},{3,2},{4,3},{5,4},{6,5},{7,6},{8,7},{9,8},{10,9... | collective-permute-start | bytes 3145736 | tf_op jit(solution)/shard_map/while/body/eval_jaxpr/ppermute | solution.py:11
  163.9 16.3 %collective-permute-start = (bf16[256,2048]{1,0:T(8,128)(2,1)S(1)}, bf16[256,2048]{1,0:T(8,128)(2,1)S(1)}, u32[]{:S(2)}, u32[]{:S(2)}) collective-permute-start(bf16[256,2048]{1,0:T(8,128)(2,1)S(1)} %get-tuple-element.157), channel_id=1, source_target_pairs={{0,31},{1,0},{2,1},{3,2},{4,3},{5,4},{6,5},{7,6},{8,7},{9,8},{10,9... | collective-permute-start | bytes 3145736 | tf_op jit(solution)/shard_map/while/body/eval_jaxpr/ppermute | solution.py:11
  181.5 16.3 %collective-permute-start = (bf16[256,2048]{1,0:T(8,128)(2,1)S(1)}, bf16[256,2048]{1,0:T(8,128)(2,1)S(1)}, u32[]{:S(2)}, u32[]{:S(2)}) collective-permute-start(bf16[256,2048]{1,0:T(8,128)(2,1)S(1)} %get-tuple-element.157), channel_id=1, source_target_pairs={{0,31},{1,0},{2,1},{3,2},{4,3},{5,4},{6,5},{7,6},{8,7},{9,8},{10,9... | collective-permute-start | bytes 3145736 | tf_op jit(solution)/shard_map/while/body/eval_jaxpr/ppermute | solution.py:11
  199.1 16.3 %collective-permute-start = (bf16[256,2048]{1,0:T(8,128)(2,1)S(1)}, bf16[256,2048]{1,0:T(8,128)(2,1)S(1)}, u32[]{:S(2)}, u32[]{:S(2)}) collective-permute-start(bf16[256,2048]{1,0:T(8,128)(2,1)S(1)} %get-tuple-element.157), channel_id=1, source_target_pairs={{0,31},{1,0},{2,1},{3,2},{4,3},{5,4},{6,5},{7,6},{8,7},{9,8},{10,9... | collective-permute-start | bytes 3145736 | tf_op jit(solution)/shard_map/while/body/eval_jaxpr/ppermute | solution.py:11
  216.8 16.3 %collective-permute-start = (bf16[256,2048]{1,0:T(8,128)(2,1)S(1)}, bf16[256,2048]{1,0:T(8,128)(2,1)S(1)}, u32[]{:S(2)}, u32[]{:S(2)}) collective-permute-start(bf16[256,2048]{1,0:T(8,128)(2,1)S(1)} %get-tuple-element.157), channel_id=1, source_target_pairs={{0,31},{1,0},{2,1},{3,2},{4,3},{5,4},{6,5},{7,6},{8,7},{9,8},{10,9... | collective-permute-start | bytes 3145736 | tf_op jit(solution)/shard_map/while/body/eval_jaxpr/ppermute | solution.py:11
  234.4 16.3 %collective-permute-start = (bf16[256,2048]{1,0:T(8,128)(2,1)S(1)}, bf16[256,2048]{1,0:T(8,128)(2,1)S(1)}, u32[]{:S(2)}, u32[]{:S(2)}) collective-permute-start(bf16[256,2048]{1,0:T(8,128)(2,1)S(1)} %get-tuple-element.157), channel_id=1, source_target_pairs={{0,31},{1,0},{2,1},{3,2},{4,3},{5,4},{6,5},{7,6},{8,7},{9,8},{10,9... | collective-permute-start | bytes 3145736 | tf_op jit(solution)/shard_map/while/body/eval_jaxpr/ppermute | solution.py:11
  252.0 16.3 %collective-permute-start = (bf16[256,2048]{1,0:T(8,128)(2,1)S(1)}, bf16[256,2048]{1,0:T(8,128)(2,1)S(1)}, u32[]{:S(2)}, u32[]{:S(2)}) collective-permute-start(bf16[256,2048]{1,0:T(8,128)(2,1)S(1)} %get-tuple-element.157), channel_id=1, source_target_pairs={{0,31},{1,0},{2,1},{3,2},{4,3},{5,4},{6,5},{7,6},{8,7},{9,8},{10,9... | collective-permute-start | bytes 3145736 | tf_op jit(solution)/shard_map/while/body/eval_jaxpr/ppermute | solution.py:11
  269.7 16.3 %collective-permute-start = (bf16[256,2048]{1,0:T(8,128)(2,1)S(1)}, bf16[256,2048]{1,0:T(8,128)(2,1)S(1)}, u32[]{:S(2)}, u32[]{:S(2)}) collective-permute-start(bf16[256,2048]{1,0:T(8,128)(2,1)S(1)} %get-tuple-element.157), channel_id=1, source_target_pairs={{0,31},{1,0},{2,1},{3,2},{4,3},{5,4},{6,5},{7,6},{8,7},{9,8},{10,9... | collective-permute-start | bytes 3145736 | tf_op jit(solution)/shard_map/while/body/eval_jaxpr/ppermute | solution.py:11
Sparse Core Ops, SparseCore 0:
  287.4 102.6 reduce-scatter.1
where the time goes:
time: 399 us
  starting transfers between devices  190 us (48%)
  waiting for transfers between devices  164 us (41%)
  matrix products  22.2 us (6%)
  between operations  13.4 us (3%)
  other arithmetic  5.07 us (1%)
  local copies, waits for them, and re-layouts  4.17 us (1%)
    ppermute x16, starting transfers between devices, from_behind(): return lax.ppermute(x, axis, [(i, (i + by) % peers) for i in range(peers)])  190 us
    reduce_scatter x1, waiting for transfers between devices, on_device(): lax.psum_scatter(partial_value, 'env', scatter_dimension=1, tiled=True)  103 us
    ppermute x16, waiting for transfers between devices, from_behind(): return lax.ppermute(x, axis, [(i, (i + by) % peers) for i in range(peers)])  61.5 us
    dot_general x17, matrix products, gram_tile(): lax.dot_general(own_kernel, moving, (((1,), (1,)), ((), ())), preferred_e...  19.5 us
  transfers between devices with their start and end apart: 17, of which 17 were waited for; matrix products, arithmetic and copies ran while one was open for 0% of the time, Pallas kernels for 0%

commit v1 on v0

v1 whole, which is shorter than its diff:
```python
import functools

import jax
import jax.numpy as jnp
from jax import lax
from jax.experimental import pallas as pl
from jax.experimental.pallas import tpu as pltpu
from jax.sharding import PartitionSpec as P


F32, BF16 = jnp.float32, jnp.bfloat16
NT = (((1,), (1,)), ((), ()))
NN = (((1,), (0,)), ((), ()))
VMEM_LIMIT = 48 * 1024 * 1024


def split_index(i):
    env, sp = divmod(i, 32)
    y_hi, x = divmod(env, 4)
    q, core = divmod(sp, 2)
    z, y_lo = divmod(q, 2)
    return y_hi, x, z, y_lo, core


def join_index(y_hi, x, z, y_lo, core):
    return ((y_hi % 2) * 4 + x % 4) * 32 + ((z % 8) * 2 + y_lo % 2) * 2 + core % 2


def fetch(value, source_of):
    pairs = []
    for i in range(256):
        pairs.append((join_index(*source_of(*split_index(i))), i))
    return lax.ppermute(value, ("env", "sp"), pairs)


def other_core(y_hi, x, z, y_lo, core):
    return y_hi, x, z, y_lo, 1 - core


def next_x(y_hi, x, z, y_lo, core):
    return y_hi, x + 1, z, y_lo, core


def previous_x(y_hi, x, z, y_lo, core):
    return y_hi, x - 1, z, y_lo, core


def next_z(y_hi, x, z, y_lo, core):
    return y_hi, x, z + 1, y_lo, core


def first_column(y_hi, x, z, y_lo, core):
    if x % 2 == 0:
        return y_hi, x, z + 1, y_lo, core
    y = (y_hi * 2 + y_lo + (1 if core == 0 else -1)) % 4
    return y // 2, x, z + y_lo, y % 2, core


def env_peer(flip, step):
    def source(y_hi, x, z, y_lo, core):
        return (y_hi + flip) % 2, x - step, z, y_lo, core

    return source


def unit(values):
    values = values.astype(F32)
    total = jnp.sum(values * values, axis=1, keepdims=True)
    return (values * lax.rsqrt(total + 1e-06)).astype(BF16)


def fourth(products):
    squares = products * products
    return (squares * squares).astype(BF16)


def own_kernel(chunk, own_env, near_a, near_b, far, own_points, sib_points, weight,
               env_hat, rows_k, own_out, sib_out):
    points = jnp.concatenate([unit(own_points[...]), unit(sib_points[...])], axis=0)
    gram = jnp.zeros((512, 256), F32)
    place = 0
    for ref in (own_env, near_a, near_b, far):
        for start in range(0, ref.shape[0], chunk):
            env = unit(ref[start:start + chunk, :])
            env_hat[place:place + chunk, :] = env
            k = fourth(lax.dot_general(points, env, NT, preferred_element_type=F32))
            rows_k[:, place:place + chunk] = k
            gram += lax.dot_general(k, k[:256], NT, preferred_element_type=F32)
            place += chunk
    gram = (gram * weight[...]).astype(BF16)
    own_out[...] = gram[:256]
    sib_out[...] = gram[256:]


def column_kernel(chunk, points, env_hat, rows_k, weight, own_out, sib_out):
    turned = unit(points[...]).T
    gram = jnp.zeros((512, 256), F32)
    for start in range(0, env_hat.shape[0], chunk):
        k = fourth(lax.dot_general(env_hat[start:start + chunk, :], turned, NN, preferred_element_type=F32))
        gram += lax.dot_general(rows_k[:, start:start + chunk], k, NN, preferred_element_type=F32)
    gram = (gram * weight[...]).astype(BF16)
    own_out[...] = gram[:256]
    sib_out[...] = gram[256:]


def pack_kernel(count, places, *refs):
    sources, outs = refs[:count], refs[count:]
    for r, out in enumerate(outs):
        start = pl.multiple_of(places[r] * 32, 32)
        for t, source in enumerate(sources):
            out[t] = source[pl.ds(start, 32), :]


def finish_kernel(flags, weights, *refs):
    pieces, out = refs[:8], refs[8]
    parity, core = flags[0], flags[1]
    same = jnp.zeros((9, 32, 256), F32)
    other = jnp.zeros((9, 32, 256), F32)
    for r in range(8):
        term = pieces[r][...].astype(F32) * weights[r][None, None, :]
        if r % 2 == 0:
            same += term
        else:
            other += term
    out[0] = jnp.where(parity == 0, same[0], other[0])
    same_odd = jnp.where(parity == core, 3, 1)
    for m in range(1, 5):
        out[4 * m - 2 * parity] = same[m]
        out[4 * m - 2 + 2 * parity] = other[m]
        out[4 * m - same_odd] = same[4 + m]
        out[4 * m - 4 + same_odd] = other[4 + m]


def spread(index):
    lanes = jnp.arange(256, dtype=jnp.int32)
    return 1.0 + ((lanes[None, :] + 64 * index[:, None]) % 256).astype(F32) / 256.0


def vmem_spec():
    return pl.BlockSpec(memory_space=pltpu.VMEM)


def smem_spec():
    return pl.BlockSpec(memory_space=pltpu.SMEM)


def shape(*dims, dtype=BF16):
    return jax.ShapeDtypeStruct(dims, dtype)


def call(body, out_shape, n_in, flops, bytes_accessed, smem=()):
    many = isinstance(out_shape, (tuple, list))
    return pl.pallas_call(
        body,
        out_shape=out_shape,
        in_specs=[smem_spec() if i in smem else vmem_spec() for i in range(n_in)],
        out_specs=[vmem_spec() for _ in out_shape] if many else vmem_spec(),
        compiler_params=pltpu.CompilerParams(vmem_limit_bytes=VMEM_LIMIT),
        cost_estimate=pl.CostEstimate(flops=flops, bytes_accessed=bytes_accessed, transcendentals=0),
    )


def on_device(descriptors, sparse_points):
    env, sp = lax.axis_index("env"), lax.axis_index("sp")
    y_hi, x, core = env // 4, env % 4, sp % 2
    parity = x % 2

    columns = [fetch(sparse_points, first_column)]
    for _ in range(3):
        columns.append(fetch(columns[-1], next_z))
    sib_points = fetch(sparse_points, other_core)
    low = lax.dynamic_slice_in_dim(descriptors, core * 512, 512, 0)
    high = lax.dynamic_slice_in_dim(descriptors, 1024 + core * 512, 512, 0)
    near_a, near_b = fetch(low, next_x), fetch(high, previous_x)
    far = fetch(jnp.concatenate([near_a, near_b], axis=0), other_core)

    group = (y_hi * 2 + x // 2)[None]
    weight = spread(group) * (16.0 / 16384.0)
    gram_pair = (shape(256, 256), shape(256, 256))
    env_hat, rows_k, own0, sib0 = call(
        functools.partial(own_kernel, 256),
        (shape(4096, 512), shape(512, 4096)) + gram_pair, 7, 2 * 1342177280, 1 << 24,
    )(descriptors, near_a, near_b, far, sparse_points, sib_points, weight)
    own, sib = [own0], [sib0]
    for points in columns:
        a, b = call(
            functools.partial(column_kernel, 512), gram_pair, 4, 2 * 1073741824, 1 << 23,
        )(points, env_hat, rows_k, weight)
        own.append(a)
        sib.append(b)

    late = jnp.logical_and(parity == 0, core == 1)
    for i in range(1, 5):
        own.append(fetch(jnp.where(late, sib[i - 1], sib[i]), other_core))

    turns = [(r // 4, r % 4) for r in range(8)]
    places = jnp.stack([((y_hi + flip) % 2) * 4 + (x + step) % 4 for flip, step in turns])
    packed = call(
        functools.partial(pack_kernel, 9), tuple(shape(9, 32, 256) for _ in range(8)), 10, 0, 1 << 21, (0,)
    )(places, *own)
    pieces = [packed[0]]
    for r in range(1, 8):
        pieces.append(fetch(packed[r], env_peer(*turns[r])))

    groups = jnp.stack([((y_hi + flip) % 2) * 2 + ((x - step) % 4) // 2 for flip, step in turns])
    flags = jnp.stack([parity, core])
    out = call(finish_kernel, shape(17, 32, 256, dtype=F32), 10, 0, 1 << 21, (0,))(
        flags, 1.0 / spread(groups), *pieces
    )
    return out[None]


def solution(mesh):
    placed = (P("env", None), P("sp", None))
    return jax.shard_map(
        on_device, mesh=mesh, in_specs=placed, out_specs=P("sp", None, "env", None), check_vma=False
    )
```

time: 399 us -> 112 us (0.28)
  starting transfers between devices: 190 us -> 35 us
  waiting for transfers between devices: 164 us -> 38.3 us
  Pallas kernels: 0 us -> 31.8 us
  matrix products: 22.2 us -> 0 us
  between operations: 13.4 us -> 0.1 us
    ppermute x16 -> x19, starting transfers between devices: 190 us -> 35 us  [fetch(): return lax.ppermute(value, ('env', 'sp'), pairs)]
    reduce_scatter x1 -> x0, waiting for transfers between devices: 103 us -> none  [on_device(): lax.psum_scatter(partial_value, 'env', scatter_dimension=1, tiled=True)]
    pallas_call x0 -> x7, Pallas kernels: none -> 31.8 us  [the longest x4 21.5 us: on_device(): call(functools.partial(column_kernel, 512), gram_pair, 4, 2 * 1073741824,...]
    ppermute x16 -> x19, waiting for transfers between devices: 61.5 us -> 38.3 us  [fetch(): return lax.ppermute(value, ('env', 'sp'), pairs)]
    dot_general x18 -> x0, matrix products: 22.2 us -> none  [the longest x17 19.5 us: gram_tile(): lax.dot_general(own_kernel, moving, (((1,), (1,)), ((), ())), preferred_e...]
  transfers between devices with their start and end apart: 17 -> 19, of which waited for: 17 -> 13; matrix products, arithmetic and copies ran while one was open for 0% -> 0% of each run, Pallas kernels for 0% -> 22%
where the time goes in v1:
time: 112 us; the launch traced here: 110 us
  waiting for transfers between devices  38.3 us (34%)
  starting transfers between devices  35 us (31%)
  Pallas kernels  31.8 us (28%)
  local copies, waits for them, and re-layouts  3.78 us (3%)
  other arithmetic  1.3 us (1%)
    ppermute x19, waiting for transfers between devices, fetch(): return lax.ppermute(value, ('env', 'sp'), pairs)  38.3 us
    ppermute x19, starting transfers between devices, fetch(): return lax.ppermute(value, ('env', 'sp'), pairs)  35 us
    pallas_call x4, Pallas kernels, on_device(): call(functools.partial(column_kernel, 512), gram_pair, 4, 2 * 1073741824,...  21.5 us
    pallas_call x1, Pallas kernels, on_device(): call(functools.partial(own_kernel, 256), (shape(4096, 512), shape(512, 40...  8.07 us
  transfers between devices with their start and end apart: 19, of which 13 were waited for; matrix products, arithmetic and copies ran while one was open for 0% of the time, Pallas kernels for 22%

profile of v1, /device:TPU:1, one launch (start us, length us, event | category | flops | bytes accessed | tf_op | source)
XLA Modules:
  0.0 110.3 jit_solution(13577830696134273662)
XLA Ops:
  0.0 0.0 copy-start.1
  0.0 1.4 %constant_dynamic-slice_fusion = (bf16[512,512]{1,0:T(8,128)(2,1)S(1)}, bf16[512,512]{1,0:T(8,128)(2,1)S(1)}) fusion(bf16[2048,512]{1,0:T(8,128)(2,1)} %own_env.1, s32[]{:T(128)S(6)} %select_n.185, s32[]{:T(128)S(6)} %select_n.184), kind=kLoop, calls=%fused_computation.25 | loop fusion | bytes 2097160 | tf_op jit(solution)/shard_map/dynamic_slice | solution.py:173
  1.4 3.4 %collective-permute-start = (bf16[512,512]{1,0:T(8,128)(2,1)S(1)}, bf16[512,512]{1,0:T(8,128)(2,1)S(1)}, u32[]{:S(2)}, u32[]{:S(2)}) collective-permute-start(bf16[512,512]{1,0:T(8,128)(2,1)S(1)} %get-tuple-element.46), channel_id=1, source_target_pairs={{32,0},{33,1},{34,2},{35,3},{36,4},{37,5},{38,6},{39,7},{40,8},{41... | collective-permute-start | bytes 1572872 | tf_op jit(solution)/shard_map/ppermute | solution.py:33
  4.8 0.0 collective-permute-start.1
  4.8 10.6 %collective-permute-done.near_a = bf16[512,512]{1,0:T(8,128)(2,1)S(1)} collective-permute-done((bf16[512,512]{1,0:T(8,128)(2,1)S(1)}, bf16[512,512]{1,0:T(8,128)(2,1)S(1)}, u32[]{:S(2)}, u32[]{:S(2)}) %collective-permute-start) | collective-permute-done | bytes 524320 | tf_op jit(solution)/shard_map/ppermute | solution.py:33
  15.4 3.1 %collective-permute-done.1.near_b = bf16[512,512]{1,0:T(8,128)(2,1)S(1)} collective-permute-done((bf16[512,512]{1,0:T(8,128)(2,1)S(1)}, bf16[512,512]{1,0:T(8,128)(2,1)S(1)}, u32[]{:S(2)}, u32[]{:S(2)}) %collective-permute-start.1) | collective-permute-done | bytes 524320 | tf_op jit(solution)/shard_map/ppermute | solution.py:33
  18.5 1.1 pad_maximum_fusion
  19.6 1.9 %collective-permute-start.2 = (bf16[1024,512]{1,0:T(8,128)(2,1)}, bf16[1024,512]{1,0:T(8,128)(2,1)}, u32[]{:S(2)}, u32[]{:S(2)}) collective-permute-start(bf16[1024,512]{1,0:T(8,128)(2,1)} %pad_maximum_fusion), channel_id=1, source_target_pairs={{1,0},{0,1},{3,2},{2,3},{5,4},{4,5},{7,6},{6,7},{9,8},{8,9},{11,10... | collective-permute-start | bytes 3145736 | tf_op jit(solution)/shard_map/ppermute | solution.py:33
  21.4 5.6 %collective-permute-start.4 = (bf16[256,512]{1,0:T(8,128)(2,1)}, bf16[256,512]{1,0:T(8,128)(2,1)S(1)}, u32[]{:S(2)}, u32[]{:S(2)}) collective-permute-start(bf16[256,512]{1,0:T(8,128)(2,1)} %own_points.1), channel_id=1, source_target_pairs={{4,0},{5,1},{6,2},{7,3},{8,4},{9,5},{10,6},{11,7},{12,8},{13,9},{1... | collective-permute-start | bytes 786440 | tf_op jit(solution)/shard_map/ppermute | solution.py:33
  27.0 6.1 %collective-permute-done.4.points = bf16[256,512]{1,0:T(8,128)(2,1)S(1)} collective-permute-done((bf16[256,512]{1,0:T(8,128)(2,1)}, bf16[256,512]{1,0:T(8,128)(2,1)S(1)}, u32[]{:S(2)}, u32[]{:S(2)}) %collective-permute-start.4) | collective-permute-done | bytes 262176 | tf_op jit(solution)/shard_map/ppermute | solution.py:33
  33.1 3.3 %collective-permute-start.5 = (bf16[256,512]{1,0:T(8,128)(2,1)S(1)}, bf16[256,512]{1,0:T(8,128)(2,1)}, u32[]{:S(2)}, u32[]{:S(2)}) collective-permute-start(bf16[256,512]{1,0:T(8,128)(2,1)S(1)} %collective-permute-done.4.points), channel_id=1, source_target_pairs={{4,0},{5,1},{6,2},{7,3},{8,4},{9,5},{10,6},{11,7},{12,8},{13,9},{1... | collective-permute-start | bytes 786440 | tf_op jit(solution)/shard_map/ppermute | solution.py:33
  36.4 4.8 %collective-permute-done.5.points = bf16[256,512]{1,0:T(8,128)(2,1)} collective-permute-done((bf16[256,512]{1,0:T(8,128)(2,1)S(1)}, bf16[256,512]{1,0:T(8,128)(2,1)}, u32[]{:S(2)}, u32[]{:S(2)}) %collective-permute-start.5) | collective-permute-done | bytes 262176 | tf_op jit(solution)/shard_map/ppermute | solution.py:33
  41.2 3.5 %collective-permute-start.6 = (bf16[256,512]{1,0:T(8,128)(2,1)}, bf16[256,512]{1,0:T(8,128)(2,1)}, u32[]{:S(2)}, u32[]{:S(2)}) collective-permute-start(bf16[256,512]{1,0:T(8,128)(2,1)} %collective-permute-done.5.points), channel_id=1, source_target_pairs={{4,0},{5,1},{6,2},{7,3},{8,4},{9,5},{10,6},{11,7},{12,8},{13,9},{1... | collective-permute-start | bytes 786440 | tf_op jit(solution)/shard_map/ppermute | solution.py:33
  44.7 2.0 %collective-permute-start.3 = (bf16[256,512]{1,0:T(8,128)(2,1)}, bf16[256,512]{1,0:T(8,128)(2,1)}, u32[]{:S(2)}, u32[]{:S(2)}) collective-permute-start(bf16[256,512]{1,0:T(8,128)(2,1)} %own_points.1), channel_id=1, source_target_pairs={{1,0},{0,1},{3,2},{2,3},{5,4},{4,5},{7,6},{6,7},{9,8},{8,9},{11,10... | collective-permute-start | bytes 786440 | tf_op jit(solution)/shard_map/ppermute | solution.py:33
  46.7 2.3 %collective-permute-done.6.points = bf16[256,512]{1,0:T(8,128)(2,1)} collective-permute-done((bf16[256,512]{1,0:T(8,128)(2,1)}, bf16[256,512]{1,0:T(8,128)(2,1)}, u32[]{:S(2)}, u32[]{:S(2)}) %collective-permute-start.6) | collective-permute-done | bytes 262176 | tf_op jit(solution)/shard_map/ppermute | solution.py:33
  49.0 3.4 %collective-permute-start.7 = (bf16[256,512]{1,0:T(8,128)(2,1)}, bf16[256,512]{1,0:T(8,128)(2,1)S(1)}, u32[]{:S(2)}, u32[]{:S(2)}) collective-permute-start(bf16[256,512]{1,0:T(8,128)(2,1)} %collective-permute-done.6.points), channel_id=1, source_target_pairs={{4,0},{5,1},{6,2},{7,3},{8,4},{9,5},{10,6},{11,7},{12,8},{13,9},{1... | collective-permute-start | bytes 786440 | tf_op jit(solution)/shard_map/ppermute | solution.py:33
  52.4 0.0 collective-permute-done.3.sib_points
  52.4 0.0 collective-permute-done.2.far
  52.4 0.0 copy-done.1
  52.4 8.1 %shard_map.28 = (bf16[4096,512]{1,0:T(8,128)(2,1)}, bf16[512,4096]{1,0:T(8,128)(2,1)}, bf16[256,256]{1,0:T(8,128)(2,1)S(1)}, bf16[256,256]{1,0:T(8,128)(2,1)S(1)}) custom-call(bf16[2048,512]{1,0:T(8,128)(2,1)S(1)} %copy-done.1, bf16[512,512]{1,0:T(8,128)(2,1)S(1)} %collective-permute-done.near_a, bf16[512,512]{1,0:T(8,128)(2,1)S(1)} %collective-permute-done.1.near_b, ...), custom_call_target="tpu_custom_call" | custom-call | flops 2684354560 | bytes 16777216 | tf_op jit(solution)/shard_map/pallas_call | solution.py:180
  60.5 0.0 copy-start
  60.5 2.2 %copy-done = bf16[4096,512]{1,0:T(8,128)(2,1)S(1)} copy-done((bf16[4096,512]{1,0:T(8,128)(2,1)S(1)}, bf16[4096,512]{1,0:T(8,128)(2,1)}, u32[]{:S(2)}) %copy-start) | copy-done | bytes 4194328
  62.7 5.4 %shard_map.31 = (bf16[256,256]{1,0:T(8,128)(2,1)S(1)}, bf16[256,256]{1,0:T(8,128)(2,1)S(1)}) custom-call(bf16[256,512]{1,0:T(8,128)(2,1)} %collective-permute-done.6.points, bf16[4096,512]{1,0:T(8,128)(2,1)S(1)} %copy-done, bf16[512,4096]{1,0:T(8,128)(2,1)} %get-tuple-element.27.rows_k, f32[1,256]{1,0:T(1,128)S(1)} %fusion.11.weight), custom_call_target="tpu_custom_call" | custom-call | flops 2147483648 | bytes 8388608 | tf_op jit(solution)/shard_map/pallas_call | solution.py:186
  68.0 5.4 %shard_map.30 = (bf16[256,256]{1,0:T(8,128)(2,1)S(1)}, bf16[256,256]{1,0:T(8,128)(2,1)S(1)}) custom-call(bf16[256,512]{1,0:T(8,128)(2,1)} %collective-permute-done.5.points, bf16[4096,512]{1,0:T(8,128)(2,1)S(1)} %copy-done, bf16[512,4096]{1,0:T(8,128)(2,1)} %get-tuple-element.27.rows_k, f32[1,256]{1,0:T(1,128)S(1)} %fusion.11.weight), custom_call_target="tpu_custom_call" | custom-call | flops 2147483648 | bytes 8388608 | tf_op jit(solution)/shard_map/pallas_call | solution.py:186
  73.4 5.3 %shard_map.29 = (bf16[256,256]{1,0:T(8,128)(2,1)S(1)}, bf16[256,256]{1,0:T(8,128)(2,1)S(1)}) custom-call(bf16[256,512]{1,0:T(8,128)(2,1)S(1)} %collective-permute-done.4.points, bf16[4096,512]{1,0:T(8,128)(2,1)S(1)} %copy-done, bf16[512,4096]{1,0:T(8,128)(2,1)} %get-tuple-element.27.rows_k, f32[1,256]{1,0:T(1,128)S(1)} %fusion.11.weight), custom_call_target="tpu_custom_call" | custom-call | flops 2147483648 | bytes 8388608 | tf_op jit(solution)/shard_map/pallas_call | solution.py:186
  78.7 0.0 collective-permute-done.7.points
  78.7 5.5 %shard_map.32 = (bf16[256,256]{1,0:T(8,128)(2,1)S(1)}, bf16[256,256]{1,0:T(8,128)(2,1)S(1)}) custom-call(bf16[256,512]{1,0:T(8,128)(2,1)S(1)} %collective-permute-done.7.points, bf16[4096,512]{1,0:T(8,128)(2,1)S(1)} %copy-done, bf16[512,4096]{1,0:T(8,128)(2,1)} %get-tuple-element.27.rows_k, f32[1,256]{1,0:T(1,128)S(1)} %fusion.11.weight), custom_call_target="tpu_custom_call" | custom-call | flops 2147483648 | bytes 8388608 | tf_op jit(solution)/shard_map/pallas_call | solution.py:186
  84.3 3.0 %collective-permute-start.10 = (bf16[256,256]{1,0:T(8,128)(2,1)S(1)}, bf16[256,256]{1,0:T(8,128)(2,1)S(1)}, u32[]{:S(2)}, u32[]{:S(2)}) collective-permute-start(bf16[256,256]{1,0:T(8,128)(2,1)S(1)} %get-tuple-element.48), channel_id=1, source_target_pairs={{1,0},{0,1},{3,2},{2,3},{5,4},{4,5},{7,6},{6,7},{9,8},{8,9},{11,10... | collective-permute-start | bytes 393224 | tf_op jit(solution)/shard_map/ppermute | solution.py:33
  87.2 0.1 collective-permute-start.11
  87.3 0.4 collective-permute-start.8
  87.7 0.1 collective-permute-start.9
  87.8 0.1 stack.83.places
  87.9 0.1 stack.74
  88.0 0.2 collective-permute-done.10.refs_7_
  88.2 0.4 collective-permute-done.11.refs_8_
  88.6 0.2 collective-permute-done.8.refs_5_
  88.8 0.3 collective-permute-done.9.refs_6_
  89.1 0.6 shard_map.33
  89.7 0.1 collective-permute-start.12
  89.8 0.1 collective-permute-start.13
  89.9 2.6 %collective-permute-start.14 = (bf16[9,32,256]{2,1,0:T(8,128)(2,1)S(1)}, bf16[9,32,256]{2,1,0:T(8,128)(2,1)S(1)}, u32[]{:S(2)}, u32[]{:S(2)}) collective-permute-start(bf16[9,32,256]{2,1,0:T(8,128)(2,1)S(1)} %get-tuple-element.40), channel_id=1, source_target_pairs={{32,0},{33,1},{34,2},{35,3},{36,4},{37,5},{38,6},{39,7},{40,8},{41... | collective-permute-start | bytes 442376 | tf_op jit(solution)/shard_map/ppermute | solution.py:33
  92.5 2.9 %collective-permute-start.15 = (bf16[9,32,256]{2,1,0:T(8,128)(2,1)S(1)}, bf16[9,32,256]{2,1,0:T(8,128)(2,1)S(1)}, u32[]{:S(2)}, u32[]{:S(2)}) collective-permute-start(bf16[9,32,256]{2,1,0:T(8,128)(2,1)S(1)} %get-tuple-element.41), channel_id=1, source_target_pairs={{128,0},{129,1},{130,2},{131,3},{132,4},{133,5},{134,6},{135,7},{1... | collective-permute-start | bytes 442376 | tf_op jit(solution)/shard_map/ppermute | solution.py:33
  95.4 0.4 collective-permute-start.16
  95.8 3.8 %collective-permute-done.12.refs_1_ = bf16[9,32,256]{2,1,0:T(8,128)(2,1)S(1)} collective-permute-done((bf16[9,32,256]{2,1,0:T(8,128)(2,1)S(1)}, bf16[9,32,256]{2,1,0:T(8,128)(2,1)S(1)}, u32[]{:S(2)}, u32[]{:S(2)}) %collective-permute-start.12) | collective-permute-done | bytes 147488 | tf_op jit(solution)/shard_map/ppermute | solution.py:33
  99.6 0.1 collective-permute-start.17
  99.7 0.0 collective-permute-done.13.refs_2_
  99.7 2.3 %collective-permute-start.18 = (bf16[9,32,256]{2,1,0:T(8,128)(2,1)S(1)}, bf16[9,32,256]{2,1,0:T(8,128)(2,1)S(1)}, u32[]{:S(2)}, u32[]{:S(2)}) collective-permute-start(bf16[9,32,256]{2,1,0:T(8,128)(2,1)S(1)} %get-tuple-element.44), channel_id=1, source_target_pairs={{160,0},{161,1},{162,2},{163,3},{164,4},{165,5},{166,6},{167,7},{1... | collective-permute-start | bytes 442376 | tf_op jit(solution)/shard_map/ppermute | solution.py:33
  102.0 0.1 fusion.4.weights
  102.1 0.1 pad_add_fusion.flags
  102.2 0.0 collective-permute-done.14.refs_3_
  102.2 0.0 collective-permute-done.15.refs_4_
  102.2 3.0 %collective-permute-done.16.refs_5_ = bf16[9,32,256]{2,1,0:T(8,128)(2,1)S(1)} collective-permute-done((bf16[9,32,256]{2,1,0:T(8,128)(2,1)S(1)}, bf16[9,32,256]{2,1,0:T(8,128)(2,1)S(1)}, u32[]{:S(2)}, u32[]{:S(2)}) %collective-permute-start.16) | collective-permute-done | bytes 147488 | tf_op jit(solution)/shard_map/ppermute | solution.py:33
  105.2 3.4 %collective-permute-done.17.refs_6_ = bf16[9,32,256]{2,1,0:T(8,128)(2,1)S(1)} collective-permute-done((bf16[9,32,256]{2,1,0:T(8,128)(2,1)S(1)}, bf16[9,32,256]{2,1,0:T(8,128)(2,1)S(1)}, u32[]{:S(2)}, u32[]{:S(2)}) %collective-permute-start.17) | collective-permute-done | bytes 147488 | tf_op jit(solution)/shard_map/ppermute | solution.py:33
  108.6 0.2 collective-permute-done.18.refs_7_
  108.8 1.6 %shard_map.34 = f32[17,32,256]{2,1,0:T(8,128)} custom-call(s32[2]{0:T(128)S(1)} %pad_add_fusion.flags, f32[8,256]{1,0:T(8,128)S(1)} %fusion.4.weights, bf16[9,32,256]{2,1,0:T(8,128)(2,1)S(1)} %get-tuple-element.37.refs_0_, bf16[9,32,256]{2,1,0:T(8,128)(2,1)S(1)} %collective-permute-done.12.refs_1_, bf16[9,32,256]{2,1,0:T(8,128)(2,1)S(1)} %collective-permute-done.13.refs_2_, ...), custom_call_target="tpu_custom_call" | custom-call | bytes 2097152 | tf_op jit(solution)/shard_map/pallas_call | solution.py:207
  (3 shorter events, 0.1 us)
Async XLA Ops:
  0.0 52.4 %copy-start.1 = (bf16[2048,512]{1,0:T(8,128)(2,1)S(1)}, bf16[2048,512]{1,0:T(8,128)(2,1)}, u32[]{:S(2)}) copy-start(bf16[2048,512]{1,0:T(8,128)(2,1)} %own_env.1) | copy-start | bytes 6291460
  1.4 14.0 %collective-permute-start = (bf16[512,512]{1,0:T(8,128)(2,1)S(1)}, bf16[512,512]{1,0:T(8,128)(2,1)S(1)}, u32[]{:S(2)}, u32[]{:S(2)}) collective-permute-start(bf16[512,512]{1,0:T(8,128)(2,1)S(1)} %get-tuple-element.46), channel_id=1, source_target_pairs={{32,0},{33,1},{34,2},{35,3},{36,4},{37,5},{38,6},{39,7},{40,8},{41... | collective-permute-start | bytes 1572872 | tf_op jit(solution)/shard_map/ppermute | solution.py:33
  4.8 13.7 %collective-permute-start.1 = (bf16[512,512]{1,0:T(8,128)(2,1)S(1)}, bf16[512,512]{1,0:T(8,128)(2,1)S(1)}, u32[]{:S(2)}, u32[]{:S(2)}) collective-permute-start(bf16[512,512]{1,0:T(8,128)(2,1)S(1)} %get-tuple-element.45), channel_id=1, source_target_pairs={{96,0},{97,1},{98,2},{99,3},{100,4},{101,5},{102,6},{103,7},{104,8... | collective-permute-start | bytes 1572872 | tf_op jit(solution)/shard_map/ppermute | solution.py:33
  19.6 32.8 %collective-permute-start.2 = (bf16[1024,512]{1,0:T(8,128)(2,1)}, bf16[1024,512]{1,0:T(8,128)(2,1)}, u32[]{:S(2)}, u32[]{:S(2)}) collective-permute-start(bf16[1024,512]{1,0:T(8,128)(2,1)} %pad_maximum_fusion), channel_id=1, source_target_pairs={{1,0},{0,1},{3,2},{2,3},{5,4},{4,5},{7,6},{6,7},{9,8},{8,9},{11,10... | collective-permute-start | bytes 3145736 | tf_op jit(solution)/shard_map/ppermute | solution.py:33
  21.4 11.6 %collective-permute-start.4 = (bf16[256,512]{1,0:T(8,128)(2,1)}, bf16[256,512]{1,0:T(8,128)(2,1)S(1)}, u32[]{:S(2)}, u32[]{:S(2)}) collective-permute-start(bf16[256,512]{1,0:T(8,128)(2,1)} %own_points.1), channel_id=1, source_target_pairs={{4,0},{5,1},{6,2},{7,3},{8,4},{9,5},{10,6},{11,7},{12,8},{13,9},{1... | collective-permute-start | bytes 786440 | tf_op jit(solution)/shard_map/ppermute | solution.py:33
  33.1 8.2 %collective-permute-start.5 = (bf16[256,512]{1,0:T(8,128)(2,1)S(1)}, bf16[256,512]{1,0:T(8,128)(2,1)}, u32[]{:S(2)}, u32[]{:S(2)}) collective-permute-start(bf16[256,512]{1,0:T(8,128)(2,1)S(1)} %collective-permute-done.4.points), channel_id=1, source_target_pairs={{4,0},{5,1},{6,2},{7,3},{8,4},{9,5},{10,6},{11,7},{12,8},{13,9},{1... | collective-permute-start | bytes 786440 | tf_op jit(solution)/shard_map/ppermute | solution.py:33
  41.2 7.8 %collective-permute-start.6 = (bf16[256,512]{1,0:T(8,128)(2,1)}, bf16[256,512]{1,0:T(8,128)(2,1)}, u32[]{:S(2)}, u32[]{:S(2)}) collective-permute-start(bf16[256,512]{1,0:T(8,128)(2,1)} %collective-permute-done.5.points), channel_id=1, source_target_pairs={{4,0},{5,1},{6,2},{7,3},{8,4},{9,5},{10,6},{11,7},{12,8},{13,9},{1... | collective-permute-start | bytes 786440 | tf_op jit(solution)/shard_map/ppermute | solution.py:33
  44.7 7.7 %collective-permute-start.3 = (bf16[256,512]{1,0:T(8,128)(2,1)}, bf16[256,512]{1,0:T(8,128)(2,1)}, u32[]{:S(2)}, u32[]{:S(2)}) collective-permute-start(bf16[256,512]{1,0:T(8,128)(2,1)} %own_points.1), channel_id=1, source_target_pairs={{1,0},{0,1},{3,2},{2,3},{5,4},{4,5},{7,6},{6,7},{9,8},{8,9},{11,10... | collective-permute-start | bytes 786440 | tf_op jit(solution)/shard_map/ppermute | solution.py:33
  49.0 29.7 %collective-permute-start.7 = (bf16[256,512]{1,0:T(8,128)(2,1)}, bf16[256,512]{1,0:T(8,128)(2,1)S(1)}, u32[]{:S(2)}, u32[]{:S(2)}) collective-permute-start(bf16[256,512]{1,0:T(8,128)(2,1)} %collective-permute-done.6.points), channel_id=1, source_target_pairs={{4,0},{5,1},{6,2},{7,3},{8,4},{9,5},{10,6},{11,7},{12,8},{13,9},{1... | collective-permute-start | bytes 786440 | tf_op jit(solution)/shard_map/ppermute | solution.py:33
  60.5 2.2 %copy-start = (bf16[4096,512]{1,0:T(8,128)(2,1)S(1)}, bf16[4096,512]{1,0:T(8,128)(2,1)}, u32[]{:S(2)}) copy-start(bf16[4096,512]{1,0:T(8,128)(2,1)} %get-tuple-element.26.env_hat) | copy-start | bytes 12582916
  84.3 3.9 %collective-permute-start.10 = (bf16[256,256]{1,0:T(8,128)(2,1)S(1)}, bf16[256,256]{1,0:T(8,128)(2,1)S(1)}, u32[]{:S(2)}, u32[]{:S(2)}) collective-permute-start(bf16[256,256]{1,0:T(8,128)(2,1)S(1)} %get-tuple-element.48), channel_id=1, source_target_pairs={{1,0},{0,1},{3,2},{2,3},{5,4},{4,5},{7,6},{6,7},{9,8},{8,9},{11,10... | collective-permute-start | bytes 393224 | tf_op jit(solution)/shard_map/ppermute | solution.py:33
  87.2 1.3 %collective-permute-start.11 = (bf16[256,256]{1,0:T(8,128)(2,1)S(1)}, bf16[256,256]{1,0:T(8,128)(2,1)S(1)}, u32[]{:S(2)}, u32[]{:S(2)}) collective-permute-start(bf16[256,256]{1,0:T(8,128)(2,1)S(1)} %get-tuple-element.47), channel_id=1, source_target_pairs={{1,0},{0,1},{3,2},{2,3},{5,4},{4,5},{7,6},{6,7},{9,8},{8,9},{11,10... | collective-permute-start | bytes 393224 | tf_op jit(solution)/shard_map/ppermute | solution.py:33
  87.3 1.4 %collective-permute-start.8 = (bf16[256,256]{1,0:T(8,128)(2,1)S(1)}, bf16[256,256]{1,0:T(8,128)(2,1)S(1)}, u32[]{:S(2)}, u32[]{:S(2)}) collective-permute-start(bf16[256,256]{1,0:T(8,128)(2,1)S(1)} %get-tuple-element.50), channel_id=1, source_target_pairs={{1,0},{0,1},{3,2},{2,3},{5,4},{4,5},{7,6},{6,7},{9,8},{8,9},{11,10... | collective-permute-start | bytes 393224 | tf_op jit(solution)/shard_map/ppermute | solution.py:33
  87.7 1.3 %collective-permute-start.9 = (bf16[256,256]{1,0:T(8,128)(2,1)S(1)}, bf16[256,256]{1,0:T(8,128)(2,1)S(1)}, u32[]{:S(2)}, u32[]{:S(2)}) collective-permute-start(bf16[256,256]{1,0:T(8,128)(2,1)S(1)} %get-tuple-element.49), channel_id=1, source_target_pairs={{1,0},{0,1},{3,2},{2,3},{5,4},{4,5},{7,6},{6,7},{9,8},{8,9},{11,10... | collective-permute-start | bytes 393224 | tf_op jit(solution)/shard_map/ppermute | solution.py:33
  89.7 9.9 %collective-permute-start.12 = (bf16[9,32,256]{2,1,0:T(8,128)(2,1)S(1)}, bf16[9,32,256]{2,1,0:T(8,128)(2,1)S(1)}, u32[]{:S(2)}, u32[]{:S(2)}) collective-permute-start(bf16[9,32,256]{2,1,0:T(8,128)(2,1)S(1)} %get-tuple-element.38), channel_id=1, source_target_pairs={{96,0},{97,1},{98,2},{99,3},{100,4},{101,5},{102,6},{103,7},{104,8... | collective-permute-start | bytes 442376 | tf_op jit(solution)/shard_map/ppermute | solution.py:33
  89.8 9.9 %collective-permute-start.13 = (bf16[9,32,256]{2,1,0:T(8,128)(2,1)S(1)}, bf16[9,32,256]{2,1,0:T(8,128)(2,1)S(1)}, u32[]{:S(2)}, u32[]{:S(2)}) collective-permute-start(bf16[9,32,256]{2,1,0:T(8,128)(2,1)S(1)} %get-tuple-element.39), channel_id=1, source_target_pairs={{64,0},{65,1},{66,2},{67,3},{68,4},{69,5},{70,6},{71,7},{72,8},{73... | collective-permute-start | bytes 442376 | tf_op jit(solution)/shard_map/ppermute | solution.py:33
  89.9 12.3 %collective-permute-start.14 = (bf16[9,32,256]{2,1,0:T(8,128)(2,1)S(1)}, bf16[9,32,256]{2,1,0:T(8,128)(2,1)S(1)}, u32[]{:S(2)}, u32[]{:S(2)}) collective-permute-start(bf16[9,32,256]{2,1,0:T(8,128)(2,1)S(1)} %get-tuple-element.40), channel_id=1, source_target_pairs={{32,0},{33,1},{34,2},{35,3},{36,4},{37,5},{38,6},{39,7},{40,8},{41... | collective-permute-start | bytes 442376 | tf_op jit(solution)/shard_map/ppermute | solution.py:33
  92.5 9.7 %collective-permute-start.15 = (bf16[9,32,256]{2,1,0:T(8,128)(2,1)S(1)}, bf16[9,32,256]{2,1,0:T(8,128)(2,1)S(1)}, u32[]{:S(2)}, u32[]{:S(2)}) collective-permute-start(bf16[9,32,256]{2,1,0:T(8,128)(2,1)S(1)} %get-tuple-element.41), channel_id=1, source_target_pairs={{128,0},{129,1},{130,2},{131,3},{132,4},{133,5},{134,6},{135,7},{1... | collective-permute-start | bytes 442376 | tf_op jit(solution)/shard_map/ppermute | solution.py:33
  95.4 9.8 %collective-permute-start.16 = (bf16[9,32,256]{2,1,0:T(8,128)(2,1)S(1)}, bf16[9,32,256]{2,1,0:T(8,128)(2,1)S(1)}, u32[]{:S(2)}, u32[]{:S(2)}) collective-permute-start(bf16[9,32,256]{2,1,0:T(8,128)(2,1)S(1)} %get-tuple-element.42), channel_id=1, source_target_pairs={{224,0},{225,1},{226,2},{227,3},{228,4},{229,5},{230,6},{231,7},{2... | collective-permute-start | bytes 442376 | tf_op jit(solution)/shard_map/ppermute | solution.py:33
  99.6 9.0 %collective-permute-start.17 = (bf16[9,32,256]{2,1,0:T(8,128)(2,1)S(1)}, bf16[9,32,256]{2,1,0:T(8,128)(2,1)S(1)}, u32[]{:S(2)}, u32[]{:S(2)}) collective-permute-start(bf16[9,32,256]{2,1,0:T(8,128)(2,1)S(1)} %get-tuple-element.43), channel_id=1, source_target_pairs={{192,0},{193,1},{194,2},{195,3},{196,4},{197,5},{198,6},{199,7},{2... | collective-permute-start | bytes 442376 | tf_op jit(solution)/shard_map/ppermute | solution.py:33
  99.7 9.1 %collective-permute-start.18 = (bf16[9,32,256]{2,1,0:T(8,128)(2,1)S(1)}, bf16[9,32,256]{2,1,0:T(8,128)(2,1)S(1)}, u32[]{:S(2)}, u32[]{:S(2)}) collective-permute-start(bf16[9,32,256]{2,1,0:T(8,128)(2,1)S(1)} %get-tuple-element.44), channel_id=1, source_target_pairs={{160,0},{161,1},{162,2},{163,3},{164,4},{165,5},{166,6},{167,7},{1... | collective-permute-start | bytes 442376 | tf_op jit(solution)/shard_map/ppermute | solution.py:33

commit v2 on v0

v2 whole, which is shorter than its diff:
```python
import functools

import jax
import jax.numpy as jnp
from jax import lax
from jax.experimental import pallas as pl
from jax.experimental.pallas import tpu as pltpu
from jax.sharding import PartitionSpec as P


F32, BF16 = jnp.float32, jnp.bfloat16
NT = (((1,), (1,)), ((), ()))
VMEM_LIMIT = 24 * 1024 * 1024


def split_index(i):
    env, sp = divmod(i, 32)
    y_hi, x = divmod(env, 4)
    q, core = divmod(sp, 2)
    z, y_lo = divmod(q, 2)
    return y_hi, x, z, y_lo, core


def join_index(y_hi, x, z, y_lo, core):
    return ((y_hi % 2) * 4 + x % 4) * 32 + ((z % 8) * 2 + y_lo % 2) * 2 + core % 2


def fetch(value, source_of):
    pairs = [(join_index(*source_of(*split_index(i))), i) for i in range(256)]
    return lax.ppermute(value, ("env", "sp"), pairs)


def other_core(y_hi, x, z, y_lo, core):
    return y_hi, x, z, y_lo, 1 - core


def near_x(y_hi, x, z, y_lo, core):
    return y_hi, x + 1 - 2 * core, z, y_lo, core


def column(first):
    def source(y_hi, x, z, y_lo, core):
        m = first + y_hi
        if x % 2 == 0:
            return y_hi, x, z + m, y_lo, core
        y = (y_hi * 2 + y_lo + 1 - 2 * core) % 4
        return y // 2, x, z + y_lo + m - 1, y % 2, core

    return source


def sharer(flip, step):
    def source(y_hi, x, z, y_lo, core):
        return (y_hi + flip) % 2, x + step, z, y_lo, core

    return source


def unit(values):
    values = values.astype(F32)
    total = jnp.sum(values * values, axis=1, keepdims=True)
    return (values * lax.rsqrt(total + 1e-06)).astype(BF16)


def fourth(products):
    squares = products * products
    return (squares * squares).astype(BF16)


def dot(a, b):
    return lax.dot_general(a, b, NT, preferred_element_type=F32)


CHUNK = 512


def rows_of(points, raw, env_hat, rows_k):
    place = 0
    for ref in raw:
        for start in range(0, ref.shape[0], CHUNK):
            env = unit(ref[start:start + CHUNK, :])
            env_hat[place:place + CHUNK, :] = env
            rows_k[:, place:place + CHUNK] = fourth(dot(points, env))
            place += CHUNK


def own_kernel(own_env, own_points, sib_points, env_hat, rows_k, points_hat, gram):
    points_hat[:256, :] = unit(own_points[...])
    points_hat[256:, :] = unit(sib_points[...])
    rows_of(points_hat[...], (own_env,), env_hat, rows_k)
    gram[...] = dot(rows_k[...], rows_k[:256, :])


def more_kernel(near, far, points_hat, gram, weight, env_hat, rows_k, own_out, sib_out):
    rows_of(points_hat[...], (near, far), env_hat, rows_k)
    total = (gram[...] + dot(rows_k[...], rows_k[:256, :])) * weight[...]
    total = total.astype(BF16)
    own_out[...] = total[:256]
    sib_out[...] = total[256:]


def quarter_kernel(first, second, out):
    out[:128, :] = unit(first[...])
    out[128:, :] = unit(second[...])


def column_kernel(points, env_a, env_b, rows_a, rows_b, weight, own_out, sib_out, kept):
    half = env_a.shape[0]
    for place in range(0, 2 * half, CHUNK):
        env, start = (env_a, place) if place < half else (env_b, place - half)
        kept[:, place:place + CHUNK] = fourth(dot(points[...], env[start:start + CHUNK, :]))
    total = dot(rows_a[...], kept[:, :half]) + dot(rows_b[...], kept[:, half:])
    total = (total * weight[...]).astype(BF16)
    own_out[...] = total[:256]
    sib_out[...] = total[256:]


def pack_kernel(flags, *refs):
    own, swapped, out = refs[:5], refs[5:10], refs[10]
    y_hi, half, late = flags[0], flags[1], flags[2]
    for e in range(8):
        rows = slice(32 * e, 32 * e + 32)
        out[e, 0] = own[0][rows, :]

    @pl.when(late == 1)
    def _():
        for e in range(8):
            out[e, 5] = swapped[0][32 * e:32 * e + 32, :]

    for v in range(4):
        which = y_hi if v < 2 else 1 - y_hi
        side = half if v % 2 == 0 else 1 - half
        lanes = pl.ds(pl.multiple_of(side * 128, 128), 128)
        for part in range(2):
            m = 1 + 2 * part + which
            cols = slice(128 * part, 128 * part + 128)
            for e in range(8):
                out[e, m, :, lanes] = own[1 + v][32 * e:32 * e + 32, cols]

            @pl.when(m + late <= 4)
            def _(v=v, m=m, cols=cols, lanes=lanes):
                for e in range(8):
                    out[e, 4 + m + late, :, lanes] = swapped[1 + v][32 * e:32 * e + 32, cols]


def finish_kernel(flags, weights, pieces, out):
    core = flags[0]
    even, odd = None, None
    for e in range(0, 8, 2):
        a = pieces[e].astype(F32) * weights[e][None, None, :]
        b = pieces[e + 1].astype(F32) * weights[e + 1][None, None, :]
        even, odd = (a, b) if even is None else (even + a, odd + b)
    out[0] = even[0]
    shift = 2 * core
    for m in range(1, 5):
        out[4 * m] = even[m]
        out[4 * m - 2] = odd[m]
        out[4 * m - 3 + shift] = even[4 + m]
        out[4 * m - 1 - shift] = odd[4 + m]


def spread(index, lanes=None):
    lanes = jnp.arange(256, dtype=jnp.int32) if lanes is None else lanes
    return 1.0 + ((lanes[None, :] + 64 * index[:, None]) % 256).astype(F32) / 256.0


def vmem_spec():
    return pl.BlockSpec(memory_space=pltpu.VMEM)


def smem_spec():
    return pl.BlockSpec(memory_space=pltpu.SMEM)


def shape(*dims, dtype=BF16):
    return jax.ShapeDtypeStruct(dims, dtype)


def call(body, out_shape, n_in, flops, bytes_accessed, smem=(), scratch=()):
    many = isinstance(out_shape, (tuple, list))
    return pl.pallas_call(
        body,
        out_shape=out_shape,
        in_specs=[smem_spec() if i in smem else vmem_spec() for i in range(n_in)],
        out_specs=[vmem_spec() for _ in out_shape] if many else vmem_spec(),
        scratch_shapes=scratch,
        compiler_params=pltpu.CompilerParams(vmem_limit_bytes=VMEM_LIMIT),
        cost_estimate=pl.CostEstimate(flops=flops, bytes_accessed=bytes_accessed, transcendentals=0),
    )


def on_device(descriptors, sparse_points):
    env, sp = lax.axis_index("env"), lax.axis_index("sp")
    y_hi, x, core = env // 4, env % 4, sp % 2
    half = x // 2

    sib_points = fetch(sparse_points, other_core)
    piece = lax.dynamic_slice_in_dim(sparse_points, half * 128, 128, 0)
    first, second = fetch(piece, column(1)), fetch(piece, column(3))
    near = fetch(lax.dynamic_slice_in_dim(descriptors, core * 1024, 1024, 0), near_x)

    env_a, rows_a, points_hat, gram = call(
        own_kernel,
        (shape(2048, 512), shape(512, 2048), shape(512, 512), shape(512, 256, dtype=F32)),
        3, 2 * 805306368, 1 << 23,
    )(descriptors, sparse_points, sib_points)
    first, second, near, env_a, rows_a, points_hat, gram = lax.optimization_barrier(
        (first, second, near, env_a, rows_a, points_hat, gram)
    )

    quarter = call(quarter_kernel, shape(256, 512), 2, 1 << 20, 1 << 19)(first, second)
    quarters = [quarter] + [fetch(quarter, sharer(*turn)) for turn in ((0, 2), (1, 0), (1, 2))]
    far = fetch(near, other_core)

    group = (y_hi * 2 + half)[None]
    weight = spread(group) * (16.0 / 16384.0)
    pair = (shape(256, 256), shape(256, 256))
    env_b, rows_b, own0, sib0 = call(
        more_kernel, (shape(2048, 512), shape(512, 2048)) + pair, 5, 2 * 805306368, 1 << 23
    )(near, far, points_hat, gram, weight)
    lanes = jnp.arange(256, dtype=jnp.int32) % 128
    sides = [spread(group, lanes + 128 * side) * (16.0 / 16384.0) for side in (half, 1 - half)]
    own, sib = [own0], [sib0]
    for v, points in enumerate(quarters):
        a, b = call(
            column_kernel, pair, 6, 2 * 1073741824, 1 << 23, scratch=(pltpu.VMEM((256, 4096), BF16),)
        )(points, env_a, env_b, rows_a, rows_b, sides[v % 2])
        own.append(a)
        sib.append(b)

    swapped = [fetch(value, other_core) for value in sib]
    late = jnp.logical_and(x % 2 == 0, core == 0).astype(jnp.int32)
    packed = call(pack_kernel, shape(8, 9, 32, 256), 11, 0, 1 << 21, (0,))(
        jnp.stack([y_hi, half, late]), *own, *swapped
    )
    pieces = lax.all_to_all(packed, "env", 0, 0, tiled=True)

    sources = jnp.arange(8, dtype=jnp.int32)
    weights = 1.0 / spread((sources // 4) * 2 + (sources % 4) // 2)
    out = call(finish_kernel, shape(17, 32, 256, dtype=F32), 3, 0, 1 << 21, (0,))(core[None], weights, pieces)
    return out[None]


def solution(mesh):
    placed = (P("env", None), P("sp", None))
    return jax.shard_map(
        on_device, mesh=mesh, in_specs=placed, out_specs=P("sp", None, "env", None), check_vma=False
    )
```

time: 399 us -> 78.3 us (0.20)
  starting transfers between devices: 190 us -> 26.6 us
  waiting for transfers between devices: 164 us -> 21.6 us
  matrix products: 22.2 us -> 0 us
  Pallas kernels: 0 us -> 20.2 us
  between operations: 13.4 us -> 0.08 us
  other arithmetic: 5.07 us -> 0.22 us
  local copies, waits for them, and re-layouts: 4.17 us -> 8.93 us
    ppermute x16 -> x13, starting transfers between devices: 190 us -> 21.9 us  [fetch(): return lax.ppermute(value, ('env', 'sp'), pairs)]
    reduce_scatter x1 -> x0, waiting for transfers between devices: 103 us -> none  [on_device(): lax.psum_scatter(partial_value, 'env', scatter_dimension=1, tiled=True)]
    ppermute x16 -> x13, waiting for transfers between devices: 61.5 us -> 2.91 us  [fetch(): return lax.ppermute(value, ('env', 'sp'), pairs)]
    dot_general x18 -> x0, matrix products: 22.2 us -> none  [the longest x17 19.5 us: gram_tile(): lax.dot_general(own_kernel, moving, (((1,), (1,)), ((), ())), preferred_e...]
    pallas_call x0 -> x9, Pallas kernels: none -> 20.2 us  [the longest x4 11.6 us: on_device(): call(column_kernel, pair, 6, 2 * 1073741824, 1 << 23, scratch=(pltpu.VMEM...]
    all_to_all x0 -> x1, waiting for transfers between devices: none -> 18.7 us  [on_device(): pieces = lax.all_to_all(packed, 'env', 0, 0, tiled=True)]
    unnamed x1 -> x16, local copies, waits for them, and re-layouts: 0.1 us -> 6.63 us
    all_to_all x0 -> x1, starting transfers between devices: none -> 4.76 us  [on_device(): pieces = lax.all_to_all(packed, 'env', 0, 0, tiled=True)]
  transfers between devices with their start and end apart: 17 -> 14, of which waited for: 17 -> 3; matrix products, arithmetic and copies ran while one was open for 0% -> 0% of each run, Pallas kernels for 0% -> 22%
where the time goes in v2:
time: 78.3 us; the launch traced here: 77.7 us
  starting transfers between devices  26.6 us (34%)
  waiting for transfers between devices  21.6 us (28%)
  Pallas kernels  20.2 us (26%)
  local copies, waits for them, and re-layouts  8.93 us (11%)
    ppermute x13, starting transfers between devices, fetch(): return lax.ppermute(value, ('env', 'sp'), pairs)  21.9 us
    all_to_all x1, waiting for transfers between devices, on_device(): pieces = lax.all_to_all(packed, 'env', 0, 0, tiled=True)  18.7 us
    pallas_call x4, Pallas kernels, on_device(): call(column_kernel, pair, 6, 2 * 1073741824, 1 << 23, scratch=(pltpu.VMEM...  11.6 us
    unnamed x16, local copies, waits for them, and re-layouts  6.63 us
    all_to_all x1, starting transfers between devices, on_device(): pieces = lax.all_to_all(packed, 'env', 0, 0, tiled=True)  4.76 us
    pallas_call x1, Pallas kernels, on_device(): call(more_kernel, (shape(2048, 512), shape(512, 2048)) + pair, 5, 2 * 805...  3.43 us
    ppermute x13, waiting for transfers between devices, fetch(): return lax.ppermute(value, ('env', 'sp'), pairs)  2.91 us
    dynamic_slice x1, local copies, waits for them, and re-layouts, on_device(): lax.dynamic_slice_in_dim(descriptors, core * 1024, 1024, 0)  2.3 us
  transfers between devices with their start and end apart: 14, of which 3 were waited for; matrix products, arithmetic and copies ran while one was open for 0% of the time, Pallas kernels for 22%

profile of v2, /device:TPU:1, one launch (start us, length us, event | category | flops | bytes accessed | tf_op | source)
XLA Modules:
  0.0 77.7 jit_solution(8231128141708698692)
XLA Ops:
  0.0 0.0 copy-start.3
  0.0 2.3 %constant_dynamic-slice_fusion = bf16[1024,512]{1,0:T(8,128)(2,1)} fusion(bf16[2048,512]{1,0:T(8,128)(2,1)} %own_env.1, s32[]{:T(128)S(6)} %select_n.127), kind=kLoop, calls=%fused_computation.49 | loop fusion | bytes 2097156 | tf_op jit(solution)/shard_map/dynamic_slice | solution.py:200
  2.3 2.0 %collective-permute-start.2 = (bf16[1024,512]{1,0:T(8,128)(2,1)}, bf16[1024,512]{1,0:T(8,128)(2,1)}, u32[]{:S(2)}, u32[]{:S(2)}) collective-permute-start(bf16[1024,512]{1,0:T(8,128)(2,1)} %constant_dynamic-slice_fusion), channel_id=1, source_target_pairs={{32,0},{97,1},{34,2},{99,3},{36,4},{101,5},{38,6},{103,7},{40,8},{... | collective-permute-start | bytes 3145736 | tf_op jit(solution)/shard_map/ppermute | solution.py:30
  4.3 0.0 copy-done.3
  4.3 2.2 %collective-permute-start.3 = (bf16[256,512]{1,0:T(8,128)(2,1)S(1)}, bf16[256,512]{1,0:T(8,128)(2,1)S(1)}, u32[]{:S(2)}, u32[]{:S(2)}) collective-permute-start(bf16[256,512]{1,0:T(8,128)(2,1)S(1)} %copy-done.3), channel_id=1, source_target_pairs={{1,0},{0,1},{3,2},{2,3},{5,4},{4,5},{7,6},{6,7},{9,8},{8,9},{11,10... | collective-permute-start | bytes 786440 | tf_op jit(solution)/shard_map/ppermute | solution.py:30
  6.6 5.7 %collective-permute-start = (bf16[128,512]{1,0:T(8,128)(2,1)S(1)}, bf16[128,512]{1,0:T(8,128)(2,1)S(1)}, u32[]{:S(2)}, u32[]{:S(2)}) collective-permute-start(bf16[128,512]{1,0:T(8,128)(2,1)S(1)} %constant_dynamic-slice_fusion.1), channel_id=1, source_target_pairs={{4,0},{5,1},{6,2},{7,3},{8,4},{9,5},{10,6},{11,7},{12,8},{13,9},{1... | collective-permute-start | bytes 393224 | tf_op jit(solution)/shard_map/ppermute | solution.py:30
  12.2 1.6 %collective-permute-start.1 = (bf16[128,512]{1,0:T(8,128)(2,1)S(1)}, bf16[128,512]{1,0:T(8,128)(2,1)S(1)}, u32[]{:S(2)}, u32[]{:S(2)}) collective-permute-start(bf16[128,512]{1,0:T(8,128)(2,1)S(1)} %constant_dynamic-slice_fusion.1), channel_id=1, source_target_pairs={{12,0},{13,1},{14,2},{15,3},{16,4},{17,5},{18,6},{19,7},{20,8},{21... | collective-permute-start | bytes 393224 | tf_op jit(solution)/shard_map/ppermute | solution.py:30
  13.8 0.0 collective-permute-done.3.sib_points
  13.9 0.0 copy-start.2
  13.9 1.6 %copy-done.2 = bf16[2048,512]{1,0:T(8,128)(2,1)S(1)} copy-done((bf16[2048,512]{1,0:T(8,128)(2,1)S(1)}, bf16[2048,512]{1,0:T(8,128)(2,1)}, u32[]{:S(2)}) %copy-start.2) | copy-done | bytes 2097176
  15.4 2.2 %shard_map.28 = (bf16[2048,512]{1,0:T(8,128)(2,1)S(1)}, bf16[512,2048]{1,0:T(8,128)(2,1)S(1)}, bf16[512,512]{1,0:T(8,128)(2,1)S(1)}, f32[512,256]{1,0:T(8,128)S(1)}) custom-call(bf16[2048,512]{1,0:T(8,128)(2,1)S(1)} %copy-done.2, bf16[256,512]{1,0:T(8,128)(2,1)S(1)} %copy-done.3, bf16[256,512]{1,0:T(8,128)(2,1)S(1)} %collective-permute-done.3.sib_points), custom_call_target="tpu_custom_call" | custom-call | flops 1610612736 | bytes 8388608 | tf_op jit(solution)/shard_map/pallas_call | solution.py:202
  17.7 0.0 copy-start
  17.7 1.3 %copy-done = bf16[512,2048]{1,0:T(8,128)(2,1)} copy-done((bf16[512,2048]{1,0:T(8,128)(2,1)}, bf16[512,2048]{1,0:T(8,128)(2,1)S(1)}, u32[]{:S(2)}) %copy-start) | copy-done | bytes 2097176
  19.0 0.0 copy-start.4
  19.0 0.8 %copy-done.4 = bf16[512,512]{1,0:T(8,128)(2,1)} copy-done((bf16[512,512]{1,0:T(8,128)(2,1)}, bf16[512,512]{1,0:T(8,128)(2,1)S(1)}, u32[]{:S(2)}) %copy-start.4) | copy-done | bytes 524312
  19.8 0.0 copy-start.6
  19.8 0.8 %copy-done.6 = f32[512,256]{1,0:T(8,128)} copy-done((f32[512,256]{1,0:T(8,128)}, f32[512,256]{1,0:T(8,128)S(1)}, u32[]{:S(2)}) %copy-start.6) | copy-done | bytes 524312
  20.6 0.0 collective-permute-done.first
  20.6 1.8 %collective-permute-done.1.second = bf16[128,512]{1,0:T(8,128)(2,1)S(1)} collective-permute-done((bf16[128,512]{1,0:T(8,128)(2,1)S(1)}, bf16[128,512]{1,0:T(8,128)(2,1)S(1)}, u32[]{:S(2)}, u32[]{:S(2)}) %collective-permute-start.1) | collective-permute-done | bytes 131104 | tf_op jit(solution)/shard_map/ppermute | solution.py:30
  22.4 0.0 collective-permute-done.2.near
  22.4 2.0 %collective-permute-start.4 = (bf16[1024,512]{1,0:T(8,128)(2,1)}, bf16[1024,512]{1,0:T(8,128)(2,1)S(1)}, u32[]{:S(2)}, u32[]{:S(2)}) collective-permute-start(bf16[1024,512]{1,0:T(8,128)(2,1)} %collective-permute-done.2.near), channel_id=1, source_target_pairs={{1,0},{0,1},{3,2},{2,3},{5,4},{4,5},{7,6},{6,7},{9,8},{8,9},{11,10... | collective-permute-start | bytes 3145736 | tf_op jit(solution)/shard_map/ppermute | solution.py:30
  24.5 0.1 shard_map.30.points
  24.6 0.0 copy-start.1
  24.6 0.6 collective-permute-start.5
  25.2 3.7 %collective-permute-start.6 = (bf16[256,512]{1,0:T(8,128)(2,1)S(1)}, bf16[256,512]{1,0:T(8,128)(2,1)S(1)}, u32[]{:S(2)}, u32[]{:S(2)}) collective-permute-start(bf16[256,512]{1,0:T(8,128)(2,1)S(1)} %shard_map.30.points), channel_id=1, source_target_pairs={{128,0},{129,1},{130,2},{131,3},{132,4},{133,5},{134,6},{135,7},{1... | collective-permute-start | bytes 786440 | tf_op jit(solution)/shard_map/ppermute | solution.py:30
  28.9 2.2 %collective-permute-start.7 = (bf16[256,512]{1,0:T(8,128)(2,1)S(1)}, bf16[256,512]{1,0:T(8,128)(2,1)S(1)}, u32[]{:S(2)}, u32[]{:S(2)}) collective-permute-start(bf16[256,512]{1,0:T(8,128)(2,1)S(1)} %shard_map.30.points), channel_id=1, source_target_pairs={{192,0},{193,1},{194,2},{195,3},{196,4},{197,5},{198,6},{199,7},{2... | collective-permute-start | bytes 786440 | tf_op jit(solution)/shard_map/ppermute | solution.py:30
  31.0 0.0 collective-permute-done.4.far
  31.0 0.0 copy-start.5
  31.0 1.0 %copy-done.5 = bf16[512,512]{1,0:T(8,128)(2,1)S(1)} copy-done((bf16[512,512]{1,0:T(8,128)(2,1)S(1)}, bf16[512,512]{1,0:T(8,128)(2,1)}, u32[]{:S(2)}) %copy-start.5) | copy-done | bytes 524312
  32.1 0.0 copy-start.7
  32.1 1.0 %copy-done.7 = f32[512,256]{1,0:T(8,128)S(1)} copy-done((f32[512,256]{1,0:T(8,128)S(1)}, f32[512,256]{1,0:T(8,128)}, u32[]{:S(2)}) %copy-start.7) | copy-done | bytes 524312
  33.1 3.4 %shard_map.29 = (bf16[2048,512]{1,0:T(8,128)(2,1)S(1)}, bf16[512,2048]{1,0:T(8,128)(2,1)S(1)}, bf16[256,256]{1,0:T(8,128)(2,1)S(1)}, bf16[256,256]{1,0:T(8,128)(2,1)S(1)}) custom-call(bf16[1024,512]{1,0:T(8,128)(2,1)} %collective-permute-done.2.near, bf16[1024,512]{1,0:T(8,128)(2,1)S(1)} %collective-permute-done.4.far, bf16[512,512]{1,0:T(8,128)(2,1)S(1)} %copy-done.5, ...), custom_call_target="tpu_custom_call" | custom-call | flops 1610612736 | bytes 8388608 | tf_op jit(solution)/shard_map/pallas_call | solution.py:218
  36.6 0.8 %collective-permute-start.8 = (bf16[256,256]{1,0:T(8,128)(2,1)S(1)}, bf16[256,256]{1,0:T(8,128)(2,1)S(1)}, u32[]{:S(2)}, u32[]{:S(2)}) collective-permute-start(bf16[256,256]{1,0:T(8,128)(2,1)S(1)} %get-tuple-element.46), channel_id=1, source_target_pairs={{1,0},{0,1},{3,2},{2,3},{5,4},{4,5},{7,6},{6,7},{9,8},{8,9},{11,10... | collective-permute-start | bytes 393224 | tf_op jit(solution)/shard_map/ppermute | solution.py:30
  37.4 0.0 copy-done.1
  37.4 2.4 %shard_map.31 = (bf16[256,256]{1,0:T(8,128)(2,1)S(1)}, bf16[256,256]{1,0:T(8,128)(2,1)S(1)}) custom-call(bf16[256,512]{1,0:T(8,128)(2,1)S(1)} %shard_map.30.points, bf16[2048,512]{1,0:T(8,128)(2,1)S(1)} %get-tuple-element.38.env_a, bf16[2048,512]{1,0:T(8,128)(2,1)S(1)} %get-tuple-element.39.env_b, bf16[512,2048]{1,0:T(8,128)(2,1)S(1)} %copy-done.1, ...), custom_call_target="tpu_custom_call" | custom-call | flops 2147483648 | bytes 8388608 | tf_op jit(solution)/shard_map/pallas_call | solution.py:225
  39.8 0.1 collective-permute-start.9
  39.9 0.0 collective-permute-done.5.points
  39.9 3.1 %shard_map.32 = (bf16[256,256]{1,0:T(8,128)(2,1)S(1)}, bf16[256,256]{1,0:T(8,128)(2,1)}) custom-call(bf16[256,512]{1,0:T(8,128)(2,1)S(1)} %collective-permute-done.5.points, bf16[2048,512]{1,0:T(8,128)(2,1)S(1)} %get-tuple-element.38.env_a, bf16[2048,512]{1,0:T(8,128)(2,1)S(1)} %get-tuple-element.39.env_b, bf16[512,2048]{1,0:T(8,128)(2,1)S(1)} %copy-done.1, ...), custom_call_target="tpu_custom_call" | custom-call | flops 2147483648 | bytes 8388608 | tf_op jit(solution)/shard_map/pallas_call | solution.py:225
  43.0 0.5 collective-permute-start.10
  43.5 0.0 collective-permute-done.6.points
  43.5 3.1 %shard_map.33 = (bf16[256,256]{1,0:T(8,128)(2,1)S(1)}, bf16[256,256]{1,0:T(8,128)(2,1)}) custom-call(bf16[256,512]{1,0:T(8,128)(2,1)S(1)} %collective-permute-done.6.points, bf16[2048,512]{1,0:T(8,128)(2,1)S(1)} %get-tuple-element.38.env_a, bf16[2048,512]{1,0:T(8,128)(2,1)S(1)} %get-tuple-element.39.env_b, bf16[512,2048]{1,0:T(8,128)(2,1)S(1)} %copy-done.1, ...), custom_call_target="tpu_custom_call" | custom-call | flops 2147483648 | bytes 8388608 | tf_op jit(solution)/shard_map/pallas_call | solution.py:225
  46.6 0.0 collective-permute-start.11
  46.6 0.0 collective-permute-done.7.points
  46.6 3.1 %shard_map.34 = (bf16[256,256]{1,0:T(8,128)(2,1)S(1)}, bf16[256,256]{1,0:T(8,128)(2,1)}) custom-call(bf16[256,512]{1,0:T(8,128)(2,1)S(1)} %collective-permute-done.7.points, bf16[2048,512]{1,0:T(8,128)(2,1)S(1)} %get-tuple-element.38.env_a, bf16[2048,512]{1,0:T(8,128)(2,1)S(1)} %get-tuple-element.39.env_b, bf16[512,2048]{1,0:T(8,128)(2,1)S(1)} %copy-done.1, ...), custom_call_target="tpu_custom_call" | custom-call | flops 2147483648 | bytes 8388608 | tf_op jit(solution)/shard_map/pallas_call | solution.py:225
  49.7 0.5 collective-permute-start.12
  50.2 0.1 pad_add_fusion.flags
  50.2 0.0 collective-permute-done.8.refs_5_
  50.2 0.0 collective-permute-done.9.refs_6_
  50.2 0.0 collective-permute-done.10.refs_7_
  50.3 0.0 collective-permute-done.11.refs_8_
  50.3 1.1 %collective-permute-done.12.refs_9_ = bf16[256,256]{1,0:T(8,128)(2,1)S(1)} collective-permute-done((bf16[256,256]{1,0:T(8,128)(2,1)}, bf16[256,256]{1,0:T(8,128)(2,1)S(1)}, u32[]{:S(2)}, u32[]{:S(2)}) %collective-permute-start.12) | collective-permute-done | bytes 131104 | tf_op jit(solution)/shard_map/ppermute | solution.py:30
  51.4 1.8 %shard_map.35 = bf16[8,9,32,256]{3,2,1,0:T(8,128)(2,1)} custom-call(s32[3]{0:T(128)S(1)} %pad_add_fusion.flags, bf16[256,256]{1,0:T(8,128)(2,1)S(1)} %get-tuple-element.35.refs_0_, bf16[256,256]{1,0:T(8,128)(2,1)S(1)} %get-tuple-element.42.refs_1_, bf16[256,256]{1,0:T(8,128)(2,1)S(1)} %get-tuple-element.43.refs_2_, ...), custom_call_target="tpu_custom_call" | custom-call | bytes 2097152 | tf_op jit(solution)/shard_map/pallas_call | solution.py:233
  53.2 4.8 %all-to-all-start = ((bf16[8,9,32,256]{3,2,1,0:T(8,128)(2,1)}), bf16[8,9,32,256]{3,2,1,0:T(8,128)(2,1)S(1)}, u32[]{:S(2)}, u32[]{:S(2)}) async-start(bf16[8,9,32,256]{3,2,1,0:T(8,128)(2,1)} %shard_map.35), calls=%async_computation | async-start | bytes 2359296 | tf_op jit(solution)/shard_map/all_to_all | solution.py:236
  57.9 0.1 fusion.4.weights
  58.0 18.7 %all-to-all-done.pieces = bf16[8,9,32,256]{3,2,1,0:T(8,128)(2,1)S(1)} async-done(((bf16[8,9,32,256]{3,2,1,0:T(8,128)(2,1)}), bf16[8,9,32,256]{3,2,1,0:T(8,128)(2,1)S(1)}, u32[]{:S(2)}, u32[]{:S(2)}) %all-to-all-start) | async-done | bytes 1179680 | tf_op jit(solution)/shard_map/all_to_all | solution.py:236
  76.7 1.0 %shard_map.36 = f32[17,32,256]{2,1,0:T(8,128)} custom-call(s32[1]{0:T(128)} %bitcast.flags, f32[8,256]{1,0:T(8,128)S(1)} %fusion.4.weights, bf16[8,9,32,256]{3,2,1,0:T(8,128)(2,1)S(1)} %all-to-all-done.pieces), custom_call_target="tpu_custom_call" | custom-call | bytes 2097152 | tf_op jit(solution)/shard_map/pallas_call | solution.py:240
  (5 shorter events, 0.1 us)
Async XLA Ops:
  0.0 4.3 %copy-start.3 = (bf16[256,512]{1,0:T(8,128)(2,1)S(1)}, bf16[256,512]{1,0:T(8,128)(2,1)}, u32[]{:S(2)}) copy-start(bf16[256,512]{1,0:T(8,128)(2,1)} %own_points.1) | copy-start | bytes 786436
  2.3 20.1 %collective-permute-start.2 = (bf16[1024,512]{1,0:T(8,128)(2,1)}, bf16[1024,512]{1,0:T(8,128)(2,1)}, u32[]{:S(2)}, u32[]{:S(2)}) collective-permute-start(bf16[1024,512]{1,0:T(8,128)(2,1)} %constant_dynamic-slice_fusion), channel_id=1, source_target_pairs={{32,0},{97,1},{34,2},{99,3},{36,4},{101,5},{38,6},{103,7},{40,8},{... | collective-permute-start | bytes 3145736 | tf_op jit(solution)/shard_map/ppermute | solution.py:30
  4.3 9.5 %collective-permute-start.3 = (bf16[256,512]{1,0:T(8,128)(2,1)S(1)}, bf16[256,512]{1,0:T(8,128)(2,1)S(1)}, u32[]{:S(2)}, u32[]{:S(2)}) collective-permute-start(bf16[256,512]{1,0:T(8,128)(2,1)S(1)} %copy-done.3), channel_id=1, source_target_pairs={{1,0},{0,1},{3,2},{2,3},{5,4},{4,5},{7,6},{6,7},{9,8},{8,9},{11,10... | collective-permute-start | bytes 786440 | tf_op jit(solution)/shard_map/ppermute | solution.py:30
  6.6 14.1 %collective-permute-start = (bf16[128,512]{1,0:T(8,128)(2,1)S(1)}, bf16[128,512]{1,0:T(8,128)(2,1)S(1)}, u32[]{:S(2)}, u32[]{:S(2)}) collective-permute-start(bf16[128,512]{1,0:T(8,128)(2,1)S(1)} %constant_dynamic-slice_fusion.1), channel_id=1, source_target_pairs={{4,0},{5,1},{6,2},{7,3},{8,4},{9,5},{10,6},{11,7},{12,8},{13,9},{1... | collective-permute-start | bytes 393224 | tf_op jit(solution)/shard_map/ppermute | solution.py:30
  12.2 10.2 %collective-permute-start.1 = (bf16[128,512]{1,0:T(8,128)(2,1)S(1)}, bf16[128,512]{1,0:T(8,128)(2,1)S(1)}, u32[]{:S(2)}, u32[]{:S(2)}) collective-permute-start(bf16[128,512]{1,0:T(8,128)(2,1)S(1)} %constant_dynamic-slice_fusion.1), channel_id=1, source_target_pairs={{12,0},{13,1},{14,2},{15,3},{16,4},{17,5},{18,6},{19,7},{20,8},{21... | collective-permute-start | bytes 393224 | tf_op jit(solution)/shard_map/ppermute | solution.py:30
  13.9 1.6 %copy-start.2 = (bf16[2048,512]{1,0:T(8,128)(2,1)S(1)}, bf16[2048,512]{1,0:T(8,128)(2,1)}, u32[]{:S(2)}) copy-start(bf16[2048,512]{1,0:T(8,128)(2,1)} %own_env.1) | copy-start | bytes 6291460
  17.7 1.3 %copy-start = (bf16[512,2048]{1,0:T(8,128)(2,1)}, bf16[512,2048]{1,0:T(8,128)(2,1)S(1)}, u32[]{:S(2)}) copy-start(bf16[512,2048]{1,0:T(8,128)(2,1)S(1)} %get-tuple-element.40.rows_a) | copy-start | bytes 6291460
  19.0 0.8 %copy-start.4 = (bf16[512,512]{1,0:T(8,128)(2,1)}, bf16[512,512]{1,0:T(8,128)(2,1)S(1)}, u32[]{:S(2)}) copy-start(bf16[512,512]{1,0:T(8,128)(2,1)S(1)} %get-tuple-element.33.points_hat) | copy-start | bytes 1572868
  19.8 0.8 %copy-start.6 = (f32[512,256]{1,0:T(8,128)}, f32[512,256]{1,0:T(8,128)S(1)}, u32[]{:S(2)}) copy-start(f32[512,256]{1,0:T(8,128)S(1)} %get-tuple-element.34.gram) | copy-start | bytes 1572868
  22.4 8.6 %collective-permute-start.4 = (bf16[1024,512]{1,0:T(8,128)(2,1)}, bf16[1024,512]{1,0:T(8,128)(2,1)S(1)}, u32[]{:S(2)}, u32[]{:S(2)}) collective-permute-start(bf16[1024,512]{1,0:T(8,128)(2,1)} %collective-permute-done.2.near), channel_id=1, source_target_pairs={{1,0},{0,1},{3,2},{2,3},{5,4},{4,5},{7,6},{6,7},{9,8},{8,9},{11,10... | collective-permute-start | bytes 3145736 | tf_op jit(solution)/shard_map/ppermute | solution.py:30
  24.6 12.8 %copy-start.1 = (bf16[512,2048]{1,0:T(8,128)(2,1)S(1)}, bf16[512,2048]{1,0:T(8,128)(2,1)}, u32[]{:S(2)}) copy-start(bf16[512,2048]{1,0:T(8,128)(2,1)} %copy-done) | copy-start | bytes 6291460
  24.6 15.3 %collective-permute-start.5 = (bf16[256,512]{1,0:T(8,128)(2,1)S(1)}, bf16[256,512]{1,0:T(8,128)(2,1)S(1)}, u32[]{:S(2)}, u32[]{:S(2)}) collective-permute-start(bf16[256,512]{1,0:T(8,128)(2,1)S(1)} %shard_map.30.points), channel_id=1, source_target_pairs={{64,0},{65,1},{66,2},{67,3},{68,4},{69,5},{70,6},{71,7},{72,8},{73... | collective-permute-start | bytes 786440 | tf_op jit(solution)/shard_map/ppermute | solution.py:30
  25.2 18.3 %collective-permute-start.6 = (bf16[256,512]{1,0:T(8,128)(2,1)S(1)}, bf16[256,512]{1,0:T(8,128)(2,1)S(1)}, u32[]{:S(2)}, u32[]{:S(2)}) collective-permute-start(bf16[256,512]{1,0:T(8,128)(2,1)S(1)} %shard_map.30.points), channel_id=1, source_target_pairs={{128,0},{129,1},{130,2},{131,3},{132,4},{133,5},{134,6},{135,7},{1... | collective-permute-start | bytes 786440 | tf_op jit(solution)/shard_map/ppermute | solution.py:30
  28.9 17.7 %collective-permute-start.7 = (bf16[256,512]{1,0:T(8,128)(2,1)S(1)}, bf16[256,512]{1,0:T(8,128)(2,1)S(1)}, u32[]{:S(2)}, u32[]{:S(2)}) collective-permute-start(bf16[256,512]{1,0:T(8,128)(2,1)S(1)} %shard_map.30.points), channel_id=1, source_target_pairs={{192,0},{193,1},{194,2},{195,3},{196,4},{197,5},{198,6},{199,7},{2... | collective-permute-start | bytes 786440 | tf_op jit(solution)/shard_map/ppermute | solution.py:30
  31.0 1.0 %copy-start.5 = (bf16[512,512]{1,0:T(8,128)(2,1)S(1)}, bf16[512,512]{1,0:T(8,128)(2,1)}, u32[]{:S(2)}) copy-start(bf16[512,512]{1,0:T(8,128)(2,1)} %copy-done.4) | copy-start | bytes 1572868
  32.1 1.0 %copy-start.7 = (f32[512,256]{1,0:T(8,128)S(1)}, f32[512,256]{1,0:T(8,128)}, u32[]{:S(2)}) copy-start(f32[512,256]{1,0:T(8,128)} %copy-done.6) | copy-start | bytes 1572868
  36.6 13.7 %collective-permute-start.8 = (bf16[256,256]{1,0:T(8,128)(2,1)S(1)}, bf16[256,256]{1,0:T(8,128)(2,1)S(1)}, u32[]{:S(2)}, u32[]{:S(2)}) collective-permute-start(bf16[256,256]{1,0:T(8,128)(2,1)S(1)} %get-tuple-element.46), channel_id=1, source_target_pairs={{1,0},{0,1},{3,2},{2,3},{5,4},{4,5},{7,6},{6,7},{9,8},{8,9},{11,10... | collective-permute-start | bytes 393224 | tf_op jit(solution)/shard_map/ppermute | solution.py:30
  39.8 10.4 %collective-permute-start.9 = (bf16[256,256]{1,0:T(8,128)(2,1)S(1)}, bf16[256,256]{1,0:T(8,128)(2,1)S(1)}, u32[]{:S(2)}, u32[]{:S(2)}) collective-permute-start(bf16[256,256]{1,0:T(8,128)(2,1)S(1)} %get-tuple-element.47), channel_id=1, source_target_pairs={{1,0},{0,1},{3,2},{2,3},{5,4},{4,5},{7,6},{6,7},{9,8},{8,9},{11,10... | collective-permute-start | bytes 393224 | tf_op jit(solution)/shard_map/ppermute | solution.py:30
  43.0 7.2 %collective-permute-start.10 = (bf16[256,256]{1,0:T(8,128)(2,1)}, bf16[256,256]{1,0:T(8,128)(2,1)S(1)}, u32[]{:S(2)}, u32[]{:S(2)}) collective-permute-start(bf16[256,256]{1,0:T(8,128)(2,1)} %get-tuple-element.48), channel_id=1, source_target_pairs={{1,0},{0,1},{3,2},{2,3},{5,4},{4,5},{7,6},{6,7},{9,8},{8,9},{11,10... | collective-permute-start | bytes 393224 | tf_op jit(solution)/shard_map/ppermute | solution.py:30
  46.6 3.7 %collective-permute-start.11 = (bf16[256,256]{1,0:T(8,128)(2,1)}, bf16[256,256]{1,0:T(8,128)(2,1)S(1)}, u32[]{:S(2)}, u32[]{:S(2)}) collective-permute-start(bf16[256,256]{1,0:T(8,128)(2,1)} %get-tuple-element.49), channel_id=1, source_target_pairs={{1,0},{0,1},{3,2},{2,3},{5,4},{4,5},{7,6},{6,7},{9,8},{8,9},{11,10... | collective-permute-start | bytes 393224 | tf_op jit(solution)/shard_map/ppermute | solution.py:30
  49.7 1.7 %collective-permute-start.12 = (bf16[256,256]{1,0:T(8,128)(2,1)}, bf16[256,256]{1,0:T(8,128)(2,1)S(1)}, u32[]{:S(2)}, u32[]{:S(2)}) collective-permute-start(bf16[256,256]{1,0:T(8,128)(2,1)} %get-tuple-element.50), channel_id=1, source_target_pairs={{1,0},{0,1},{3,2},{2,3},{5,4},{4,5},{7,6},{6,7},{9,8},{8,9},{11,10... | collective-permute-start | bytes 393224 | tf_op jit(solution)/shard_map/ppermute | solution.py:30
  53.2 23.5 %all-to-all-start = ((bf16[8,9,32,256]{3,2,1,0:T(8,128)(2,1)}), bf16[8,9,32,256]{3,2,1,0:T(8,128)(2,1)S(1)}, u32[]{:S(2)}, u32[]{:S(2)}) async-start(bf16[8,9,32,256]{3,2,1,0:T(8,128)(2,1)} %shard_map.35), calls=%async_computation | async-start | bytes 2359296 | tf_op jit(solution)/shard_map/all_to_all | solution.py:236

commit v3 on v0

v3 whole, which is shorter than its diff:
```python
import functools

import jax
import jax.numpy as jnp
from jax import lax
from jax.experimental import pallas as pl
from jax.experimental.pallas import tpu as pltpu
from jax.sharding import PartitionSpec as P


F32, BF16 = jnp.float32, jnp.bfloat16
NT = (((1,), (1,)), ((), ()))
VMEM_LIMIT = 20 * 1024 * 1024


def split_index(i):
    env, sp = divmod(i, 32)
    y_hi, x = divmod(env, 4)
    q, core = divmod(sp, 2)
    z, y_lo = divmod(q, 2)
    return y_hi, x, z, y_lo, core


def join_index(y_hi, x, z, y_lo, core):
    return ((y_hi % 2) * 4 + x % 4) * 32 + ((z % 8) * 2 + y_lo % 2) * 2 + core % 2


def fetch(value, source_of):
    pairs = [(join_index(*source_of(*split_index(i))), i) for i in range(256)]
    return lax.ppermute(value, ("env", "sp"), pairs)


def other_core(y_hi, x, z, y_lo, core):
    return y_hi, x, z, y_lo, 1 - core


def near_x(y_hi, x, z, y_lo, core):
    return y_hi, x + 1 - 2 * core, z, y_lo, core


def next_z(y_hi, x, z, y_lo, core):
    return y_hi, x, z + 1, y_lo, core


def first_column(y_hi, x, z, y_lo, core):
    if x % 2 == 0:
        return y_hi, x, z + 1, y_lo, core
    y = (y_hi * 2 + y_lo + 1 - 2 * core) % 4
    return y // 2, x, z + y_lo, y % 2, core


def unit(values):
    values = values.astype(F32)
    total = jnp.sum(values * values, axis=1, keepdims=True)
    return (values * lax.rsqrt(total + 1e-06)).astype(BF16)


def fourth(products):
    squares = products * products
    return (squares * squares).astype(BF16)


def dot(a, b):
    return lax.dot_general(a, b, NT, preferred_element_type=F32)


CHUNK = 512


def weight_row():
    env = lax.axis_index("env")
    group = (env // 4) * 2 + (env % 4) // 2
    lanes = lax.broadcasted_iota(jnp.int32, (1, 256), 1)
    return (1.0 + ((lanes + 64 * group) % 256).astype(F32) / 256.0) * (16.0 / 16384.0)


def source_weight(e):
    group = (e // 4) * 2 + (e % 4) // 2
    lanes = lax.broadcasted_iota(jnp.int32, (1, 256), 1)
    return 1.0 / (1.0 + ((lanes + 64 * group) % 256).astype(F32) / 256.0)


def rows_of(points, raw, env_hat, rows_k):
    place = 0
    for ref in raw:
        for start in range(0, ref.shape[0], CHUNK):
            env = unit(ref[start:start + CHUNK, :])
            env_hat[place:place + CHUNK, :] = env
            rows_k[:, place:place + CHUNK] = fourth(dot(points, env))
            place += CHUNK


def slice_kernel(descriptors, first_out, second_out, sems):
    start = pl.multiple_of((lax.axis_index("sp") % 2) * 1024, 1024)
    copies = []
    for i, out in enumerate((first_out, second_out)):
        copies.append(pltpu.make_async_copy(descriptors.at[pl.ds(start + 512 * i, 512), :], out, sems.at[i]))
        copies[i].start()
    for copy in copies:
        copy.wait()


def own_kernel(own_env, own_points, sib_points, env_hat, rows_k, gram, points_hat):
    points_hat[:256, :] = unit(own_points[...])
    points_hat[256:, :] = unit(sib_points[...])
    rows_of(points_hat[...], (own_env,), env_hat, rows_k)
    gram[...] = dot(rows_k[...], rows_k[:256, :])


def more_kernel(near, far, points_hat, gram, env_hat, rows_k, gram_out):
    rows_of(points_hat[...], (near, far), env_hat, rows_k)
    gram_out[...] = gram[...] + dot(rows_k[...], rows_k[:256, :])


def last_kernel(near, far, points_hat, gram, env_hat, rows_k, own_out, sib_out):
    rows_of(points_hat[...], (near, far), env_hat, rows_k)
    total = ((gram[...] + dot(rows_k[...], rows_k[:256, :])) * weight_row()).astype(BF16)
    own_out[...] = total[:256]
    sib_out[...] = total[256:]


def column_kernel(points, *refs):
    envs, rows, own_out, sib_out, kept = refs[:3], refs[3:6], refs[6], refs[7], refs[8]
    point_hat = unit(points[...])
    total, place = None, 0
    for env in envs:
        for start in range(0, env.shape[0], CHUNK):
            kept[:, place:place + CHUNK] = fourth(dot(point_hat, env[start:start + CHUNK, :]))
            place += CHUNK
    place = 0
    for row in rows:
        term = dot(row[...], kept[:, place:place + row.shape[1]])
        total = term if total is None else total + term
        place += row.shape[1]
    total = (total * weight_row()).astype(BF16)
    own_out[...] = total[:256]
    sib_out[...] = total[256:]


def pack_kernel(*refs):
    own, swapped, out = refs[:5], refs[5:10], refs[10]
    even_x = lax.axis_index("env") % 2 == 0
    shift = jnp.logical_and(even_x, lax.axis_index("sp") % 2 == 0)
    for e in range(8):
        rows = slice(32 * e, 32 * e + 32)
        for m in range(5):
            out[e, m] = own[m][rows, :]
        for m in range(1, 5):
            out[e, 4 + m] = jnp.where(shift, swapped[m - 1][rows, :], swapped[m][rows, :])


def finish_kernel(pieces, out):
    core = lax.axis_index("sp") % 2

    def total(parity, slot):
        value = None
        for e in range(parity, 8, 2):
            term = pieces[e, slot].astype(F32) * source_weight(e)
            value = term if value is None else value + term
        return value

    out[0] = total(0, 0)
    for m in range(1, 5):
        out[4 * m] = total(0, m)
        out[4 * m - 2] = total(1, m)
        out[4 * m - 3 + 2 * core] = total(0, 4 + m)
        out[4 * m - 1 - 2 * core] = total(1, 4 + m)


def vmem_spec():
    return pl.BlockSpec(memory_space=pltpu.VMEM)


def shape(*dims, dtype=BF16):
    return jax.ShapeDtypeStruct(dims, dtype)


def call(body, out_shape, n_in, flops, bytes_accessed, scratch=(), in_place=False):
    many = isinstance(out_shape, (tuple, list))
    return pl.pallas_call(
        body,
        out_shape=out_shape,
        in_specs=[pl.BlockSpec(memory_space=pl.ANY) if in_place else vmem_spec() for _ in range(n_in)],
        out_specs=[vmem_spec() for _ in out_shape] if many else vmem_spec(),
        scratch_shapes=scratch,
        compiler_params=pltpu.CompilerParams(vmem_limit_bytes=VMEM_LIMIT),
        cost_estimate=pl.CostEstimate(flops=flops, bytes_accessed=bytes_accessed, transcendentals=0),
    )


def on_device(descriptors, sparse_points):
    barrier = lax.optimization_barrier

    def rows(body, envs, sums, n_in, *args):
        return call(body, (shape(envs, 512), shape(512, envs)) + sums, n_in, envs * 786432, envs << 12)(*args)

    gram_shape = shape(512, 256, dtype=F32)
    pair = (shape(256, 256), shape(256, 256))

    column = fetch(sparse_points, first_column)
    sib_points = fetch(sparse_points, other_core)
    low, high = call(
        slice_kernel, (shape(512, 512), shape(512, 512)), 1, 0, 1 << 21, (pltpu.SemaphoreType.DMA((2,)),), True
    )(descriptors)
    near = fetch(low, near_x)
    env_a, rows_a, gram, points_hat = rows(
        own_kernel, 2048, (gram_shape, shape(512, 512)), 3, descriptors, sparse_points, sib_points
    )
    columns = [column]
    column, near, high, env_a, rows_a, gram, points_hat = barrier(
        (column, near, high, env_a, rows_a, gram, points_hat)
    )

    far = fetch(near, other_core)
    columns.append(fetch(column, next_z))
    near_b = fetch(high, near_x)
    env_b, rows_b, gram = rows(more_kernel, 1024, (gram_shape,), 4, near, far, points_hat, gram)
    column, near_b, env_b, rows_b, gram = barrier((columns[1], near_b, env_b, rows_b, gram))

    columns.append(fetch(column, next_z))
    env_c, rows_c, own, sib = rows(
        last_kernel, 1024, pair, 4, near_b, fetch(near_b, other_core), points_hat, gram
    )
    owns, sibs = [own], [sib]

    def take(points):
        own, sib = call(
            column_kernel, pair, 7, 2 * 1073741824, 1 << 23, (pltpu.VMEM((256, 4096), BF16),)
        )(points, env_a, env_b, env_c, rows_a, rows_b, rows_c)
        owns.append(own)
        sibs.append(sib)

    take(columns[0])
    column, owns[1], sibs[1] = barrier((columns[2], owns[1], sibs[1]))

    columns.append(fetch(column, next_z))
    for points in columns[1:]:
        take(points)

    swapped = [fetch(sib, other_core) for sib in sibs]
    packed = call(pack_kernel, shape(8, 9, 32, 256), 10, 0, 1 << 21)(*owns, *swapped)
    pieces = lax.all_to_all(packed, "env", 0, 0, tiled=True)
    return call(finish_kernel, shape(17, 32, 256, dtype=F32), 1, 0, 1 << 21)(pieces)[None]


def solution(mesh):
    placed = (P("env", None), P("sp", None))
    return jax.shard_map(
        on_device, mesh=mesh, in_specs=placed, out_specs=P("sp", None, "env", None), check_vma=False
    )
```

time: 399 us -> 75.8 us (0.19)
  starting transfers between devices: 190 us -> 24.1 us
  waiting for transfers between devices: 164 us -> 10.9 us
  blocking collectives: 0 us -> 23.3 us
  matrix products: 22.2 us -> 0 us
  Pallas kernels: 0 us -> 15.6 us
  between operations: 13.4 us -> 0.08 us
  other arithmetic: 5.07 us -> 0 us
    ppermute x16 -> x14, starting transfers between devices: 190 us -> 24.1 us  [fetch(): return lax.ppermute(value, ('env', 'sp'), pairs)]
    reduce_scatter x1 -> x0, waiting for transfers between devices: 103 us -> none  [on_device(): lax.psum_scatter(partial_value, 'env', scatter_dimension=1, tiled=True)]
    ppermute x16 -> x14, waiting for transfers between devices: 61.5 us -> 10.9 us  [fetch(): return lax.ppermute(value, ('env', 'sp'), pairs)]
    all_to_all x0 -> x1, blocking collectives: none -> 23.3 us  [on_device(): pieces = lax.all_to_all(packed, 'env', 0, 0, tiled=True)]
    dot_general x18 -> x0, matrix products: 22.2 us -> none  [the longest x17 19.5 us: gram_tile(): lax.dot_general(own_kernel, moving, (((1,), (1,)), ((), ())), preferred_e...]
    pallas_call x0 -> x10, Pallas kernels: none -> 15.6 us  [the longest x4 9.62 us: take(): call(column_kernel, pair, 7, 2 * 1073741824, 1 << 23, (pltpu.VMEM((256, 4...]
  transfers between devices with their start and end apart: 17 -> 14, of which waited for: 17 -> 5; matrix products, arithmetic and copies ran while one was open for 0% -> 0% of each run, Pallas kernels for 0% -> 19%
where the time goes in v3:
time: 75.8 us; the launch traced here: 75.7 us
  starting transfers between devices  24.1 us (32%)
  blocking collectives  23.3 us (31%)
  Pallas kernels  15.6 us (21%)
  waiting for transfers between devices  10.9 us (14%)
  local copies, waits for them, and re-layouts  1.59 us (2%)
    ppermute x14, starting transfers between devices, fetch(): return lax.ppermute(value, ('env', 'sp'), pairs)  24.1 us
    all_to_all x1, blocking collectives, on_device(): pieces = lax.all_to_all(packed, 'env', 0, 0, tiled=True)  23.3 us
    ppermute x14, waiting for transfers between devices, fetch(): return lax.ppermute(value, ('env', 'sp'), pairs)  10.9 us
    pallas_call x4, Pallas kernels, take(): call(column_kernel, pair, 7, 2 * 1073741824, 1 << 23, (pltpu.VMEM((256, 4...  9.62 us
    pallas_call x3, Pallas kernels, rows(): call(body, (shape(envs, 512), shape(512, envs)) + sums, n_in, envs * 7864...  4.83 us
    unnamed x4, local copies, waits for them, and re-layouts  1.59 us
  transfers between devices with their start and end apart: 14, of which 5 were waited for; matrix products, arithmetic and copies ran while one was open for 0% of the time, Pallas kernels for 19%

profile of v3, /device:TPU:1, one launch (start us, length us, event | category | flops | bytes accessed | tf_op | source)
XLA Modules:
  0.0 75.7 jit_solution(4090832936589363809)
XLA Ops:
  0.0 0.0 copy-start
  0.0 1.6 %copy-done = bf16[2048,512]{1,0:T(8,128)(2,1)S(1)} copy-done((bf16[2048,512]{1,0:T(8,128)(2,1)S(1)}, bf16[2048,512]{1,0:T(8,128)(2,1)}, u32[]{:S(2)}) %copy-start) | copy-done | bytes 2097176
  1.6 0.0 copy-start.1
  1.6 0.1 shard_map.28
  1.7 2.1 %collective-permute-start.1 = (bf16[512,512]{1,0:T(8,128)(2,1)S(1)}, bf16[512,512]{1,0:T(8,128)(2,1)S(1)}, u32[]{:S(2)}, u32[]{:S(2)}) collective-permute-start(bf16[512,512]{1,0:T(8,128)(2,1)S(1)} %get-tuple-element.41), channel_id=1, source_target_pairs={{32,0},{97,1},{34,2},{99,3},{36,4},{101,5},{38,6},{103,7},{40,8},{... | collective-permute-start | bytes 1572872 | tf_op jit(solution)/shard_map/ppermute | solution.py:30
  3.8 0.0 copy-done.1
  3.8 2.2 %collective-permute-start.2 = (bf16[256,512]{1,0:T(8,128)(2,1)S(1)}, bf16[256,512]{1,0:T(8,128)(2,1)S(1)}, u32[]{:S(2)}, u32[]{:S(2)}) collective-permute-start(bf16[256,512]{1,0:T(8,128)(2,1)S(1)} %copy-done.1), channel_id=1, source_target_pairs={{1,0},{0,1},{3,2},{2,3},{5,4},{4,5},{7,6},{6,7},{9,8},{8,9},{11,10... | collective-permute-start | bytes 786440 | tf_op jit(solution)/shard_map/ppermute | solution.py:30
  6.0 5.6 %collective-permute-start = (bf16[256,512]{1,0:T(8,128)(2,1)S(1)}, bf16[256,512]{1,0:T(8,128)(2,1)S(1)}, u32[]{:S(2)}, u32[]{:S(2)}) collective-permute-start(bf16[256,512]{1,0:T(8,128)(2,1)S(1)} %copy-done.1), channel_id=1, source_target_pairs={{4,0},{5,1},{6,2},{7,3},{8,4},{9,5},{10,6},{11,7},{12,8},{13,9},{1... | collective-permute-start | bytes 786440 | tf_op jit(solution)/shard_map/ppermute | solution.py:30
  11.6 0.0 collective-permute-done.2.sib_points
  11.6 2.2 %shard_map.29 = (bf16[2048,512]{1,0:T(8,128)(2,1)S(1)}, bf16[512,2048]{1,0:T(8,128)(2,1)S(1)}, f32[512,256]{1,0:T(8,128)S(1)}, bf16[512,512]{1,0:T(8,128)(2,1)S(1)}) custom-call(bf16[2048,512]{1,0:T(8,128)(2,1)S(1)} %copy-done, bf16[256,512]{1,0:T(8,128)(2,1)S(1)} %copy-done.1, bf16[256,512]{1,0:T(8,128)(2,1)S(1)} %collective-permute-done.2.sib_points), custom_call_target="tpu_custom_call" | custom-call | flops 1610612736 | bytes 8388608 | tf_op jit(solution)/shard_map/pallas_call | solution.py:195
  13.9 3.5 %collective-permute-done.points = bf16[256,512]{1,0:T(8,128)(2,1)S(1)} collective-permute-done((bf16[256,512]{1,0:T(8,128)(2,1)S(1)}, bf16[256,512]{1,0:T(8,128)(2,1)S(1)}, u32[]{:S(2)}, u32[]{:S(2)}) %collective-permute-start) | collective-permute-done | bytes 262176 | tf_op jit(solution)/shard_map/ppermute | solution.py:30
  17.4 0.0 collective-permute-done.1.near
  17.4 0.8 %collective-permute-start.5 = (bf16[512,512]{1,0:T(8,128)(2,1)S(1)}, bf16[512,512]{1,0:T(8,128)(2,1)S(1)}, u32[]{:S(2)}, u32[]{:S(2)}) collective-permute-start(bf16[512,512]{1,0:T(8,128)(2,1)S(1)} %collective-permute-done.1.near), channel_id=1, source_target_pairs={{1,0},{0,1},{3,2},{2,3},{5,4},{4,5},{7,6},{6,7},{9,8},{8,9},{11,10... | collective-permute-start | bytes 1572872 | tf_op jit(solution)/shard_map/ppermute | solution.py:30
  18.1 0.2 collective-permute-start.4
  18.4 3.2 %collective-permute-start.3 = (bf16[256,512]{1,0:T(8,128)(2,1)S(1)}, bf16[256,512]{1,0:T(8,128)(2,1)S(1)}, u32[]{:S(2)}, u32[]{:S(2)}) collective-permute-start(bf16[256,512]{1,0:T(8,128)(2,1)S(1)} %collective-permute-done.points), channel_id=1, source_target_pairs={{4,0},{5,1},{6,2},{7,3},{8,4},{9,5},{10,6},{11,7},{12,8},{13,9},{1... | collective-permute-start | bytes 786440 | tf_op jit(solution)/shard_map/ppermute | solution.py:30
  21.6 0.0 collective-permute-done.5.far
  21.6 1.3 %shard_map.30 = (bf16[1024,512]{1,0:T(8,128)(2,1)S(1)}, bf16[512,1024]{1,0:T(8,128)(2,1)S(1)}, f32[512,256]{1,0:T(8,128)S(1)}) custom-call(bf16[512,512]{1,0:T(8,128)(2,1)S(1)} %collective-permute-done.1.near, bf16[512,512]{1,0:T(8,128)(2,1)S(1)} %collective-permute-done.5.far, bf16[512,512]{1,0:T(8,128)(2,1)S(1)} %get-tuple-element.50.points_hat, ...), custom_call_target="tpu_custom_call" | custom-call | flops 805306368 | bytes 4194304 | tf_op jit(solution)/shard_map/pallas_call | solution.py:195
  22.9 3.9 %collective-permute-done.3.points = bf16[256,512]{1,0:T(8,128)(2,1)S(1)} collective-permute-done((bf16[256,512]{1,0:T(8,128)(2,1)S(1)}, bf16[256,512]{1,0:T(8,128)(2,1)S(1)}, u32[]{:S(2)}, u32[]{:S(2)}) %collective-permute-start.3) | collective-permute-done | bytes 262176 | tf_op jit(solution)/shard_map/ppermute | solution.py:30
  26.8 0.6 collective-permute-done.4.near
  27.4 0.7 collective-permute-start.6
  28.1 3.4 %collective-permute-start.7 = (bf16[256,512]{1,0:T(8,128)(2,1)S(1)}, bf16[256,512]{1,0:T(8,128)(2,1)S(1)}, u32[]{:S(2)}, u32[]{:S(2)}) collective-permute-start(bf16[256,512]{1,0:T(8,128)(2,1)S(1)} %collective-permute-done.3.points), channel_id=1, source_target_pairs={{4,0},{5,1},{6,2},{7,3},{8,4},{9,5},{10,6},{11,7},{12,8},{13,9},{1... | collective-permute-start | bytes 786440 | tf_op jit(solution)/shard_map/ppermute | solution.py:30
  31.5 0.0 collective-permute-done.6.far
  31.5 1.3 %shard_map.31 = (bf16[1024,512]{1,0:T(8,128)(2,1)S(1)}, bf16[512,1024]{1,0:T(8,128)(2,1)S(1)}, bf16[256,256]{1,0:T(8,128)(2,1)S(1)}, bf16[256,256]{1,0:T(8,128)(2,1)S(1)}) custom-call(bf16[512,512]{1,0:T(8,128)(2,1)S(1)} %collective-permute-done.4.near, bf16[512,512]{1,0:T(8,128)(2,1)S(1)} %collective-permute-done.6.far, ...), custom_call_target="tpu_custom_call" | custom-call | flops 805306368 | bytes 4194304 | tf_op jit(solution)/shard_map/pallas_call | solution.py:195
  32.8 2.4 %shard_map.32 = (bf16[256,256]{1,0:T(8,128)(2,1)S(1)}, bf16[256,256]{1,0:T(8,128)(2,1)S(1)}) custom-call(bf16[256,512]{1,0:T(8,128)(2,1)S(1)} %collective-permute-done.points, bf16[2048,512]{1,0:T(8,128)(2,1)S(1)} %get-tuple-element.59.refs_0_, bf16[1024,512]{1,0:T(8,128)(2,1)S(1)} %get-tuple-element.60.refs_1_, ...), custom_call_target="tpu_custom_call" | custom-call | flops 2147483648 | bytes 8388608 | tf_op jit(solution)/shard_map/pallas_call | solution.py:227
  35.2 1.9 %collective-permute-done.7.points = bf16[256,512]{1,0:T(8,128)(2,1)S(1)} collective-permute-done((bf16[256,512]{1,0:T(8,128)(2,1)S(1)}, bf16[256,512]{1,0:T(8,128)(2,1)S(1)}, u32[]{:S(2)}, u32[]{:S(2)}) %collective-permute-start.7) | collective-permute-done | bytes 262176 | tf_op jit(solution)/shard_map/ppermute | solution.py:30
  37.2 3.4 %collective-permute-start.8 = (bf16[256,512]{1,0:T(8,128)(2,1)S(1)}, bf16[256,512]{1,0:T(8,128)(2,1)S(1)}, u32[]{:S(2)}, u32[]{:S(2)}) collective-permute-start(bf16[256,512]{1,0:T(8,128)(2,1)S(1)} %collective-permute-done.7.points), channel_id=1, source_target_pairs={{4,0},{5,1},{6,2},{7,3},{8,4},{9,5},{10,6},{11,7},{12,8},{13,9},{1... | collective-permute-start | bytes 786440 | tf_op jit(solution)/shard_map/ppermute | solution.py:30
  40.6 2.4 %shard_map.34 = (bf16[256,256]{1,0:T(8,128)(2,1)S(1)}, bf16[256,256]{1,0:T(8,128)(2,1)S(1)}) custom-call(bf16[256,512]{1,0:T(8,128)(2,1)S(1)} %collective-permute-done.7.points, bf16[2048,512]{1,0:T(8,128)(2,1)S(1)} %get-tuple-element.59.refs_0_, bf16[1024,512]{1,0:T(8,128)(2,1)S(1)} %get-tuple-element.60.refs_1_, ...), custom_call_target="tpu_custom_call" | custom-call | flops 2147483648 | bytes 8388608 | tf_op jit(solution)/shard_map/pallas_call | solution.py:227
  43.0 1.2 %collective-permute-start.12 = (bf16[256,256]{1,0:T(8,128)(2,1)S(1)}, bf16[256,256]{1,0:T(8,128)(2,1)S(1)}, u32[]{:S(2)}, u32[]{:S(2)}) collective-permute-start(bf16[256,256]{1,0:T(8,128)(2,1)S(1)} %get-tuple-element.75), channel_id=1, source_target_pairs={{1,0},{0,1},{3,2},{2,3},{5,4},{4,5},{7,6},{6,7},{9,8},{8,9},{11,10... | collective-permute-start | bytes 393224 | tf_op jit(solution)/shard_map/ppermute | solution.py:30
  44.2 2.4 %shard_map.33 = (bf16[256,256]{1,0:T(8,128)(2,1)S(1)}, bf16[256,256]{1,0:T(8,128)(2,1)S(1)}) custom-call(bf16[256,512]{1,0:T(8,128)(2,1)S(1)} %collective-permute-done.3.points, bf16[2048,512]{1,0:T(8,128)(2,1)S(1)} %get-tuple-element.59.refs_0_, bf16[1024,512]{1,0:T(8,128)(2,1)S(1)} %get-tuple-element.60.refs_1_, ...), custom_call_target="tpu_custom_call" | custom-call | flops 2147483648 | bytes 8388608 | tf_op jit(solution)/shard_map/pallas_call | solution.py:227
  46.6 0.1 collective-permute-start.11
  46.7 0.5 collective-permute-start.10
  47.2 0.1 collective-permute-start.9
  47.3 0.0 collective-permute-done.8.points
  47.3 2.4 %shard_map.35 = (bf16[256,256]{1,0:T(8,128)(2,1)S(1)}, bf16[256,256]{1,0:T(8,128)(2,1)S(1)}) custom-call(bf16[256,512]{1,0:T(8,128)(2,1)S(1)} %collective-permute-done.8.points, bf16[2048,512]{1,0:T(8,128)(2,1)S(1)} %get-tuple-element.59.refs_0_, bf16[1024,512]{1,0:T(8,128)(2,1)S(1)} %get-tuple-element.60.refs_1_, ...), custom_call_target="tpu_custom_call" | custom-call | flops 2147483648 | bytes 8388608 | tf_op jit(solution)/shard_map/pallas_call | solution.py:227
  49.8 0.5 collective-permute-start.13
  50.3 0.0 collective-permute-done.12.refs_8_
  50.3 0.0 collective-permute-done.11.refs_7_
  50.3 0.0 collective-permute-done.10.refs_6_
  50.3 0.0 collective-permute-done.9.refs_5_
  50.3 1.0 %collective-permute-done.13.refs_9_ = bf16[256,256]{1,0:T(8,128)(2,1)S(1)} collective-permute-done((bf16[256,256]{1,0:T(8,128)(2,1)S(1)}, bf16[256,256]{1,0:T(8,128)(2,1)S(1)}, u32[]{:S(2)}, u32[]{:S(2)}) %collective-permute-start.13) | collective-permute-done | bytes 131104 | tf_op jit(solution)/shard_map/ppermute | solution.py:30
  51.2 0.1 shard_map.36
  51.3 23.3 %all_to_all.5.pieces = bf16[8,9,32,256]{3,2,1,0:T(8,128)(2,1)S(1)} all-to-all(bf16[8,9,32,256]{3,2,1,0:T(8,128)(2,1)S(1)} %shard_map.36), channel_id=1, replica_groups=mesh['env'=8,'sp'=32] {'env'}, dimensions={0} | all-to-all | bytes 2359296 | tf_op jit(solution)/shard_map/all_to_all | solution.py:242
  74.7 1.0 %shard_map.37 = f32[17,32,256]{2,1,0:T(8,128)} custom-call(bf16[8,9,32,256]{3,2,1,0:T(8,128)(2,1)S(1)} %all_to_all.5.pieces), custom_call_target="tpu_custom_call" | custom-call | bytes 2097152 | tf_op jit(solution)/shard_map/pallas_call | solution.py:243
Async XLA Ops:
  0.0 1.6 %copy-start = (bf16[2048,512]{1,0:T(8,128)(2,1)S(1)}, bf16[2048,512]{1,0:T(8,128)(2,1)}, u32[]{:S(2)}) copy-start(bf16[2048,512]{1,0:T(8,128)(2,1)} %own_env.1) | copy-start | bytes 6291460
  1.6 2.2 %copy-start.1 = (bf16[256,512]{1,0:T(8,128)(2,1)S(1)}, bf16[256,512]{1,0:T(8,128)(2,1)}, u32[]{:S(2)}) copy-start(bf16[256,512]{1,0:T(8,128)(2,1)} %own_points.1) | copy-start | bytes 786436
  1.7 15.7 %collective-permute-start.1 = (bf16[512,512]{1,0:T(8,128)(2,1)S(1)}, bf16[512,512]{1,0:T(8,128)(2,1)S(1)}, u32[]{:S(2)}, u32[]{:S(2)}) collective-permute-start(bf16[512,512]{1,0:T(8,128)(2,1)S(1)} %get-tuple-element.41), channel_id=1, source_target_pairs={{32,0},{97,1},{34,2},{99,3},{36,4},{101,5},{38,6},{103,7},{40,8},{... | collective-permute-start | bytes 1572872 | tf_op jit(solution)/shard_map/ppermute | solution.py:30
  3.8 7.8 %collective-permute-start.2 = (bf16[256,512]{1,0:T(8,128)(2,1)S(1)}, bf16[256,512]{1,0:T(8,128)(2,1)S(1)}, u32[]{:S(2)}, u32[]{:S(2)}) collective-permute-start(bf16[256,512]{1,0:T(8,128)(2,1)S(1)} %copy-done.1), channel_id=1, source_target_pairs={{1,0},{0,1},{3,2},{2,3},{5,4},{4,5},{7,6},{6,7},{9,8},{8,9},{11,10... | collective-permute-start | bytes 786440 | tf_op jit(solution)/shard_map/ppermute | solution.py:30
  6.0 11.3 %collective-permute-start = (bf16[256,512]{1,0:T(8,128)(2,1)S(1)}, bf16[256,512]{1,0:T(8,128)(2,1)S(1)}, u32[]{:S(2)}, u32[]{:S(2)}) collective-permute-start(bf16[256,512]{1,0:T(8,128)(2,1)S(1)} %copy-done.1), channel_id=1, source_target_pairs={{4,0},{5,1},{6,2},{7,3},{8,4},{9,5},{10,6},{11,7},{12,8},{13,9},{1... | collective-permute-start | bytes 786440 | tf_op jit(solution)/shard_map/ppermute | solution.py:30
  17.4 4.2 %collective-permute-start.5 = (bf16[512,512]{1,0:T(8,128)(2,1)S(1)}, bf16[512,512]{1,0:T(8,128)(2,1)S(1)}, u32[]{:S(2)}, u32[]{:S(2)}) collective-permute-start(bf16[512,512]{1,0:T(8,128)(2,1)S(1)} %collective-permute-done.1.near), channel_id=1, source_target_pairs={{1,0},{0,1},{3,2},{2,3},{5,4},{4,5},{7,6},{6,7},{9,8},{8,9},{11,10... | collective-permute-start | bytes 1572872 | tf_op jit(solution)/shard_map/ppermute | solution.py:30
  18.1 9.2 %collective-permute-start.4 = (bf16[512,512]{1,0:T(8,128)(2,1)S(1)}, bf16[512,512]{1,0:T(8,128)(2,1)S(1)}, u32[]{:S(2)}, u32[]{:S(2)}) collective-permute-start(bf16[512,512]{1,0:T(8,128)(2,1)S(1)} %get-tuple-element.48), channel_id=1, source_target_pairs={{32,0},{97,1},{34,2},{99,3},{36,4},{101,5},{38,6},{103,7},{40,8},{... | collective-permute-start | bytes 1572872 | tf_op jit(solution)/shard_map/ppermute | solution.py:30
  18.4 8.4 %collective-permute-start.3 = (bf16[256,512]{1,0:T(8,128)(2,1)S(1)}, bf16[256,512]{1,0:T(8,128)(2,1)S(1)}, u32[]{:S(2)}, u32[]{:S(2)}) collective-permute-start(bf16[256,512]{1,0:T(8,128)(2,1)S(1)} %collective-permute-done.points), channel_id=1, source_target_pairs={{4,0},{5,1},{6,2},{7,3},{8,4},{9,5},{10,6},{11,7},{12,8},{13,9},{1... | collective-permute-start | bytes 786440 | tf_op jit(solution)/shard_map/ppermute | solution.py:30
  27.4 4.1 %collective-permute-start.6 = (bf16[512,512]{1,0:T(8,128)(2,1)S(1)}, bf16[512,512]{1,0:T(8,128)(2,1)S(1)}, u32[]{:S(2)}, u32[]{:S(2)}) collective-permute-start(bf16[512,512]{1,0:T(8,128)(2,1)S(1)} %collective-permute-done.4.near), channel_id=1, source_target_pairs={{1,0},{0,1},{3,2},{2,3},{5,4},{4,5},{7,6},{6,7},{9,8},{8,9},{11,10... | collective-permute-start | bytes 1572872 | tf_op jit(solution)/shard_map/ppermute | solution.py:30
  28.1 9.1 %collective-permute-start.7 = (bf16[256,512]{1,0:T(8,128)(2,1)S(1)}, bf16[256,512]{1,0:T(8,128)(2,1)S(1)}, u32[]{:S(2)}, u32[]{:S(2)}) collective-permute-start(bf16[256,512]{1,0:T(8,128)(2,1)S(1)} %collective-permute-done.3.points), channel_id=1, source_target_pairs={{4,0},{5,1},{6,2},{7,3},{8,4},{9,5},{10,6},{11,7},{12,8},{13,9},{1... | collective-permute-start | bytes 786440 | tf_op jit(solution)/shard_map/ppermute | solution.py:30
  37.2 10.2 %collective-permute-start.8 = (bf16[256,512]{1,0:T(8,128)(2,1)S(1)}, bf16[256,512]{1,0:T(8,128)(2,1)S(1)}, u32[]{:S(2)}, u32[]{:S(2)}) collective-permute-start(bf16[256,512]{1,0:T(8,128)(2,1)S(1)} %collective-permute-done.7.points), channel_id=1, source_target_pairs={{4,0},{5,1},{6,2},{7,3},{8,4},{9,5},{10,6},{11,7},{12,8},{13,9},{1... | collective-permute-start | bytes 786440 | tf_op jit(solution)/shard_map/ppermute | solution.py:30
  43.0 7.3 %collective-permute-start.12 = (bf16[256,256]{1,0:T(8,128)(2,1)S(1)}, bf16[256,256]{1,0:T(8,128)(2,1)S(1)}, u32[]{:S(2)}, u32[]{:S(2)}) collective-permute-start(bf16[256,256]{1,0:T(8,128)(2,1)S(1)} %get-tuple-element.75), channel_id=1, source_target_pairs={{1,0},{0,1},{3,2},{2,3},{5,4},{4,5},{7,6},{6,7},{9,8},{8,9},{11,10... | collective-permute-start | bytes 393224 | tf_op jit(solution)/shard_map/ppermute | solution.py:30
  46.6 3.6 %collective-permute-start.11 = (bf16[256,256]{1,0:T(8,128)(2,1)S(1)}, bf16[256,256]{1,0:T(8,128)(2,1)S(1)}, u32[]{:S(2)}, u32[]{:S(2)}) collective-permute-start(bf16[256,256]{1,0:T(8,128)(2,1)S(1)} %get-tuple-element.74), channel_id=1, source_target_pairs={{1,0},{0,1},{3,2},{2,3},{5,4},{4,5},{7,6},{6,7},{9,8},{8,9},{11,10... | collective-permute-start | bytes 393224 | tf_op jit(solution)/shard_map/ppermute | solution.py:30
  46.7 3.5 %collective-permute-start.10 = (bf16[256,256]{1,0:T(8,128)(2,1)S(1)}, bf16[256,256]{1,0:T(8,128)(2,1)S(1)}, u32[]{:S(2)}, u32[]{:S(2)}) collective-permute-start(bf16[256,256]{1,0:T(8,128)(2,1)S(1)} %get-tuple-element.73), channel_id=1, source_target_pairs={{1,0},{0,1},{3,2},{2,3},{5,4},{4,5},{7,6},{6,7},{9,8},{8,9},{11,10... | collective-permute-start | bytes 393224 | tf_op jit(solution)/shard_map/ppermute | solution.py:30
  47.2 3.0 %collective-permute-start.9 = (bf16[256,256]{1,0:T(8,128)(2,1)S(1)}, bf16[256,256]{1,0:T(8,128)(2,1)S(1)}, u32[]{:S(2)}, u32[]{:S(2)}) collective-permute-start(bf16[256,256]{1,0:T(8,128)(2,1)S(1)} %get-tuple-element.72), channel_id=1, source_target_pairs={{1,0},{0,1},{3,2},{2,3},{5,4},{4,5},{7,6},{6,7},{9,8},{8,9},{11,10... | collective-permute-start | bytes 393224 | tf_op jit(solution)/shard_map/ppermute | solution.py:30
  49.8 1.5 %collective-permute-start.13 = (bf16[256,256]{1,0:T(8,128)(2,1)S(1)}, bf16[256,256]{1,0:T(8,128)(2,1)S(1)}, u32[]{:S(2)}, u32[]{:S(2)}) collective-permute-start(bf16[256,256]{1,0:T(8,128)(2,1)S(1)} %get-tuple-element.76), channel_id=1, source_target_pairs={{1,0},{0,1},{3,2},{2,3},{5,4},{4,5},{7,6},{6,7},{9,8},{8,9},{11,10... | collective-permute-start | bytes 393224 | tf_op jit(solution)/shard_map/ppermute | solution.py:30

commit v4 on v3

v4 whole, which is shorter than its diff:
```python
import functools

import jax
import jax.numpy as jnp
from jax import lax
from jax.experimental import pallas as pl
from jax.experimental.pallas import tpu as pltpu
from jax.sharding import PartitionSpec as P


F32, BF16 = jnp.float32, jnp.bfloat16
NT = (((1,), (1,)), ((), ()))
VMEM_LIMIT = 20 * 1024 * 1024


def split_index(i):
    env, sp = divmod(i, 32)
    y_hi, x = divmod(env, 4)
    q, core = divmod(sp, 2)
    z, y_lo = divmod(q, 2)
    return y_hi, x, z, y_lo, core


def join_index(y_hi, x, z, y_lo, core):
    return ((y_hi % 2) * 4 + x % 4) * 32 + ((z % 8) * 2 + y_lo % 2) * 2 + core % 2


def fetch(value, source_of):
    pairs = [(join_index(*source_of(*split_index(i))), i) for i in range(256)]
    return lax.ppermute(value, ("env", "sp"), pairs)


def other_core(y_hi, x, z, y_lo, core):
    return y_hi, x, z, y_lo, 1 - core


def y_partner(y_hi, x, z, y_lo, core):
    return 1 - y_hi, x, z, 1 - y_lo, core


def column(first):
    def source(y_hi, x, z, y_lo, core):
        m = first + x // 2
        if y_hi == 0:
            return y_hi, x, z + m, y_lo, core
        return y_hi, x, z + y_lo + m - 1, 1 - y_lo, core

    return source


def along_x(step):
    def source(y_hi, x, z, y_lo, core):
        return y_hi, x + step, z, y_lo, core

    return source


def unit(values):
    values = values.astype(F32)
    total = jnp.sum(values * values, axis=1, keepdims=True)
    return (values * lax.rsqrt(total + 1e-06)).astype(BF16)


def fourth(products):
    squares = products * products
    return (squares * squares).astype(BF16)


def dot(a, b):
    return lax.dot_general(a, b, NT, preferred_element_type=F32)


CHUNK = 512


def spread(group):
    lanes = lax.broadcasted_iota(jnp.int32, (1, 256), 1)
    return 1.0 + ((lanes + 64 * group) % 256).astype(F32) / 256.0


def weight_row():
    return spread(lax.axis_index("env") % 4) * (16.0 / 16384.0)


def rows_of(points, raw, env_hat, rows_k):
    place = 0
    for ref in raw:
        for start in range(0, ref.shape[0], CHUNK):
            env = unit(ref[start:start + CHUNK, :])
            env_hat[place:place + CHUNK, :] = env
            rows_k[:, place:place + CHUNK] = fourth(dot(points, env))
            place += CHUNK


def piece_kernel(points, out, sem):
    start = pl.multiple_of((lax.axis_index("env") % 2) * 128, 128)
    copy = pltpu.make_async_copy(points.at[pl.ds(start, 128), :], out, sem)
    copy.start()
    copy.wait()


def slice_kernel(descriptors, first_out, second_out, sems):
    start = pl.multiple_of((lax.axis_index("sp") % 2) * 1024, 1024)
    copies = []
    for i, out in enumerate((first_out, second_out)):
        copies.append(pltpu.make_async_copy(descriptors.at[pl.ds(start + 512 * i, 512), :], out, sems.at[i]))
        copies[i].start()
    for copy in copies:
        copy.wait()


def own_kernel(own_env, own_points, sib_points, env_hat, rows_k, gram, points_hat):
    points_hat[:256, :] = unit(own_points[...])
    points_hat[256:, :] = unit(sib_points[...])
    rows_of(points_hat[...], (own_env,), env_hat, rows_k)
    gram[...] = dot(rows_k[...], rows_k[:256, :])


def more_kernel(near, far, points_hat, gram, env_hat, rows_k, gram_out):
    rows_of(points_hat[...], (near, far), env_hat, rows_k)
    gram_out[...] = gram[...] + dot(rows_k[...], rows_k[:256, :])


def quarter_kernel(first, second, out):
    out[:128, :] = unit(first[...])
    out[128:, :] = unit(second[...])


def column_kernel(points, env_a, env_b, rows_a, rows_b, gram, kept):
    total, place = None, 0
    for env in (env_a, env_b):
        for start in range(0, env.shape[0], CHUNK):
            kept[:, place:place + CHUNK] = fourth(dot(points[...], env[start:start + CHUNK, :]))
            place += CHUNK
    size = env_a.shape[0]
    gram[...] = dot(rows_a[...], kept[:, :size]) + dot(rows_b[...], kept[:, size:])


def last_kernel(near, far, points_hat, *refs):
    grams, quarters, own_out, sib_out, env_hat, rows_k, kept = refs[:5], refs[5:9], *refs[9:]
    rows_of(points_hat[...], (near, far), env_hat, rows_k)
    weight = weight_row()
    for t in range(5):
        if t == 0:
            columns = rows_k[:256, :]
        else:
            for start in range(0, env_hat.shape[0], CHUNK):
                kept[:, start:start + CHUNK] = fourth(dot(quarters[t - 1][...], env_hat[start:start + CHUNK, :]))
            columns = kept[...]
        total = ((grams[t][...] + dot(rows_k[...], columns)) * weight).astype(BF16)
        own_out[t] = total[:256]
        sib_out[t] = total[256:]


def pack_kernel(own, swapped, out):
    x = lax.axis_index("env") % 4
    shift = jnp.logical_and(lax.axis_index("env") < 4, lax.axis_index("sp") % 2 == 0)
    for e in range(8):
        rows = slice(32 * e, 32 * e + 32)
        out[e, 0] = own[0, rows, :]
        for v in range(4):
            out[e, 1 + v] = own[1 + v, rows, :]
            out[e, 5 + v, :, :128] = swapped[1 + v, rows, :128]
            start = jnp.where(x % 2 == v % 2, swapped[0, rows, :128], swapped[0, rows, 128:])
            instead = jnp.logical_and(shift, (x + v) % 4 >= 2)
            out[e, 5 + v, :, 128:] = jnp.where(instead, start, swapped[1 + v, rows, 128:])


def finish_kernel(pieces, out):
    core = lax.axis_index("sp") % 2
    inverse = [1.0 / spread(x) for x in range(4)]

    def total(odd, which, side, base, lanes, weight_lanes):
        value = None
        for x in range(4):
            slot = base + (2 * which + side - x) % 4
            term = pieces[4 * odd + x, slot, :, lanes].astype(F32) * inverse[x][:, weight_lanes]
            value = term if value is None else value + term
        return value

    value = None
    for x in range(4):
        term = pieces[x, 0].astype(F32) * inverse[x]
        value = term if value is None else value + term
    out[0] = value
    for m in range(1, 5):
        which, part = (m - 1) % 2, (m - 1) // 2
        lanes = slice(128 * part, 128 * part + 128)
        for side in range(2):
            place = slice(128 * side, 128 * side + 128)
            out[4 * m, :, place] = total(0, which, side, 1, lanes, lanes)
            out[4 * m - 2, :, place] = total(1, which, side, 1, lanes, lanes)
            out[4 * m - 1 - 2 * core, :, place] = total(1, which, side, 5, lanes, lanes)
            if m < 4:
                out[4 * m + 1 - 2 * core, :, place] = total(0, which, side, 5, lanes, lanes)
            else:

                @pl.when(core == 0)
                def _(which=which, side=side, lanes=lanes, place=place):
                    out[1, :, place] = total(0, which, side, 5, lanes, place)

                @pl.when(core == 1)
                def _(which=which, side=side, lanes=lanes, place=place):
                    out[15, :, place] = total(0, which, side, 5, lanes, lanes)


def vmem_spec():
    return pl.BlockSpec(memory_space=pltpu.VMEM)


def shape(*dims, dtype=BF16):
    return jax.ShapeDtypeStruct(dims, dtype)


def call(body, out_shape, n_in, flops, bytes_accessed, scratch=(), in_place=False):
    many = isinstance(out_shape, (tuple, list))
    return pl.pallas_call(
        body,
        out_shape=out_shape,
        in_specs=[pl.BlockSpec(memory_space=pl.ANY) if in_place else vmem_spec() for _ in range(n_in)],
        out_specs=[vmem_spec() for _ in out_shape] if many else vmem_spec(),
        scratch_shapes=scratch,
        compiler_params=pltpu.CompilerParams(vmem_limit_bytes=VMEM_LIMIT),
        cost_estimate=pl.CostEstimate(flops=flops, bytes_accessed=bytes_accessed, transcendentals=0),
    )


def on_device(descriptors, sparse_points):
    barrier = lax.optimization_barrier

    def rows(body, envs, sums, n_in, *args):
        return call(body, (shape(envs, 512), shape(512, envs)) + sums, n_in, envs * 786432, envs << 12)(*args)

    gram_shape = shape(512, 256, dtype=F32)

    sib_points = fetch(sparse_points, other_core)
    piece = call(piece_kernel, shape(128, 512), 1, 0, 1 << 18, (pltpu.SemaphoreType.DMA,), True)(sparse_points)
    first, second = fetch(piece, column(1)), fetch(piece, column(3))
    low, high = call(
        slice_kernel, (shape(512, 512), shape(512, 512)), 1, 0, 1 << 21, (pltpu.SemaphoreType.DMA((2,)),), True
    )(descriptors)
    near = fetch(low, y_partner)
    env_a, rows_a, gram, points_hat = rows(
        own_kernel, 2048, (gram_shape, shape(512, 512)), 3, descriptors, sparse_points, sib_points
    )
    first, second, near, high, env_a, rows_a, gram, points_hat = barrier(
        (first, second, near, high, env_a, rows_a, gram, points_hat)
    )

    near_b = fetch(high, y_partner)
    quarter = call(quarter_kernel, shape(256, 512), 2, 1 << 20, 1 << 19)(first, second)
    quarters = [quarter] + [fetch(quarter, along_x(step)) for step in range(1, 4)]
    env_b, rows_b, gram = rows(more_kernel, 1024, (gram_shape,), 4, near, fetch(near, other_core), points_hat, gram)
    grams = [gram]
    for points in quarters:
        grams.append(
            call(column_kernel, gram_shape, 5, 2 * 805306368, 1 << 23, (pltpu.VMEM((256, 3072), BF16),))(
                points, env_a, env_b, rows_a, rows_b
            )
        )
    near_b, grams[1], grams[2] = barrier((near_b, grams[1], grams[2]))
    scratch = (pltpu.VMEM((1024, 512), BF16), pltpu.VMEM((512, 1024), BF16), pltpu.VMEM((256, 1024), BF16))
    own, sib = call(last_kernel, (shape(5, 256, 256), shape(5, 256, 256)), 12, 2 * 1744830464, 1 << 23, scratch)(
        near_b, fetch(near_b, other_core), points_hat, *grams, *quarters
    )

    packed = call(pack_kernel, shape(8, 9, 32, 256), 2, 0, 1 << 21)(own, fetch(sib, other_core))
    pieces = lax.all_to_all(packed, "env", 0, 0, tiled=True)
    return call(finish_kernel, shape(17, 32, 256, dtype=F32), 1, 0, 1 << 21)(pieces)[None]


def solution(mesh):
    placed = (P("env", None), P("sp", None))
    return jax.shard_map(
        on_device, mesh=mesh, in_specs=placed, out_specs=P("sp", None, "env", None), check_vma=False
    )
```

time: 75.8 us -> 84.4 us (1.11)
  waiting for transfers between devices: 10.9 us -> 20 us
  local copies, waits for them, and re-layouts: 1.59 us -> 2.54 us
  blocking collectives: 23.3 us -> 22.4 us
  starting transfers between devices: 24.1 us -> 23.2 us
    ppermute x14 -> x11, waiting for transfers between devices: 10.9 us -> 20 us  [fetch(): return lax.ppermute(value, ('env', 'sp'), pairs)]
    pallas_call x5 -> x8, Pallas kernels: 9.7 us -> 11.3 us  [the longest x4 7.3 us: on_device(): call(column_kernel, gram_shape, 5, 2 * 805306368, 1 << 23, (pltpu.VMEM((2...]
    pallas_call x3 -> x2, Pallas kernels: 4.83 us -> 3.53 us  [rows(): call(body, (shape(envs, 512), shape(512, envs)) + sums, n_in, envs * 7864...]
    unnamed x4 -> x6, local copies, waits for them, and re-layouts: 1.59 us -> 2.54 us
    all_to_all x1, blocking collectives: 23.3 us -> 22.4 us  [on_device(): pieces = lax.all_to_all(packed, 'env', 0, 0, tiled=True)]
    ppermute x14 -> x11, starting transfers between devices: 24.1 us -> 23.2 us  [fetch(): return lax.ppermute(value, ('env', 'sp'), pairs)]
  transfers between devices with their start and end apart: 14 -> 11, of which waited for: 5 -> 6; matrix products, arithmetic and copies ran while one was open for 0% -> 0% of each run, Pallas kernels for 19% -> 13%
where the time goes in v4:
time: 84.4 us; the launch traced here: 84.2 us
  starting transfers between devices  23.2 us (27%)
  blocking collectives  22.4 us (27%)
  waiting for transfers between devices  20 us (24%)
  Pallas kernels  15.9 us (19%)
  local copies, waits for them, and re-layouts  2.54 us (3%)
    ppermute x11, starting transfers between devices, fetch(): return lax.ppermute(value, ('env', 'sp'), pairs)  23.2 us
    all_to_all x1, blocking collectives, on_device(): pieces = lax.all_to_all(packed, 'env', 0, 0, tiled=True)  22.4 us
    ppermute x11, waiting for transfers between devices, fetch(): return lax.ppermute(value, ('env', 'sp'), pairs)  20 us
    pallas_call x4, Pallas kernels, on_device(): call(column_kernel, gram_shape, 5, 2 * 805306368, 1 << 23, (pltpu.VMEM((2...  7.3 us
    pallas_call x1, Pallas kernels, on_device(): call(last_kernel, (shape(5, 256, 256), shape(5, 256, 256)), 12, 2 * 17448...  3.58 us
    pallas_call x2, Pallas kernels, rows(): call(body, (shape(envs, 512), shape(512, envs)) + sums, n_in, envs * 7864...  3.53 us
    unnamed x6, local copies, waits for them, and re-layouts  2.54 us
  transfers between devices with their start and end apart: 11, of which 6 were waited for; matrix products, arithmetic and copies ran while one was open for 0% of the time, Pallas kernels for 13%

profile of v4, /device:TPU:1, one launch (start us, length us, event | category | flops | bytes accessed | tf_op | source)
XLA Modules:
  0.0 84.2 jit_solution(11963685584452179440)
XLA Ops:
  0.0 0.0 copy-start
  0.0 1.6 %copy-done = bf16[2048,512]{1,0:T(8,128)(2,1)S(1)} copy-done((bf16[2048,512]{1,0:T(8,128)(2,1)S(1)}, bf16[2048,512]{1,0:T(8,128)(2,1)}, u32[]{:S(2)}) %copy-start) | copy-done | bytes 2097176
  1.6 0.0 copy-start.1
  1.6 0.1 shard_map.29
  1.7 3.7 %collective-permute-start.2 = (bf16[512,512]{1,0:T(8,128)(2,1)S(1)}, bf16[512,512]{1,0:T(8,128)(2,1)S(1)}, u32[]{:S(2)}, u32[]{:S(2)}) collective-permute-start(bf16[512,512]{1,0:T(8,128)(2,1)S(1)} %get-tuple-element.27), channel_id=1, source_target_pairs={{130,0},{131,1},{128,2},{129,3},{134,4},{135,5},{132,6},{133,7},{1... | collective-permute-start | bytes 1572872 | tf_op jit(solution)/shard_map/ppermute | solution.py:30
  5.3 1.0 %collective-permute-start.3 = (bf16[256,512]{1,0:T(8,128)(2,1)}, bf16[256,512]{1,0:T(8,128)(2,1)S(1)}, u32[]{:S(2)}, u32[]{:S(2)}) collective-permute-start(bf16[256,512]{1,0:T(8,128)(2,1)} %own_points.1), channel_id=1, source_target_pairs={{1,0},{0,1},{3,2},{2,3},{5,4},{4,5},{7,6},{6,7},{9,8},{8,9},{11,10... | collective-permute-start | bytes 786440 | tf_op jit(solution)/shard_map/ppermute | solution.py:30
  6.3 0.0 copy-start.2
  6.3 0.9 %copy-done.2 = bf16[256,512]{1,0:T(8,128)(2,1)S(1)} copy-done((bf16[256,512]{1,0:T(8,128)(2,1)S(1)}, bf16[256,512]{1,0:T(8,128)(2,1)}, u32[]{:S(2)}) %copy-start.2) | copy-done | bytes 262168
  7.3 0.1 shard_map.28
  7.4 6.5 %collective-permute-start.1 = (bf16[128,512]{1,0:T(8,128)(2,1)S(1)}, bf16[128,512]{1,0:T(8,128)(2,1)S(1)}, u32[]{:S(2)}, u32[]{:S(2)}) collective-permute-start(bf16[128,512]{1,0:T(8,128)(2,1)S(1)} %shard_map.28), channel_id=1, source_target_pairs={{12,0},{13,1},{14,2},{15,3},{16,4},{17,5},{18,6},{19,7},{20,8},{21... | collective-permute-start | bytes 393224 | tf_op jit(solution)/shard_map/ppermute | solution.py:30
  13.9 0.7 collective-permute-start
  14.7 0.0 collective-permute-done.3.sib_points
  14.7 0.0 copy-done.1
  14.7 2.2 %shard_map.30 = (bf16[2048,512]{1,0:T(8,128)(2,1)S(1)}, bf16[512,2048]{1,0:T(8,128)(2,1)S(1)}, f32[512,256]{1,0:T(8,128)S(1)}, bf16[512,512]{1,0:T(8,128)(2,1)S(1)}) custom-call(bf16[2048,512]{1,0:T(8,128)(2,1)S(1)} %copy-done.1, bf16[256,512]{1,0:T(8,128)(2,1)S(1)} %copy-done.2, bf16[256,512]{1,0:T(8,128)(2,1)S(1)} %collective-permute-done.3.sib_points), custom_call_target="tpu_custom_call" | custom-call | flops 1610612736 | bytes 8388608 | tf_op jit(solution)/shard_map/pallas_call | solution.py:232
  16.9 5.6 %collective-permute-done.1.second = bf16[128,512]{1,0:T(8,128)(2,1)S(1)} collective-permute-done((bf16[128,512]{1,0:T(8,128)(2,1)S(1)}, bf16[128,512]{1,0:T(8,128)(2,1)S(1)}, u32[]{:S(2)}, u32[]{:S(2)}) %collective-permute-start.1) | collective-permute-done | bytes 131104 | tf_op jit(solution)/shard_map/ppermute | solution.py:30
  22.5 2.8 %collective-permute-done.first = bf16[128,512]{1,0:T(8,128)(2,1)S(1)} collective-permute-done((bf16[128,512]{1,0:T(8,128)(2,1)S(1)}, bf16[128,512]{1,0:T(8,128)(2,1)S(1)}, u32[]{:S(2)}, u32[]{:S(2)}) %collective-permute-start) | collective-permute-done | bytes 131104 | tf_op jit(solution)/shard_map/ppermute | solution.py:30
  25.3 0.0 collective-permute-done.2.near
  25.3 0.8 collective-permute-start.5
  26.1 0.8 collective-permute-start.4
  26.9 0.1 shard_map.31.points.refs_5_
  27.1 3.8 %collective-permute-start.6 = (bf16[256,512]{1,0:T(8,128)(2,1)S(1)}, bf16[256,512]{1,0:T(8,128)(2,1)S(1)}, u32[]{:S(2)}, u32[]{:S(2)}) collective-permute-start(bf16[256,512]{1,0:T(8,128)(2,1)S(1)} %shard_map.31.points.refs_5_), channel_id=1, source_target_pairs={{32,0},{33,1},{34,2},{35,3},{36,4},{37,5},{38,6},{39,7},{40,8},{41... | collective-permute-start | bytes 786440 | tf_op jit(solution)/shard_map/ppermute | solution.py:30
  30.9 0.0 collective-permute-start.9
  30.9 0.0 collective-permute-done.5.far
  30.9 1.3 %shard_map.32 = (bf16[1024,512]{1,0:T(8,128)(2,1)S(1)}, bf16[512,1024]{1,0:T(8,128)(2,1)S(1)}, f32[512,256]{1,0:T(8,128)S(1)}) custom-call(bf16[512,512]{1,0:T(8,128)(2,1)S(1)} %collective-permute-done.2.near, bf16[512,512]{1,0:T(8,128)(2,1)S(1)} %collective-permute-done.5.far, bf16[512,512]{1,0:T(8,128)(2,1)S(1)} %get-tuple-element.38.points_hat, ...), custom_call_target="tpu_custom_call" | custom-call | flops 805306368 | bytes 4194304 | tf_op jit(solution)/shard_map/pallas_call | solution.py:232
  32.2 1.8 %shard_map.33.refs_1_ = f32[512,256]{1,0:T(8,128)S(1)} custom-call(bf16[256,512]{1,0:T(8,128)(2,1)S(1)} %shard_map.31.points.refs_5_, bf16[2048,512]{1,0:T(8,128)(2,1)S(1)} %get-tuple-element.36.env_a, bf16[1024,512]{1,0:T(8,128)(2,1)S(1)} %get-tuple-element.40.env_b, bf16[512,2048]{1,0:T(8,128)(2,1)S(1)} %get-tuple-element.41.rows_a, ...), custom_call_target="tpu_custom_call" | custom-call | flops 1610612736 | bytes 8388608 | tf_op jit(solution)/shard_map/pallas_call | solution.py:257
  34.0 2.3 %collective-permute-done.6.points.refs_6_ = bf16[256,512]{1,0:T(8,128)(2,1)S(1)} collective-permute-done((bf16[256,512]{1,0:T(8,128)(2,1)S(1)}, bf16[256,512]{1,0:T(8,128)(2,1)S(1)}, u32[]{:S(2)}, u32[]{:S(2)}) %collective-permute-start.6) | collective-permute-done | bytes 262176 | tf_op jit(solution)/shard_map/ppermute | solution.py:30
  36.3 1.8 %shard_map.34.refs_2_ = f32[512,256]{1,0:T(8,128)S(1)} custom-call(bf16[256,512]{1,0:T(8,128)(2,1)S(1)} %collective-permute-done.6.points.refs_6_, bf16[2048,512]{1,0:T(8,128)(2,1)S(1)} %get-tuple-element.36.env_a, bf16[1024,512]{1,0:T(8,128)(2,1)S(1)} %get-tuple-element.40.env_b, bf16[512,2048]{1,0:T(8,128)(2,1)S(1)} %get-tuple-element.41.rows_a, ...), custom_call_target="tpu_custom_call" | custom-call | flops 1610612736 | bytes 8388608 | tf_op jit(solution)/shard_map/pallas_call | solution.py:257
  38.1 2.7 %collective-permute-done.4.near = bf16[512,512]{1,0:T(8,128)(2,1)S(1)} collective-permute-done((bf16[512,512]{1,0:T(8,128)(2,1)S(1)}, bf16[512,512]{1,0:T(8,128)(2,1)S(1)}, u32[]{:S(2)}, u32[]{:S(2)}) %collective-permute-start.4) | collective-permute-done | bytes 524320 | tf_op jit(solution)/shard_map/ppermute | solution.py:30
  40.9 0.8 collective-permute-start.7
  41.6 4.5 %collective-permute-start.8 = (bf16[256,512]{1,0:T(8,128)(2,1)S(1)}, bf16[256,512]{1,0:T(8,128)(2,1)S(1)}, u32[]{:S(2)}, u32[]{:S(2)}) collective-permute-start(bf16[256,512]{1,0:T(8,128)(2,1)S(1)} %shard_map.31.points.refs_5_), channel_id=1, source_target_pairs={{64,0},{65,1},{66,2},{67,3},{68,4},{69,5},{70,6},{71,7},{72,8},{73... | collective-permute-start | bytes 786440 | tf_op jit(solution)/shard_map/ppermute | solution.py:30
  46.1 0.0 collective-permute-done.9.points.refs_8_
  46.1 1.8 %shard_map.36.refs_4_ = f32[512,256]{1,0:T(8,128)S(1)} custom-call(bf16[256,512]{1,0:T(8,128)(2,1)S(1)} %collective-permute-done.9.points.refs_8_, bf16[2048,512]{1,0:T(8,128)(2,1)S(1)} %get-tuple-element.36.env_a, bf16[1024,512]{1,0:T(8,128)(2,1)S(1)} %get-tuple-element.40.env_b, bf16[512,2048]{1,0:T(8,128)(2,1)S(1)} %get-tuple-element.41.rows_a, ...), custom_call_target="tpu_custom_call" | custom-call | flops 1610612736 | bytes 8388608 | tf_op jit(solution)/shard_map/pallas_call | solution.py:257
  48.0 4.8 %collective-permute-done.8.points.refs_7_ = bf16[256,512]{1,0:T(8,128)(2,1)S(1)} collective-permute-done((bf16[256,512]{1,0:T(8,128)(2,1)S(1)}, bf16[256,512]{1,0:T(8,128)(2,1)S(1)}, u32[]{:S(2)}, u32[]{:S(2)}) %collective-permute-start.8) | collective-permute-done | bytes 262176 | tf_op jit(solution)/shard_map/ppermute | solution.py:30
  52.8 1.8 %shard_map.35.refs_3_ = f32[512,256]{1,0:T(8,128)S(1)} custom-call(bf16[256,512]{1,0:T(8,128)(2,1)S(1)} %collective-permute-done.8.points.refs_7_, bf16[2048,512]{1,0:T(8,128)(2,1)S(1)} %get-tuple-element.36.env_a, bf16[1024,512]{1,0:T(8,128)(2,1)S(1)} %get-tuple-element.40.env_b, bf16[512,2048]{1,0:T(8,128)(2,1)S(1)} %get-tuple-element.41.rows_a, ...), custom_call_target="tpu_custom_call" | custom-call | flops 1610612736 | bytes 8388608 | tf_op jit(solution)/shard_map/pallas_call | solution.py:257
  54.6 0.0 collective-permute-done.7.far
  54.6 3.6 %shard_map.37 = (bf16[5,256,256]{2,1,0:T(8,128)(2,1)S(1)}, bf16[5,256,256]{2,1,0:T(8,128)(2,1)S(1)}) custom-call(bf16[512,512]{1,0:T(8,128)(2,1)S(1)} %collective-permute-done.4.near, bf16[512,512]{1,0:T(8,128)(2,1)S(1)} %collective-permute-done.7.far, bf16[512,512]{1,0:T(8,128)(2,1)S(1)} %get-tuple-element.38.points_hat, ...), custom_call_target="tpu_custom_call" | custom-call | flops 3489660928 | bytes 8388608 | tf_op jit(solution)/shard_map/pallas_call | solution.py:263
  58.2 0.7 collective-permute-start.10
  58.9 1.7 %collective-permute-done.10.swapped = bf16[5,256,256]{2,1,0:T(8,128)(2,1)S(1)} collective-permute-done((bf16[5,256,256]{2,1,0:T(8,128)(2,1)S(1)}, bf16[5,256,256]{2,1,0:T(8,128)(2,1)S(1)}, u32[]{:S(2)}, u32[]{:S(2)}) %collective-permute-start.10) | collective-permute-done | bytes 655392 | tf_op jit(solution)/shard_map/ppermute | solution.py:30
  60.6 0.1 shard_map.38
  60.8 22.4 %all_to_all.5.pieces = bf16[8,9,32,256]{3,2,1,0:T(8,128)(2,1)S(1)} all-to-all(bf16[8,9,32,256]{3,2,1,0:T(8,128)(2,1)S(1)} %shard_map.38), channel_id=1, replica_groups=mesh['env'=8,'sp'=32] {'env'}, dimensions={0} | all-to-all | bytes 2359296 | tf_op jit(solution)/shard_map/all_to_all | solution.py:268
  83.2 1.0 %shard_map.39 = f32[17,32,256]{2,1,0:T(8,128)} custom-call(bf16[8,9,32,256]{3,2,1,0:T(8,128)(2,1)S(1)} %all_to_all.5.pieces), custom_call_target="tpu_custom_call" | custom-call | bytes 2097152 | tf_op jit(solution)/shard_map/pallas_call | solution.py:269
Async XLA Ops:
  0.0 1.6 %copy-start = (bf16[2048,512]{1,0:T(8,128)(2,1)S(1)}, bf16[2048,512]{1,0:T(8,128)(2,1)}, u32[]{:S(2)}) copy-start(bf16[2048,512]{1,0:T(8,128)(2,1)} %own_env.1) | copy-start | bytes 6291460
  1.6 13.1 %copy-start.1 = (bf16[2048,512]{1,0:T(8,128)(2,1)S(1)}, bf16[2048,512]{1,0:T(8,128)(2,1)}, u32[]{:S(2)}) copy-start(bf16[2048,512]{1,0:T(8,128)(2,1)} %own_env.1) | copy-start | bytes 6291460
  1.7 23.6 %collective-permute-start.2 = (bf16[512,512]{1,0:T(8,128)(2,1)S(1)}, bf16[512,512]{1,0:T(8,128)(2,1)S(1)}, u32[]{:S(2)}, u32[]{:S(2)}) collective-permute-start(bf16[512,512]{1,0:T(8,128)(2,1)S(1)} %get-tuple-element.27), channel_id=1, source_target_pairs={{130,0},{131,1},{128,2},{129,3},{134,4},{135,5},{132,6},{133,7},{1... | collective-permute-start | bytes 1572872 | tf_op jit(solution)/shard_map/ppermute | solution.py:30
  5.3 9.3 %collective-permute-start.3 = (bf16[256,512]{1,0:T(8,128)(2,1)}, bf16[256,512]{1,0:T(8,128)(2,1)S(1)}, u32[]{:S(2)}, u32[]{:S(2)}) collective-permute-start(bf16[256,512]{1,0:T(8,128)(2,1)} %own_points.1), channel_id=1, source_target_pairs={{1,0},{0,1},{3,2},{2,3},{5,4},{4,5},{7,6},{6,7},{9,8},{8,9},{11,10... | collective-permute-start | bytes 786440 | tf_op jit(solution)/shard_map/ppermute | solution.py:30
  6.3 0.9 %copy-start.2 = (bf16[256,512]{1,0:T(8,128)(2,1)S(1)}, bf16[256,512]{1,0:T(8,128)(2,1)}, u32[]{:S(2)}) copy-start(bf16[256,512]{1,0:T(8,128)(2,1)} %own_points.1) | copy-start | bytes 786436
  7.4 15.1 %collective-permute-start.1 = (bf16[128,512]{1,0:T(8,128)(2,1)S(1)}, bf16[128,512]{1,0:T(8,128)(2,1)S(1)}, u32[]{:S(2)}, u32[]{:S(2)}) collective-permute-start(bf16[128,512]{1,0:T(8,128)(2,1)S(1)} %shard_map.28), channel_id=1, source_target_pairs={{12,0},{13,1},{14,2},{15,3},{16,4},{17,5},{18,6},{19,7},{20,8},{21... | collective-permute-start | bytes 393224 | tf_op jit(solution)/shard_map/ppermute | solution.py:30
  13.9 11.4 %collective-permute-start = (bf16[128,512]{1,0:T(8,128)(2,1)S(1)}, bf16[128,512]{1,0:T(8,128)(2,1)S(1)}, u32[]{:S(2)}, u32[]{:S(2)}) collective-permute-start(bf16[128,512]{1,0:T(8,128)(2,1)S(1)} %shard_map.28), channel_id=1, source_target_pairs={{4,0},{5,1},{6,2},{7,3},{8,4},{9,5},{10,6},{11,7},{12,8},{13,9},{1... | collective-permute-start | bytes 393224 | tf_op jit(solution)/shard_map/ppermute | solution.py:30
  25.3 5.6 %collective-permute-start.5 = (bf16[512,512]{1,0:T(8,128)(2,1)S(1)}, bf16[512,512]{1,0:T(8,128)(2,1)S(1)}, u32[]{:S(2)}, u32[]{:S(2)}) collective-permute-start(bf16[512,512]{1,0:T(8,128)(2,1)S(1)} %collective-permute-done.2.near), channel_id=1, source_target_pairs={{1,0},{0,1},{3,2},{2,3},{5,4},{4,5},{7,6},{6,7},{9,8},{8,9},{11,10... | collective-permute-start | bytes 1572872 | tf_op jit(solution)/shard_map/ppermute | solution.py:30
  26.1 14.8 %collective-permute-start.4 = (bf16[512,512]{1,0:T(8,128)(2,1)S(1)}, bf16[512,512]{1,0:T(8,128)(2,1)S(1)}, u32[]{:S(2)}, u32[]{:S(2)}) collective-permute-start(bf16[512,512]{1,0:T(8,128)(2,1)S(1)} %get-tuple-element.33), channel_id=1, source_target_pairs={{130,0},{131,1},{128,2},{129,3},{134,4},{135,5},{132,6},{133,7},{1... | collective-permute-start | bytes 1572872 | tf_op jit(solution)/shard_map/ppermute | solution.py:30
  27.1 9.2 %collective-permute-start.6 = (bf16[256,512]{1,0:T(8,128)(2,1)S(1)}, bf16[256,512]{1,0:T(8,128)(2,1)S(1)}, u32[]{:S(2)}, u32[]{:S(2)}) collective-permute-start(bf16[256,512]{1,0:T(8,128)(2,1)S(1)} %shard_map.31.points.refs_5_), channel_id=1, source_target_pairs={{32,0},{33,1},{34,2},{35,3},{36,4},{37,5},{38,6},{39,7},{40,8},{41... | collective-permute-start | bytes 786440 | tf_op jit(solution)/shard_map/ppermute | solution.py:30
  30.9 15.3 %collective-permute-start.9 = (bf16[256,512]{1,0:T(8,128)(2,1)S(1)}, bf16[256,512]{1,0:T(8,128)(2,1)S(1)}, u32[]{:S(2)}, u32[]{:S(2)}) collective-permute-start(bf16[256,512]{1,0:T(8,128)(2,1)S(1)} %shard_map.31.points.refs_5_), channel_id=1, source_target_pairs={{96,0},{97,1},{98,2},{99,3},{100,4},{101,5},{102,6},{103,7},{104,8... | collective-permute-start | bytes 786440 | tf_op jit(solution)/shard_map/ppermute | solution.py:30
  40.9 13.8 %collective-permute-start.7 = (bf16[512,512]{1,0:T(8,128)(2,1)S(1)}, bf16[512,512]{1,0:T(8,128)(2,1)S(1)}, u32[]{:S(2)}, u32[]{:S(2)}) collective-permute-start(bf16[512,512]{1,0:T(8,128)(2,1)S(1)} %collective-permute-done.4.near), channel_id=1, source_target_pairs={{1,0},{0,1},{3,2},{2,3},{5,4},{4,5},{7,6},{6,7},{9,8},{8,9},{11,10... | collective-permute-start | bytes 1572872 | tf_op jit(solution)/shard_map/ppermute | solution.py:30
  41.6 11.2 %collective-permute-start.8 = (bf16[256,512]{1,0:T(8,128)(2,1)S(1)}, bf16[256,512]{1,0:T(8,128)(2,1)S(1)}, u32[]{:S(2)}, u32[]{:S(2)}) collective-permute-start(bf16[256,512]{1,0:T(8,128)(2,1)S(1)} %shard_map.31.points.refs_5_), channel_id=1, source_target_pairs={{64,0},{65,1},{66,2},{67,3},{68,4},{69,5},{70,6},{71,7},{72,8},{73... | collective-permute-start | bytes 786440 | tf_op jit(solution)/shard_map/ppermute | solution.py:30
  58.2 2.4 %collective-permute-start.10 = (bf16[5,256,256]{2,1,0:T(8,128)(2,1)S(1)}, bf16[5,256,256]{2,1,0:T(8,128)(2,1)S(1)}, u32[]{:S(2)}, u32[]{:S(2)}) collective-permute-start(bf16[5,256,256]{2,1,0:T(8,128)(2,1)S(1)} %get-tuple-element.48), channel_id=1, source_target_pairs={{1,0},{0,1},{3,2},{2,3},{5,4},{4,5},{7,6},{6,7},{9,8},{8,9},{11,10... | collective-permute-start | bytes 1966088 | tf_op jit(solution)/shard_map/ppermute | solution.py:30

commit v5 on v4

--- a/solution.py
+++ b/solution.py
@@ -70,7 +70,11 @@
     return lax.dot_general(a, b, NT, preferred_element_type=F32)
 
 
-CHUNK = 512
+FIRST = 768
+
+
+def chunks(rows):
+    return [(start, min(512, rows - start)) for start in range(0, rows, 512)]
 
 
 def spread(group):
@@ -85,28 +89,22 @@
 def rows_of(points, raw, env_hat, rows_k):
     place = 0
     for ref in raw:
-        for start in range(0, ref.shape[0], CHUNK):
-            env = unit(ref[start:start + CHUNK, :])
-            env_hat[place:place + CHUNK, :] = env
-            rows_k[:, place:place + CHUNK] = fourth(dot(points, env))
-            place += CHUNK
-
-
-def piece_kernel(points, out, sem):
+        for start, size in chunks(ref.shape[0]):
+            env = unit(ref[start:start + size, :])
+            env_hat[place:place + size, :] = env
+            rows_k[:, place:place + size] = fourth(dot(points, env))
+            place += size
+
+
+def piece_kernel(points, out):
     start = pl.multiple_of((lax.axis_index("env") % 2) * 128, 128)
-    copy = pltpu.make_async_copy(points.at[pl.ds(start, 128), :], out, sem)
-    copy.start()
-    copy.wait()
-
-
-def slice_kernel(descriptors, first_out, second_out, sems):
-    start = pl.multiple_of((lax.axis_index("sp") % 2) * 1024, 1024)
-    copies = []
-    for i, out in enumerate((first_out, second_out)):
-        copies.append(pltpu.make_async_copy(descriptors.at[pl.ds(start + 512 * i, 512), :], out, sems.at[i]))
-        copies[i].start()
-    for copy in copies:
-        copy.wait()
+    out[...] = points[pl.ds(start, 128), :]
+
+
+def slice_kernel(descriptors, first_out, second_out):
+    half = pl.multiple_of((lax.axis_index("sp") % 2) * 1024, 1024)
+    first_out[...] = descriptors[pl.ds(half, FIRST), :]
+    second_out[...] = descriptors[pl.ds(half + FIRST, 1024 - FIRST), :]
 
 
 def own_kernel(own_env, own_points, sib_points, env_hat, rows_k, gram, points_hat):
@@ -129,9 +127,9 @@
 def column_kernel(points, env_a, env_b, rows_a, rows_b, gram, kept):
     total, place = None, 0
     for env in (env_a, env_b):
-        for start in range(0, env.shape[0], CHUNK):
-            kept[:, place:place + CHUNK] = fourth(dot(points[...], env[start:start + CHUNK, :]))
-            place += CHUNK
+        for start, size in chunks(env.shape[0]):
+            kept[:, place:place + size] = fourth(dot(points[...], env[start:start + size, :]))
+            place += size
     size = env_a.shape[0]
     gram[...] = dot(rows_a[...], kept[:, :size]) + dot(rows_b[...], kept[:, size:])
 
@@ -144,8 +142,8 @@
         if t == 0:
             columns = rows_k[:256, :]
         else:
-            for start in range(0, env_hat.shape[0], CHUNK):
-                kept[:, start:start + CHUNK] = fourth(dot(quarters[t - 1][...], env_hat[start:start + CHUNK, :]))
+            for start, size in chunks(env_hat.shape[0]):
+                kept[:, start:start + size] = fourth(dot(quarters[t - 1][...], env_hat[start:start + size, :]))
             columns = kept[...]
         total = ((grams[t][...] + dot(rows_k[...], columns)) * weight).astype(BF16)
         own_out[t] = total[:256]
@@ -212,12 +210,12 @@
     return jax.ShapeDtypeStruct(dims, dtype)
 
 
-def call(body, out_shape, n_in, flops, bytes_accessed, scratch=(), in_place=False):
+def call(body, out_shape, n_in, flops, bytes_accessed, scratch=()):
     many = isinstance(out_shape, (tuple, list))
     return pl.pallas_call(
         body,
         out_shape=out_shape,
-        in_specs=[pl.BlockSpec(memory_space=pl.ANY) if in_place else vmem_spec() for _ in range(n_in)],
+        in_specs=[vmem_spec() for _ in range(n_in)],
         out_specs=[vmem_spec() for _ in out_shape] if many else vmem_spec(),
         scratch_shapes=scratch,
         compiler_params=pltpu.CompilerParams(vmem_limit_bytes=VMEM_LIMIT),
@@ -234,10 +232,10 @@
     gram_shape = shape(512, 256, dtype=F32)
 
     sib_points = fetch(sparse_points, other_core)
-    piece = call(piece_kernel, shape(128, 512), 1, 0, 1 << 18, (pltpu.SemaphoreType.DMA,), True)(sparse_points)
+    piece = call(piece_kernel, shape(128, 512), 1, 0, 1 << 18)(sparse_points)
     first, second = fetch(piece, column(1)), fetch(piece, column(3))
     low, high = call(
-        slice_kernel, (shape(512, 512), shape(512, 512)), 1, 0, 1 << 21, (pltpu.SemaphoreType.DMA((2,)),), True
+        slice_kernel, (shape(FIRST, 512), shape(1024 - FIRST, 512)), 1, 0, 1 << 21
     )(descriptors)
     near = fetch(low, y_partner)
     env_a, rows_a, gram, points_hat = rows(
@@ -250,16 +248,19 @@
     near_b = fetch(high, y_partner)
     quarter = call(quarter_kernel, shape(256, 512), 2, 1 << 20, 1 << 19)(first, second)
     quarters = [quarter] + [fetch(quarter, along_x(step)) for step in range(1, 4)]
-    env_b, rows_b, gram = rows(more_kernel, 1024, (gram_shape,), 4, near, fetch(near, other_core), points_hat, gram)
+    env_b, rows_b, gram = rows(more_kernel, 2 * FIRST, (gram_shape,), 4, near, fetch(near, other_core), points_hat, gram)
     grams = [gram]
-    for points in quarters:
+    for v, points in enumerate(quarters):
+        if v == 2:
+            near_b, points, grams[1], grams[2] = barrier((near_b, points, grams[1], grams[2]))
+            quarters[2] = points
         grams.append(
-            call(column_kernel, gram_shape, 5, 2 * 805306368, 1 << 23, (pltpu.VMEM((256, 3072), BF16),))(
+            call(column_kernel, gram_shape, 5, (2048 + 2 * FIRST) << 19, 1 << 23, (pltpu.VMEM((256, 2048 + 2 * FIRST), BF16),))(
                 points, env_a, env_b, rows_a, rows_b
             )
         )
-    near_b, grams[1], grams[2] = barrier((near_b, grams[1], grams[2]))
-    scratch = (pltpu.VMEM((1024, 512), BF16), pltpu.VMEM((512, 1024), BF16), pltpu.VMEM((256, 1024), BF16))
+    rest = 2048 - 2 * FIRST
+    scratch = (pltpu.VMEM((rest, 512), BF16), pltpu.VMEM((512, rest), BF16), pltpu.VMEM((256, rest), BF16))
     own, sib = call(last_kernel, (shape(5, 256, 256), shape(5, 256, 256)), 12, 2 * 1744830464, 1 << 23, scratch)(
         near_b, fetch(near_b, other_core), points_hat, *grams, *quarters
     )

time: 84.4 us -> 77.5 us (0.918)
  waiting for transfers between devices: 20 us -> 15.7 us
  starting transfers between devices: 23.2 us -> 20.3 us
    ppermute x11, waiting for transfers between devices: 20 us -> 15.7 us  [fetch(): return lax.ppermute(value, ('env', 'sp'), pairs)]
    ppermute x11, starting transfers between devices: 23.2 us -> 20.3 us  [fetch(): return lax.ppermute(value, ('env', 'sp'), pairs)]
    pallas_call x1, Pallas kernels: 3.58 us -> 2.06 us  [on_device(): call(last_kernel, (shape(5, 256, 256), shape(5, 256, 256)), 12, 2 * 17448...]
    pallas_call x6, Pallas kernels: 7.53 us -> 8.46 us  [the longest x4 8.39 us: on_device(): call(column_kernel, gram_shape, 5, 2048 + 2 * FIRST << 19, 1 << 23, (pltp...]
  transfers between devices with their start and end apart: 11 -> 11, of which waited for: 6 -> 5; matrix products, arithmetic and copies ran while one was open for 0% -> 0% of each run, Pallas kernels for 13% -> 16%
where the time goes in v5:
time: 77.5 us; the launch traced here: 77.4 us
  blocking collectives  22.9 us (30%)
  starting transfers between devices  20.3 us (26%)
  Pallas kernels  15.8 us (20%)
  waiting for transfers between devices  15.7 us (20%)
  local copies, waits for them, and re-layouts  2.54 us (3%)
    all_to_all x1, blocking collectives, on_device(): pieces = lax.all_to_all(packed, 'env', 0, 0, tiled=True)  22.9 us
    ppermute x11, starting transfers between devices, fetch(): return lax.ppermute(value, ('env', 'sp'), pairs)  20.3 us
    ppermute x11, waiting for transfers between devices, fetch(): return lax.ppermute(value, ('env', 'sp'), pairs)  15.7 us
    pallas_call x4, Pallas kernels, on_device(): call(column_kernel, gram_shape, 5, 2048 + 2 * FIRST << 19, 1 << 23, (pltp...  8.39 us
    pallas_call x2, Pallas kernels, rows(): call(body, (shape(envs, 512), shape(512, envs)) + sums, n_in, envs * 7864...  3.95 us
    unnamed x6, local copies, waits for them, and re-layouts  2.54 us
    pallas_call x1, Pallas kernels, on_device(): call(last_kernel, (shape(5, 256, 256), shape(5, 256, 256)), 12, 2 * 17448...  2.06 us
  transfers between devices with their start and end apart: 11, of which 5 were waited for; matrix products, arithmetic and copies ran while one was open for 0% of the time, Pallas kernels for 16%

profile of v5, /device:TPU:1, one launch (start us, length us, event | category | flops | bytes accessed | tf_op | source)
XLA Modules:
  0.0 77.4 jit_solution(6992096787025088348)
XLA Ops:
  0.0 0.0 copy-start
  0.0 1.6 %copy-done = bf16[2048,512]{1,0:T(8,128)(2,1)S(1)} copy-done((bf16[2048,512]{1,0:T(8,128)(2,1)S(1)}, bf16[2048,512]{1,0:T(8,128)(2,1)}, u32[]{:S(2)}) %copy-start) | copy-done | bytes 2097176
  1.6 0.0 copy-start.1
  1.6 0.1 shard_map.29
  1.7 3.7 %collective-permute-start.2 = (bf16[768,512]{1,0:T(8,128)(2,1)S(1)}, bf16[768,512]{1,0:T(8,128)(2,1)S(1)}, u32[]{:S(2)}, u32[]{:S(2)}) collective-permute-start(bf16[768,512]{1,0:T(8,128)(2,1)S(1)} %get-tuple-element.28), channel_id=1, source_target_pairs={{130,0},{131,1},{128,2},{129,3},{134,4},{135,5},{132,6},{133,7},{1... | collective-permute-start | bytes 2359304 | tf_op jit(solution)/shard_map/ppermute | solution.py:30
  5.3 1.0 %collective-permute-start.3 = (bf16[256,512]{1,0:T(8,128)(2,1)}, bf16[256,512]{1,0:T(8,128)(2,1)S(1)}, u32[]{:S(2)}, u32[]{:S(2)}) collective-permute-start(bf16[256,512]{1,0:T(8,128)(2,1)} %own_points.1), channel_id=1, source_target_pairs={{1,0},{0,1},{3,2},{2,3},{5,4},{4,5},{7,6},{6,7},{9,8},{8,9},{11,10... | collective-permute-start | bytes 786440 | tf_op jit(solution)/shard_map/ppermute | solution.py:30
  6.3 0.0 copy-start.2
  6.3 0.9 %copy-done.2 = bf16[256,512]{1,0:T(8,128)(2,1)S(1)} copy-done((bf16[256,512]{1,0:T(8,128)(2,1)S(1)}, bf16[256,512]{1,0:T(8,128)(2,1)}, u32[]{:S(2)}) %copy-start.2) | copy-done | bytes 262168
  7.2 6.5 %collective-permute-start.1 = (bf16[128,512]{1,0:T(8,128)(2,1)S(1)}, bf16[128,512]{1,0:T(8,128)(2,1)S(1)}, u32[]{:S(2)}, u32[]{:S(2)}) collective-permute-start(bf16[128,512]{1,0:T(8,128)(2,1)S(1)} %shard_map.28), channel_id=1, source_target_pairs={{12,0},{13,1},{14,2},{15,3},{16,4},{17,5},{18,6},{19,7},{20,8},{21... | collective-permute-start | bytes 393224 | tf_op jit(solution)/shard_map/ppermute | solution.py:30
  13.8 0.7 collective-permute-start
  14.5 0.0 collective-permute-done.3.sib_points
  14.5 0.0 copy-done.1
  14.5 2.2 %shard_map.30 = (bf16[2048,512]{1,0:T(8,128)(2,1)S(1)}, bf16[512,2048]{1,0:T(8,128)(2,1)S(1)}, f32[512,256]{1,0:T(8,128)S(1)}, bf16[512,512]{1,0:T(8,128)(2,1)S(1)}) custom-call(bf16[2048,512]{1,0:T(8,128)(2,1)S(1)} %copy-done.1, bf16[256,512]{1,0:T(8,128)(2,1)S(1)} %copy-done.2, bf16[256,512]{1,0:T(8,128)(2,1)S(1)} %collective-permute-done.3.sib_points), custom_call_target="tpu_custom_call" | custom-call | flops 1610612736 | bytes 8388608 | tf_op jit(solution)/shard_map/pallas_call | solution.py:230
  16.7 5.6 %collective-permute-done.1.second = bf16[128,512]{1,0:T(8,128)(2,1)S(1)} collective-permute-done((bf16[128,512]{1,0:T(8,128)(2,1)S(1)}, bf16[128,512]{1,0:T(8,128)(2,1)S(1)}, u32[]{:S(2)}, u32[]{:S(2)}) %collective-permute-start.1) | collective-permute-done | bytes 131104 | tf_op jit(solution)/shard_map/ppermute | solution.py:30
  22.3 2.8 %collective-permute-done.first = bf16[128,512]{1,0:T(8,128)(2,1)S(1)} collective-permute-done((bf16[128,512]{1,0:T(8,128)(2,1)S(1)}, bf16[128,512]{1,0:T(8,128)(2,1)S(1)}, u32[]{:S(2)}, u32[]{:S(2)}) %collective-permute-start) | collective-permute-done | bytes 131104 | tf_op jit(solution)/shard_map/ppermute | solution.py:30
  25.1 0.0 collective-permute-done.2.near
  25.1 0.8 collective-permute-start.6
  25.9 0.1 shard_map.31.points.refs_5_
  26.1 1.3 %collective-permute-start.9 = (bf16[256,512]{1,0:T(8,128)(2,1)S(1)}, bf16[256,512]{1,0:T(8,128)(2,1)S(1)}, u32[]{:S(2)}, u32[]{:S(2)}) collective-permute-start(bf16[256,512]{1,0:T(8,128)(2,1)S(1)} %shard_map.31.points.refs_5_), channel_id=1, source_target_pairs={{96,0},{97,1},{98,2},{99,3},{100,4},{101,5},{102,6},{103,7},{104,8... | collective-permute-start | bytes 786440 | tf_op jit(solution)/shard_map/ppermute | solution.py:30
  27.3 3.1 %collective-permute-start.7 = (bf16[256,512]{1,0:T(8,128)(2,1)S(1)}, bf16[256,512]{1,0:T(8,128)(2,1)S(1)}, u32[]{:S(2)}, u32[]{:S(2)}) collective-permute-start(bf16[256,512]{1,0:T(8,128)(2,1)S(1)} %shard_map.31.points.refs_5_), channel_id=1, source_target_pairs={{32,0},{33,1},{34,2},{35,3},{36,4},{37,5},{38,6},{39,7},{40,8},{41... | collective-permute-start | bytes 786440 | tf_op jit(solution)/shard_map/ppermute | solution.py:30
  30.4 1.6 %collective-permute-start.5 = (bf16[256,512]{1,0:T(8,128)(2,1)S(1)}, bf16[256,512]{1,0:T(8,128)(2,1)S(1)}, u32[]{:S(2)}, u32[]{:S(2)}) collective-permute-start(bf16[256,512]{1,0:T(8,128)(2,1)S(1)} %shard_map.31.points.refs_5_), channel_id=1, source_target_pairs={{64,0},{65,1},{66,2},{67,3},{68,4},{69,5},{70,6},{71,7},{72,8},{73... | collective-permute-start | bytes 786440 | tf_op jit(solution)/shard_map/ppermute | solution.py:30
  32.1 0.4 collective-permute-start.4
  32.4 0.0 collective-permute-done.6.far
  32.4 1.7 %shard_map.32 = (bf16[1536,512]{1,0:T(8,128)(2,1)S(1)}, bf16[512,1536]{1,0:T(8,128)(2,1)S(1)}, f32[512,256]{1,0:T(8,128)S(1)}) custom-call(bf16[768,512]{1,0:T(8,128)(2,1)S(1)} %collective-permute-done.2.near, bf16[768,512]{1,0:T(8,128)(2,1)S(1)} %collective-permute-done.6.far, bf16[512,512]{1,0:T(8,128)(2,1)S(1)} %get-tuple-element.39.points_hat, ...), custom_call_target="tpu_custom_call" | custom-call | flops 1207959552 | bytes 6291456 | tf_op jit(solution)/shard_map/pallas_call | solution.py:230
  34.2 2.1 %shard_map.33.refs_1_ = f32[512,256]{1,0:T(8,128)S(1)} custom-call(bf16[256,512]{1,0:T(8,128)(2,1)S(1)} %shard_map.31.points.refs_5_, bf16[2048,512]{1,0:T(8,128)(2,1)S(1)} %get-tuple-element.37.env_a, bf16[1536,512]{1,0:T(8,128)(2,1)S(1)} %get-tuple-element.41.env_b, bf16[512,2048]{1,0:T(8,128)(2,1)S(1)} %get-tuple-element.42.rows_a, ...), custom_call_target="tpu_custom_call" | custom-call | flops 1879048192 | bytes 8388608 | tf_op jit(solution)/shard_map/pallas_call | solution.py:258
  36.3 0.5 collective-permute-done.7.points.refs_6_
  36.8 2.1 %shard_map.34.refs_2_ = f32[512,256]{1,0:T(8,128)S(1)} custom-call(bf16[256,512]{1,0:T(8,128)(2,1)S(1)} %collective-permute-done.7.points.refs_6_, bf16[2048,512]{1,0:T(8,128)(2,1)S(1)} %get-tuple-element.37.env_a, bf16[1536,512]{1,0:T(8,128)(2,1)S(1)} %get-tuple-element.41.env_b, bf16[512,2048]{1,0:T(8,128)(2,1)S(1)} %get-tuple-element.42.rows_a, ...), custom_call_target="tpu_custom_call" | custom-call | flops 1879048192 | bytes 8388608 | tf_op jit(solution)/shard_map/pallas_call | solution.py:258
  38.9 4.8 %collective-permute-done.5.points.refs_7_ = bf16[256,512]{1,0:T(8,128)(2,1)S(1)} collective-permute-done((bf16[256,512]{1,0:T(8,128)(2,1)S(1)}, bf16[256,512]{1,0:T(8,128)(2,1)S(1)}, u32[]{:S(2)}, u32[]{:S(2)}) %collective-permute-start.5) | collective-permute-done | bytes 262176 | tf_op jit(solution)/shard_map/ppermute | solution.py:30
  43.6 0.0 collective-permute-done.4.near
  43.6 1.2 %collective-permute-start.8 = (bf16[256,512]{1,0:T(8,128)(2,1)S(1)}, bf16[256,512]{1,0:T(8,128)(2,1)S(1)}, u32[]{:S(2)}, u32[]{:S(2)}) collective-permute-start(bf16[256,512]{1,0:T(8,128)(2,1)S(1)} %collective-permute-done.4.near), channel_id=1, source_target_pairs={{1,0},{0,1},{3,2},{2,3},{5,4},{4,5},{7,6},{6,7},{9,8},{8,9},{11,10... | collective-permute-start | bytes 786440 | tf_op jit(solution)/shard_map/ppermute | solution.py:30
  44.8 2.1 %shard_map.35.refs_3_ = f32[512,256]{1,0:T(8,128)S(1)} custom-call(bf16[256,512]{1,0:T(8,128)(2,1)S(1)} %collective-permute-done.5.points.refs_7_, bf16[2048,512]{1,0:T(8,128)(2,1)S(1)} %get-tuple-element.37.env_a, bf16[1536,512]{1,0:T(8,128)(2,1)S(1)} %get-tuple-element.41.env_b, bf16[512,2048]{1,0:T(8,128)(2,1)S(1)} %get-tuple-element.42.rows_a, ...), custom_call_target="tpu_custom_call" | custom-call | flops 1879048192 | bytes 8388608 | tf_op jit(solution)/shard_map/pallas_call | solution.py:258
  46.9 0.0 collective-permute-done.9.points.refs_8_
  46.9 2.1 %shard_map.36.refs_4_ = f32[512,256]{1,0:T(8,128)S(1)} custom-call(bf16[256,512]{1,0:T(8,128)(2,1)S(1)} %collective-permute-done.9.points.refs_8_, bf16[2048,512]{1,0:T(8,128)(2,1)S(1)} %get-tuple-element.37.env_a, bf16[1536,512]{1,0:T(8,128)(2,1)S(1)} %get-tuple-element.41.env_b, bf16[512,2048]{1,0:T(8,128)(2,1)S(1)} %get-tuple-element.42.rows_a, ...), custom_call_target="tpu_custom_call" | custom-call | flops 1879048192 | bytes 8388608 | tf_op jit(solution)/shard_map/pallas_call | solution.py:258
  49.0 0.0 collective-permute-done.8.far
  49.1 2.1 %shard_map.37 = (bf16[5,256,256]{2,1,0:T(8,128)(2,1)S(1)}, bf16[5,256,256]{2,1,0:T(8,128)(2,1)S(1)}) custom-call(bf16[256,512]{1,0:T(8,128)(2,1)S(1)} %collective-permute-done.4.near, bf16[256,512]{1,0:T(8,128)(2,1)S(1)} %collective-permute-done.8.far, bf16[512,512]{1,0:T(8,128)(2,1)S(1)} %get-tuple-element.39.points_hat, ...), custom_call_target="tpu_custom_call" | custom-call | flops 3489660928 | bytes 8388608 | tf_op jit(solution)/shard_map/pallas_call | solution.py:264
  51.1 0.1 collective-permute-start.10
  51.2 2.1 %collective-permute-done.10.swapped = bf16[5,256,256]{2,1,0:T(8,128)(2,1)S(1)} collective-permute-done((bf16[5,256,256]{2,1,0:T(8,128)(2,1)S(1)}, bf16[5,256,256]{2,1,0:T(8,128)(2,1)S(1)}, u32[]{:S(2)}, u32[]{:S(2)}) %collective-permute-start.10) | collective-permute-done | bytes 655392 | tf_op jit(solution)/shard_map/ppermute | solution.py:30
  53.3 0.1 shard_map.38
  53.5 22.9 %all_to_all.5.pieces = bf16[8,9,32,256]{3,2,1,0:T(8,128)(2,1)S(1)} all-to-all(bf16[8,9,32,256]{3,2,1,0:T(8,128)(2,1)S(1)} %shard_map.38), channel_id=1, replica_groups=mesh['env'=8,'sp'=32] {'env'}, dimensions={0} | all-to-all | bytes 2359296 | tf_op jit(solution)/shard_map/all_to_all | solution.py:269
  76.3 1.0 %shard_map.39 = f32[17,32,256]{2,1,0:T(8,128)} custom-call(bf16[8,9,32,256]{3,2,1,0:T(8,128)(2,1)S(1)} %all_to_all.5.pieces), custom_call_target="tpu_custom_call" | custom-call | bytes 2097152 | tf_op jit(solution)/shard_map/pallas_call | solution.py:270
  (1 shorter events, 0.0 us)
Async XLA Ops:
  0.0 1.6 %copy-start = (bf16[2048,512]{1,0:T(8,128)(2,1)S(1)}, bf16[2048,512]{1,0:T(8,128)(2,1)}, u32[]{:S(2)}) copy-start(bf16[2048,512]{1,0:T(8,128)(2,1)} %own_env.1) | copy-start | bytes 6291460
  1.6 12.9 %copy-start.1 = (bf16[2048,512]{1,0:T(8,128)(2,1)S(1)}, bf16[2048,512]{1,0:T(8,128)(2,1)}, u32[]{:S(2)}) copy-start(bf16[2048,512]{1,0:T(8,128)(2,1)} %own_env.1) | copy-start | bytes 6291460
  1.7 23.5 %collective-permute-start.2 = (bf16[768,512]{1,0:T(8,128)(2,1)S(1)}, bf16[768,512]{1,0:T(8,128)(2,1)S(1)}, u32[]{:S(2)}, u32[]{:S(2)}) collective-permute-start(bf16[768,512]{1,0:T(8,128)(2,1)S(1)} %get-tuple-element.28), channel_id=1, source_target_pairs={{130,0},{131,1},{128,2},{129,3},{134,4},{135,5},{132,6},{133,7},{1... | collective-permute-start | bytes 2359304 | tf_op jit(solution)/shard_map/ppermute | solution.py:30
  5.3 9.2 %collective-permute-start.3 = (bf16[256,512]{1,0:T(8,128)(2,1)}, bf16[256,512]{1,0:T(8,128)(2,1)S(1)}, u32[]{:S(2)}, u32[]{:S(2)}) collective-permute-start(bf16[256,512]{1,0:T(8,128)(2,1)} %own_points.1), channel_id=1, source_target_pairs={{1,0},{0,1},{3,2},{2,3},{5,4},{4,5},{7,6},{6,7},{9,8},{8,9},{11,10... | collective-permute-start | bytes 786440 | tf_op jit(solution)/shard_map/ppermute | solution.py:30
  6.3 0.9 %copy-start.2 = (bf16[256,512]{1,0:T(8,128)(2,1)S(1)}, bf16[256,512]{1,0:T(8,128)(2,1)}, u32[]{:S(2)}) copy-start(bf16[256,512]{1,0:T(8,128)(2,1)} %own_points.1) | copy-start | bytes 786436
  7.2 15.1 %collective-permute-start.1 = (bf16[128,512]{1,0:T(8,128)(2,1)S(1)}, bf16[128,512]{1,0:T(8,128)(2,1)S(1)}, u32[]{:S(2)}, u32[]{:S(2)}) collective-permute-start(bf16[128,512]{1,0:T(8,128)(2,1)S(1)} %shard_map.28), channel_id=1, source_target_pairs={{12,0},{13,1},{14,2},{15,3},{16,4},{17,5},{18,6},{19,7},{20,8},{21... | collective-permute-start | bytes 393224 | tf_op jit(solution)/shard_map/ppermute | solution.py:30
  13.8 11.4 %collective-permute-start = (bf16[128,512]{1,0:T(8,128)(2,1)S(1)}, bf16[128,512]{1,0:T(8,128)(2,1)S(1)}, u32[]{:S(2)}, u32[]{:S(2)}) collective-permute-start(bf16[128,512]{1,0:T(8,128)(2,1)S(1)} %shard_map.28), channel_id=1, source_target_pairs={{4,0},{5,1},{6,2},{7,3},{8,4},{9,5},{10,6},{11,7},{12,8},{13,9},{1... | collective-permute-start | bytes 393224 | tf_op jit(solution)/shard_map/ppermute | solution.py:30
  25.1 7.3 %collective-permute-start.6 = (bf16[768,512]{1,0:T(8,128)(2,1)S(1)}, bf16[768,512]{1,0:T(8,128)(2,1)S(1)}, u32[]{:S(2)}, u32[]{:S(2)}) collective-permute-start(bf16[768,512]{1,0:T(8,128)(2,1)S(1)} %collective-permute-done.2.near), channel_id=1, source_target_pairs={{1,0},{0,1},{3,2},{2,3},{5,4},{4,5},{7,6},{6,7},{9,8},{8,9},{11,10... | collective-permute-start | bytes 2359304 | tf_op jit(solution)/shard_map/ppermute | solution.py:30
  26.1 20.9 %collective-permute-start.9 = (bf16[256,512]{1,0:T(8,128)(2,1)S(1)}, bf16[256,512]{1,0:T(8,128)(2,1)S(1)}, u32[]{:S(2)}, u32[]{:S(2)}) collective-permute-start(bf16[256,512]{1,0:T(8,128)(2,1)S(1)} %shard_map.31.points.refs_5_), channel_id=1, source_target_pairs={{96,0},{97,1},{98,2},{99,3},{100,4},{101,5},{102,6},{103,7},{104,8... | collective-permute-start | bytes 786440 | tf_op jit(solution)/shard_map/ppermute | solution.py:30
  27.3 9.4 %collective-permute-start.7 = (bf16[256,512]{1,0:T(8,128)(2,1)S(1)}, bf16[256,512]{1,0:T(8,128)(2,1)S(1)}, u32[]{:S(2)}, u32[]{:S(2)}) collective-permute-start(bf16[256,512]{1,0:T(8,128)(2,1)S(1)} %shard_map.31.points.refs_5_), channel_id=1, source_target_pairs={{32,0},{33,1},{34,2},{35,3},{36,4},{37,5},{38,6},{39,7},{40,8},{41... | collective-permute-start | bytes 786440 | tf_op jit(solution)/shard_map/ppermute | solution.py:30
  30.4 13.2 %collective-permute-start.5 = (bf16[256,512]{1,0:T(8,128)(2,1)S(1)}, bf16[256,512]{1,0:T(8,128)(2,1)S(1)}, u32[]{:S(2)}, u32[]{:S(2)}) collective-permute-start(bf16[256,512]{1,0:T(8,128)(2,1)S(1)} %shard_map.31.points.refs_5_), channel_id=1, source_target_pairs={{64,0},{65,1},{66,2},{67,3},{68,4},{69,5},{70,6},{71,7},{72,8},{73... | collective-permute-start | bytes 786440 | tf_op jit(solution)/shard_map/ppermute | solution.py:30
  32.1 11.5 %collective-permute-start.4 = (bf16[256,512]{1,0:T(8,128)(2,1)S(1)}, bf16[256,512]{1,0:T(8,128)(2,1)S(1)}, u32[]{:S(2)}, u32[]{:S(2)}) collective-permute-start(bf16[256,512]{1,0:T(8,128)(2,1)S(1)} %get-tuple-element.34), channel_id=1, source_target_pairs={{130,0},{131,1},{128,2},{129,3},{134,4},{135,5},{132,6},{133,7},{1... | collective-permute-start | bytes 786440 | tf_op jit(solution)/shard_map/ppermute | solution.py:30
  43.6 5.4 %collective-permute-start.8 = (bf16[256,512]{1,0:T(8,128)(2,1)S(1)}, bf16[256,512]{1,0:T(8,128)(2,1)S(1)}, u32[]{:S(2)}, u32[]{:S(2)}) collective-permute-start(bf16[256,512]{1,0:T(8,128)(2,1)S(1)} %collective-permute-done.4.near), channel_id=1, source_target_pairs={{1,0},{0,1},{3,2},{2,3},{5,4},{4,5},{7,6},{6,7},{9,8},{8,9},{11,10... | collective-permute-start | bytes 786440 | tf_op jit(solution)/shard_map/ppermute | solution.py:30
  51.1 2.2 %collective-permute-start.10 = (bf16[5,256,256]{2,1,0:T(8,128)(2,1)S(1)}, bf16[5,256,256]{2,1,0:T(8,128)(2,1)S(1)}, u32[]{:S(2)}, u32[]{:S(2)}) collective-permute-start(bf16[5,256,256]{2,1,0:T(8,128)(2,1)S(1)} %get-tuple-element.50), channel_id=1, source_target_pairs={{1,0},{0,1},{3,2},{2,3},{5,4},{4,5},{7,6},{6,7},{9,8},{8,9},{11,10... | collective-permute-start | bytes 1966088 | tf_op jit(solution)/shard_map/ppermute | solution.py:30

commit v6 on v3

--- a/solution.py
+++ b/solution.py
@@ -90,14 +90,10 @@
             place += CHUNK
 
 
-def slice_kernel(descriptors, first_out, second_out, sems):
-    start = pl.multiple_of((lax.axis_index("sp") % 2) * 1024, 1024)
-    copies = []
-    for i, out in enumerate((first_out, second_out)):
-        copies.append(pltpu.make_async_copy(descriptors.at[pl.ds(start + 512 * i, 512), :], out, sems.at[i]))
-        copies[i].start()
-    for copy in copies:
-        copy.wait()
+def slice_kernel(descriptors, first_out, second_out):
+    half = pl.multiple_of((lax.axis_index("sp") % 2) * 1024, 1024)
+    first_out[...] = descriptors[pl.ds(half, 512), :]
+    second_out[...] = descriptors[pl.ds(half + 512, 512), :]
 
 
 def own_kernel(own_env, own_points, sib_points, env_hat, rows_k, gram, points_hat):
@@ -175,12 +171,12 @@
     return jax.ShapeDtypeStruct(dims, dtype)
 
 
-def call(body, out_shape, n_in, flops, bytes_accessed, scratch=(), in_place=False):
+def call(body, out_shape, n_in, flops, bytes_accessed, scratch=()):
     many = isinstance(out_shape, (tuple, list))
     return pl.pallas_call(
         body,
         out_shape=out_shape,
-        in_specs=[pl.BlockSpec(memory_space=pl.ANY) if in_place else vmem_spec() for _ in range(n_in)],
+        in_specs=[vmem_spec() for _ in range(n_in)],
         out_specs=[vmem_spec() for _ in out_shape] if many else vmem_spec(),
         scratch_shapes=scratch,
         compiler_params=pltpu.CompilerParams(vmem_limit_bytes=VMEM_LIMIT),
@@ -199,23 +195,23 @@
 
     column = fetch(sparse_points, first_column)
     sib_points = fetch(sparse_points, other_core)
-    low, high = call(
-        slice_kernel, (shape(512, 512), shape(512, 512)), 1, 0, 1 << 21, (pltpu.SemaphoreType.DMA((2,)),), True
-    )(descriptors)
-    near = fetch(low, near_x)
     env_a, rows_a, gram, points_hat = rows(
         own_kernel, 2048, (gram_shape, shape(512, 512)), 3, descriptors, sparse_points, sib_points
     )
     columns = [column]
-    column, near, high, env_a, rows_a, gram, points_hat = barrier(
-        (column, near, high, env_a, rows_a, gram, points_hat)
-    )
-
-    far = fetch(near, other_core)
+    column, later, env_a, rows_a, gram, points_hat = barrier(
+        (column, descriptors, env_a, rows_a, gram, points_hat)
+    )
+
+    columns.append(fetch(column, next_z))
+    low, high = call(slice_kernel, (shape(512, 512), shape(512, 512)), 1, 0, 1 << 21)(later)
+    near, high, column = barrier((fetch(low, near_x), high, columns[1]))
+
     columns.append(fetch(column, next_z))
     near_b = fetch(high, near_x)
+    far = fetch(near, other_core)
     env_b, rows_b, gram = rows(more_kernel, 1024, (gram_shape,), 4, near, far, points_hat, gram)
-    column, near_b, env_b, rows_b, gram = barrier((columns[1], near_b, env_b, rows_b, gram))
+    near_b, column, env_b, rows_b, gram = barrier((near_b, columns[2], env_b, rows_b, gram))
 
     columns.append(fetch(column, next_z))
     env_c, rows_c, own, sib = rows(
@@ -230,12 +226,10 @@
         owns.append(own)
         sibs.append(sib)
 
-    take(columns[0])
-    column, owns[1], sibs[1] = barrier((columns[2], owns[1], sibs[1]))
-
-    columns.append(fetch(column, next_z))
-    for points in columns[1:]:
+    for points in columns[:3]:
         take(points)
+    column, *owns = barrier((columns[3], *owns))
+    take(column)
 
     swapped = [fetch(sib, other_core) for sib in sibs]
     packed = call(pack_kernel, shape(8, 9, 32, 256), 10, 0, 1 << 21)(*owns, *swapped)

time: 75.8 us -> 77.2 us (1.018)
  waiting for transfers between devices: 10.9 us -> 12.4 us
  starting transfers between devices: 24.1 us -> 22.8 us
  local copies, waits for them, and re-layouts: 1.59 us -> 2.54 us
    ppermute x14, waiting for transfers between devices: 10.9 us -> 12.4 us  [fetch(): return lax.ppermute(value, ('env', 'sp'), pairs)]
    ppermute x14, starting transfers between devices: 24.1 us -> 22.8 us  [fetch(): return lax.ppermute(value, ('env', 'sp'), pairs)]
    unnamed x4, local copies, waits for them, and re-layouts: 1.59 us -> 2.54 us
  transfers between devices with their start and end apart: 14 -> 14, of which waited for: 5 -> 9; matrix products, arithmetic and copies ran while one was open for 0% -> 0% of each run, Pallas kernels for 19% -> 16%
where the time goes in v6:
time: 77.2 us; the launch traced here: 77 us
  blocking collectives  23.5 us (30%)
  starting transfers between devices  22.8 us (30%)
  Pallas kernels  15.6 us (20%)
  waiting for transfers between devices  12.4 us (16%)
  local copies, waits for them, and re-layouts  2.54 us (3%)
    all_to_all x1, blocking collectives, on_device(): pieces = lax.all_to_all(packed, 'env', 0, 0, tiled=True)  23.5 us
    ppermute x14, starting transfers between devices, fetch(): return lax.ppermute(value, ('env', 'sp'), pairs)  22.8 us
    ppermute x14, waiting for transfers between devices, fetch(): return lax.ppermute(value, ('env', 'sp'), pairs)  12.4 us
    pallas_call x4, Pallas kernels, take(): call(column_kernel, pair, 7, 2 * 1073741824, 1 << 23, (pltpu.VMEM((256, 4...  9.63 us
    pallas_call x3, Pallas kernels, rows(): call(body, (shape(envs, 512), shape(512, envs)) + sums, n_in, envs * 7864...  4.83 us
    unnamed x4, local copies, waits for them, and re-layouts  2.54 us
  transfers between devices with their start and end apart: 14, of which 9 were waited for; matrix products, arithmetic and copies ran while one was open for 0% of the time, Pallas kernels for 16%

profile of v6, /device:TPU:1, one launch (start us, length us, event | category | flops | bytes accessed | tf_op | source)
XLA Modules:
  0.0 77.0 jit_solution(14886862184071417992)
XLA Ops:
  0.0 3.2 %collective-permute-start.1 = (bf16[256,512]{1,0:T(8,128)(2,1)}, bf16[256,512]{1,0:T(8,128)(2,1)S(1)}, u32[]{:S(2)}, u32[]{:S(2)}) collective-permute-start(bf16[256,512]{1,0:T(8,128)(2,1)} %own_points.1), channel_id=1, source_target_pairs={{1,0},{0,1},{3,2},{2,3},{5,4},{4,5},{7,6},{6,7},{9,8},{8,9},{11,10... | collective-permute-start | bytes 786440 | tf_op jit(solution)/shard_map/ppermute | solution.py:30
  3.2 3.8 %collective-permute-start = (bf16[256,512]{1,0:T(8,128)(2,1)}, bf16[256,512]{1,0:T(8,128)(2,1)S(1)}, u32[]{:S(2)}, u32[]{:S(2)}) collective-permute-start(bf16[256,512]{1,0:T(8,128)(2,1)} %own_points.1), channel_id=1, source_target_pairs={{4,0},{5,1},{6,2},{7,3},{8,4},{9,5},{10,6},{11,7},{12,8},{13,9},{1... | collective-permute-start | bytes 786440 | tf_op jit(solution)/shard_map/ppermute | solution.py:30
  7.1 0.0 collective-permute-done.1.sib_points
  7.1 0.0 copy-start
  7.1 1.6 %copy-done = bf16[2048,512]{1,0:T(8,128)(2,1)S(1)} copy-done((bf16[2048,512]{1,0:T(8,128)(2,1)S(1)}, bf16[2048,512]{1,0:T(8,128)(2,1)}, u32[]{:S(2)}) %copy-start) | copy-done | bytes 2097176
  8.7 0.0 copy-start.1
  8.7 0.9 %copy-done.1 = bf16[256,512]{1,0:T(8,128)(2,1)S(1)} copy-done((bf16[256,512]{1,0:T(8,128)(2,1)S(1)}, bf16[256,512]{1,0:T(8,128)(2,1)}, u32[]{:S(2)}) %copy-start.1) | copy-done | bytes 262168
  9.6 2.2 %shard_map.28 = (bf16[2048,512]{1,0:T(8,128)(2,1)S(1)}, bf16[512,2048]{1,0:T(8,128)(2,1)S(1)}, f32[512,256]{1,0:T(8,128)S(1)}, bf16[512,512]{1,0:T(8,128)(2,1)S(1)}) custom-call(bf16[2048,512]{1,0:T(8,128)(2,1)S(1)} %copy-done, bf16[256,512]{1,0:T(8,128)(2,1)S(1)} %copy-done.1, bf16[256,512]{1,0:T(8,128)(2,1)S(1)} %collective-permute-done.1.sib_points), custom_call_target="tpu_custom_call" | custom-call | flops 1610612736 | bytes 8388608 | tf_op jit(solution)/shard_map/pallas_call | solution.py:191
  11.9 1.3 %collective-permute-done.points = bf16[256,512]{1,0:T(8,128)(2,1)S(1)} collective-permute-done((bf16[256,512]{1,0:T(8,128)(2,1)}, bf16[256,512]{1,0:T(8,128)(2,1)S(1)}, u32[]{:S(2)}, u32[]{:S(2)}) %collective-permute-start) | collective-permute-done | bytes 262176 | tf_op jit(solution)/shard_map/ppermute | solution.py:30
  13.1 0.1 shard_map.29
  13.2 1.1 %collective-permute-start.2 = (bf16[512,512]{1,0:T(8,128)(2,1)S(1)}, bf16[512,512]{1,0:T(8,128)(2,1)S(1)}, u32[]{:S(2)}, u32[]{:S(2)}) collective-permute-start(bf16[512,512]{1,0:T(8,128)(2,1)S(1)} %get-tuple-element.50), channel_id=1, source_target_pairs={{32,0},{97,1},{34,2},{99,3},{36,4},{101,5},{38,6},{103,7},{40,8},{... | collective-permute-start | bytes 1572872 | tf_op jit(solution)/shard_map/ppermute | solution.py:30
  14.3 2.4 %collective-permute-start.3 = (bf16[256,512]{1,0:T(8,128)(2,1)S(1)}, bf16[256,512]{1,0:T(8,128)(2,1)S(1)}, u32[]{:S(2)}, u32[]{:S(2)}) collective-permute-start(bf16[256,512]{1,0:T(8,128)(2,1)S(1)} %collective-permute-done.points), channel_id=1, source_target_pairs={{4,0},{5,1},{6,2},{7,3},{8,4},{9,5},{10,6},{11,7},{12,8},{13,9},{1... | collective-permute-start | bytes 786440 | tf_op jit(solution)/shard_map/ppermute | solution.py:30
  16.7 3.7 %collective-permute-done.3.points = bf16[256,512]{1,0:T(8,128)(2,1)S(1)} collective-permute-done((bf16[256,512]{1,0:T(8,128)(2,1)S(1)}, bf16[256,512]{1,0:T(8,128)(2,1)S(1)}, u32[]{:S(2)}, u32[]{:S(2)}) %collective-permute-start.3) | collective-permute-done | bytes 262176 | tf_op jit(solution)/shard_map/ppermute | solution.py:30
  20.4 2.1 %collective-permute-done.2.near = bf16[512,512]{1,0:T(8,128)(2,1)S(1)} collective-permute-done((bf16[512,512]{1,0:T(8,128)(2,1)S(1)}, bf16[512,512]{1,0:T(8,128)(2,1)S(1)}, u32[]{:S(2)}, u32[]{:S(2)}) %collective-permute-start.2) | collective-permute-done | bytes 524320 | tf_op jit(solution)/shard_map/ppermute | solution.py:30
  22.5 2.0 %collective-permute-start.6 = (bf16[512,512]{1,0:T(8,128)(2,1)S(1)}, bf16[512,512]{1,0:T(8,128)(2,1)S(1)}, u32[]{:S(2)}, u32[]{:S(2)}) collective-permute-start(bf16[512,512]{1,0:T(8,128)(2,1)S(1)} %collective-permute-done.2.near), channel_id=1, source_target_pairs={{1,0},{0,1},{3,2},{2,3},{5,4},{4,5},{7,6},{6,7},{9,8},{8,9},{11,10... | collective-permute-start | bytes 1572872 | tf_op jit(solution)/shard_map/ppermute | solution.py:30
  24.5 1.0 %collective-permute-start.4 = (bf16[512,512]{1,0:T(8,128)(2,1)S(1)}, bf16[512,512]{1,0:T(8,128)(2,1)S(1)}, u32[]{:S(2)}, u32[]{:S(2)}) collective-permute-start(bf16[512,512]{1,0:T(8,128)(2,1)S(1)} %get-tuple-element.53), channel_id=1, source_target_pairs={{32,0},{97,1},{34,2},{99,3},{36,4},{101,5},{38,6},{103,7},{40,8},{... | collective-permute-start | bytes 1572872 | tf_op jit(solution)/shard_map/ppermute | solution.py:30
  25.6 3.4 %collective-permute-start.5 = (bf16[256,512]{1,0:T(8,128)(2,1)S(1)}, bf16[256,512]{1,0:T(8,128)(2,1)S(1)}, u32[]{:S(2)}, u32[]{:S(2)}) collective-permute-start(bf16[256,512]{1,0:T(8,128)(2,1)S(1)} %collective-permute-done.3.points), channel_id=1, source_target_pairs={{4,0},{5,1},{6,2},{7,3},{8,4},{9,5},{10,6},{11,7},{12,8},{13,9},{1... | collective-permute-start | bytes 786440 | tf_op jit(solution)/shard_map/ppermute | solution.py:30
  29.0 0.0 collective-permute-done.6.far
  29.0 1.3 %shard_map.30 = (bf16[1024,512]{1,0:T(8,128)(2,1)S(1)}, bf16[512,1024]{1,0:T(8,128)(2,1)S(1)}, f32[512,256]{1,0:T(8,128)S(1)}) custom-call(bf16[512,512]{1,0:T(8,128)(2,1)S(1)} %collective-permute-done.2.near, bf16[512,512]{1,0:T(8,128)(2,1)S(1)} %collective-permute-done.6.far, bf16[512,512]{1,0:T(8,128)(2,1)S(1)} %get-tuple-element.56.points_hat, ...), custom_call_target="tpu_custom_call" | custom-call | flops 805306368 | bytes 4194304 | tf_op jit(solution)/shard_map/pallas_call | solution.py:191
  30.3 3.9 %collective-permute-done.5.points = bf16[256,512]{1,0:T(8,128)(2,1)S(1)} collective-permute-done((bf16[256,512]{1,0:T(8,128)(2,1)S(1)}, bf16[256,512]{1,0:T(8,128)(2,1)S(1)}, u32[]{:S(2)}, u32[]{:S(2)}) %collective-permute-start.5) | collective-permute-done | bytes 262176 | tf_op jit(solution)/shard_map/ppermute | solution.py:30
  34.1 0.4 collective-permute-done.4.near
  34.5 1.0 %collective-permute-start.8 = (bf16[512,512]{1,0:T(8,128)(2,1)S(1)}, bf16[512,512]{1,0:T(8,128)(2,1)S(1)}, u32[]{:S(2)}, u32[]{:S(2)}) collective-permute-start(bf16[512,512]{1,0:T(8,128)(2,1)S(1)} %collective-permute-done.4.near), channel_id=1, source_target_pairs={{1,0},{0,1},{3,2},{2,3},{5,4},{4,5},{7,6},{6,7},{9,8},{8,9},{11,10... | collective-permute-start | bytes 1572872 | tf_op jit(solution)/shard_map/ppermute | solution.py:30
  35.5 3.4 %collective-permute-start.7 = (bf16[256,512]{1,0:T(8,128)(2,1)S(1)}, bf16[256,512]{1,0:T(8,128)(2,1)S(1)}, u32[]{:S(2)}, u32[]{:S(2)}) collective-permute-start(bf16[256,512]{1,0:T(8,128)(2,1)S(1)} %collective-permute-done.5.points), channel_id=1, source_target_pairs={{4,0},{5,1},{6,2},{7,3},{8,4},{9,5},{10,6},{11,7},{12,8},{13,9},{1... | collective-permute-start | bytes 786440 | tf_op jit(solution)/shard_map/ppermute | solution.py:30
  38.9 0.0 collective-permute-done.8.far
  38.9 1.3 %shard_map.31 = (bf16[1024,512]{1,0:T(8,128)(2,1)S(1)}, bf16[512,1024]{1,0:T(8,128)(2,1)S(1)}, bf16[256,256]{1,0:T(8,128)(2,1)S(1)}, bf16[256,256]{1,0:T(8,128)(2,1)S(1)}) custom-call(bf16[512,512]{1,0:T(8,128)(2,1)S(1)} %collective-permute-done.4.near, bf16[512,512]{1,0:T(8,128)(2,1)S(1)} %collective-permute-done.8.far, ...), custom_call_target="tpu_custom_call" | custom-call | flops 805306368 | bytes 4194304 | tf_op jit(solution)/shard_map/pallas_call | solution.py:191
  40.2 2.4 %shard_map.34 = (bf16[256,256]{1,0:T(8,128)(2,1)S(1)}, bf16[256,256]{1,0:T(8,128)(2,1)S(1)}) custom-call(bf16[256,512]{1,0:T(8,128)(2,1)S(1)} %collective-permute-done.5.points, bf16[2048,512]{1,0:T(8,128)(2,1)S(1)} %get-tuple-element.65.refs_0_, bf16[1024,512]{1,0:T(8,128)(2,1)S(1)} %get-tuple-element.66.refs_1_, ...), custom_call_target="tpu_custom_call" | custom-call | flops 2147483648 | bytes 8388608 | tf_op jit(solution)/shard_map/pallas_call | solution.py:223
  42.6 2.4 %shard_map.33 = (bf16[256,256]{1,0:T(8,128)(2,1)S(1)}, bf16[256,256]{1,0:T(8,128)(2,1)S(1)}) custom-call(bf16[256,512]{1,0:T(8,128)(2,1)S(1)} %collective-permute-done.3.points, bf16[2048,512]{1,0:T(8,128)(2,1)S(1)} %get-tuple-element.65.refs_0_, bf16[1024,512]{1,0:T(8,128)(2,1)S(1)} %get-tuple-element.66.refs_1_, ...), custom_call_target="tpu_custom_call" | custom-call | flops 2147483648 | bytes 8388608 | tf_op jit(solution)/shard_map/pallas_call | solution.py:223
  45.1 2.4 %shard_map.32 = (bf16[256,256]{1,0:T(8,128)(2,1)S(1)}, bf16[256,256]{1,0:T(8,128)(2,1)S(1)}) custom-call(bf16[256,512]{1,0:T(8,128)(2,1)S(1)} %collective-permute-done.points, bf16[2048,512]{1,0:T(8,128)(2,1)S(1)} %get-tuple-element.65.refs_0_, bf16[1024,512]{1,0:T(8,128)(2,1)S(1)} %get-tuple-element.66.refs_1_, ...), custom_call_target="tpu_custom_call" | custom-call | flops 2147483648 | bytes 8388608 | tf_op jit(solution)/shard_map/pallas_call | solution.py:223
  47.5 0.0 collective-permute-done.7.points
  47.5 2.4 %shard_map.35 = (bf16[256,256]{1,0:T(8,128)(2,1)S(1)}, bf16[256,256]{1,0:T(8,128)(2,1)S(1)}) custom-call(bf16[256,512]{1,0:T(8,128)(2,1)S(1)} %collective-permute-done.7.points, bf16[2048,512]{1,0:T(8,128)(2,1)S(1)} %get-tuple-element.65.refs_0_, bf16[1024,512]{1,0:T(8,128)(2,1)S(1)} %get-tuple-element.66.refs_1_, ...), custom_call_target="tpu_custom_call" | custom-call | flops 2147483648 | bytes 8388608 | tf_op jit(solution)/shard_map/pallas_call | solution.py:223
  49.9 0.4 collective-permute-start.13
  50.3 0.2 collective-permute-start.12
  50.5 0.3 collective-permute-start.11
  50.8 0.2 collective-permute-start.10
  51.0 0.3 collective-permute-start.9
  51.3 0.0 collective-permute-done.13.refs_9_
  51.3 0.3 collective-permute-done.12.refs_8_
  51.6 0.2 collective-permute-done.11.refs_7_
  51.8 0.3 collective-permute-done.10.refs_6_
  52.1 0.2 collective-permute-done.9.refs_5_
  52.4 0.1 shard_map.36
  52.4 23.5 %all_to_all.5.pieces = bf16[8,9,32,256]{3,2,1,0:T(8,128)(2,1)S(1)} all-to-all(bf16[8,9,32,256]{3,2,1,0:T(8,128)(2,1)S(1)} %shard_map.36), channel_id=1, replica_groups=mesh['env'=8,'sp'=32] {'env'}, dimensions={0} | all-to-all | bytes 2359296 | tf_op jit(solution)/shard_map/all_to_all | solution.py:236
  76.0 1.0 %shard_map.37 = f32[17,32,256]{2,1,0:T(8,128)} custom-call(bf16[8,9,32,256]{3,2,1,0:T(8,128)(2,1)S(1)} %all_to_all.5.pieces), custom_call_target="tpu_custom_call" | custom-call | bytes 2097152 | tf_op jit(solution)/shard_map/pallas_call | solution.py:237
Async XLA Ops:
  0.0 7.1 %collective-permute-start.1 = (bf16[256,512]{1,0:T(8,128)(2,1)}, bf16[256,512]{1,0:T(8,128)(2,1)S(1)}, u32[]{:S(2)}, u32[]{:S(2)}) collective-permute-start(bf16[256,512]{1,0:T(8,128)(2,1)} %own_points.1), channel_id=1, source_target_pairs={{1,0},{0,1},{3,2},{2,3},{5,4},{4,5},{7,6},{6,7},{9,8},{8,9},{11,10... | collective-permute-start | bytes 786440 | tf_op jit(solution)/shard_map/ppermute | solution.py:30
  3.2 9.9 %collective-permute-start = (bf16[256,512]{1,0:T(8,128)(2,1)}, bf16[256,512]{1,0:T(8,128)(2,1)S(1)}, u32[]{:S(2)}, u32[]{:S(2)}) collective-permute-start(bf16[256,512]{1,0:T(8,128)(2,1)} %own_points.1), channel_id=1, source_target_pairs={{4,0},{5,1},{6,2},{7,3},{8,4},{9,5},{10,6},{11,7},{12,8},{13,9},{1... | collective-permute-start | bytes 786440 | tf_op jit(solution)/shard_map/ppermute | solution.py:30
  7.1 1.6 %copy-start = (bf16[2048,512]{1,0:T(8,128)(2,1)S(1)}, bf16[2048,512]{1,0:T(8,128)(2,1)}, u32[]{:S(2)}) copy-start(bf16[2048,512]{1,0:T(8,128)(2,1)} %descriptors) | copy-start | bytes 6291460
  8.7 0.9 %copy-start.1 = (bf16[256,512]{1,0:T(8,128)(2,1)S(1)}, bf16[256,512]{1,0:T(8,128)(2,1)}, u32[]{:S(2)}) copy-start(bf16[256,512]{1,0:T(8,128)(2,1)} %own_points.1) | copy-start | bytes 786436
  13.2 9.3 %collective-permute-start.2 = (bf16[512,512]{1,0:T(8,128)(2,1)S(1)}, bf16[512,512]{1,0:T(8,128)(2,1)S(1)}, u32[]{:S(2)}, u32[]{:S(2)}) collective-permute-start(bf16[512,512]{1,0:T(8,128)(2,1)S(1)} %get-tuple-element.50), channel_id=1, source_target_pairs={{32,0},{97,1},{34,2},{99,3},{36,4},{101,5},{38,6},{103,7},{40,8},{... | collective-permute-start | bytes 1572872 | tf_op jit(solution)/shard_map/ppermute | solution.py:30
  14.3 6.1 %collective-permute-start.3 = (bf16[256,512]{1,0:T(8,128)(2,1)S(1)}, bf16[256,512]{1,0:T(8,128)(2,1)S(1)}, u32[]{:S(2)}, u32[]{:S(2)}) collective-permute-start(bf16[256,512]{1,0:T(8,128)(2,1)S(1)} %collective-permute-done.points), channel_id=1, source_target_pairs={{4,0},{5,1},{6,2},{7,3},{8,4},{9,5},{10,6},{11,7},{12,8},{13,9},{1... | collective-permute-start | bytes 786440 | tf_op jit(solution)/shard_map/ppermute | solution.py:30
  22.5 6.5 %collective-permute-start.6 = (bf16[512,512]{1,0:T(8,128)(2,1)S(1)}, bf16[512,512]{1,0:T(8,128)(2,1)S(1)}, u32[]{:S(2)}, u32[]{:S(2)}) collective-permute-start(bf16[512,512]{1,0:T(8,128)(2,1)S(1)} %collective-permute-done.2.near), channel_id=1, source_target_pairs={{1,0},{0,1},{3,2},{2,3},{5,4},{4,5},{7,6},{6,7},{9,8},{8,9},{11,10... | collective-permute-start | bytes 1572872 | tf_op jit(solution)/shard_map/ppermute | solution.py:30
  24.5 10.0 %collective-permute-start.4 = (bf16[512,512]{1,0:T(8,128)(2,1)S(1)}, bf16[512,512]{1,0:T(8,128)(2,1)S(1)}, u32[]{:S(2)}, u32[]{:S(2)}) collective-permute-start(bf16[512,512]{1,0:T(8,128)(2,1)S(1)} %get-tuple-element.53), channel_id=1, source_target_pairs={{32,0},{97,1},{34,2},{99,3},{36,4},{101,5},{38,6},{103,7},{40,8},{... | collective-permute-start | bytes 1572872 | tf_op jit(solution)/shard_map/ppermute | solution.py:30
  25.6 8.6 %collective-permute-start.5 = (bf16[256,512]{1,0:T(8,128)(2,1)S(1)}, bf16[256,512]{1,0:T(8,128)(2,1)S(1)}, u32[]{:S(2)}, u32[]{:S(2)}) collective-permute-start(bf16[256,512]{1,0:T(8,128)(2,1)S(1)} %collective-permute-done.3.points), channel_id=1, source_target_pairs={{4,0},{5,1},{6,2},{7,3},{8,4},{9,5},{10,6},{11,7},{12,8},{13,9},{1... | collective-permute-start | bytes 786440 | tf_op jit(solution)/shard_map/ppermute | solution.py:30
  34.5 4.4 %collective-permute-start.8 = (bf16[512,512]{1,0:T(8,128)(2,1)S(1)}, bf16[512,512]{1,0:T(8,128)(2,1)S(1)}, u32[]{:S(2)}, u32[]{:S(2)}) collective-permute-start(bf16[512,512]{1,0:T(8,128)(2,1)S(1)} %collective-permute-done.4.near), channel_id=1, source_target_pairs={{1,0},{0,1},{3,2},{2,3},{5,4},{4,5},{7,6},{6,7},{9,8},{8,9},{11,10... | collective-permute-start | bytes 1572872 | tf_op jit(solution)/shard_map/ppermute | solution.py:30
  35.5 12.0 %collective-permute-start.7 = (bf16[256,512]{1,0:T(8,128)(2,1)S(1)}, bf16[256,512]{1,0:T(8,128)(2,1)S(1)}, u32[]{:S(2)}, u32[]{:S(2)}) collective-permute-start(bf16[256,512]{1,0:T(8,128)(2,1)S(1)} %collective-permute-done.5.points), channel_id=1, source_target_pairs={{4,0},{5,1},{6,2},{7,3},{8,4},{9,5},{10,6},{11,7},{12,8},{13,9},{1... | collective-permute-start | bytes 786440 | tf_op jit(solution)/shard_map/ppermute | solution.py:30
  49.9 1.4 %collective-permute-start.13 = (bf16[256,256]{1,0:T(8,128)(2,1)S(1)}, bf16[256,256]{1,0:T(8,128)(2,1)S(1)}, u32[]{:S(2)}, u32[]{:S(2)}) collective-permute-start(bf16[256,256]{1,0:T(8,128)(2,1)S(1)} %get-tuple-element.84), channel_id=1, source_target_pairs={{1,0},{0,1},{3,2},{2,3},{5,4},{4,5},{7,6},{6,7},{9,8},{8,9},{11,10... | collective-permute-start | bytes 393224 | tf_op jit(solution)/shard_map/ppermute | solution.py:30
  50.3 1.3 %collective-permute-start.12 = (bf16[256,256]{1,0:T(8,128)(2,1)S(1)}, bf16[256,256]{1,0:T(8,128)(2,1)S(1)}, u32[]{:S(2)}, u32[]{:S(2)}) collective-permute-start(bf16[256,256]{1,0:T(8,128)(2,1)S(1)} %get-tuple-element.83), channel_id=1, source_target_pairs={{1,0},{0,1},{3,2},{2,3},{5,4},{4,5},{7,6},{6,7},{9,8},{8,9},{11,10... | collective-permute-start | bytes 393224 | tf_op jit(solution)/shard_map/ppermute | solution.py:30
  50.5 1.3 %collective-permute-start.11 = (bf16[256,256]{1,0:T(8,128)(2,1)S(1)}, bf16[256,256]{1,0:T(8,128)(2,1)S(1)}, u32[]{:S(2)}, u32[]{:S(2)}) collective-permute-start(bf16[256,256]{1,0:T(8,128)(2,1)S(1)} %get-tuple-element.82), channel_id=1, source_target_pairs={{1,0},{0,1},{3,2},{2,3},{5,4},{4,5},{7,6},{6,7},{9,8},{8,9},{11,10... | collective-permute-start | bytes 393224 | tf_op jit(solution)/shard_map/ppermute | solution.py:30
  50.8 1.3 %collective-permute-start.10 = (bf16[256,256]{1,0:T(8,128)(2,1)S(1)}, bf16[256,256]{1,0:T(8,128)(2,1)S(1)}, u32[]{:S(2)}, u32[]{:S(2)}) collective-permute-start(bf16[256,256]{1,0:T(8,128)(2,1)S(1)} %get-tuple-element.81), channel_id=1, source_target_pairs={{1,0},{0,1},{3,2},{2,3},{5,4},{4,5},{7,6},{6,7},{9,8},{8,9},{11,10... | collective-permute-start | bytes 393224 | tf_op jit(solution)/shard_map/ppermute | solution.py:30
  51.0 1.3 %collective-permute-start.9 = (bf16[256,256]{1,0:T(8,128)(2,1)S(1)}, bf16[256,256]{1,0:T(8,128)(2,1)S(1)}, u32[]{:S(2)}, u32[]{:S(2)}) collective-permute-start(bf16[256,256]{1,0:T(8,128)(2,1)S(1)} %get-tuple-element.80), channel_id=1, source_target_pairs={{1,0},{0,1},{3,2},{2,3},{5,4},{4,5},{7,6},{6,7},{9,8},{8,9},{11,10... | collective-permute-start | bytes 393224 | tf_op jit(solution)/shard_map/ppermute | solution.py:30

commit v7 on v6

--- a/solution.py
+++ b/solution.py
@@ -108,29 +108,47 @@
     gram_out[...] = gram[...] + dot(rows_k[...], rows_k[:256, :])
 
 
-def last_kernel(near, far, points_hat, gram, env_hat, rows_k, own_out, sib_out):
-    rows_of(points_hat[...], (near, far), env_hat, rows_k)
-    total = ((gram[...] + dot(rows_k[...], rows_k[:256, :])) * weight_row()).astype(BF16)
-    own_out[...] = total[:256]
-    sib_out[...] = total[256:]
-
-
-def column_kernel(points, *refs):
-    envs, rows, own_out, sib_out, kept = refs[:3], refs[3:6], refs[6], refs[7], refs[8]
-    point_hat = unit(points[...])
-    total, place = None, 0
+def kernel_values(point_hat, envs, kept):
+    place = 0
     for env in envs:
         for start in range(0, env.shape[0], CHUNK):
             kept[:, place:place + CHUNK] = fourth(dot(point_hat, env[start:start + CHUNK, :]))
             place += CHUNK
-    place = 0
+
+
+def products(rows, kept):
+    total, place = None, 0
     for row in rows:
         term = dot(row[...], kept[:, place:place + row.shape[1]])
         total = term if total is None else total + term
         place += row.shape[1]
-    total = (total * weight_row()).astype(BF16)
+    return total
+
+
+def give(gram, own_out, sib_out):
+    total = (gram * weight_row()).astype(BF16)
     own_out[...] = total[:256]
     sib_out[...] = total[256:]
+
+
+def begin_kernel(points, env_a, env_b, rows_a, rows_b, point_hat, gram, kept):
+    point_hat[...] = unit(points[...])
+    kernel_values(point_hat[...], (env_a, env_b), kept)
+    gram[...] = products((rows_a, rows_b), kept)
+
+
+def last_kernel(near, far, points_hat, gram, first_hat, first_gram, second_hat, second_gram,
+                env_hat, rows_k, own0, sib0, own1, sib1, own2, sib2, kept):
+    rows_of(points_hat[...], (near, far), env_hat, rows_k)
+    give(gram[...] + dot(rows_k[...], rows_k[:256, :]), own0, sib0)
+    for point_hat, begun, own, sib in ((first_hat, first_gram, own1, sib1), (second_hat, second_gram, own2, sib2)):
+        kernel_values(point_hat[...], (env_hat,), kept)
+        give(begun[...] + products((rows_k,), kept), own, sib)
+
+
+def column_kernel(points, *refs):
+    kernel_values(unit(points[...]), refs[:3], refs[8])
+    give(products(refs[3:6], refs[8]), refs[6], refs[7])
 
 
 def pack_kernel(*refs):
@@ -211,28 +229,31 @@
     near_b = fetch(high, near_x)
     far = fetch(near, other_core)
     env_b, rows_b, gram = rows(more_kernel, 1024, (gram_shape,), 4, near, far, points_hat, gram)
-    near_b, column, env_b, rows_b, gram = barrier((near_b, columns[2], env_b, rows_b, gram))
-
-    columns.append(fetch(column, next_z))
-    env_c, rows_c, own, sib = rows(
-        last_kernel, 1024, pair, 4, near_b, fetch(near_b, other_core), points_hat, gram
-    )
-    owns, sibs = [own], [sib]
+    begun = []
+    for points in columns[:2]:
+        begun += call(
+            begin_kernel, (shape(256, 512), gram_shape), 5, 2 * 805306368, 1 << 23, (pltpu.VMEM((256, 3072), BF16),)
+        )(points, env_a, env_b, rows_a, rows_b)
+    near_b, column, env_b, rows_b, gram, *begun = barrier((near_b, columns[2], env_b, rows_b, gram, *begun))
+
+    last = fetch(column, next_z)
+    env_c, rows_c, *sums = call(
+        last_kernel, (shape(1024, 512), shape(512, 1024)) + 3 * pair, 8, 2 * 1207959552, 1 << 23,
+        (pltpu.VMEM((256, 1024), BF16),)
+    )(near_b, fetch(near_b, other_core), points_hat, gram, *begun)
 
     def take(points):
-        own, sib = call(
+        return call(
             column_kernel, pair, 7, 2 * 1073741824, 1 << 23, (pltpu.VMEM((256, 4096), BF16),)
         )(points, env_a, env_b, env_c, rows_a, rows_b, rows_c)
-        owns.append(own)
-        sibs.append(sib)
-
-    for points in columns[:3]:
-        take(points)
-    column, *owns = barrier((columns[3], *owns))
-    take(column)
-
-    swapped = [fetch(sib, other_core) for sib in sibs]
-    packed = call(pack_kernel, shape(8, 9, 32, 256), 10, 0, 1 << 21)(*owns, *swapped)
+
+    sums += take(column)
+    owns, swapped = sums[0::2], [fetch(sib, other_core) for sib in sums[1::2]]
+    last, *sums = barrier((last, *owns, *swapped))
+    owns, swapped = sums[:4], sums[4:]
+
+    own, sib = take(last)
+    packed = call(pack_kernel, shape(8, 9, 32, 256), 10, 0, 1 << 21)(*owns, own, *swapped, fetch(sib, other_core))
     pieces = lax.all_to_all(packed, "env", 0, 0, tiled=True)
     return call(finish_kernel, shape(17, 32, 256, dtype=F32), 1, 0, 1 << 21)(pieces)[None]
 

time: 77.2 us -> 74.7 us (0.968)
  waiting for transfers between devices: 12.4 us -> 9.85 us
    pallas_call x1 -> x4, Pallas kernels: 0.08 us -> 6.3 us  [the longest x2 3.72 us: on_device(): call(begin_kernel, (shape(256, 512), gram_shape), 5, 2 * 805306368, 1 <<...]
    pallas_call x4 -> x2, Pallas kernels: 9.63 us -> 4.81 us  [take(): call(column_kernel, pair, 7, 2 * 1073741824, 1 << 23, (pltpu.VMEM((256, 4...]
    ppermute x14, waiting for transfers between devices: 12.4 us -> 9.85 us  [fetch(): return lax.ppermute(value, ('env', 'sp'), pairs)]
    pallas_call x3 -> x2, Pallas kernels: 4.83 us -> 3.53 us  [rows(): call(body, (shape(envs, 512), shape(512, envs)) + sums, n_in, envs * 7864...]
  transfers between devices with their start and end apart: 14 -> 14, of which waited for: 9 -> 10; matrix products, arithmetic and copies ran while one was open for 0% -> 0% of each run, Pallas kernels for 16% -> 16%
where the time goes in v7:
time: 74.7 us; the launch traced here: 74.6 us
  blocking collectives  23.5 us (31%)
  starting transfers between devices  22.8 us (31%)
  Pallas kernels  15.7 us (21%)
  waiting for transfers between devices  9.85 us (13%)
  local copies, waits for them, and re-layouts  2.54 us (3%)
    all_to_all x1, blocking collectives, on_device(): pieces = lax.all_to_all(packed, 'env', 0, 0, tiled=True)  23.5 us
    ppermute x14, starting transfers between devices, fetch(): return lax.ppermute(value, ('env', 'sp'), pairs)  22.8 us
    ppermute x14, waiting for transfers between devices, fetch(): return lax.ppermute(value, ('env', 'sp'), pairs)  9.85 us
    pallas_call x2, Pallas kernels, take(): call(column_kernel, pair, 7, 2 * 1073741824, 1 << 23, (pltpu.VMEM((256, 4...  4.81 us
    pallas_call x2, Pallas kernels, on_device(): call(begin_kernel, (shape(256, 512), gram_shape), 5, 2 * 805306368, 1 <<...  3.72 us
    pallas_call x2, Pallas kernels, rows(): call(body, (shape(envs, 512), shape(512, envs)) + sums, n_in, envs * 7864...  3.53 us
    unnamed x4, local copies, waits for them, and re-layouts  2.54 us
    pallas_call x1, Pallas kernels, on_device(): call(last_kernel, (shape(1024, 512), shape(512, 1024)) + 3 * pair, 8, 2 *...  2.5 us
  transfers between devices with their start and end apart: 14, of which 10 were waited for; matrix products, arithmetic and copies ran while one was open for 0% of the time, Pallas kernels for 16%

profile of v7, /device:TPU:1, one launch (start us, length us, event | category | flops | bytes accessed | tf_op | source)
XLA Modules:
  0.0 74.6 jit_solution(12237368784931353713)
XLA Ops:
  0.0 3.2 %collective-permute-start.1 = (bf16[256,512]{1,0:T(8,128)(2,1)}, bf16[256,512]{1,0:T(8,128)(2,1)S(1)}, u32[]{:S(2)}, u32[]{:S(2)}) collective-permute-start(bf16[256,512]{1,0:T(8,128)(2,1)} %own_points.1), channel_id=1, source_target_pairs={{1,0},{0,1},{3,2},{2,3},{5,4},{4,5},{7,6},{6,7},{9,8},{8,9},{11,10... | collective-permute-start | bytes 786440 | tf_op jit(solution)/shard_map/ppermute | solution.py:30
  3.2 3.8 %collective-permute-start = (bf16[256,512]{1,0:T(8,128)(2,1)}, bf16[256,512]{1,0:T(8,128)(2,1)S(1)}, u32[]{:S(2)}, u32[]{:S(2)}) collective-permute-start(bf16[256,512]{1,0:T(8,128)(2,1)} %own_points.1), channel_id=1, source_target_pairs={{4,0},{5,1},{6,2},{7,3},{8,4},{9,5},{10,6},{11,7},{12,8},{13,9},{1... | collective-permute-start | bytes 786440 | tf_op jit(solution)/shard_map/ppermute | solution.py:30
  7.1 0.0 collective-permute-done.1.sib_points
  7.1 0.0 copy-start
  7.1 1.6 %copy-done = bf16[2048,512]{1,0:T(8,128)(2,1)S(1)} copy-done((bf16[2048,512]{1,0:T(8,128)(2,1)S(1)}, bf16[2048,512]{1,0:T(8,128)(2,1)}, u32[]{:S(2)}) %copy-start) | copy-done | bytes 2097176
  8.7 0.0 copy-start.1
  8.7 0.9 %copy-done.1 = bf16[256,512]{1,0:T(8,128)(2,1)S(1)} copy-done((bf16[256,512]{1,0:T(8,128)(2,1)S(1)}, bf16[256,512]{1,0:T(8,128)(2,1)}, u32[]{:S(2)}) %copy-start.1) | copy-done | bytes 262168
  9.6 2.2 %shard_map.28 = (bf16[2048,512]{1,0:T(8,128)(2,1)S(1)}, bf16[512,2048]{1,0:T(8,128)(2,1)S(1)}, f32[512,256]{1,0:T(8,128)S(1)}, bf16[512,512]{1,0:T(8,128)(2,1)S(1)}) custom-call(bf16[2048,512]{1,0:T(8,128)(2,1)S(1)} %copy-done, bf16[256,512]{1,0:T(8,128)(2,1)S(1)} %copy-done.1, bf16[256,512]{1,0:T(8,128)(2,1)S(1)} %collective-permute-done.1.sib_points), custom_call_target="tpu_custom_call" | custom-call | flops 1610612736 | bytes 8388608 | tf_op jit(solution)/shard_map/pallas_call | solution.py:209
  11.9 1.3 %collective-permute-done.points = bf16[256,512]{1,0:T(8,128)(2,1)S(1)} collective-permute-done((bf16[256,512]{1,0:T(8,128)(2,1)}, bf16[256,512]{1,0:T(8,128)(2,1)S(1)}, u32[]{:S(2)}, u32[]{:S(2)}) %collective-permute-start) | collective-permute-done | bytes 262176 | tf_op jit(solution)/shard_map/ppermute | solution.py:30
  13.1 0.1 shard_map.29
  13.2 1.1 %collective-permute-start.2 = (bf16[512,512]{1,0:T(8,128)(2,1)S(1)}, bf16[512,512]{1,0:T(8,128)(2,1)S(1)}, u32[]{:S(2)}, u32[]{:S(2)}) collective-permute-start(bf16[512,512]{1,0:T(8,128)(2,1)S(1)} %get-tuple-element.62), channel_id=1, source_target_pairs={{32,0},{97,1},{34,2},{99,3},{36,4},{101,5},{38,6},{103,7},{40,8},{... | collective-permute-start | bytes 1572872 | tf_op jit(solution)/shard_map/ppermute | solution.py:30
  14.3 2.4 %collective-permute-start.3 = (bf16[256,512]{1,0:T(8,128)(2,1)S(1)}, bf16[256,512]{1,0:T(8,128)(2,1)S(1)}, u32[]{:S(2)}, u32[]{:S(2)}) collective-permute-start(bf16[256,512]{1,0:T(8,128)(2,1)S(1)} %collective-permute-done.points), channel_id=1, source_target_pairs={{4,0},{5,1},{6,2},{7,3},{8,4},{9,5},{10,6},{11,7},{12,8},{13,9},{1... | collective-permute-start | bytes 786440 | tf_op jit(solution)/shard_map/ppermute | solution.py:30
  16.7 3.7 %collective-permute-done.3.points = bf16[256,512]{1,0:T(8,128)(2,1)S(1)} collective-permute-done((bf16[256,512]{1,0:T(8,128)(2,1)S(1)}, bf16[256,512]{1,0:T(8,128)(2,1)S(1)}, u32[]{:S(2)}, u32[]{:S(2)}) %collective-permute-start.3) | collective-permute-done | bytes 262176 | tf_op jit(solution)/shard_map/ppermute | solution.py:30
  20.4 2.1 %collective-permute-done.2.near = bf16[512,512]{1,0:T(8,128)(2,1)S(1)} collective-permute-done((bf16[512,512]{1,0:T(8,128)(2,1)S(1)}, bf16[512,512]{1,0:T(8,128)(2,1)S(1)}, u32[]{:S(2)}, u32[]{:S(2)}) %collective-permute-start.2) | collective-permute-done | bytes 524320 | tf_op jit(solution)/shard_map/ppermute | solution.py:30
  22.5 2.0 %collective-permute-start.6 = (bf16[512,512]{1,0:T(8,128)(2,1)S(1)}, bf16[512,512]{1,0:T(8,128)(2,1)S(1)}, u32[]{:S(2)}, u32[]{:S(2)}) collective-permute-start(bf16[512,512]{1,0:T(8,128)(2,1)S(1)} %collective-permute-done.2.near), channel_id=1, source_target_pairs={{1,0},{0,1},{3,2},{2,3},{5,4},{4,5},{7,6},{6,7},{9,8},{8,9},{11,10... | collective-permute-start | bytes 1572872 | tf_op jit(solution)/shard_map/ppermute | solution.py:30
  24.5 1.0 %collective-permute-start.4 = (bf16[512,512]{1,0:T(8,128)(2,1)S(1)}, bf16[512,512]{1,0:T(8,128)(2,1)S(1)}, u32[]{:S(2)}, u32[]{:S(2)}) collective-permute-start(bf16[512,512]{1,0:T(8,128)(2,1)S(1)} %get-tuple-element.65), channel_id=1, source_target_pairs={{32,0},{97,1},{34,2},{99,3},{36,4},{101,5},{38,6},{103,7},{40,8},{... | collective-permute-start | bytes 1572872 | tf_op jit(solution)/shard_map/ppermute | solution.py:30
  25.6 3.4 %collective-permute-start.5 = (bf16[256,512]{1,0:T(8,128)(2,1)S(1)}, bf16[256,512]{1,0:T(8,128)(2,1)S(1)}, u32[]{:S(2)}, u32[]{:S(2)}) collective-permute-start(bf16[256,512]{1,0:T(8,128)(2,1)S(1)} %collective-permute-done.3.points), channel_id=1, source_target_pairs={{4,0},{5,1},{6,2},{7,3},{8,4},{9,5},{10,6},{11,7},{12,8},{13,9},{1... | collective-permute-start | bytes 786440 | tf_op jit(solution)/shard_map/ppermute | solution.py:30
  29.0 0.0 collective-permute-done.6.far
  29.0 1.3 %shard_map.30 = (bf16[1024,512]{1,0:T(8,128)(2,1)S(1)}, bf16[512,1024]{1,0:T(8,128)(2,1)S(1)}, f32[512,256]{1,0:T(8,128)S(1)}) custom-call(bf16[512,512]{1,0:T(8,128)(2,1)S(1)} %collective-permute-done.2.near, bf16[512,512]{1,0:T(8,128)(2,1)S(1)} %collective-permute-done.6.far, bf16[512,512]{1,0:T(8,128)(2,1)S(1)} %get-tuple-element.68.points_hat, ...), custom_call_target="tpu_custom_call" | custom-call | flops 805306368 | bytes 4194304 | tf_op jit(solution)/shard_map/pallas_call | solution.py:209
  30.3 1.9 %shard_map.32 = (bf16[256,512]{1,0:T(8,128)(2,1)S(1)}, f32[512,256]{1,0:T(8,128)S(1)}) custom-call(bf16[256,512]{1,0:T(8,128)(2,1)S(1)} %collective-permute-done.3.points, bf16[2048,512]{1,0:T(8,128)(2,1)S(1)} %get-tuple-element.73.env_a.refs_0_, bf16[1024,512]{1,0:T(8,128)(2,1)S(1)} %get-tuple-element.89.env_b.refs_1_, ...), custom_call_target="tpu_custom_call" | custom-call | flops 1610612736 | bytes 8388608 | tf_op jit(solution)/shard_map/pallas_call | solution.py:234
  32.2 1.9 %shard_map.31 = (bf16[256,512]{1,0:T(8,128)(2,1)S(1)}, f32[512,256]{1,0:T(8,128)S(1)}) custom-call(bf16[256,512]{1,0:T(8,128)(2,1)S(1)} %collective-permute-done.points, bf16[2048,512]{1,0:T(8,128)(2,1)S(1)} %get-tuple-element.73.env_a.refs_0_, bf16[1024,512]{1,0:T(8,128)(2,1)S(1)} %get-tuple-element.89.env_b.refs_1_, ...), custom_call_target="tpu_custom_call" | custom-call | flops 1610612736 | bytes 8388608 | tf_op jit(solution)/shard_map/pallas_call | solution.py:234
  34.0 0.1 collective-permute-done.5.points
  34.1 0.4 collective-permute-done.4.near
  34.5 1.0 %collective-permute-start.8 = (bf16[512,512]{1,0:T(8,128)(2,1)S(1)}, bf16[512,512]{1,0:T(8,128)(2,1)S(1)}, u32[]{:S(2)}, u32[]{:S(2)}) collective-permute-start(bf16[512,512]{1,0:T(8,128)(2,1)S(1)} %collective-permute-done.4.near), channel_id=1, source_target_pairs={{1,0},{0,1},{3,2},{2,3},{5,4},{4,5},{7,6},{6,7},{9,8},{8,9},{11,10... | collective-permute-start | bytes 1572872 | tf_op jit(solution)/shard_map/ppermute | solution.py:30
  35.5 3.4 %collective-permute-start.7 = (bf16[256,512]{1,0:T(8,128)(2,1)S(1)}, bf16[256,512]{1,0:T(8,128)(2,1)S(1)}, u32[]{:S(2)}, u32[]{:S(2)}) collective-permute-start(bf16[256,512]{1,0:T(8,128)(2,1)S(1)} %collective-permute-done.5.points), channel_id=1, source_target_pairs={{4,0},{5,1},{6,2},{7,3},{8,4},{9,5},{10,6},{11,7},{12,8},{13,9},{1... | collective-permute-start | bytes 786440 | tf_op jit(solution)/shard_map/ppermute | solution.py:30
  38.9 0.0 collective-permute-done.8.far
  38.9 2.5 %shard_map.33 = (bf16[1024,512]{1,0:T(8,128)(2,1)S(1)}, bf16[512,1024]{1,0:T(8,128)(2,1)S(1)}, bf16[256,256]{1,0:T(8,128)(2,1)S(1)}, bf16[256,256]{1,0:T(8,128)(...) custom-call(bf16[512,512]{1,0:T(8,128)(2,1)S(1)} %collective-permute, ...), custom_call_target="tpu_custom_call" | custom-call | flops 2415919104 | bytes 8388608 | tf_op jit(solution)/shard_map/pallas_call | solution.py:240
  41.4 2.4 %shard_map.34 = (bf16[256,256]{1,0:T(8,128)(2,1)S(1)}, bf16[256,256]{1,0:T(8,128)(2,1)S(1)}) custom-call(bf16[256,512]{1,0:T(8,128)(2,1)S(1)} %collective-permute-done.5.points, bf16[2048,512]{1,0:T(8,128)(2,1)S(1)} %get-tuple-element.73.env_a.refs_0_, bf16[1024,512]{1,0:T(8,128)(2,1)S(1)} %get-tuple-element.89.env_b.refs_1_, ...), custom_call_target="tpu_custom_call" | custom-call | flops 2147483648 | bytes 8388608 | tf_op jit(solution)/shard_map/pallas_call | solution.py:246
  43.8 0.4 collective-permute-start.12
  44.2 0.2 collective-permute-start.10
  44.4 0.3 collective-permute-start.11
  44.7 0.2 collective-permute-start.9
  44.9 0.0 collective-permute-done.7.points
  45.0 0.3 collective-permute-done.12.refs_8_
  45.3 0.3 collective-permute-done.10.refs_6_
  45.6 0.2 collective-permute-done.11.refs_7_
  45.8 0.3 collective-permute-done.9.refs_5_
  46.1 2.4 %shard_map.35 = (bf16[256,256]{1,0:T(8,128)(2,1)S(1)}, bf16[256,256]{1,0:T(8,128)(2,1)S(1)}) custom-call(bf16[256,512]{1,0:T(8,128)(2,1)S(1)} %collective-permute-done.7.points, bf16[2048,512]{1,0:T(8,128)(2,1)S(1)} %get-tuple-element.73.env_a.refs_0_, bf16[1024,512]{1,0:T(8,128)(2,1)S(1)} %get-tuple-element.89.env_b.refs_1_, ...), custom_call_target="tpu_custom_call" | custom-call | flops 2147483648 | bytes 8388608 | tf_op jit(solution)/shard_map/pallas_call | solution.py:246
  48.5 0.3 collective-permute-start.13
  48.8 1.1 %collective-permute-done.13.refs_9_ = bf16[256,256]{1,0:T(8,128)(2,1)S(1)} collective-permute-done((bf16[256,256]{1,0:T(8,128)(2,1)S(1)}, bf16[256,256]{1,0:T(8,128)(2,1)S(1)}, u32[]{:S(2)}, u32[]{:S(2)}) %collective-permute-start.13) | collective-permute-done | bytes 131104 | tf_op jit(solution)/shard_map/ppermute | solution.py:30
  49.9 0.1 shard_map.36
  50.0 23.5 %all_to_all.5.pieces = bf16[8,9,32,256]{3,2,1,0:T(8,128)(2,1)S(1)} all-to-all(bf16[8,9,32,256]{3,2,1,0:T(8,128)(2,1)S(1)} %shard_map.36), channel_id=1, replica_groups=mesh['env'=8,'sp'=32] {'env'}, dimensions={0} | all-to-all | bytes 2359296 | tf_op jit(solution)/shard_map/all_to_all | solution.py:257
  73.5 1.0 %shard_map.37 = f32[17,32,256]{2,1,0:T(8,128)} custom-call(bf16[8,9,32,256]{3,2,1,0:T(8,128)(2,1)S(1)} %all_to_all.5.pieces), custom_call_target="tpu_custom_call" | custom-call | bytes 2097152 | tf_op jit(solution)/shard_map/pallas_call | solution.py:258
Async XLA Ops:
  0.0 7.1 %collective-permute-start.1 = (bf16[256,512]{1,0:T(8,128)(2,1)}, bf16[256,512]{1,0:T(8,128)(2,1)S(1)}, u32[]{:S(2)}, u32[]{:S(2)}) collective-permute-start(bf16[256,512]{1,0:T(8,128)(2,1)} %own_points.1), channel_id=1, source_target_pairs={{1,0},{0,1},{3,2},{2,3},{5,4},{4,5},{7,6},{6,7},{9,8},{8,9},{11,10... | collective-permute-start | bytes 786440 | tf_op jit(solution)/shard_map/ppermute | solution.py:30
  3.2 9.9 %collective-permute-start = (bf16[256,512]{1,0:T(8,128)(2,1)}, bf16[256,512]{1,0:T(8,128)(2,1)S(1)}, u32[]{:S(2)}, u32[]{:S(2)}) collective-permute-start(bf16[256,512]{1,0:T(8,128)(2,1)} %own_points.1), channel_id=1, source_target_pairs={{4,0},{5,1},{6,2},{7,3},{8,4},{9,5},{10,6},{11,7},{12,8},{13,9},{1... | collective-permute-start | bytes 786440 | tf_op jit(solution)/shard_map/ppermute | solution.py:30
  7.1 1.6 %copy-start = (bf16[2048,512]{1,0:T(8,128)(2,1)S(1)}, bf16[2048,512]{1,0:T(8,128)(2,1)}, u32[]{:S(2)}) copy-start(bf16[2048,512]{1,0:T(8,128)(2,1)} %descriptors) | copy-start | bytes 6291460
  8.7 0.9 %copy-start.1 = (bf16[256,512]{1,0:T(8,128)(2,1)S(1)}, bf16[256,512]{1,0:T(8,128)(2,1)}, u32[]{:S(2)}) copy-start(bf16[256,512]{1,0:T(8,128)(2,1)} %own_points.1) | copy-start | bytes 786436
  13.2 9.3 %collective-permute-start.2 = (bf16[512,512]{1,0:T(8,128)(2,1)S(1)}, bf16[512,512]{1,0:T(8,128)(2,1)S(1)}, u32[]{:S(2)}, u32[]{:S(2)}) collective-permute-start(bf16[512,512]{1,0:T(8,128)(2,1)S(1)} %get-tuple-element.62), channel_id=1, source_target_pairs={{32,0},{97,1},{34,2},{99,3},{36,4},{101,5},{38,6},{103,7},{40,8},{... | collective-permute-start | bytes 1572872 | tf_op jit(solution)/shard_map/ppermute | solution.py:30
  14.3 6.1 %collective-permute-start.3 = (bf16[256,512]{1,0:T(8,128)(2,1)S(1)}, bf16[256,512]{1,0:T(8,128)(2,1)S(1)}, u32[]{:S(2)}, u32[]{:S(2)}) collective-permute-start(bf16[256,512]{1,0:T(8,128)(2,1)S(1)} %collective-permute-done.points), channel_id=1, source_target_pairs={{4,0},{5,1},{6,2},{7,3},{8,4},{9,5},{10,6},{11,7},{12,8},{13,9},{1... | collective-permute-start | bytes 786440 | tf_op jit(solution)/shard_map/ppermute | solution.py:30
  22.5 6.5 %collective-permute-start.6 = (bf16[512,512]{1,0:T(8,128)(2,1)S(1)}, bf16[512,512]{1,0:T(8,128)(2,1)S(1)}, u32[]{:S(2)}, u32[]{:S(2)}) collective-permute-start(bf16[512,512]{1,0:T(8,128)(2,1)S(1)} %collective-permute-done.2.near), channel_id=1, source_target_pairs={{1,0},{0,1},{3,2},{2,3},{5,4},{4,5},{7,6},{6,7},{9,8},{8,9},{11,10... | collective-permute-start | bytes 1572872 | tf_op jit(solution)/shard_map/ppermute | solution.py:30
  24.5 10.0 %collective-permute-start.4 = (bf16[512,512]{1,0:T(8,128)(2,1)S(1)}, bf16[512,512]{1,0:T(8,128)(2,1)S(1)}, u32[]{:S(2)}, u32[]{:S(2)}) collective-permute-start(bf16[512,512]{1,0:T(8,128)(2,1)S(1)} %get-tuple-element.65), channel_id=1, source_target_pairs={{32,0},{97,1},{34,2},{99,3},{36,4},{101,5},{38,6},{103,7},{40,8},{... | collective-permute-start | bytes 1572872 | tf_op jit(solution)/shard_map/ppermute | solution.py:30
  25.6 8.6 %collective-permute-start.5 = (bf16[256,512]{1,0:T(8,128)(2,1)S(1)}, bf16[256,512]{1,0:T(8,128)(2,1)S(1)}, u32[]{:S(2)}, u32[]{:S(2)}) collective-permute-start(bf16[256,512]{1,0:T(8,128)(2,1)S(1)} %collective-permute-done.3.points), channel_id=1, source_target_pairs={{4,0},{5,1},{6,2},{7,3},{8,4},{9,5},{10,6},{11,7},{12,8},{13,9},{1... | collective-permute-start | bytes 786440 | tf_op jit(solution)/shard_map/ppermute | solution.py:30
  34.5 4.4 %collective-permute-start.8 = (bf16[512,512]{1,0:T(8,128)(2,1)S(1)}, bf16[512,512]{1,0:T(8,128)(2,1)S(1)}, u32[]{:S(2)}, u32[]{:S(2)}) collective-permute-start(bf16[512,512]{1,0:T(8,128)(2,1)S(1)} %collective-permute-done.4.near), channel_id=1, source_target_pairs={{1,0},{0,1},{3,2},{2,3},{5,4},{4,5},{7,6},{6,7},{9,8},{8,9},{11,10... | collective-permute-start | bytes 1572872 | tf_op jit(solution)/shard_map/ppermute | solution.py:30
  35.5 9.5 %collective-permute-start.7 = (bf16[256,512]{1,0:T(8,128)(2,1)S(1)}, bf16[256,512]{1,0:T(8,128)(2,1)S(1)}, u32[]{:S(2)}, u32[]{:S(2)}) collective-permute-start(bf16[256,512]{1,0:T(8,128)(2,1)S(1)} %collective-permute-done.5.points), channel_id=1, source_target_pairs={{4,0},{5,1},{6,2},{7,3},{8,4},{9,5},{10,6},{11,7},{12,8},{13,9},{1... | collective-permute-start | bytes 786440 | tf_op jit(solution)/shard_map/ppermute | solution.py:30
  43.8 1.4 %collective-permute-start.12 = (bf16[256,256]{1,0:T(8,128)(2,1)S(1)}, bf16[256,256]{1,0:T(8,128)(2,1)S(1)}, u32[]{:S(2)}, u32[]{:S(2)}) collective-permute-start(bf16[256,256]{1,0:T(8,128)(2,1)S(1)} %get-tuple-element.97), channel_id=1, source_target_pairs={{1,0},{0,1},{3,2},{2,3},{5,4},{4,5},{7,6},{6,7},{9,8},{8,9},{11,10... | collective-permute-start | bytes 393224 | tf_op jit(solution)/shard_map/ppermute | solution.py:30
  44.2 1.3 %collective-permute-start.10 = (bf16[256,256]{1,0:T(8,128)(2,1)S(1)}, bf16[256,256]{1,0:T(8,128)(2,1)S(1)}, u32[]{:S(2)}, u32[]{:S(2)}) collective-permute-start(bf16[256,256]{1,0:T(8,128)(2,1)S(1)} %get-tuple-element.95), channel_id=1, source_target_pairs={{1,0},{0,1},{3,2},{2,3},{5,4},{4,5},{7,6},{6,7},{9,8},{8,9},{11,10... | collective-permute-start | bytes 393224 | tf_op jit(solution)/shard_map/ppermute | solution.py:30
  44.4 1.3 %collective-permute-start.11 = (bf16[256,256]{1,0:T(8,128)(2,1)S(1)}, bf16[256,256]{1,0:T(8,128)(2,1)S(1)}, u32[]{:S(2)}, u32[]{:S(2)}) collective-permute-start(bf16[256,256]{1,0:T(8,128)(2,1)S(1)} %get-tuple-element.96), channel_id=1, source_target_pairs={{1,0},{0,1},{3,2},{2,3},{5,4},{4,5},{7,6},{6,7},{9,8},{8,9},{11,10... | collective-permute-start | bytes 393224 | tf_op jit(solution)/shard_map/ppermute | solution.py:30
  44.7 1.3 %collective-permute-start.9 = (bf16[256,256]{1,0:T(8,128)(2,1)S(1)}, bf16[256,256]{1,0:T(8,128)(2,1)S(1)}, u32[]{:S(2)}, u32[]{:S(2)}) collective-permute-start(bf16[256,256]{1,0:T(8,128)(2,1)S(1)} %get-tuple-element.94), channel_id=1, source_target_pairs={{1,0},{0,1},{3,2},{2,3},{5,4},{4,5},{7,6},{6,7},{9,8},{8,9},{11,10... | collective-permute-start | bytes 393224 | tf_op jit(solution)/shard_map/ppermute | solution.py:30
  48.5 1.4 %collective-permute-start.13 = (bf16[256,256]{1,0:T(8,128)(2,1)S(1)}, bf16[256,256]{1,0:T(8,128)(2,1)S(1)}, u32[]{:S(2)}, u32[]{:S(2)}) collective-permute-start(bf16[256,256]{1,0:T(8,128)(2,1)S(1)} %get-tuple-element.108), channel_id=1, source_target_pairs={{1,0},{0,1},{3,2},{2,3},{5,4},{4,5},{7,6},{6,7},{9,8},{8,9},{11,10... | collective-permute-start | bytes 393224 | tf_op jit(solution)/shard_map/ppermute | solution.py:30

commit v8 on v7

--- a/solution.py
+++ b/solution.py
@@ -65,6 +65,7 @@
 
 
 CHUNK = 512
+PIECES = 4
 
 
 def weight_row():
@@ -84,16 +85,22 @@
     place = 0
     for ref in raw:
         for start in range(0, ref.shape[0], CHUNK):
-            env = unit(ref[start:start + CHUNK, :])
-            env_hat[place:place + CHUNK, :] = env
-            rows_k[:, place:place + CHUNK] = fourth(dot(points, env))
-            place += CHUNK
-
-
-def slice_kernel(descriptors, first_out, second_out):
+            size = min(CHUNK, ref.shape[0] - start)
+            env = unit(ref[start:start + size, :])
+            env_hat[place:place + size, :] = env
+            rows_k[:, place:place + size] = fourth(dot(points, env))
+            place += size
+
+
+def slice_kernel(descriptors, out):
     half = pl.multiple_of((lax.axis_index("sp") % 2) * 1024, 1024)
-    first_out[...] = descriptors[pl.ds(half, 512), :]
-    second_out[...] = descriptors[pl.ds(half + 512, 512), :]
+    out[...] = descriptors[pl.ds(half, 1024), :]
+
+
+def split_kernel(near, *outs):
+    size = near.shape[0] // len(outs)
+    for i, out in enumerate(outs):
+        out[...] = near[size * i:size * i + size, :]
 
 
 def own_kernel(own_env, own_points, sib_points, env_hat, rows_k, gram, points_hat):
@@ -101,11 +108,6 @@
     points_hat[256:, :] = unit(sib_points[...])
     rows_of(points_hat[...], (own_env,), env_hat, rows_k)
     gram[...] = dot(rows_k[...], rows_k[:256, :])
-
-
-def more_kernel(near, far, points_hat, gram, env_hat, rows_k, gram_out):
-    rows_of(points_hat[...], (near, far), env_hat, rows_k)
-    gram_out[...] = gram[...] + dot(rows_k[...], rows_k[:256, :])
 
 
 def kernel_values(point_hat, envs, kept):
@@ -131,24 +133,15 @@
     sib_out[...] = total[256:]
 
 
-def begin_kernel(points, env_a, env_b, rows_a, rows_b, point_hat, gram, kept):
-    point_hat[...] = unit(points[...])
-    kernel_values(point_hat[...], (env_a, env_b), kept)
-    gram[...] = products((rows_a, rows_b), kept)
-
-
-def last_kernel(near, far, points_hat, gram, first_hat, first_gram, second_hat, second_gram,
-                env_hat, rows_k, own0, sib0, own1, sib1, own2, sib2, kept):
-    rows_of(points_hat[...], (near, far), env_hat, rows_k)
-    give(gram[...] + dot(rows_k[...], rows_k[:256, :]), own0, sib0)
-    for point_hat, begun, own, sib in ((first_hat, first_gram, own1, sib1), (second_hat, second_gram, own2, sib2)):
-        kernel_values(point_hat[...], (env_hat,), kept)
-        give(begun[...] + products((rows_k,), kept), own, sib)
+def more_kernel(*refs):
+    points_hat, gram, env_hat, rows_k, own_out, sib_out = refs[2 * PIECES:]
+    rows_of(points_hat[...], refs[:2 * PIECES], env_hat, rows_k)
+    give(gram[...] + dot(rows_k[...], rows_k[:256, :]), own_out, sib_out)
 
 
 def column_kernel(points, *refs):
-    kernel_values(unit(points[...]), refs[:3], refs[8])
-    give(products(refs[3:6], refs[8]), refs[6], refs[7])
+    kernel_values(unit(points[...]), refs[:2], refs[6])
+    give(products(refs[2:4], refs[6]), refs[4], refs[5])
 
 
 def pack_kernel(*refs):
@@ -222,32 +215,25 @@
     )
 
     columns.append(fetch(column, next_z))
-    low, high = call(slice_kernel, (shape(512, 512), shape(512, 512)), 1, 0, 1 << 21)(later)
-    near, high, column = barrier((fetch(low, near_x), high, columns[1]))
-
-    columns.append(fetch(column, next_z))
-    near_b = fetch(high, near_x)
-    far = fetch(near, other_core)
-    env_b, rows_b, gram = rows(more_kernel, 1024, (gram_shape,), 4, near, far, points_hat, gram)
-    begun = []
-    for points in columns[:2]:
-        begun += call(
-            begin_kernel, (shape(256, 512), gram_shape), 5, 2 * 805306368, 1 << 23, (pltpu.VMEM((256, 3072), BF16),)
-        )(points, env_a, env_b, rows_a, rows_b)
-    near_b, column, env_b, rows_b, gram, *begun = barrier((near_b, columns[2], env_b, rows_b, gram, *begun))
-
-    last = fetch(column, next_z)
-    env_c, rows_c, *sums = call(
-        last_kernel, (shape(1024, 512), shape(512, 1024)) + 3 * pair, 8, 2 * 1207959552, 1 << 23,
-        (pltpu.VMEM((256, 1024), BF16),)
-    )(near_b, fetch(near_b, other_core), points_hat, gram, *begun)
+    near = fetch(call(slice_kernel, shape(1024, 512), 1, 0, 1 << 21)(later), near_x)
+    near, _ = barrier((near, columns[1]))
+
+    columns.append(fetch(columns[1], next_z))
+    near = call(split_kernel, PIECES * (shape(1024 // PIECES, 512),), 1, 0, 1 << 21)(near)
+    far = [fetch(piece, other_core) for piece in near]
+    env_b, rows_b, own, sib = rows(more_kernel, 2048, pair, 2 * PIECES + 2, *near, *far, points_hat, gram)
 
     def take(points):
         return call(
-            column_kernel, pair, 7, 2 * 1073741824, 1 << 23, (pltpu.VMEM((256, 4096), BF16),)
-        )(points, env_a, env_b, env_c, rows_a, rows_b, rows_c)
-
-    sums += take(column)
+            column_kernel, pair, 5, 2 * 1073741824, 1 << 23, (pltpu.VMEM((256, 4096), BF16),)
+        )(points, env_a, env_b, rows_a, rows_b)
+
+    sums = [own, sib]
+    column = columns[2]
+
+    last = fetch(column, next_z)
+    for points in columns[:3]:
+        sums += take(points)
     owns, swapped = sums[0::2], [fetch(sib, other_core) for sib in sums[1::2]]
     last, *sums = barrier((last, *owns, *swapped))
     owns, swapped = sums[:4], sums[4:]

time: 74.7 us -> 77.9 us (1.043); the launches traced: 74.6 us -> 76.9 us
  blocking collectives: 23.5 us -> 26 us
  waiting for transfers between devices: 9.85 us -> 11.4 us
  starting transfers between devices: 22.8 us -> 21.7 us
    all_to_all x1, blocking collectives: 23.5 us -> 26 us  [on_device(): pieces = lax.all_to_all(packed, 'env', 0, 0, tiled=True)]
    ppermute x14 -> x15, waiting for transfers between devices: 9.85 us -> 11.4 us  [fetch(): return lax.ppermute(value, ('env', 'sp'), pairs)]
    pallas_call x6, Pallas kernels: 11.1 us -> 9.76 us  [the longest x4 9.62 us: take(): call(column_kernel, pair, 5, 2 * 1073741824, 1 << 23, (pltpu.VMEM((256, 4...]
    ppermute x14 -> x15, starting transfers between devices: 22.8 us -> 21.7 us  [fetch(): return lax.ppermute(value, ('env', 'sp'), pairs)]
    pallas_call x2, Pallas kernels: 3.53 us -> 4.41 us  [rows(): call(body, (shape(envs, 512), shape(512, envs)) + sums, n_in, envs * 7864...]
  transfers between devices with their start and end apart: 14 -> 15, of which waited for: 10 -> 6; matrix products, arithmetic and copies ran while one was open for 0% -> 0% of each run, Pallas kernels for 16% -> 15%
where the time goes in v8:
time: 77.9 us; the launch traced here: 76.9 us
  blocking collectives  26 us (33%)
  starting transfers between devices  21.7 us (28%)
  Pallas kernels  15.3 us (20%)
  waiting for transfers between devices  11.4 us (15%)
  local copies, waits for them, and re-layouts  2.54 us (3%)
    all_to_all x1, blocking collectives, on_device(): pieces = lax.all_to_all(packed, 'env', 0, 0, tiled=True)  26 us
    ppermute x15, starting transfers between devices, fetch(): return lax.ppermute(value, ('env', 'sp'), pairs)  21.7 us
    ppermute x15, waiting for transfers between devices, fetch(): return lax.ppermute(value, ('env', 'sp'), pairs)  11.4 us
    pallas_call x4, Pallas kernels, take(): call(column_kernel, pair, 5, 2 * 1073741824, 1 << 23, (pltpu.VMEM((256, 4...  9.62 us
    pallas_call x2, Pallas kernels, rows(): call(body, (shape(envs, 512), shape(512, envs)) + sums, n_in, envs * 7864...  4.41 us
    unnamed x4, local copies, waits for them, and re-layouts  2.54 us
  transfers between devices with their start and end apart: 15, of which 6 were waited for; matrix products, arithmetic and copies ran while one was open for 0% of the time, Pallas kernels for 15%

profile of v8, /device:TPU:1, one launch (start us, length us, event | category | flops | bytes accessed | tf_op | source)
XLA Modules:
  0.0 76.9 jit_solution(16380163369284146912)
XLA Ops:
  0.0 3.2 %collective-permute-start.1 = (bf16[256,512]{1,0:T(8,128)(2,1)}, bf16[256,512]{1,0:T(8,128)(2,1)S(1)}, u32[]{:S(2)}, u32[]{:S(2)}) collective-permute-start(bf16[256,512]{1,0:T(8,128)(2,1)} %own_points.1), channel_id=1, source_target_pairs={{1,0},{0,1},{3,2},{2,3},{5,4},{4,5},{7,6},{6,7},{9,8},{8,9},{11,10... | collective-permute-start | bytes 786440 | tf_op jit(solution)/shard_map/ppermute | solution.py:30
  3.2 3.8 %collective-permute-start = (bf16[256,512]{1,0:T(8,128)(2,1)}, bf16[256,512]{1,0:T(8,128)(2,1)S(1)}, u32[]{:S(2)}, u32[]{:S(2)}) collective-permute-start(bf16[256,512]{1,0:T(8,128)(2,1)} %own_points.1), channel_id=1, source_target_pairs={{4,0},{5,1},{6,2},{7,3},{8,4},{9,5},{10,6},{11,7},{12,8},{13,9},{1... | collective-permute-start | bytes 786440 | tf_op jit(solution)/shard_map/ppermute | solution.py:30
  7.1 0.0 collective-permute-done.1.sib_points
  7.1 0.0 copy-start
  7.1 1.6 %copy-done = bf16[2048,512]{1,0:T(8,128)(2,1)S(1)} copy-done((bf16[2048,512]{1,0:T(8,128)(2,1)S(1)}, bf16[2048,512]{1,0:T(8,128)(2,1)}, u32[]{:S(2)}) %copy-start) | copy-done | bytes 2097176
  8.7 0.0 copy-start.1
  8.7 0.9 %copy-done.1 = bf16[256,512]{1,0:T(8,128)(2,1)S(1)} copy-done((bf16[256,512]{1,0:T(8,128)(2,1)S(1)}, bf16[256,512]{1,0:T(8,128)(2,1)}, u32[]{:S(2)}) %copy-start.1) | copy-done | bytes 262168
  9.6 2.2 %shard_map.28 = (bf16[2048,512]{1,0:T(8,128)(2,1)S(1)}, bf16[512,2048]{1,0:T(8,128)(2,1)S(1)}, f32[512,256]{1,0:T(8,128)S(1)}, bf16[512,512]{1,0:T(8,128)(2,1)S(1)}) custom-call(bf16[2048,512]{1,0:T(8,128)(2,1)S(1)} %copy-done, bf16[256,512]{1,0:T(8,128)(2,1)S(1)} %copy-done.1, bf16[256,512]{1,0:T(8,128)(2,1)S(1)} %collective-permute-done.1.sib_points), custom_call_target="tpu_custom_call" | custom-call | flops 1610612736 | bytes 8388608 | tf_op jit(solution)/shard_map/pallas_call | solution.py:202
  11.9 1.3 %collective-permute-done.points = bf16[256,512]{1,0:T(8,128)(2,1)S(1)} collective-permute-done((bf16[256,512]{1,0:T(8,128)(2,1)}, bf16[256,512]{1,0:T(8,128)(2,1)S(1)}, u32[]{:S(2)}, u32[]{:S(2)}) %collective-permute-start) | collective-permute-done | bytes 262176 | tf_op jit(solution)/shard_map/ppermute | solution.py:30
  13.1 0.1 shard_map.29
  13.2 1.1 %collective-permute-start.5 = (bf16[1024,512]{1,0:T(8,128)(2,1)S(1)}, bf16[1024,512]{1,0:T(8,128)(2,1)S(1)}, u32[]{:S(2)}, u32[]{:S(2)}) collective-permute-start(bf16[1024,512]{1,0:T(8,128)(2,1)S(1)} %shard_map.29), channel_id=1, source_target_pairs={{32,0},{97,1},{34,2},{99,3},{36,4},{101,5},{38,6},{103,7},{40,8},{... | collective-permute-start | bytes 3145736 | tf_op jit(solution)/shard_map/ppermute | solution.py:30
  14.3 2.4 %collective-permute-start.2 = (bf16[256,512]{1,0:T(8,128)(2,1)S(1)}, bf16[256,512]{1,0:T(8,128)(2,1)S(1)}, u32[]{:S(2)}, u32[]{:S(2)}) collective-permute-start(bf16[256,512]{1,0:T(8,128)(2,1)S(1)} %collective-permute-done.points), channel_id=1, source_target_pairs={{4,0},{5,1},{6,2},{7,3},{8,4},{9,5},{10,6},{11,7},{12,8},{13,9},{1... | collective-permute-start | bytes 786440 | tf_op jit(solution)/shard_map/ppermute | solution.py:30
  16.7 3.7 %collective-permute-done.2.points = bf16[256,512]{1,0:T(8,128)(2,1)S(1)} collective-permute-done((bf16[256,512]{1,0:T(8,128)(2,1)S(1)}, bf16[256,512]{1,0:T(8,128)(2,1)S(1)}, u32[]{:S(2)}, u32[]{:S(2)}) %collective-permute-start.2) | collective-permute-done | bytes 262176 | tf_op jit(solution)/shard_map/ppermute | solution.py:30
  20.4 3.4 %collective-permute-start.3 = (bf16[256,512]{1,0:T(8,128)(2,1)S(1)}, bf16[256,512]{1,0:T(8,128)(2,1)S(1)}, u32[]{:S(2)}, u32[]{:S(2)}) collective-permute-start(bf16[256,512]{1,0:T(8,128)(2,1)S(1)} %collective-permute-done.2.points), channel_id=1, source_target_pairs={{4,0},{5,1},{6,2},{7,3},{8,4},{9,5},{10,6},{11,7},{12,8},{13,9},{1... | collective-permute-start | bytes 786440 | tf_op jit(solution)/shard_map/ppermute | solution.py:30
  23.8 4.3 %collective-permute-done.5.near = bf16[1024,512]{1,0:T(8,128)(2,1)S(1)} collective-permute-done((bf16[1024,512]{1,0:T(8,128)(2,1)S(1)}, bf16[1024,512]{1,0:T(8,128)(2,1)S(1)}, u32[]{:S(2)}, u32[]{:S(2)}) %collective-permute-start.5) | collective-permute-done | bytes 1048608 | tf_op jit(solution)/shard_map/ppermute | solution.py:30
  28.1 0.1 shard_map.30
  28.2 2.1 %collective-permute-start.6 = (bf16[256,512]{1,0:T(8,128)(2,1)S(1)}, bf16[256,512]{1,0:T(8,128)(2,1)S(1)}, u32[]{:S(2)}, u32[]{:S(2)}) collective-permute-start(bf16[256,512]{1,0:T(8,128)(2,1)S(1)} %get-tuple-element.48.refs_0_), channel_id=1, source_target_pairs={{1,0},{0,1},{3,2},{2,3},{5,4},{4,5},{7,6},{6,7},{9,8},{8,9},{11,10... | collective-permute-start | bytes 786440 | tf_op jit(solution)/shard_map/ppermute | solution.py:30
  30.3 0.1 collective-permute-start.7
  30.4 0.4 collective-permute-start.8
  30.8 0.1 collective-permute-start.9
  30.9 0.0 collective-permute-done.3.points
  30.9 2.0 %collective-permute-start.4 = (bf16[256,512]{1,0:T(8,128)(2,1)S(1)}, bf16[256,512]{1,0:T(8,128)(2,1)S(1)}, u32[]{:S(2)}, u32[]{:S(2)}) collective-permute-start(bf16[256,512]{1,0:T(8,128)(2,1)S(1)} %collective-permute-done.3.points), channel_id=1, source_target_pairs={{4,0},{5,1},{6,2},{7,3},{8,4},{9,5},{10,6},{11,7},{12,8},{13,9},{1... | collective-permute-start | bytes 786440 | tf_op jit(solution)/shard_map/ppermute | solution.py:30
  32.9 0.0 collective-permute-done.6.refs_4_
  33.0 0.0 collective-permute-done.7.refs_5_
  33.0 0.0 collective-permute-done.8.refs_6_
  33.0 0.0 collective-permute-done.9.refs_7_
  33.0 2.2 %shard_map.31 = (bf16[2048,512]{1,0:T(8,128)(2,1)S(1)}, bf16[512,2048]{1,0:T(8,128)(2,1)S(1)}, bf16[256,256]{1,0:T(8,128)(2,1)S(1)}, bf16[256,256]{1,0:T(8,128)(2,1)S(1)}) custom-call(bf16[256,512]{1,0:T(8,128)(2,1)S(1)} %get-tuple-element.48.refs_0_, bf16[256,512]{1,0:T(8,128)(2,1)S(1)} %get-tuple-element.49.refs_1_, ...), custom_call_target="tpu_custom_call" | custom-call | flops 1610612736 | bytes 8388608 | tf_op jit(solution)/shard_map/pallas_call | solution.py:202
  35.2 2.4 %shard_map.34 = (bf16[256,256]{1,0:T(8,128)(2,1)S(1)}, bf16[256,256]{1,0:T(8,128)(2,1)S(1)}) custom-call(bf16[256,512]{1,0:T(8,128)(2,1)S(1)} %collective-permute-done.3.points, bf16[2048,512]{1,0:T(8,128)(2,1)S(1)} %get-tuple-element.55.refs_0_, bf16[2048,512]{1,0:T(8,128)(2,1)S(1)} %get-tuple-element.56.refs_1_, ...), custom_call_target="tpu_custom_call" | custom-call | flops 2147483648 | bytes 8388608 | tf_op jit(solution)/shard_map/pallas_call | solution.py:227
  37.6 1.6 %collective-permute-start.13 = (bf16[256,256]{1,0:T(8,128)(2,1)S(1)}, bf16[256,256]{1,0:T(8,128)(2,1)S(1)}, u32[]{:S(2)}, u32[]{:S(2)}) collective-permute-start(bf16[256,256]{1,0:T(8,128)(2,1)S(1)} %get-tuple-element.65), channel_id=1, source_target_pairs={{1,0},{0,1},{3,2},{2,3},{5,4},{4,5},{7,6},{6,7},{9,8},{8,9},{11,10... | collective-permute-start | bytes 393224 | tf_op jit(solution)/shard_map/ppermute | solution.py:30
  39.2 2.4 %shard_map.33 = (bf16[256,256]{1,0:T(8,128)(2,1)S(1)}, bf16[256,256]{1,0:T(8,128)(2,1)S(1)}) custom-call(bf16[256,512]{1,0:T(8,128)(2,1)S(1)} %collective-permute-done.2.points, bf16[2048,512]{1,0:T(8,128)(2,1)S(1)} %get-tuple-element.55.refs_0_, bf16[2048,512]{1,0:T(8,128)(2,1)S(1)} %get-tuple-element.56.refs_1_, ...), custom_call_target="tpu_custom_call" | custom-call | flops 2147483648 | bytes 8388608 | tf_op jit(solution)/shard_map/pallas_call | solution.py:227
  41.6 0.1 collective-permute-start.12
  41.7 2.4 %shard_map.32 = (bf16[256,256]{1,0:T(8,128)(2,1)S(1)}, bf16[256,256]{1,0:T(8,128)(2,1)S(1)}) custom-call(bf16[256,512]{1,0:T(8,128)(2,1)S(1)} %collective-permute-done.points, bf16[2048,512]{1,0:T(8,128)(2,1)S(1)} %get-tuple-element.55.refs_0_, bf16[2048,512]{1,0:T(8,128)(2,1)S(1)} %get-tuple-element.56.refs_1_, ...), custom_call_target="tpu_custom_call" | custom-call | flops 2147483648 | bytes 8388608 | tf_op jit(solution)/shard_map/pallas_call | solution.py:227
  44.1 0.6 collective-permute-start.11
  44.7 0.3 collective-permute-start.10
  45.0 0.0 collective-permute-done.4.points
  45.0 0.0 collective-permute-done.13.refs_8_
  45.0 0.0 collective-permute-done.12.refs_7_
  45.0 0.7 collective-permute-done.11.refs_6_
  45.7 0.4 collective-permute-done.10.refs_5_
  46.0 2.4 %shard_map.35 = (bf16[256,256]{1,0:T(8,128)(2,1)S(1)}, bf16[256,256]{1,0:T(8,128)(2,1)S(1)}) custom-call(bf16[256,512]{1,0:T(8,128)(2,1)S(1)} %collective-permute-done.4.points, bf16[2048,512]{1,0:T(8,128)(2,1)S(1)} %get-tuple-element.55.refs_0_, bf16[2048,512]{1,0:T(8,128)(2,1)S(1)} %get-tuple-element.56.refs_1_, ...), custom_call_target="tpu_custom_call" | custom-call | flops 2147483648 | bytes 8388608 | tf_op jit(solution)/shard_map/pallas_call | solution.py:227
  48.5 0.4 collective-permute-start.14
  48.9 1.0 %collective-permute-done.14.refs_9_ = bf16[256,256]{1,0:T(8,128)(2,1)S(1)} collective-permute-done((bf16[256,256]{1,0:T(8,128)(2,1)S(1)}, bf16[256,256]{1,0:T(8,128)(2,1)S(1)}, u32[]{:S(2)}, u32[]{:S(2)}) %collective-permute-start.14) | collective-permute-done | bytes 131104 | tf_op jit(solution)/shard_map/ppermute | solution.py:30
  49.9 0.1 shard_map.36
  50.0 26.0 %all_to_all.5.pieces = bf16[8,9,32,256]{3,2,1,0:T(8,128)(2,1)S(1)} all-to-all(bf16[8,9,32,256]{3,2,1,0:T(8,128)(2,1)S(1)} %shard_map.36), channel_id=1, replica_groups=mesh['env'=8,'sp'=32] {'env'}, dimensions={0} | all-to-all | bytes 2359296 | tf_op jit(solution)/shard_map/all_to_all | solution.py:243
  75.9 1.0 %shard_map.37 = f32[17,32,256]{2,1,0:T(8,128)} custom-call(bf16[8,9,32,256]{3,2,1,0:T(8,128)(2,1)S(1)} %all_to_all.5.pieces), custom_call_target="tpu_custom_call" | custom-call | bytes 2097152 | tf_op jit(solution)/shard_map/pallas_call | solution.py:244
Async XLA Ops:
  0.0 7.1 %collective-permute-start.1 = (bf16[256,512]{1,0:T(8,128)(2,1)}, bf16[256,512]{1,0:T(8,128)(2,1)S(1)}, u32[]{:S(2)}, u32[]{:S(2)}) collective-permute-start(bf16[256,512]{1,0:T(8,128)(2,1)} %own_points.1), channel_id=1, source_target_pairs={{1,0},{0,1},{3,2},{2,3},{5,4},{4,5},{7,6},{6,7},{9,8},{8,9},{11,10... | collective-permute-start | bytes 786440 | tf_op jit(solution)/shard_map/ppermute | solution.py:30
  3.2 9.9 %collective-permute-start = (bf16[256,512]{1,0:T(8,128)(2,1)}, bf16[256,512]{1,0:T(8,128)(2,1)S(1)}, u32[]{:S(2)}, u32[]{:S(2)}) collective-permute-start(bf16[256,512]{1,0:T(8,128)(2,1)} %own_points.1), channel_id=1, source_target_pairs={{4,0},{5,1},{6,2},{7,3},{8,4},{9,5},{10,6},{11,7},{12,8},{13,9},{1... | collective-permute-start | bytes 786440 | tf_op jit(solution)/shard_map/ppermute | solution.py:30
  7.1 1.6 %copy-start = (bf16[2048,512]{1,0:T(8,128)(2,1)S(1)}, bf16[2048,512]{1,0:T(8,128)(2,1)}, u32[]{:S(2)}) copy-start(bf16[2048,512]{1,0:T(8,128)(2,1)} %descriptors) | copy-start | bytes 6291460
  8.7 0.9 %copy-start.1 = (bf16[256,512]{1,0:T(8,128)(2,1)S(1)}, bf16[256,512]{1,0:T(8,128)(2,1)}, u32[]{:S(2)}) copy-start(bf16[256,512]{1,0:T(8,128)(2,1)} %own_points.1) | copy-start | bytes 786436
  13.2 14.9 %collective-permute-start.5 = (bf16[1024,512]{1,0:T(8,128)(2,1)S(1)}, bf16[1024,512]{1,0:T(8,128)(2,1)S(1)}, u32[]{:S(2)}, u32[]{:S(2)}) collective-permute-start(bf16[1024,512]{1,0:T(8,128)(2,1)S(1)} %shard_map.29), channel_id=1, source_target_pairs={{32,0},{97,1},{34,2},{99,3},{36,4},{101,5},{38,6},{103,7},{40,8},{... | collective-permute-start | bytes 3145736 | tf_op jit(solution)/shard_map/ppermute | solution.py:30
  14.3 6.1 %collective-permute-start.2 = (bf16[256,512]{1,0:T(8,128)(2,1)S(1)}, bf16[256,512]{1,0:T(8,128)(2,1)S(1)}, u32[]{:S(2)}, u32[]{:S(2)}) collective-permute-start(bf16[256,512]{1,0:T(8,128)(2,1)S(1)} %collective-permute-done.points), channel_id=1, source_target_pairs={{4,0},{5,1},{6,2},{7,3},{8,4},{9,5},{10,6},{11,7},{12,8},{13,9},{1... | collective-permute-start | bytes 786440 | tf_op jit(solution)/shard_map/ppermute | solution.py:30
  20.4 10.5 %collective-permute-start.3 = (bf16[256,512]{1,0:T(8,128)(2,1)S(1)}, bf16[256,512]{1,0:T(8,128)(2,1)S(1)}, u32[]{:S(2)}, u32[]{:S(2)}) collective-permute-start(bf16[256,512]{1,0:T(8,128)(2,1)S(1)} %collective-permute-done.2.points), channel_id=1, source_target_pairs={{4,0},{5,1},{6,2},{7,3},{8,4},{9,5},{10,6},{11,7},{12,8},{13,9},{1... | collective-permute-start | bytes 786440 | tf_op jit(solution)/shard_map/ppermute | solution.py:30
  28.2 4.7 %collective-permute-start.6 = (bf16[256,512]{1,0:T(8,128)(2,1)S(1)}, bf16[256,512]{1,0:T(8,128)(2,1)S(1)}, u32[]{:S(2)}, u32[]{:S(2)}) collective-permute-start(bf16[256,512]{1,0:T(8,128)(2,1)S(1)} %get-tuple-element.48.refs_0_), channel_id=1, source_target_pairs={{1,0},{0,1},{3,2},{2,3},{5,4},{4,5},{7,6},{6,7},{9,8},{8,9},{11,10... | collective-permute-start | bytes 786440 | tf_op jit(solution)/shard_map/ppermute | solution.py:30
  30.3 2.6 %collective-permute-start.7 = (bf16[256,512]{1,0:T(8,128)(2,1)S(1)}, bf16[256,512]{1,0:T(8,128)(2,1)S(1)}, u32[]{:S(2)}, u32[]{:S(2)}) collective-permute-start(bf16[256,512]{1,0:T(8,128)(2,1)S(1)} %get-tuple-element.49.refs_1_), channel_id=1, source_target_pairs={{1,0},{0,1},{3,2},{2,3},{5,4},{4,5},{7,6},{6,7},{9,8},{8,9},{11,10... | collective-permute-start | bytes 786440 | tf_op jit(solution)/shard_map/ppermute | solution.py:30
  30.4 2.5 %collective-permute-start.8 = (bf16[256,512]{1,0:T(8,128)(2,1)S(1)}, bf16[256,512]{1,0:T(8,128)(2,1)S(1)}, u32[]{:S(2)}, u32[]{:S(2)}) collective-permute-start(bf16[256,512]{1,0:T(8,128)(2,1)S(1)} %get-tuple-element.50.refs_2_), channel_id=1, source_target_pairs={{1,0},{0,1},{3,2},{2,3},{5,4},{4,5},{7,6},{6,7},{9,8},{8,9},{11,10... | collective-permute-start | bytes 786440 | tf_op jit(solution)/shard_map/ppermute | solution.py:30
  30.8 2.1 %collective-permute-start.9 = (bf16[256,512]{1,0:T(8,128)(2,1)S(1)}, bf16[256,512]{1,0:T(8,128)(2,1)S(1)}, u32[]{:S(2)}, u32[]{:S(2)}) collective-permute-start(bf16[256,512]{1,0:T(8,128)(2,1)S(1)} %get-tuple-element.51.refs_3_), channel_id=1, source_target_pairs={{1,0},{0,1},{3,2},{2,3},{5,4},{4,5},{7,6},{6,7},{9,8},{8,9},{11,10... | collective-permute-start | bytes 786440 | tf_op jit(solution)/shard_map/ppermute | solution.py:30
  30.9 14.1 %collective-permute-start.4 = (bf16[256,512]{1,0:T(8,128)(2,1)S(1)}, bf16[256,512]{1,0:T(8,128)(2,1)S(1)}, u32[]{:S(2)}, u32[]{:S(2)}) collective-permute-start(bf16[256,512]{1,0:T(8,128)(2,1)S(1)} %collective-permute-done.3.points), channel_id=1, source_target_pairs={{4,0},{5,1},{6,2},{7,3},{8,4},{9,5},{10,6},{11,7},{12,8},{13,9},{1... | collective-permute-start | bytes 786440 | tf_op jit(solution)/shard_map/ppermute | solution.py:30
  37.6 7.5 %collective-permute-start.13 = (bf16[256,256]{1,0:T(8,128)(2,1)S(1)}, bf16[256,256]{1,0:T(8,128)(2,1)S(1)}, u32[]{:S(2)}, u32[]{:S(2)}) collective-permute-start(bf16[256,256]{1,0:T(8,128)(2,1)S(1)} %get-tuple-element.65), channel_id=1, source_target_pairs={{1,0},{0,1},{3,2},{2,3},{5,4},{4,5},{7,6},{6,7},{9,8},{8,9},{11,10... | collective-permute-start | bytes 393224 | tf_op jit(solution)/shard_map/ppermute | solution.py:30
  41.6 3.4 %collective-permute-start.12 = (bf16[256,256]{1,0:T(8,128)(2,1)S(1)}, bf16[256,256]{1,0:T(8,128)(2,1)S(1)}, u32[]{:S(2)}, u32[]{:S(2)}) collective-permute-start(bf16[256,256]{1,0:T(8,128)(2,1)S(1)} %get-tuple-element.64), channel_id=1, source_target_pairs={{1,0},{0,1},{3,2},{2,3},{5,4},{4,5},{7,6},{6,7},{9,8},{8,9},{11,10... | collective-permute-start | bytes 393224 | tf_op jit(solution)/shard_map/ppermute | solution.py:30
  44.1 1.6 %collective-permute-start.11 = (bf16[256,256]{1,0:T(8,128)(2,1)S(1)}, bf16[256,256]{1,0:T(8,128)(2,1)S(1)}, u32[]{:S(2)}, u32[]{:S(2)}) collective-permute-start(bf16[256,256]{1,0:T(8,128)(2,1)S(1)} %get-tuple-element.63), channel_id=1, source_target_pairs={{1,0},{0,1},{3,2},{2,3},{5,4},{4,5},{7,6},{6,7},{9,8},{8,9},{11,10... | collective-permute-start | bytes 393224 | tf_op jit(solution)/shard_map/ppermute | solution.py:30
  44.7 1.3 %collective-permute-start.10 = (bf16[256,256]{1,0:T(8,128)(2,1)S(1)}, bf16[256,256]{1,0:T(8,128)(2,1)S(1)}, u32[]{:S(2)}, u32[]{:S(2)}) collective-permute-start(bf16[256,256]{1,0:T(8,128)(2,1)S(1)} %get-tuple-element.62), channel_id=1, source_target_pairs={{1,0},{0,1},{3,2},{2,3},{5,4},{4,5},{7,6},{6,7},{9,8},{8,9},{11,10... | collective-permute-start | bytes 393224 | tf_op jit(solution)/shard_map/ppermute | solution.py:30
  48.5 1.4 %collective-permute-start.14 = (bf16[256,256]{1,0:T(8,128)(2,1)S(1)}, bf16[256,256]{1,0:T(8,128)(2,1)S(1)}, u32[]{:S(2)}, u32[]{:S(2)}) collective-permute-start(bf16[256,256]{1,0:T(8,128)(2,1)S(1)} %get-tuple-element.76), channel_id=1, source_target_pairs={{1,0},{0,1},{3,2},{2,3},{5,4},{4,5},{7,6},{6,7},{9,8},{8,9},{11,10... | collective-permute-start | bytes 393224 | tf_op jit(solution)/shard_map/ppermute | solution.py:30

commit v9 on v8

--- a/solution.py
+++ b/solution.py
@@ -133,10 +133,20 @@
     sib_out[...] = total[256:]
 
 
+def begin_kernel(points, env_a, rows_a, point_hat, gram, kept):
+    point_hat[...] = unit(points[...])
+    kernel_values(point_hat[...], (env_a,), kept)
+    gram[...] = products((rows_a,), kept)
+
+
 def more_kernel(*refs):
-    points_hat, gram, env_hat, rows_k, own_out, sib_out = refs[2 * PIECES:]
+    points_hat, gram, first_hat, first_gram, second_hat, second_gram = refs[2 * PIECES:2 * PIECES + 6]
+    env_hat, rows_k, own0, sib0, own1, sib1, own2, sib2, kept = refs[2 * PIECES + 6:]
     rows_of(points_hat[...], refs[:2 * PIECES], env_hat, rows_k)
-    give(gram[...] + dot(rows_k[...], rows_k[:256, :]), own_out, sib_out)
+    give(gram[...] + dot(rows_k[...], rows_k[:256, :]), own0, sib0)
+    for point_hat, begun, own, sib in ((first_hat, first_gram, own1, sib1), (second_hat, second_gram, own2, sib2)):
+        kernel_values(point_hat[...], (env_hat,), kept)
+        give(begun[...] + products((rows_k,), kept), own, sib)
 
 
 def column_kernel(points, *refs):
@@ -214,26 +224,32 @@
         (column, descriptors, env_a, rows_a, gram, points_hat)
     )
 
+    kept = (pltpu.VMEM((256, 2048), BF16),)
+
+    def begin(points):
+        return call(begin_kernel, (shape(256, 512), gram_shape), 3, 1 << 30, 1 << 22, kept)(points, env_a, rows_a)
+
     columns.append(fetch(column, next_z))
     near = fetch(call(slice_kernel, shape(1024, 512), 1, 0, 1 << 21)(later), near_x)
-    near, _ = barrier((near, columns[1]))
-
-    columns.append(fetch(columns[1], next_z))
+    column, *begun = barrier((columns[1], *begin(columns[0])))
+
+    columns.append(fetch(column, next_z))
+    near, *others = barrier((near, *begin(column)))
+    begun += others
     near = call(split_kernel, PIECES * (shape(1024 // PIECES, 512),), 1, 0, 1 << 21)(near)
     far = [fetch(piece, other_core) for piece in near]
-    env_b, rows_b, own, sib = rows(more_kernel, 2048, pair, 2 * PIECES + 2, *near, *far, points_hat, gram)
+
+    last = fetch(columns[2], next_z)
+    env_b, rows_b, *sums = call(
+        more_kernel, (shape(2048, 512), shape(512, 2048)) + 3 * pair, 2 * PIECES + 6, 7 << 29, 1 << 23, kept
+    )(*near, *far, points_hat, gram, *begun)
 
     def take(points):
         return call(
             column_kernel, pair, 5, 2 * 1073741824, 1 << 23, (pltpu.VMEM((256, 4096), BF16),)
         )(points, env_a, env_b, rows_a, rows_b)
 
-    sums = [own, sib]
-    column = columns[2]
-
-    last = fetch(column, next_z)
-    for points in columns[:3]:
-        sums += take(points)
+    sums += take(columns[2])
     owns, swapped = sums[0::2], [fetch(sib, other_core) for sib in sums[1::2]]
     last, *sums = barrier((last, *owns, *swapped))
     owns, swapped = sums[:4], sums[4:]

time: 77.9 us -> 75.2 us (0.965)
  waiting for transfers between devices: 11.4 us -> 9.11 us
    pallas_call x0 -> x3, Pallas kernels: none -> 7.07 us  [the longest x1 4.44 us: on_device(): call(more_kernel, (shape(2048, 512), shape(512, 2048)) + 3 * pair, 2 * PI...]
    pallas_call x4 -> x2, Pallas kernels: 9.62 us -> 4.82 us  [take(): call(column_kernel, pair, 5, 2 * 1073741824, 1 << 23, (pltpu.VMEM((256, 4...]
    ppermute x15, waiting for transfers between devices: 11.4 us -> 9.11 us  [fetch(): return lax.ppermute(value, ('env', 'sp'), pairs)]
    pallas_call x2 -> x1, Pallas kernels: 4.41 us -> 2.23 us  [rows(): call(body, (shape(envs, 512), shape(512, envs)) + sums, n_in, envs * 7864...]
  transfers between devices with their start and end apart: 15 -> 15, of which waited for: 6 -> 8; matrix products, arithmetic and copies ran while one was open for 0% -> 0% of each run, Pallas kernels for 15% -> 16%
where the time goes in v9:
time: 75.2 us; the launch traced here: 74.2 us
  blocking collectives  26 us (35%)
  starting transfers between devices  21.2 us (28%)
  Pallas kernels  15.3 us (20%)
  waiting for transfers between devices  9.11 us (12%)
  local copies, waits for them, and re-layouts  2.54 us (3%)
    all_to_all x1, blocking collectives, on_device(): pieces = lax.all_to_all(packed, 'env', 0, 0, tiled=True)  26 us
    ppermute x15, starting transfers between devices, fetch(): return lax.ppermute(value, ('env', 'sp'), pairs)  21.2 us
    ppermute x15, waiting for transfers between devices, fetch(): return lax.ppermute(value, ('env', 'sp'), pairs)  9.11 us
    pallas_call x2, Pallas kernels, take(): call(column_kernel, pair, 5, 2 * 1073741824, 1 << 23, (pltpu.VMEM((256, 4...  4.82 us
    pallas_call x1, Pallas kernels, on_device(): call(more_kernel, (shape(2048, 512), shape(512, 2048)) + 3 * pair, 2 * PI...  4.44 us
    pallas_call x2, Pallas kernels, begin(): call(begin_kernel, (shape(256, 512), gram_shape), 3, 1 << 30, 1 << 22, kept)  2.63 us
    unnamed x4, local copies, waits for them, and re-layouts  2.54 us
    pallas_call x1, Pallas kernels, rows(): call(body, (shape(envs, 512), shape(512, envs)) + sums, n_in, envs * 7864...  2.23 us
  transfers between devices with their start and end apart: 15, of which 8 were waited for; matrix products, arithmetic and copies ran while one was open for 0% of the time, Pallas kernels for 16%

profile of v9, /device:TPU:1, one launch (start us, length us, event | category | flops | bytes accessed | tf_op | source)
XLA Modules:
  0.0 74.2 jit_solution(14200535185901784084)
XLA Ops:
  0.0 3.2 %collective-permute-start.1 = (bf16[256,512]{1,0:T(8,128)(2,1)}, bf16[256,512]{1,0:T(8,128)(2,1)S(1)}, u32[]{:S(2)}, u32[]{:S(2)}) collective-permute-start(bf16[256,512]{1,0:T(8,128)(2,1)} %own_points.1), channel_id=1, source_target_pairs={{1,0},{0,1},{3,2},{2,3},{5,4},{4,5},{7,6},{6,7},{9,8},{8,9},{11,10... | collective-permute-start | bytes 786440 | tf_op jit(solution)/shard_map/ppermute | solution.py:30
  3.2 3.8 %collective-permute-start = (bf16[256,512]{1,0:T(8,128)(2,1)}, bf16[256,512]{1,0:T(8,128)(2,1)S(1)}, u32[]{:S(2)}, u32[]{:S(2)}) collective-permute-start(bf16[256,512]{1,0:T(8,128)(2,1)} %own_points.1), channel_id=1, source_target_pairs={{4,0},{5,1},{6,2},{7,3},{8,4},{9,5},{10,6},{11,7},{12,8},{13,9},{1... | collective-permute-start | bytes 786440 | tf_op jit(solution)/shard_map/ppermute | solution.py:30
  7.1 0.0 collective-permute-done.1.sib_points
  7.1 0.0 copy-start
  7.1 1.6 %copy-done = bf16[2048,512]{1,0:T(8,128)(2,1)S(1)} copy-done((bf16[2048,512]{1,0:T(8,128)(2,1)S(1)}, bf16[2048,512]{1,0:T(8,128)(2,1)}, u32[]{:S(2)}) %copy-start) | copy-done | bytes 2097176
  8.7 0.0 copy-start.1
  8.7 0.9 %copy-done.1 = bf16[256,512]{1,0:T(8,128)(2,1)S(1)} copy-done((bf16[256,512]{1,0:T(8,128)(2,1)S(1)}, bf16[256,512]{1,0:T(8,128)(2,1)}, u32[]{:S(2)}) %copy-start.1) | copy-done | bytes 262168
  9.6 2.2 %shard_map.28 = (bf16[2048,512]{1,0:T(8,128)(2,1)S(1)}, bf16[512,2048]{1,0:T(8,128)(2,1)S(1)}, f32[512,256]{1,0:T(8,128)S(1)}, bf16[512,512]{1,0:T(8,128)(2,1)S(1)}) custom-call(bf16[2048,512]{1,0:T(8,128)(2,1)S(1)} %copy-done, bf16[256,512]{1,0:T(8,128)(2,1)S(1)} %copy-done.1, bf16[256,512]{1,0:T(8,128)(2,1)S(1)} %collective-permute-done.1.sib_points), custom_call_target="tpu_custom_call" | custom-call | flops 1610612736 | bytes 8388608 | tf_op jit(solution)/shard_map/pallas_call | solution.py:212
  11.9 1.3 %collective-permute-done.points = bf16[256,512]{1,0:T(8,128)(2,1)S(1)} collective-permute-done((bf16[256,512]{1,0:T(8,128)(2,1)}, bf16[256,512]{1,0:T(8,128)(2,1)S(1)}, u32[]{:S(2)}, u32[]{:S(2)}) %collective-permute-start) | collective-permute-done | bytes 262176 | tf_op jit(solution)/shard_map/ppermute | solution.py:30
  13.1 0.1 shard_map.30
  13.2 1.1 %collective-permute-start.5 = (bf16[1024,512]{1,0:T(8,128)(2,1)S(1)}, bf16[1024,512]{1,0:T(8,128)(2,1)S(1)}, u32[]{:S(2)}, u32[]{:S(2)}) collective-permute-start(bf16[1024,512]{1,0:T(8,128)(2,1)S(1)} %shard_map.30), channel_id=1, source_target_pairs={{32,0},{97,1},{34,2},{99,3},{36,4},{101,5},{38,6},{103,7},{40,8},{... | collective-permute-start | bytes 3145736 | tf_op jit(solution)/shard_map/ppermute | solution.py:30
  14.3 2.4 %collective-permute-start.2 = (bf16[256,512]{1,0:T(8,128)(2,1)S(1)}, bf16[256,512]{1,0:T(8,128)(2,1)S(1)}, u32[]{:S(2)}, u32[]{:S(2)}) collective-permute-start(bf16[256,512]{1,0:T(8,128)(2,1)S(1)} %collective-permute-done.points), channel_id=1, source_target_pairs={{4,0},{5,1},{6,2},{7,3},{8,4},{9,5},{10,6},{11,7},{12,8},{13,9},{1... | collective-permute-start | bytes 786440 | tf_op jit(solution)/shard_map/ppermute | solution.py:30
  16.7 1.3 %shard_map.29 = (bf16[256,512]{1,0:T(8,128)(2,1)S(1)}, f32[512,256]{1,0:T(8,128)S(1)}) custom-call(bf16[256,512]{1,0:T(8,128)(2,1)S(1)} %collective-permute-done.points, bf16[2048,512]{1,0:T(8,128)(2,1)S(1)} %get-tuple-element.55.env_a.refs_0_, bf16[512,2048]{1,0:T(8,128)(2,1)S(1)} %get-tuple-element.56.rows_a.refs_2_), custom_call_target="tpu_custom_call" | custom-call | flops 1073741824 | bytes 4194304 | tf_op jit(solution)/shard_map/pallas_call | solution.py:230
  18.0 2.4 %collective-permute-done.2.points = bf16[256,512]{1,0:T(8,128)(2,1)S(1)} collective-permute-done((bf16[256,512]{1,0:T(8,128)(2,1)S(1)}, bf16[256,512]{1,0:T(8,128)(2,1)S(1)}, u32[]{:S(2)}, u32[]{:S(2)}) %collective-permute-start.2) | collective-permute-done | bytes 262176 | tf_op jit(solution)/shard_map/ppermute | solution.py:30
  20.4 3.4 %collective-permute-start.3 = (bf16[256,512]{1,0:T(8,128)(2,1)S(1)}, bf16[256,512]{1,0:T(8,128)(2,1)S(1)}, u32[]{:S(2)}, u32[]{:S(2)}) collective-permute-start(bf16[256,512]{1,0:T(8,128)(2,1)S(1)} %collective-permute-done.2.points), channel_id=1, source_target_pairs={{4,0},{5,1},{6,2},{7,3},{8,4},{9,5},{10,6},{11,7},{12,8},{13,9},{1... | collective-permute-start | bytes 786440 | tf_op jit(solution)/shard_map/ppermute | solution.py:30
  23.8 1.3 %shard_map.31 = (bf16[256,512]{1,0:T(8,128)(2,1)S(1)}, f32[512,256]{1,0:T(8,128)S(1)}) custom-call(bf16[256,512]{1,0:T(8,128)(2,1)S(1)} %collective-permute-done.2.points, bf16[2048,512]{1,0:T(8,128)(2,1)S(1)} %get-tuple-element.55.env_a.refs_0_, bf16[512,2048]{1,0:T(8,128)(2,1)S(1)} %get-tuple-element.56.rows_a.refs_2_), custom_call_target="tpu_custom_call" | custom-call | flops 1073741824 | bytes 4194304 | tf_op jit(solution)/shard_map/pallas_call | solution.py:230
  25.1 3.0 %collective-permute-done.5.near = bf16[1024,512]{1,0:T(8,128)(2,1)S(1)} collective-permute-done((bf16[1024,512]{1,0:T(8,128)(2,1)S(1)}, bf16[1024,512]{1,0:T(8,128)(2,1)S(1)}, u32[]{:S(2)}, u32[]{:S(2)}) %collective-permute-start.5) | collective-permute-done | bytes 1048608 | tf_op jit(solution)/shard_map/ppermute | solution.py:30
  28.1 0.1 shard_map.32
  28.2 2.1 %collective-permute-start.6 = (bf16[256,512]{1,0:T(8,128)(2,1)S(1)}, bf16[256,512]{1,0:T(8,128)(2,1)S(1)}, u32[]{:S(2)}, u32[]{:S(2)}) collective-permute-start(bf16[256,512]{1,0:T(8,128)(2,1)S(1)} %get-tuple-element.64.refs_0_), channel_id=1, source_target_pairs={{1,0},{0,1},{3,2},{2,3},{5,4},{4,5},{7,6},{6,7},{9,8},{8,9},{11,10... | collective-permute-start | bytes 786440 | tf_op jit(solution)/shard_map/ppermute | solution.py:30
  30.3 0.1 collective-permute-start.7
  30.4 0.4 collective-permute-start.8
  30.8 0.1 collective-permute-start.9
  30.9 0.0 collective-permute-done.3.points
  30.9 2.0 %collective-permute-start.4 = (bf16[256,512]{1,0:T(8,128)(2,1)S(1)}, bf16[256,512]{1,0:T(8,128)(2,1)S(1)}, u32[]{:S(2)}, u32[]{:S(2)}) collective-permute-start(bf16[256,512]{1,0:T(8,128)(2,1)S(1)} %collective-permute-done.3.points), channel_id=1, source_target_pairs={{4,0},{5,1},{6,2},{7,3},{8,4},{9,5},{10,6},{11,7},{12,8},{13,9},{1... | collective-permute-start | bytes 786440 | tf_op jit(solution)/shard_map/ppermute | solution.py:30
  32.9 0.0 collective-permute-done.6.refs_4_
  33.0 0.0 collective-permute-done.7.refs_5_
  33.0 0.0 collective-permute-done.8.refs_6_
  33.0 0.0 collective-permute-done.9.refs_7_
  33.0 4.4 %shard_map.33 = (bf16[2048,512]{1,0:T(8,128)(2,1)S(1)}, bf16[512,2048]{1,0:T(8,128)(2,1)S(1)}, bf16[256,256]{1,0:T(8,128)(2,1)S(1)}, bf16[256,256]{1,0:T(8,128)(...) custom-call(bf16[256,512]{1,0:T(8,128)(2,1)S(1)} %get-tuple-element., ...), custom_call_target="tpu_custom_call" | custom-call | flops 3758096384 | bytes 8388608 | tf_op jit(solution)/shard_map/pallas_call | solution.py:243
  37.4 2.4 %shard_map.34 = (bf16[256,256]{1,0:T(8,128)(2,1)S(1)}, bf16[256,256]{1,0:T(8,128)(2,1)S(1)}) custom-call(bf16[256,512]{1,0:T(8,128)(2,1)S(1)} %collective-permute-done.3.points, bf16[2048,512]{1,0:T(8,128)(2,1)S(1)} %get-tuple-element.55.env_a.refs_0_, bf16[2048,512]{1,0:T(8,128)(2,1)S(1)} %get-tuple-element.77.refs_1_, ...), custom_call_target="tpu_custom_call" | custom-call | flops 2147483648 | bytes 8388608 | tf_op jit(solution)/shard_map/pallas_call | solution.py:248
  39.8 1.6 %collective-permute-start.13 = (bf16[256,256]{1,0:T(8,128)(2,1)S(1)}, bf16[256,256]{1,0:T(8,128)(2,1)S(1)}, u32[]{:S(2)}, u32[]{:S(2)}) collective-permute-start(bf16[256,256]{1,0:T(8,128)(2,1)S(1)} %get-tuple-element.83), channel_id=1, source_target_pairs={{1,0},{0,1},{3,2},{2,3},{5,4},{4,5},{7,6},{6,7},{9,8},{8,9},{11,10... | collective-permute-start | bytes 393224 | tf_op jit(solution)/shard_map/ppermute | solution.py:30
  41.4 0.1 collective-permute-start.10
  41.5 0.4 collective-permute-start.11
  42.0 0.1 collective-permute-start.12
  42.1 0.0 collective-permute-done.4.points
  42.1 0.4 collective-permute-done.13.refs_8_
  42.4 0.4 collective-permute-done.10.refs_5_
  42.8 0.2 collective-permute-done.11.refs_6_
  43.0 0.3 collective-permute-done.12.refs_7_
  43.3 2.4 %shard_map.35 = (bf16[256,256]{1,0:T(8,128)(2,1)S(1)}, bf16[256,256]{1,0:T(8,128)(2,1)S(1)}) custom-call(bf16[256,512]{1,0:T(8,128)(2,1)S(1)} %collective-permute-done.4.points, bf16[2048,512]{1,0:T(8,128)(2,1)S(1)} %get-tuple-element.55.env_a.refs_0_, bf16[2048,512]{1,0:T(8,128)(2,1)S(1)} %get-tuple-element.77.refs_1_, ...), custom_call_target="tpu_custom_call" | custom-call | flops 2147483648 | bytes 8388608 | tf_op jit(solution)/shard_map/pallas_call | solution.py:248
  45.7 0.3 collective-permute-start.14
  46.0 1.2 %collective-permute-done.14.refs_9_ = bf16[256,256]{1,0:T(8,128)(2,1)S(1)} collective-permute-done((bf16[256,256]{1,0:T(8,128)(2,1)S(1)}, bf16[256,256]{1,0:T(8,128)(2,1)S(1)}, u32[]{:S(2)}, u32[]{:S(2)}) %collective-permute-start.14) | collective-permute-done | bytes 131104 | tf_op jit(solution)/shard_map/ppermute | solution.py:30
  47.2 0.1 shard_map.36
  47.2 26.0 %all_to_all.5.pieces = bf16[8,9,32,256]{3,2,1,0:T(8,128)(2,1)S(1)} all-to-all(bf16[8,9,32,256]{3,2,1,0:T(8,128)(2,1)S(1)} %shard_map.36), channel_id=1, replica_groups=mesh['env'=8,'sp'=32] {'env'}, dimensions={0} | all-to-all | bytes 2359296 | tf_op jit(solution)/shard_map/all_to_all | solution.py:259
  73.2 1.0 %shard_map.37 = f32[17,32,256]{2,1,0:T(8,128)} custom-call(bf16[8,9,32,256]{3,2,1,0:T(8,128)(2,1)S(1)} %all_to_all.5.pieces), custom_call_target="tpu_custom_call" | custom-call | bytes 2097152 | tf_op jit(solution)/shard_map/pallas_call | solution.py:260
Async XLA Ops:
  0.0 7.1 %collective-permute-start.1 = (bf16[256,512]{1,0:T(8,128)(2,1)}, bf16[256,512]{1,0:T(8,128)(2,1)S(1)}, u32[]{:S(2)}, u32[]{:S(2)}) collective-permute-start(bf16[256,512]{1,0:T(8,128)(2,1)} %own_points.1), channel_id=1, source_target_pairs={{1,0},{0,1},{3,2},{2,3},{5,4},{4,5},{7,6},{6,7},{9,8},{8,9},{11,10... | collective-permute-start | bytes 786440 | tf_op jit(solution)/shard_map/ppermute | solution.py:30
  3.2 9.9 %collective-permute-start = (bf16[256,512]{1,0:T(8,128)(2,1)}, bf16[256,512]{1,0:T(8,128)(2,1)S(1)}, u32[]{:S(2)}, u32[]{:S(2)}) collective-permute-start(bf16[256,512]{1,0:T(8,128)(2,1)} %own_points.1), channel_id=1, source_target_pairs={{4,0},{5,1},{6,2},{7,3},{8,4},{9,5},{10,6},{11,7},{12,8},{13,9},{1... | collective-permute-start | bytes 786440 | tf_op jit(solution)/shard_map/ppermute | solution.py:30
  7.1 1.6 %copy-start = (bf16[2048,512]{1,0:T(8,128)(2,1)S(1)}, bf16[2048,512]{1,0:T(8,128)(2,1)}, u32[]{:S(2)}) copy-start(bf16[2048,512]{1,0:T(8,128)(2,1)} %descriptors) | copy-start | bytes 6291460
  8.7 0.9 %copy-start.1 = (bf16[256,512]{1,0:T(8,128)(2,1)S(1)}, bf16[256,512]{1,0:T(8,128)(2,1)}, u32[]{:S(2)}) copy-start(bf16[256,512]{1,0:T(8,128)(2,1)} %own_points.1) | copy-start | bytes 786436
  13.2 14.9 %collective-permute-start.5 = (bf16[1024,512]{1,0:T(8,128)(2,1)S(1)}, bf16[1024,512]{1,0:T(8,128)(2,1)S(1)}, u32[]{:S(2)}, u32[]{:S(2)}) collective-permute-start(bf16[1024,512]{1,0:T(8,128)(2,1)S(1)} %shard_map.30), channel_id=1, source_target_pairs={{32,0},{97,1},{34,2},{99,3},{36,4},{101,5},{38,6},{103,7},{40,8},{... | collective-permute-start | bytes 3145736 | tf_op jit(solution)/shard_map/ppermute | solution.py:30
  14.3 6.1 %collective-permute-start.2 = (bf16[256,512]{1,0:T(8,128)(2,1)S(1)}, bf16[256,512]{1,0:T(8,128)(2,1)S(1)}, u32[]{:S(2)}, u32[]{:S(2)}) collective-permute-start(bf16[256,512]{1,0:T(8,128)(2,1)S(1)} %collective-permute-done.points), channel_id=1, source_target_pairs={{4,0},{5,1},{6,2},{7,3},{8,4},{9,5},{10,6},{11,7},{12,8},{13,9},{1... | collective-permute-start | bytes 786440 | tf_op jit(solution)/shard_map/ppermute | solution.py:30
  20.4 10.5 %collective-permute-start.3 = (bf16[256,512]{1,0:T(8,128)(2,1)S(1)}, bf16[256,512]{1,0:T(8,128)(2,1)S(1)}, u32[]{:S(2)}, u32[]{:S(2)}) collective-permute-start(bf16[256,512]{1,0:T(8,128)(2,1)S(1)} %collective-permute-done.2.points), channel_id=1, source_target_pairs={{4,0},{5,1},{6,2},{7,3},{8,4},{9,5},{10,6},{11,7},{12,8},{13,9},{1... | collective-permute-start | bytes 786440 | tf_op jit(solution)/shard_map/ppermute | solution.py:30
  28.2 4.7 %collective-permute-start.6 = (bf16[256,512]{1,0:T(8,128)(2,1)S(1)}, bf16[256,512]{1,0:T(8,128)(2,1)S(1)}, u32[]{:S(2)}, u32[]{:S(2)}) collective-permute-start(bf16[256,512]{1,0:T(8,128)(2,1)S(1)} %get-tuple-element.64.refs_0_), channel_id=1, source_target_pairs={{1,0},{0,1},{3,2},{2,3},{5,4},{4,5},{7,6},{6,7},{9,8},{8,9},{11,10... | collective-permute-start | bytes 786440 | tf_op jit(solution)/shard_map/ppermute | solution.py:30
  30.3 2.6 %collective-permute-start.7 = (bf16[256,512]{1,0:T(8,128)(2,1)S(1)}, bf16[256,512]{1,0:T(8,128)(2,1)S(1)}, u32[]{:S(2)}, u32[]{:S(2)}) collective-permute-start(bf16[256,512]{1,0:T(8,128)(2,1)S(1)} %get-tuple-element.65.refs_1_), channel_id=1, source_target_pairs={{1,0},{0,1},{3,2},{2,3},{5,4},{4,5},{7,6},{6,7},{9,8},{8,9},{11,10... | collective-permute-start | bytes 786440 | tf_op jit(solution)/shard_map/ppermute | solution.py:30
  30.4 2.5 %collective-permute-start.8 = (bf16[256,512]{1,0:T(8,128)(2,1)S(1)}, bf16[256,512]{1,0:T(8,128)(2,1)S(1)}, u32[]{:S(2)}, u32[]{:S(2)}) collective-permute-start(bf16[256,512]{1,0:T(8,128)(2,1)S(1)} %get-tuple-element.66.refs_2_), channel_id=1, source_target_pairs={{1,0},{0,1},{3,2},{2,3},{5,4},{4,5},{7,6},{6,7},{9,8},{8,9},{11,10... | collective-permute-start | bytes 786440 | tf_op jit(solution)/shard_map/ppermute | solution.py:30
  30.8 2.1 %collective-permute-start.9 = (bf16[256,512]{1,0:T(8,128)(2,1)S(1)}, bf16[256,512]{1,0:T(8,128)(2,1)S(1)}, u32[]{:S(2)}, u32[]{:S(2)}) collective-permute-start(bf16[256,512]{1,0:T(8,128)(2,1)S(1)} %get-tuple-element.67.refs_3_), channel_id=1, source_target_pairs={{1,0},{0,1},{3,2},{2,3},{5,4},{4,5},{7,6},{6,7},{9,8},{8,9},{11,10... | collective-permute-start | bytes 786440 | tf_op jit(solution)/shard_map/ppermute | solution.py:30
  30.9 11.1 %collective-permute-start.4 = (bf16[256,512]{1,0:T(8,128)(2,1)S(1)}, bf16[256,512]{1,0:T(8,128)(2,1)S(1)}, u32[]{:S(2)}, u32[]{:S(2)}) collective-permute-start(bf16[256,512]{1,0:T(8,128)(2,1)S(1)} %collective-permute-done.3.points), channel_id=1, source_target_pairs={{4,0},{5,1},{6,2},{7,3},{8,4},{9,5},{10,6},{11,7},{12,8},{13,9},{1... | collective-permute-start | bytes 786440 | tf_op jit(solution)/shard_map/ppermute | solution.py:30
  39.8 2.6 %collective-permute-start.13 = (bf16[256,256]{1,0:T(8,128)(2,1)S(1)}, bf16[256,256]{1,0:T(8,128)(2,1)S(1)}, u32[]{:S(2)}, u32[]{:S(2)}) collective-permute-start(bf16[256,256]{1,0:T(8,128)(2,1)S(1)} %get-tuple-element.83), channel_id=1, source_target_pairs={{1,0},{0,1},{3,2},{2,3},{5,4},{4,5},{7,6},{6,7},{9,8},{8,9},{11,10... | collective-permute-start | bytes 393224 | tf_op jit(solution)/shard_map/ppermute | solution.py:30
  41.4 1.3 %collective-permute-start.10 = (bf16[256,256]{1,0:T(8,128)(2,1)S(1)}, bf16[256,256]{1,0:T(8,128)(2,1)S(1)}, u32[]{:S(2)}, u32[]{:S(2)}) collective-permute-start(bf16[256,256]{1,0:T(8,128)(2,1)S(1)} %get-tuple-element.80), channel_id=1, source_target_pairs={{1,0},{0,1},{3,2},{2,3},{5,4},{4,5},{7,6},{6,7},{9,8},{8,9},{11,10... | collective-permute-start | bytes 393224 | tf_op jit(solution)/shard_map/ppermute | solution.py:30
  41.5 1.4 %collective-permute-start.11 = (bf16[256,256]{1,0:T(8,128)(2,1)S(1)}, bf16[256,256]{1,0:T(8,128)(2,1)S(1)}, u32[]{:S(2)}, u32[]{:S(2)}) collective-permute-start(bf16[256,256]{1,0:T(8,128)(2,1)S(1)} %get-tuple-element.81), channel_id=1, source_target_pairs={{1,0},{0,1},{3,2},{2,3},{5,4},{4,5},{7,6},{6,7},{9,8},{8,9},{11,10... | collective-permute-start | bytes 393224 | tf_op jit(solution)/shard_map/ppermute | solution.py:30
  42.0 1.3 %collective-permute-start.12 = (bf16[256,256]{1,0:T(8,128)(2,1)S(1)}, bf16[256,256]{1,0:T(8,128)(2,1)S(1)}, u32[]{:S(2)}, u32[]{:S(2)}) collective-permute-start(bf16[256,256]{1,0:T(8,128)(2,1)S(1)} %get-tuple-element.82), channel_id=1, source_target_pairs={{1,0},{0,1},{3,2},{2,3},{5,4},{4,5},{7,6},{6,7},{9,8},{8,9},{11,10... | collective-permute-start | bytes 393224 | tf_op jit(solution)/shard_map/ppermute | solution.py:30
  45.7 1.4 %collective-permute-start.14 = (bf16[256,256]{1,0:T(8,128)(2,1)S(1)}, bf16[256,256]{1,0:T(8,128)(2,1)S(1)}, u32[]{:S(2)}, u32[]{:S(2)}) collective-permute-start(bf16[256,256]{1,0:T(8,128)(2,1)S(1)} %get-tuple-element.94), channel_id=1, source_target_pairs={{1,0},{0,1},{3,2},{2,3},{5,4},{4,5},{7,6},{6,7},{9,8},{8,9},{11,10... | collective-permute-start | bytes 393224 | tf_op jit(solution)/shard_map/ppermute | solution.py:30

commit v10 on v9

--- a/solution.py
+++ b/solution.py
@@ -127,10 +127,10 @@
     return total
 
 
-def give(gram, own_out, sib_out):
+def give(gram, own_out, sib_out, t=slice(None)):
     total = (gram * weight_row()).astype(BF16)
-    own_out[...] = total[:256]
-    sib_out[...] = total[256:]
+    own_out[t] = total[:256]
+    sib_out[t] = total[256:]
 
 
 def begin_kernel(points, env_a, rows_a, point_hat, gram, kept):
@@ -140,13 +140,16 @@
 
 
 def more_kernel(*refs):
-    points_hat, gram, first_hat, first_gram, second_hat, second_gram = refs[2 * PIECES:2 * PIECES + 6]
-    env_hat, rows_k, own0, sib0, own1, sib1, own2, sib2, kept = refs[2 * PIECES + 6:]
+    points_hat, gram, first_hat, first_gram, second_hat, second_gram, third, env_a, rows_a = refs[2 * PIECES:-5]
+    env_hat, rows_k, own, sib, kept = refs[-5:]
+    half = env_hat.shape[0]
     rows_of(points_hat[...], refs[:2 * PIECES], env_hat, rows_k)
-    give(gram[...] + dot(rows_k[...], rows_k[:256, :]), own0, sib0)
-    for point_hat, begun, own, sib in ((first_hat, first_gram, own1, sib1), (second_hat, second_gram, own2, sib2)):
+    give(gram[...] + dot(rows_k[...], rows_k[:256, :]), own, sib, 0)
+    for t, (point_hat, begun) in enumerate(((first_hat, first_gram), (second_hat, second_gram))):
         kernel_values(point_hat[...], (env_hat,), kept)
-        give(begun[...] + products((rows_k,), kept), own, sib)
+        give(begun[...] + products((rows_k,), kept), own, sib, 1 + t)
+    kernel_values(unit(third[...]), (env_a, env_hat), kept)
+    give(products((rows_a, rows_k), kept), own, sib, 3)
 
 
 def column_kernel(points, *refs):
@@ -154,16 +157,17 @@
     give(products(refs[2:4], refs[6]), refs[4], refs[5])
 
 
-def pack_kernel(*refs):
-    own, swapped, out = refs[:5], refs[5:10], refs[10]
+def pack_kernel(own, own_last, swapped, swapped_last, out):
     even_x = lax.axis_index("env") % 2 == 0
     shift = jnp.logical_and(even_x, lax.axis_index("sp") % 2 == 0)
     for e in range(8):
         rows = slice(32 * e, 32 * e + 32)
-        for m in range(5):
-            out[e, m] = own[m][rows, :]
-        for m in range(1, 5):
-            out[e, 4 + m] = jnp.where(shift, swapped[m - 1][rows, :], swapped[m][rows, :])
+        for m in range(4):
+            out[e, m] = own[m, rows, :]
+        out[e, 4] = own_last[rows, :]
+        for m in range(1, 4):
+            out[e, 4 + m] = jnp.where(shift, swapped[m - 1, rows, :], swapped[m, rows, :])
+        out[e, 8] = jnp.where(shift, swapped[3, rows, :], swapped_last[rows, :])
 
 
 def finish_kernel(pieces, out):
@@ -240,22 +244,20 @@
     far = [fetch(piece, other_core) for piece in near]
 
     last = fetch(columns[2], next_z)
-    env_b, rows_b, *sums = call(
-        more_kernel, (shape(2048, 512), shape(512, 2048)) + 3 * pair, 2 * PIECES + 6, 7 << 29, 1 << 23, kept
-    )(*near, *far, points_hat, gram, *begun)
-
-    def take(points):
-        return call(
-            column_kernel, pair, 5, 2 * 1073741824, 1 << 23, (pltpu.VMEM((256, 4096), BF16),)
-        )(points, env_a, env_b, rows_a, rows_b)
-
-    sums += take(columns[2])
-    owns, swapped = sums[0::2], [fetch(sib, other_core) for sib in sums[1::2]]
-    last, *sums = barrier((last, *owns, *swapped))
-    owns, swapped = sums[:4], sums[4:]
-
-    own, sib = take(last)
-    packed = call(pack_kernel, shape(8, 9, 32, 256), 10, 0, 1 << 21)(*owns, own, *swapped, fetch(sib, other_core))
+    four = (shape(4, 256, 256), shape(4, 256, 256))
+    env_b, rows_b, own, sib = call(
+        more_kernel, (shape(2048, 512), shape(512, 2048)) + four, 2 * PIECES + 9, 11 << 29, 1 << 24,
+        (pltpu.VMEM((256, 4096), BF16),)
+    )(*near, *far, points_hat, gram, *begun, columns[2], env_a, rows_a)
+    swapped = fetch(sib, other_core)
+    last, own = barrier((last, own))
+
+    own_last, sib_last = call(
+        column_kernel, pair, 5, 2 * 1073741824, 1 << 23, (pltpu.VMEM((256, 4096), BF16),)
+    )(last, env_a, env_b, rows_a, rows_b)
+    packed = call(pack_kernel, shape(8, 9, 32, 256), 4, 0, 1 << 21)(
+        own, own_last, swapped, fetch(sib_last, other_core)
+    )
     pieces = lax.all_to_all(packed, "env", 0, 0, tiled=True)
     return call(finish_kernel, shape(17, 32, 256, dtype=F32), 1, 0, 1 << 21)(pieces)[None]
 

time: 75.2 us -> 74.5 us (level)
  Pallas kernels: 15.3 us -> 16.6 us
  waiting for transfers between devices: 9.11 us -> 8.03 us
  starting transfers between devices: 21.2 us -> 20.4 us
    pallas_call x4 -> x3, Pallas kernels: 9.34 us -> 10.5 us  [the longest x1 8.05 us: on_device(): call(more_kernel, (shape(2048, 512), shape(512, 2048)) + four, 2 * PIECES...]
    ppermute x15 -> x12, waiting for transfers between devices: 9.11 us -> 8.03 us  [fetch(): return lax.ppermute(value, ('env', 'sp'), pairs)]
    ppermute x15 -> x12, starting transfers between devices: 21.2 us -> 20.4 us  [fetch(): return lax.ppermute(value, ('env', 'sp'), pairs)]
  transfers between devices with their start and end apart: 15 -> 12, of which waited for: 8 -> 4; matrix products, arithmetic and copies ran while one was open for 0% -> 0% of each run, Pallas kernels for 16% -> 21%
where the time goes in v10:
time: 74.5 us; the launch traced here: 73.6 us
  blocking collectives  26 us (35%)
  starting transfers between devices  20.4 us (27%)
  Pallas kernels  16.6 us (22%)
  waiting for transfers between devices  8.03 us (11%)
  local copies, waits for them, and re-layouts  2.54 us (3%)
    all_to_all x1, blocking collectives, on_device(): pieces = lax.all_to_all(packed, 'env', 0, 0, tiled=True)  26 us
    ppermute x12, starting transfers between devices, fetch(): return lax.ppermute(value, ('env', 'sp'), pairs)  20.4 us
    pallas_call x1, Pallas kernels, on_device(): call(more_kernel, (shape(2048, 512), shape(512, 2048)) + four, 2 * PIECES...  8.05 us
    ppermute x12, waiting for transfers between devices, fetch(): return lax.ppermute(value, ('env', 'sp'), pairs)  8.03 us
    pallas_call x2, Pallas kernels, begin(): call(begin_kernel, (shape(256, 512), gram_shape), 3, 1 << 30, 1 << 22, kept)  2.63 us
    unnamed x4, local copies, waits for them, and re-layouts  2.54 us
    pallas_call x1, Pallas kernels, on_device(): call(column_kernel, pair, 5, 2 * 1073741824, 1 << 23, (pltpu.VMEM((256, 4...  2.41 us
    pallas_call x1, Pallas kernels, rows(): call(body, (shape(envs, 512), shape(512, envs)) + sums, n_in, envs * 7864...  2.23 us
  transfers between devices with their start and end apart: 12, of which 4 were waited for; matrix products, arithmetic and copies ran while one was open for 0% of the time, Pallas kernels for 21%

profile of v10, /device:TPU:1, one launch (start us, length us, event | category | flops | bytes accessed | tf_op | source)
XLA Modules:
  0.0 73.6 jit_solution(11679948587209529891)
XLA Ops:
  0.0 3.2 %collective-permute-start.1 = (bf16[256,512]{1,0:T(8,128)(2,1)}, bf16[256,512]{1,0:T(8,128)(2,1)S(1)}, u32[]{:S(2)}, u32[]{:S(2)}) collective-permute-start(bf16[256,512]{1,0:T(8,128)(2,1)} %own_points.1), channel_id=1, source_target_pairs={{1,0},{0,1},{3,2},{2,3},{5,4},{4,5},{7,6},{6,7},{9,8},{8,9},{11,10... | collective-permute-start | bytes 786440 | tf_op jit(solution)/shard_map/ppermute | solution.py:30
  3.2 3.8 %collective-permute-start = (bf16[256,512]{1,0:T(8,128)(2,1)}, bf16[256,512]{1,0:T(8,128)(2,1)S(1)}, u32[]{:S(2)}, u32[]{:S(2)}) collective-permute-start(bf16[256,512]{1,0:T(8,128)(2,1)} %own_points.1), channel_id=1, source_target_pairs={{4,0},{5,1},{6,2},{7,3},{8,4},{9,5},{10,6},{11,7},{12,8},{13,9},{1... | collective-permute-start | bytes 786440 | tf_op jit(solution)/shard_map/ppermute | solution.py:30
  7.1 0.0 collective-permute-done.1.sib_points
  7.1 0.0 copy-start
  7.1 1.6 %copy-done = bf16[2048,512]{1,0:T(8,128)(2,1)S(1)} copy-done((bf16[2048,512]{1,0:T(8,128)(2,1)S(1)}, bf16[2048,512]{1,0:T(8,128)(2,1)}, u32[]{:S(2)}) %copy-start) | copy-done | bytes 2097176
  8.7 0.0 copy-start.1
  8.7 0.9 %copy-done.1 = bf16[256,512]{1,0:T(8,128)(2,1)S(1)} copy-done((bf16[256,512]{1,0:T(8,128)(2,1)S(1)}, bf16[256,512]{1,0:T(8,128)(2,1)}, u32[]{:S(2)}) %copy-start.1) | copy-done | bytes 262168
  9.6 2.2 %shard_map.28 = (bf16[2048,512]{1,0:T(8,128)(2,1)S(1)}, bf16[512,2048]{1,0:T(8,128)(2,1)S(1)}, f32[512,256]{1,0:T(8,128)S(1)}, bf16[512,512]{1,0:T(8,128)(2,1)S(1)}) custom-call(bf16[2048,512]{1,0:T(8,128)(2,1)S(1)} %copy-done, bf16[256,512]{1,0:T(8,128)(2,1)S(1)} %copy-done.1, bf16[256,512]{1,0:T(8,128)(2,1)S(1)} %collective-permute-done.1.sib_points), custom_call_target="tpu_custom_call" | custom-call | flops 1610612736 | bytes 8388608 | tf_op jit(solution)/shard_map/pallas_call | solution.py:216
  11.9 1.3 %collective-permute-done.points = bf16[256,512]{1,0:T(8,128)(2,1)S(1)} collective-permute-done((bf16[256,512]{1,0:T(8,128)(2,1)}, bf16[256,512]{1,0:T(8,128)(2,1)S(1)}, u32[]{:S(2)}, u32[]{:S(2)}) %collective-permute-start) | collective-permute-done | bytes 262176 | tf_op jit(solution)/shard_map/ppermute | solution.py:30
  13.1 0.1 shard_map.30
  13.2 1.1 %collective-permute-start.5 = (bf16[1024,512]{1,0:T(8,128)(2,1)S(1)}, bf16[1024,512]{1,0:T(8,128)(2,1)S(1)}, u32[]{:S(2)}, u32[]{:S(2)}) collective-permute-start(bf16[1024,512]{1,0:T(8,128)(2,1)S(1)} %shard_map.30), channel_id=1, source_target_pairs={{32,0},{97,1},{34,2},{99,3},{36,4},{101,5},{38,6},{103,7},{40,8},{... | collective-permute-start | bytes 3145736 | tf_op jit(solution)/shard_map/ppermute | solution.py:30
  14.3 2.4 %collective-permute-start.2 = (bf16[256,512]{1,0:T(8,128)(2,1)S(1)}, bf16[256,512]{1,0:T(8,128)(2,1)S(1)}, u32[]{:S(2)}, u32[]{:S(2)}) collective-permute-start(bf16[256,512]{1,0:T(8,128)(2,1)S(1)} %collective-permute-done.points), channel_id=1, source_target_pairs={{4,0},{5,1},{6,2},{7,3},{8,4},{9,5},{10,6},{11,7},{12,8},{13,9},{1... | collective-permute-start | bytes 786440 | tf_op jit(solution)/shard_map/ppermute | solution.py:30
  16.7 1.3 %shard_map.29 = (bf16[256,512]{1,0:T(8,128)(2,1)S(1)}, f32[512,256]{1,0:T(8,128)S(1)}) custom-call(bf16[256,512]{1,0:T(8,128)(2,1)S(1)} %collective-permute-done.points, bf16[2048,512]{1,0:T(8,128)(2,1)S(1)} %get-tuple-element.42.env_a.refs_15_.refs_0_, bf16[512,2048]{1,0:T(8,128)(2,1)S(1)} %get-tuple-element.43.rows_a.refs_16_.refs_2_), custom_call_target="tpu_custom_call" | custom-call | flops 1073741824 | bytes 4194304 | tf_op jit(solution)/shard_map/pallas_call | solution.py:234
  18.0 2.4 %collective-permute-done.2.points = bf16[256,512]{1,0:T(8,128)(2,1)S(1)} collective-permute-done((bf16[256,512]{1,0:T(8,128)(2,1)S(1)}, bf16[256,512]{1,0:T(8,128)(2,1)S(1)}, u32[]{:S(2)}, u32[]{:S(2)}) %collective-permute-start.2) | collective-permute-done | bytes 262176 | tf_op jit(solution)/shard_map/ppermute | solution.py:30
  20.4 3.4 %collective-permute-start.3 = (bf16[256,512]{1,0:T(8,128)(2,1)S(1)}, bf16[256,512]{1,0:T(8,128)(2,1)S(1)}, u32[]{:S(2)}, u32[]{:S(2)}) collective-permute-start(bf16[256,512]{1,0:T(8,128)(2,1)S(1)} %collective-permute-done.2.points), channel_id=1, source_target_pairs={{4,0},{5,1},{6,2},{7,3},{8,4},{9,5},{10,6},{11,7},{12,8},{13,9},{1... | collective-permute-start | bytes 786440 | tf_op jit(solution)/shard_map/ppermute | solution.py:30
  23.8 1.3 %shard_map.31 = (bf16[256,512]{1,0:T(8,128)(2,1)S(1)}, f32[512,256]{1,0:T(8,128)S(1)}) custom-call(bf16[256,512]{1,0:T(8,128)(2,1)S(1)} %collective-permute-done.2.points, bf16[2048,512]{1,0:T(8,128)(2,1)S(1)} %get-tuple-element.42.env_a.refs_15_.refs_0_, bf16[512,2048]{1,0:T(8,128)(2,1)S(1)} %get-tuple-element.43.rows_a.refs_16_.refs_2_), custom_call_target="tpu_custom_call" | custom-call | flops 1073741824 | bytes 4194304 | tf_op jit(solution)/shard_map/pallas_call | solution.py:234
  25.1 3.0 %collective-permute-done.5.near = bf16[1024,512]{1,0:T(8,128)(2,1)S(1)} collective-permute-done((bf16[1024,512]{1,0:T(8,128)(2,1)S(1)}, bf16[1024,512]{1,0:T(8,128)(2,1)S(1)}, u32[]{:S(2)}, u32[]{:S(2)}) %collective-permute-start.5) | collective-permute-done | bytes 1048608 | tf_op jit(solution)/shard_map/ppermute | solution.py:30
  28.1 0.1 shard_map.32
  28.2 2.1 %collective-permute-start.6 = (bf16[256,512]{1,0:T(8,128)(2,1)S(1)}, bf16[256,512]{1,0:T(8,128)(2,1)S(1)}, u32[]{:S(2)}, u32[]{:S(2)}) collective-permute-start(bf16[256,512]{1,0:T(8,128)(2,1)S(1)} %get-tuple-element.51.refs_0_), channel_id=1, source_target_pairs={{1,0},{0,1},{3,2},{2,3},{5,4},{4,5},{7,6},{6,7},{9,8},{8,9},{11,10... | collective-permute-start | bytes 786440 | tf_op jit(solution)/shard_map/ppermute | solution.py:30
  30.3 0.1 collective-permute-start.7
  30.4 0.4 collective-permute-start.8
  30.8 0.1 collective-permute-start.9
  30.9 0.0 collective-permute-done.3.refs_14_
  30.9 2.0 %collective-permute-start.4 = (bf16[256,512]{1,0:T(8,128)(2,1)S(1)}, bf16[256,512]{1,0:T(8,128)(2,1)S(1)}, u32[]{:S(2)}, u32[]{:S(2)}) collective-permute-start(bf16[256,512]{1,0:T(8,128)(2,1)S(1)} %collective-permute-done.3.refs_14_), channel_id=1, source_target_pairs={{4,0},{5,1},{6,2},{7,3},{8,4},{9,5},{10,6},{11,7},{12,8},{13,9},{1... | collective-permute-start | bytes 786440 | tf_op jit(solution)/shard_map/ppermute | solution.py:30
  32.9 0.0 collective-permute-done.6.refs_4_
  33.0 0.0 collective-permute-done.7.refs_5_
  33.0 0.0 collective-permute-done.8.refs_6_
  33.0 0.0 collective-permute-done.9.refs_7_
  33.0 8.1 %shard_map.33 = (bf16[2048,512]{1,0:T(8,128)(2,1)S(1)}, bf16[512,2048]{1,0:T(8,128)(2,1)S(1)}, bf16[4,256,256]{2,1,0:T(8,128)(2,1)S(1)}, bf16[4,256,256]{2,1,0:T(8,128)(2,1)S(1)}) custom-call(bf16[256,512]{1,0:T(8,128)(2,1)S(1)} %get-tuple-element.51.refs_0_, bf16[256,512]{1,0:T(8,128)(2,1)S(1)} %get-tuple-element.52.refs_1_, ...), custom_call_target="tpu_custom_call" | custom-call | flops 5905580032 | bytes 16777216 | tf_op jit(solution)/shard_map/pallas_call | solution.py:248
  41.0 1.6 %collective-permute-start.10 = (bf16[4,256,256]{2,1,0:T(8,128)(2,1)S(1)}, bf16[4,256,256]{2,1,0:T(8,128)(2,1)S(1)}, u32[]{:S(2)}, u32[]{:S(2)}) collective-permute-start(bf16[4,256,256]{2,1,0:T(8,128)(2,1)S(1)} %get-tuple-element.67), channel_id=1, source_target_pairs={{1,0},{0,1},{3,2},{2,3},{5,4},{4,5},{7,6},{6,7},{9,8},{8,9},{11,10... | collective-permute-start | bytes 1572872 | tf_op jit(solution)/shard_map/ppermute | solution.py:30
  42.6 0.0 collective-permute-done.4.points
  42.7 2.4 %shard_map.34 = (bf16[256,256]{1,0:T(8,128)(2,1)S(1)}, bf16[256,256]{1,0:T(8,128)(2,1)S(1)}) custom-call(bf16[256,512]{1,0:T(8,128)(2,1)S(1)} %collective-permute-done.4.points, bf16[2048,512]{1,0:T(8,128)(2,1)S(1)} %get-tuple-element.42.env_a.refs_15_.refs_0_, bf16[2048,512]{1,0:T(8,128)(2,1)S(1)} %get-tuple-element.64.refs_1_, ...), custom_call_target="tpu_custom_call" | custom-call | flops 2147483648 | bytes 8388608 | tf_op jit(solution)/shard_map/pallas_call | solution.py:255
  45.1 0.1 collective-permute-start.11
  45.2 1.3 %collective-permute-done.11.swapped_last = bf16[256,256]{1,0:T(8,128)(2,1)S(1)} collective-permute-done((bf16[256,256]{1,0:T(8,128)(2,1)S(1)}, bf16[256,256]{1,0:T(8,128)(2,1)S(1)}, u32[]{:S(2)}, u32[]{:S(2)}) %collective-permute-start.11) | collective-permute-done | bytes 131104 | tf_op jit(solution)/shard_map/ppermute | solution.py:30
  46.5 0.0 collective-permute-done.10.swapped
  46.5 0.1 shard_map.35
  46.6 26.0 %all_to_all.5.pieces = bf16[8,9,32,256]{3,2,1,0:T(8,128)(2,1)S(1)} all-to-all(bf16[8,9,32,256]{3,2,1,0:T(8,128)(2,1)S(1)} %shard_map.35), channel_id=1, replica_groups=mesh['env'=8,'sp'=32] {'env'}, dimensions={0} | all-to-all | bytes 2359296 | tf_op jit(solution)/shard_map/all_to_all | solution.py:261
  72.6 1.0 %shard_map.36 = f32[17,32,256]{2,1,0:T(8,128)} custom-call(bf16[8,9,32,256]{3,2,1,0:T(8,128)(2,1)S(1)} %all_to_all.5.pieces), custom_call_target="tpu_custom_call" | custom-call | bytes 2097152 | tf_op jit(solution)/shard_map/pallas_call | solution.py:262
Async XLA Ops:
  0.0 7.1 %collective-permute-start.1 = (bf16[256,512]{1,0:T(8,128)(2,1)}, bf16[256,512]{1,0:T(8,128)(2,1)S(1)}, u32[]{:S(2)}, u32[]{:S(2)}) collective-permute-start(bf16[256,512]{1,0:T(8,128)(2,1)} %own_points.1), channel_id=1, source_target_pairs={{1,0},{0,1},{3,2},{2,3},{5,4},{4,5},{7,6},{6,7},{9,8},{8,9},{11,10... | collective-permute-start | bytes 786440 | tf_op jit(solution)/shard_map/ppermute | solution.py:30
  3.2 9.9 %collective-permute-start = (bf16[256,512]{1,0:T(8,128)(2,1)}, bf16[256,512]{1,0:T(8,128)(2,1)S(1)}, u32[]{:S(2)}, u32[]{:S(2)}) collective-permute-start(bf16[256,512]{1,0:T(8,128)(2,1)} %own_points.1), channel_id=1, source_target_pairs={{4,0},{5,1},{6,2},{7,3},{8,4},{9,5},{10,6},{11,7},{12,8},{13,9},{1... | collective-permute-start | bytes 786440 | tf_op jit(solution)/shard_map/ppermute | solution.py:30
  7.1 1.6 %copy-start = (bf16[2048,512]{1,0:T(8,128)(2,1)S(1)}, bf16[2048,512]{1,0:T(8,128)(2,1)}, u32[]{:S(2)}) copy-start(bf16[2048,512]{1,0:T(8,128)(2,1)} %descriptors) | copy-start | bytes 6291460
  8.7 0.9 %copy-start.1 = (bf16[256,512]{1,0:T(8,128)(2,1)S(1)}, bf16[256,512]{1,0:T(8,128)(2,1)}, u32[]{:S(2)}) copy-start(bf16[256,512]{1,0:T(8,128)(2,1)} %own_points.1) | copy-start | bytes 786436
  13.2 14.9 %collective-permute-start.5 = (bf16[1024,512]{1,0:T(8,128)(2,1)S(1)}, bf16[1024,512]{1,0:T(8,128)(2,1)S(1)}, u32[]{:S(2)}, u32[]{:S(2)}) collective-permute-start(bf16[1024,512]{1,0:T(8,128)(2,1)S(1)} %shard_map.30), channel_id=1, source_target_pairs={{32,0},{97,1},{34,2},{99,3},{36,4},{101,5},{38,6},{103,7},{40,8},{... | collective-permute-start | bytes 3145736 | tf_op jit(solution)/shard_map/ppermute | solution.py:30
  14.3 6.1 %collective-permute-start.2 = (bf16[256,512]{1,0:T(8,128)(2,1)S(1)}, bf16[256,512]{1,0:T(8,128)(2,1)S(1)}, u32[]{:S(2)}, u32[]{:S(2)}) collective-permute-start(bf16[256,512]{1,0:T(8,128)(2,1)S(1)} %collective-permute-done.points), channel_id=1, source_target_pairs={{4,0},{5,1},{6,2},{7,3},{8,4},{9,5},{10,6},{11,7},{12,8},{13,9},{1... | collective-permute-start | bytes 786440 | tf_op jit(solution)/shard_map/ppermute | solution.py:30
  20.4 10.5 %collective-permute-start.3 = (bf16[256,512]{1,0:T(8,128)(2,1)S(1)}, bf16[256,512]{1,0:T(8,128)(2,1)S(1)}, u32[]{:S(2)}, u32[]{:S(2)}) collective-permute-start(bf16[256,512]{1,0:T(8,128)(2,1)S(1)} %collective-permute-done.2.points), channel_id=1, source_target_pairs={{4,0},{5,1},{6,2},{7,3},{8,4},{9,5},{10,6},{11,7},{12,8},{13,9},{1... | collective-permute-start | bytes 786440 | tf_op jit(solution)/shard_map/ppermute | solution.py:30
  28.2 4.7 %collective-permute-start.6 = (bf16[256,512]{1,0:T(8,128)(2,1)S(1)}, bf16[256,512]{1,0:T(8,128)(2,1)S(1)}, u32[]{:S(2)}, u32[]{:S(2)}) collective-permute-start(bf16[256,512]{1,0:T(8,128)(2,1)S(1)} %get-tuple-element.51.refs_0_), channel_id=1, source_target_pairs={{1,0},{0,1},{3,2},{2,3},{5,4},{4,5},{7,6},{6,7},{9,8},{8,9},{11,10... | collective-permute-start | bytes 786440 | tf_op jit(solution)/shard_map/ppermute | solution.py:30
  30.3 2.6 %collective-permute-start.7 = (bf16[256,512]{1,0:T(8,128)(2,1)S(1)}, bf16[256,512]{1,0:T(8,128)(2,1)S(1)}, u32[]{:S(2)}, u32[]{:S(2)}) collective-permute-start(bf16[256,512]{1,0:T(8,128)(2,1)S(1)} %get-tuple-element.52.refs_1_), channel_id=1, source_target_pairs={{1,0},{0,1},{3,2},{2,3},{5,4},{4,5},{7,6},{6,7},{9,8},{8,9},{11,10... | collective-permute-start | bytes 786440 | tf_op jit(solution)/shard_map/ppermute | solution.py:30
  30.4 2.5 %collective-permute-start.8 = (bf16[256,512]{1,0:T(8,128)(2,1)S(1)}, bf16[256,512]{1,0:T(8,128)(2,1)S(1)}, u32[]{:S(2)}, u32[]{:S(2)}) collective-permute-start(bf16[256,512]{1,0:T(8,128)(2,1)S(1)} %get-tuple-element.53.refs_2_), channel_id=1, source_target_pairs={{1,0},{0,1},{3,2},{2,3},{5,4},{4,5},{7,6},{6,7},{9,8},{8,9},{11,10... | collective-permute-start | bytes 786440 | tf_op jit(solution)/shard_map/ppermute | solution.py:30
  30.8 2.1 %collective-permute-start.9 = (bf16[256,512]{1,0:T(8,128)(2,1)S(1)}, bf16[256,512]{1,0:T(8,128)(2,1)S(1)}, u32[]{:S(2)}, u32[]{:S(2)}) collective-permute-start(bf16[256,512]{1,0:T(8,128)(2,1)S(1)} %get-tuple-element.54.refs_3_), channel_id=1, source_target_pairs={{1,0},{0,1},{3,2},{2,3},{5,4},{4,5},{7,6},{6,7},{9,8},{8,9},{11,10... | collective-permute-start | bytes 786440 | tf_op jit(solution)/shard_map/ppermute | solution.py:30
  30.9 11.7 %collective-permute-start.4 = (bf16[256,512]{1,0:T(8,128)(2,1)S(1)}, bf16[256,512]{1,0:T(8,128)(2,1)S(1)}, u32[]{:S(2)}, u32[]{:S(2)}) collective-permute-start(bf16[256,512]{1,0:T(8,128)(2,1)S(1)} %collective-permute-done.3.refs_14_), channel_id=1, source_target_pairs={{4,0},{5,1},{6,2},{7,3},{8,4},{9,5},{10,6},{11,7},{12,8},{13,9},{1... | collective-permute-start | bytes 786440 | tf_op jit(solution)/shard_map/ppermute | solution.py:30
  41.0 5.5 %collective-permute-start.10 = (bf16[4,256,256]{2,1,0:T(8,128)(2,1)S(1)}, bf16[4,256,256]{2,1,0:T(8,128)(2,1)S(1)}, u32[]{:S(2)}, u32[]{:S(2)}) collective-permute-start(bf16[4,256,256]{2,1,0:T(8,128)(2,1)S(1)} %get-tuple-element.67), channel_id=1, source_target_pairs={{1,0},{0,1},{3,2},{2,3},{5,4},{4,5},{7,6},{6,7},{9,8},{8,9},{11,10... | collective-permute-start | bytes 1572872 | tf_op jit(solution)/shard_map/ppermute | solution.py:30
  45.1 1.4 %collective-permute-start.11 = (bf16[256,256]{1,0:T(8,128)(2,1)S(1)}, bf16[256,256]{1,0:T(8,128)(2,1)S(1)}, u32[]{:S(2)}, u32[]{:S(2)}) collective-permute-start(bf16[256,256]{1,0:T(8,128)(2,1)S(1)} %get-tuple-element.68), channel_id=1, source_target_pairs={{1,0},{0,1},{3,2},{2,3},{5,4},{4,5},{7,6},{6,7},{9,8},{8,9},{11,10... | collective-permute-start | bytes 393224 | tf_op jit(solution)/shard_map/ppermute | solution.py:30

commit v11 on v8

--- a/solution.py
+++ b/solution.py
@@ -92,9 +92,11 @@
             place += size
 
 
-def slice_kernel(descriptors, out):
+def slice_kernel(descriptors, out, sem):
     half = pl.multiple_of((lax.axis_index("sp") % 2) * 1024, 1024)
-    out[...] = descriptors[pl.ds(half, 1024), :]
+    copy = pltpu.make_async_copy(descriptors.at[pl.ds(half, 1024), :], out, sem)
+    copy.start()
+    copy.wait()
 
 
 def split_kernel(near, *outs):
@@ -204,36 +206,40 @@
     gram_shape = shape(512, 256, dtype=F32)
     pair = (shape(256, 256), shape(256, 256))
 
-    column = fetch(sparse_points, first_column)
+    columns = [fetch(sparse_points, first_column)]
     sib_points = fetch(sparse_points, other_core)
+    near = pl.pallas_call(
+        slice_kernel,
+        out_shape=shape(1024, 512),
+        in_specs=[pl.BlockSpec(memory_space=pl.ANY)],
+        out_specs=vmem_spec(),
+        scratch_shapes=(pltpu.SemaphoreType.DMA,),
+        compiler_params=pltpu.CompilerParams(vmem_limit_bytes=61 * 1024 * 1024),
+        cost_estimate=pl.CostEstimate(flops=0, bytes_accessed=1 << 21, transcendentals=0),
+    )(descriptors)
+    near = fetch(near, near_x)
     env_a, rows_a, gram, points_hat = rows(
         own_kernel, 2048, (gram_shape, shape(512, 512)), 3, descriptors, sparse_points, sib_points
     )
-    columns = [column]
-    column, later, env_a, rows_a, gram, points_hat = barrier(
-        (column, descriptors, env_a, rows_a, gram, points_hat)
-    )
+    column, env_a, rows_a, gram, points_hat = barrier((columns[0], env_a, rows_a, gram, points_hat))
+    near, _ = barrier((near, column))
 
     columns.append(fetch(column, next_z))
-    near = fetch(call(slice_kernel, shape(1024, 512), 1, 0, 1 << 21)(later), near_x)
-    near, _ = barrier((near, columns[1]))
-
-    columns.append(fetch(columns[1], next_z))
     near = call(split_kernel, PIECES * (shape(1024 // PIECES, 512),), 1, 0, 1 << 21)(near)
     far = [fetch(piece, other_core) for piece in near]
-    env_b, rows_b, own, sib = rows(more_kernel, 2048, pair, 2 * PIECES + 2, *near, *far, points_hat, gram)
+    env_b, rows_b, *sums = rows(more_kernel, 2048, pair, 2 * PIECES + 2, *near, *far, points_hat, gram)
 
     def take(points):
         return call(
             column_kernel, pair, 5, 2 * 1073741824, 1 << 23, (pltpu.VMEM((256, 4096), BF16),)
         )(points, env_a, env_b, rows_a, rows_b)
 
-    sums = [own, sib]
-    column = columns[2]
+    columns.append(fetch(columns[1], next_z))
+    sums += take(columns[0]) + take(columns[1])
+    column, *sums = barrier((columns[2], *sums))
 
     last = fetch(column, next_z)
-    for points in columns[:3]:
-        sums += take(points)
+    sums += take(column)
     owns, swapped = sums[0::2], [fetch(sib, other_core) for sib in sums[1::2]]
     last, *sums = barrier((last, *owns, *swapped))
     owns, swapped = sums[:4], sums[4:]

time: 77.9 us -> 72.9 us (0.936)
  blocking collectives: 26 us -> 22.4 us
  waiting for transfers between devices: 11.4 us -> 8.76 us
  local copies, waits for them, and re-layouts: 2.54 us -> 0.01 us
  Pallas kernels: 15.3 us -> 17.6 us
  starting transfers between devices: 21.7 us -> 23.7 us
    all_to_all x1, blocking collectives: 26 us -> 22.4 us  [on_device(): pieces = lax.all_to_all(packed, 'env', 0, 0, tiled=True)]
    ppermute x15, waiting for transfers between devices: 11.4 us -> 8.76 us  [fetch(): return lax.ppermute(value, ('env', 'sp'), pairs)]
    unnamed x4, local copies, waits for them, and re-layouts: 2.54 us -> 0.01 us
    pallas_call x1, Pallas kernels: 0.07 us -> 2.38 us  [on_device(): pl.pallas_call(slice_kernel, out_shape=shape(1024, 512), in_specs=[pl.Blo...]
    ppermute x15, starting transfers between devices: 21.7 us -> 23.7 us  [fetch(): return lax.ppermute(value, ('env', 'sp'), pairs)]
  transfers between devices with their start and end apart: 15 -> 15, of which waited for: 6 -> 7; matrix products, arithmetic and copies ran while one was open for 0% -> 0% of each run, Pallas kernels for 15% -> 16%
where the time goes in v11:
time: 72.9 us; the launch traced here: 72.6 us
  starting transfers between devices  23.7 us (33%)
  blocking collectives  22.4 us (31%)
  Pallas kernels  17.6 us (24%)
  waiting for transfers between devices  8.76 us (12%)
    ppermute x15, starting transfers between devices, fetch(): return lax.ppermute(value, ('env', 'sp'), pairs)  23.7 us
    all_to_all x1, blocking collectives, on_device(): pieces = lax.all_to_all(packed, 'env', 0, 0, tiled=True)  22.4 us
    pallas_call x4, Pallas kernels, take(): call(column_kernel, pair, 5, 2 * 1073741824, 1 << 23, (pltpu.VMEM((256, 4...  9.62 us
    ppermute x15, waiting for transfers between devices, fetch(): return lax.ppermute(value, ('env', 'sp'), pairs)  8.76 us
    pallas_call x2, Pallas kernels, rows(): call(body, (shape(envs, 512), shape(512, envs)) + sums, n_in, envs * 7864...  4.41 us
    pallas_call x1, Pallas kernels, on_device(): pl.pallas_call(slice_kernel, out_shape=shape(1024, 512), in_specs=[pl.Blo...  2.38 us
  transfers between devices with their start and end apart: 15, of which 7 were waited for; matrix products, arithmetic and copies ran while one was open for 0% of the time, Pallas kernels for 16%

profile of v11, /device:TPU:1, one launch (start us, length us, event | category | flops | bytes accessed | tf_op | source)
XLA Modules:
  0.0 72.6 jit_solution(9055512796151990303)
XLA Ops:
  0.0 0.0 copy-start
  0.0 0.0 copy-start.1
  0.0 2.4 %shard_map.29 = bf16[1024,512]{1,0:T(8,128)(2,1)} custom-call(bf16[2048,512]{1,0:T(8,128)(2,1)} %descriptors.1), custom_call_target="tpu_custom_call" | custom-call | bytes 2097152 | tf_op jit(solution)/shard_map/pallas_call | solution.py:211
  2.4 2.1 %collective-permute-start.4 = (bf16[1024,512]{1,0:T(8,128)(2,1)}, bf16[1024,512]{1,0:T(8,128)(2,1)S(1)}, u32[]{:S(2)}, u32[]{:S(2)}) collective-permute-start(bf16[1024,512]{1,0:T(8,128)(2,1)} %shard_map.29), channel_id=1, source_target_pairs={{32,0},{97,1},{34,2},{99,3},{36,4},{101,5},{38,6},{103,7},{40,8},{... | collective-permute-start | bytes 3145736 | tf_op jit(solution)/shard_map/ppermute | solution.py:30
  4.5 0.0 copy-done.1
  4.5 2.2 %collective-permute-start.1 = (bf16[256,512]{1,0:T(8,128)(2,1)S(1)}, bf16[256,512]{1,0:T(8,128)(2,1)S(1)}, u32[]{:S(2)}, u32[]{:S(2)}) collective-permute-start(bf16[256,512]{1,0:T(8,128)(2,1)S(1)} %copy-done.1), channel_id=1, source_target_pairs={{1,0},{0,1},{3,2},{2,3},{5,4},{4,5},{7,6},{6,7},{9,8},{8,9},{11,10... | collective-permute-start | bytes 786440 | tf_op jit(solution)/shard_map/ppermute | solution.py:30
  6.7 5.6 %collective-permute-start = (bf16[256,512]{1,0:T(8,128)(2,1)S(1)}, bf16[256,512]{1,0:T(8,128)(2,1)S(1)}, u32[]{:S(2)}, u32[]{:S(2)}) collective-permute-start(bf16[256,512]{1,0:T(8,128)(2,1)S(1)} %copy-done.1), channel_id=1, source_target_pairs={{4,0},{5,1},{6,2},{7,3},{8,4},{9,5},{10,6},{11,7},{12,8},{13,9},{1... | collective-permute-start | bytes 786440 | tf_op jit(solution)/shard_map/ppermute | solution.py:30
  12.3 0.0 collective-permute-done.1.sib_points
  12.3 0.0 copy-done
  12.3 2.2 %shard_map.28 = (bf16[2048,512]{1,0:T(8,128)(2,1)S(1)}, bf16[512,2048]{1,0:T(8,128)(2,1)S(1)}, f32[512,256]{1,0:T(8,128)S(1)}, bf16[512,512]{1,0:T(8,128)(2,1)S(1)}) custom-call(bf16[2048,512]{1,0:T(8,128)(2,1)S(1)} %copy-done, bf16[256,512]{1,0:T(8,128)(2,1)S(1)} %copy-done.1, bf16[256,512]{1,0:T(8,128)(2,1)S(1)} %collective-permute-done.1.sib_points), custom_call_target="tpu_custom_call" | custom-call | flops 1610612736 | bytes 8388608 | tf_op jit(solution)/shard_map/pallas_call | solution.py:204
  14.6 3.5 %collective-permute-done.points = bf16[256,512]{1,0:T(8,128)(2,1)S(1)} collective-permute-done((bf16[256,512]{1,0:T(8,128)(2,1)S(1)}, bf16[256,512]{1,0:T(8,128)(2,1)S(1)}, u32[]{:S(2)}, u32[]{:S(2)}) %collective-permute-start) | collective-permute-done | bytes 262176 | tf_op jit(solution)/shard_map/ppermute | solution.py:30
  18.1 3.4 %collective-permute-start.2 = (bf16[256,512]{1,0:T(8,128)(2,1)S(1)}, bf16[256,512]{1,0:T(8,128)(2,1)S(1)}, u32[]{:S(2)}, u32[]{:S(2)}) collective-permute-start(bf16[256,512]{1,0:T(8,128)(2,1)S(1)} %collective-permute-done.points), channel_id=1, source_target_pairs={{4,0},{5,1},{6,2},{7,3},{8,4},{9,5},{10,6},{11,7},{12,8},{13,9},{1... | collective-permute-start | bytes 786440 | tf_op jit(solution)/shard_map/ppermute | solution.py:30
  21.5 0.0 collective-permute-done.4.near
  21.5 0.1 shard_map.30
  21.5 1.2 %collective-permute-start.5 = (bf16[256,512]{1,0:T(8,128)(2,1)S(1)}, bf16[256,512]{1,0:T(8,128)(2,1)S(1)}, u32[]{:S(2)}, u32[]{:S(2)}) collective-permute-start(bf16[256,512]{1,0:T(8,128)(2,1)S(1)} %get-tuple-element.53.refs_0_), channel_id=1, source_target_pairs={{1,0},{0,1},{3,2},{2,3},{5,4},{4,5},{7,6},{6,7},{9,8},{8,9},{11,10... | collective-permute-start | bytes 786440 | tf_op jit(solution)/shard_map/ppermute | solution.py:30
  22.7 0.1 collective-permute-start.6
  22.8 0.4 collective-permute-start.7
  23.2 0.1 collective-permute-start.8
  23.3 3.0 %collective-permute-done.2.points = bf16[256,512]{1,0:T(8,128)(2,1)S(1)} collective-permute-done((bf16[256,512]{1,0:T(8,128)(2,1)S(1)}, bf16[256,512]{1,0:T(8,128)(2,1)S(1)}, u32[]{:S(2)}, u32[]{:S(2)}) %collective-permute-start.2) | collective-permute-done | bytes 262176 | tf_op jit(solution)/shard_map/ppermute | solution.py:30
  26.3 3.4 %collective-permute-start.3 = (bf16[256,512]{1,0:T(8,128)(2,1)S(1)}, bf16[256,512]{1,0:T(8,128)(2,1)S(1)}, u32[]{:S(2)}, u32[]{:S(2)}) collective-permute-start(bf16[256,512]{1,0:T(8,128)(2,1)S(1)} %collective-permute-done.2.points), channel_id=1, source_target_pairs={{4,0},{5,1},{6,2},{7,3},{8,4},{9,5},{10,6},{11,7},{12,8},{13,9},{1... | collective-permute-start | bytes 786440 | tf_op jit(solution)/shard_map/ppermute | solution.py:30
  29.7 0.0 collective-permute-done.5.refs_4_
  29.7 0.0 collective-permute-done.6.refs_5_
  29.7 0.0 collective-permute-done.7.refs_6_
  29.7 0.0 collective-permute-done.8.refs_7_
  29.7 2.2 %shard_map.31 = (bf16[2048,512]{1,0:T(8,128)(2,1)S(1)}, bf16[512,2048]{1,0:T(8,128)(2,1)S(1)}, bf16[256,256]{1,0:T(8,128)(2,1)S(1)}, bf16[256,256]{1,0:T(8,128)(2,1)S(1)}) custom-call(bf16[256,512]{1,0:T(8,128)(2,1)S(1)} %get-tuple-element.53.refs_0_, bf16[256,512]{1,0:T(8,128)(2,1)S(1)} %get-tuple-element.54.refs_1_, ...), custom_call_target="tpu_custom_call" | custom-call | flops 1610612736 | bytes 8388608 | tf_op jit(solution)/shard_map/pallas_call | solution.py:204
  31.9 2.4 %shard_map.33 = (bf16[256,256]{1,0:T(8,128)(2,1)S(1)}, bf16[256,256]{1,0:T(8,128)(2,1)S(1)}) custom-call(bf16[256,512]{1,0:T(8,128)(2,1)S(1)} %collective-permute-done.2.points, bf16[2048,512]{1,0:T(8,128)(2,1)S(1)} %get-tuple-element.61.refs_0_, bf16[2048,512]{1,0:T(8,128)(2,1)S(1)} %get-tuple-element.62.refs_1_, ...), custom_call_target="tpu_custom_call" | custom-call | flops 2147483648 | bytes 8388608 | tf_op jit(solution)/shard_map/pallas_call | solution.py:233
  34.3 2.4 %shard_map.32 = (bf16[256,256]{1,0:T(8,128)(2,1)S(1)}, bf16[256,256]{1,0:T(8,128)(2,1)S(1)}) custom-call(bf16[256,512]{1,0:T(8,128)(2,1)S(1)} %collective-permute-done.points, bf16[2048,512]{1,0:T(8,128)(2,1)S(1)} %get-tuple-element.61.refs_0_, bf16[2048,512]{1,0:T(8,128)(2,1)S(1)} %get-tuple-element.62.refs_1_, ...), custom_call_target="tpu_custom_call" | custom-call | flops 2147483648 | bytes 8388608 | tf_op jit(solution)/shard_map/pallas_call | solution.py:233
  36.8 0.0 collective-permute-done.3.points
  36.8 0.3 collective-permute-start.9
  37.1 2.4 %shard_map.34 = (bf16[256,256]{1,0:T(8,128)(2,1)S(1)}, bf16[256,256]{1,0:T(8,128)(2,1)S(1)}) custom-call(bf16[256,512]{1,0:T(8,128)(2,1)S(1)} %collective-permute-done.3.points, bf16[2048,512]{1,0:T(8,128)(2,1)S(1)} %get-tuple-element.61.refs_0_, bf16[2048,512]{1,0:T(8,128)(2,1)S(1)} %get-tuple-element.62.refs_1_, ...), custom_call_target="tpu_custom_call" | custom-call | flops 2147483648 | bytes 8388608 | tf_op jit(solution)/shard_map/pallas_call | solution.py:233
  39.5 3.0 %collective-permute-start.13 = (bf16[256,256]{1,0:T(8,128)(2,1)S(1)}, bf16[256,256]{1,0:T(8,128)(2,1)S(1)}, u32[]{:S(2)}, u32[]{:S(2)}) collective-permute-start(bf16[256,256]{1,0:T(8,128)(2,1)S(1)} %get-tuple-element.77), channel_id=1, source_target_pairs={{1,0},{0,1},{3,2},{2,3},{5,4},{4,5},{7,6},{6,7},{9,8},{8,9},{11,10... | collective-permute-start | bytes 393224 | tf_op jit(solution)/shard_map/ppermute | solution.py:30
  42.4 0.1 collective-permute-start.10
  42.5 0.4 collective-permute-start.11
  42.9 0.1 collective-permute-start.12
  43.0 0.4 collective-permute-done.13.refs_8_
  43.4 0.4 collective-permute-done.10.refs_5_
  43.8 0.2 collective-permute-done.11.refs_6_
  44.0 0.3 collective-permute-done.12.refs_7_
  44.3 0.0 collective-permute-done.9.points
  44.3 2.4 %shard_map.35 = (bf16[256,256]{1,0:T(8,128)(2,1)S(1)}, bf16[256,256]{1,0:T(8,128)(2,1)S(1)}) custom-call(bf16[256,512]{1,0:T(8,128)(2,1)S(1)} %collective-permute-done.9.points, bf16[2048,512]{1,0:T(8,128)(2,1)S(1)} %get-tuple-element.61.refs_0_, bf16[2048,512]{1,0:T(8,128)(2,1)S(1)} %get-tuple-element.62.refs_1_, ...), custom_call_target="tpu_custom_call" | custom-call | flops 2147483648 | bytes 8388608 | tf_op jit(solution)/shard_map/pallas_call | solution.py:233
  46.7 1.4 %collective-permute-start.14 = (bf16[256,256]{1,0:T(8,128)(2,1)S(1)}, bf16[256,256]{1,0:T(8,128)(2,1)S(1)}, u32[]{:S(2)}, u32[]{:S(2)}) collective-permute-start(bf16[256,256]{1,0:T(8,128)(2,1)S(1)} %get-tuple-element.88), channel_id=1, source_target_pairs={{1,0},{0,1},{3,2},{2,3},{5,4},{4,5},{7,6},{6,7},{9,8},{8,9},{11,10... | collective-permute-start | bytes 393224 | tf_op jit(solution)/shard_map/ppermute | solution.py:30
  48.1 1.0 %collective-permute-done.14.refs_9_ = bf16[256,256]{1,0:T(8,128)(2,1)S(1)} collective-permute-done((bf16[256,256]{1,0:T(8,128)(2,1)S(1)}, bf16[256,256]{1,0:T(8,128)(2,1)S(1)}, u32[]{:S(2)}, u32[]{:S(2)}) %collective-permute-start.14) | collective-permute-done | bytes 131104 | tf_op jit(solution)/shard_map/ppermute | solution.py:30
  49.1 0.1 shard_map.36
  49.1 22.4 %all_to_all.5.pieces = bf16[8,9,32,256]{3,2,1,0:T(8,128)(2,1)S(1)} all-to-all(bf16[8,9,32,256]{3,2,1,0:T(8,128)(2,1)S(1)} %shard_map.36), channel_id=1, replica_groups=mesh['env'=8,'sp'=32] {'env'}, dimensions={0} | all-to-all | bytes 2359296 | tf_op jit(solution)/shard_map/all_to_all | solution.py:249
  71.5 1.0 %shard_map.37 = f32[17,32,256]{2,1,0:T(8,128)} custom-call(bf16[8,9,32,256]{3,2,1,0:T(8,128)(2,1)S(1)} %all_to_all.5.pieces), custom_call_target="tpu_custom_call" | custom-call | bytes 2097152 | tf_op jit(solution)/shard_map/pallas_call | solution.py:250
Async XLA Ops:
  0.0 12.3 %copy-start = (bf16[2048,512]{1,0:T(8,128)(2,1)S(1)}, bf16[2048,512]{1,0:T(8,128)(2,1)}, u32[]{:S(2)}) copy-start(bf16[2048,512]{1,0:T(8,128)(2,1)} %descriptors.1) | copy-start | bytes 6291460
  0.0 4.5 %copy-start.1 = (bf16[256,512]{1,0:T(8,128)(2,1)S(1)}, bf16[256,512]{1,0:T(8,128)(2,1)}, u32[]{:S(2)}) copy-start(bf16[256,512]{1,0:T(8,128)(2,1)} %own_points.1) | copy-start | bytes 786436
  2.4 19.1 %collective-permute-start.4 = (bf16[1024,512]{1,0:T(8,128)(2,1)}, bf16[1024,512]{1,0:T(8,128)(2,1)S(1)}, u32[]{:S(2)}, u32[]{:S(2)}) collective-permute-start(bf16[1024,512]{1,0:T(8,128)(2,1)} %shard_map.29), channel_id=1, source_target_pairs={{32,0},{97,1},{34,2},{99,3},{36,4},{101,5},{38,6},{103,7},{40,8},{... | collective-permute-start | bytes 3145736 | tf_op jit(solution)/shard_map/ppermute | solution.py:30
  4.5 7.8 %collective-permute-start.1 = (bf16[256,512]{1,0:T(8,128)(2,1)S(1)}, bf16[256,512]{1,0:T(8,128)(2,1)S(1)}, u32[]{:S(2)}, u32[]{:S(2)}) collective-permute-start(bf16[256,512]{1,0:T(8,128)(2,1)S(1)} %copy-done.1), channel_id=1, source_target_pairs={{1,0},{0,1},{3,2},{2,3},{5,4},{4,5},{7,6},{6,7},{9,8},{8,9},{11,10... | collective-permute-start | bytes 786440 | tf_op jit(solution)/shard_map/ppermute | solution.py:30
  6.7 11.3 %collective-permute-start = (bf16[256,512]{1,0:T(8,128)(2,1)S(1)}, bf16[256,512]{1,0:T(8,128)(2,1)S(1)}, u32[]{:S(2)}, u32[]{:S(2)}) collective-permute-start(bf16[256,512]{1,0:T(8,128)(2,1)S(1)} %copy-done.1), channel_id=1, source_target_pairs={{4,0},{5,1},{6,2},{7,3},{8,4},{9,5},{10,6},{11,7},{12,8},{13,9},{1... | collective-permute-start | bytes 786440 | tf_op jit(solution)/shard_map/ppermute | solution.py:30
  18.1 8.3 %collective-permute-start.2 = (bf16[256,512]{1,0:T(8,128)(2,1)S(1)}, bf16[256,512]{1,0:T(8,128)(2,1)S(1)}, u32[]{:S(2)}, u32[]{:S(2)}) collective-permute-start(bf16[256,512]{1,0:T(8,128)(2,1)S(1)} %collective-permute-done.points), channel_id=1, source_target_pairs={{4,0},{5,1},{6,2},{7,3},{8,4},{9,5},{10,6},{11,7},{12,8},{13,9},{1... | collective-permute-start | bytes 786440 | tf_op jit(solution)/shard_map/ppermute | solution.py:30
  21.5 8.2 %collective-permute-start.5 = (bf16[256,512]{1,0:T(8,128)(2,1)S(1)}, bf16[256,512]{1,0:T(8,128)(2,1)S(1)}, u32[]{:S(2)}, u32[]{:S(2)}) collective-permute-start(bf16[256,512]{1,0:T(8,128)(2,1)S(1)} %get-tuple-element.53.refs_0_), channel_id=1, source_target_pairs={{1,0},{0,1},{3,2},{2,3},{5,4},{4,5},{7,6},{6,7},{9,8},{8,9},{11,10... | collective-permute-start | bytes 786440 | tf_op jit(solution)/shard_map/ppermute | solution.py:30
  22.7 7.0 %collective-permute-start.6 = (bf16[256,512]{1,0:T(8,128)(2,1)S(1)}, bf16[256,512]{1,0:T(8,128)(2,1)S(1)}, u32[]{:S(2)}, u32[]{:S(2)}) collective-permute-start(bf16[256,512]{1,0:T(8,128)(2,1)S(1)} %get-tuple-element.54.refs_1_), channel_id=1, source_target_pairs={{1,0},{0,1},{3,2},{2,3},{5,4},{4,5},{7,6},{6,7},{9,8},{8,9},{11,10... | collective-permute-start | bytes 786440 | tf_op jit(solution)/shard_map/ppermute | solution.py:30
  22.8 6.9 %collective-permute-start.7 = (bf16[256,512]{1,0:T(8,128)(2,1)S(1)}, bf16[256,512]{1,0:T(8,128)(2,1)S(1)}, u32[]{:S(2)}, u32[]{:S(2)}) collective-permute-start(bf16[256,512]{1,0:T(8,128)(2,1)S(1)} %get-tuple-element.55.refs_2_), channel_id=1, source_target_pairs={{1,0},{0,1},{3,2},{2,3},{5,4},{4,5},{7,6},{6,7},{9,8},{8,9},{11,10... | collective-permute-start | bytes 786440 | tf_op jit(solution)/shard_map/ppermute | solution.py:30
  23.2 6.5 %collective-permute-start.8 = (bf16[256,512]{1,0:T(8,128)(2,1)S(1)}, bf16[256,512]{1,0:T(8,128)(2,1)S(1)}, u32[]{:S(2)}, u32[]{:S(2)}) collective-permute-start(bf16[256,512]{1,0:T(8,128)(2,1)S(1)} %get-tuple-element.56.refs_3_), channel_id=1, source_target_pairs={{1,0},{0,1},{3,2},{2,3},{5,4},{4,5},{7,6},{6,7},{9,8},{8,9},{11,10... | collective-permute-start | bytes 786440 | tf_op jit(solution)/shard_map/ppermute | solution.py:30
  26.3 10.4 %collective-permute-start.3 = (bf16[256,512]{1,0:T(8,128)(2,1)S(1)}, bf16[256,512]{1,0:T(8,128)(2,1)S(1)}, u32[]{:S(2)}, u32[]{:S(2)}) collective-permute-start(bf16[256,512]{1,0:T(8,128)(2,1)S(1)} %collective-permute-done.2.points), channel_id=1, source_target_pairs={{4,0},{5,1},{6,2},{7,3},{8,4},{9,5},{10,6},{11,7},{12,8},{13,9},{1... | collective-permute-start | bytes 786440 | tf_op jit(solution)/shard_map/ppermute | solution.py:30
  36.8 7.5 %collective-permute-start.9 = (bf16[256,512]{1,0:T(8,128)(2,1)S(1)}, bf16[256,512]{1,0:T(8,128)(2,1)S(1)}, u32[]{:S(2)}, u32[]{:S(2)}) collective-permute-start(bf16[256,512]{1,0:T(8,128)(2,1)S(1)} %collective-permute-done.3.points), channel_id=1, source_target_pairs={{4,0},{5,1},{6,2},{7,3},{8,4},{9,5},{10,6},{11,7},{12,8},{13,9},{1... | collective-permute-start | bytes 786440 | tf_op jit(solution)/shard_map/ppermute | solution.py:30
  39.5 3.9 %collective-permute-start.13 = (bf16[256,256]{1,0:T(8,128)(2,1)S(1)}, bf16[256,256]{1,0:T(8,128)(2,1)S(1)}, u32[]{:S(2)}, u32[]{:S(2)}) collective-permute-start(bf16[256,256]{1,0:T(8,128)(2,1)S(1)} %get-tuple-element.77), channel_id=1, source_target_pairs={{1,0},{0,1},{3,2},{2,3},{5,4},{4,5},{7,6},{6,7},{9,8},{8,9},{11,10... | collective-permute-start | bytes 393224 | tf_op jit(solution)/shard_map/ppermute | solution.py:30
  42.4 1.3 %collective-permute-start.10 = (bf16[256,256]{1,0:T(8,128)(2,1)S(1)}, bf16[256,256]{1,0:T(8,128)(2,1)S(1)}, u32[]{:S(2)}, u32[]{:S(2)}) collective-permute-start(bf16[256,256]{1,0:T(8,128)(2,1)S(1)} %get-tuple-element.74), channel_id=1, source_target_pairs={{1,0},{0,1},{3,2},{2,3},{5,4},{4,5},{7,6},{6,7},{9,8},{8,9},{11,10... | collective-permute-start | bytes 393224 | tf_op jit(solution)/shard_map/ppermute | solution.py:30
  42.5 1.4 %collective-permute-start.11 = (bf16[256,256]{1,0:T(8,128)(2,1)S(1)}, bf16[256,256]{1,0:T(8,128)(2,1)S(1)}, u32[]{:S(2)}, u32[]{:S(2)}) collective-permute-start(bf16[256,256]{1,0:T(8,128)(2,1)S(1)} %get-tuple-element.75), channel_id=1, source_target_pairs={{1,0},{0,1},{3,2},{2,3},{5,4},{4,5},{7,6},{6,7},{9,8},{8,9},{11,10... | collective-permute-start | bytes 393224 | tf_op jit(solution)/shard_map/ppermute | solution.py:30
  42.9 1.3 %collective-permute-start.12 = (bf16[256,256]{1,0:T(8,128)(2,1)S(1)}, bf16[256,256]{1,0:T(8,128)(2,1)S(1)}, u32[]{:S(2)}, u32[]{:S(2)}) collective-permute-start(bf16[256,256]{1,0:T(8,128)(2,1)S(1)} %get-tuple-element.76), channel_id=1, source_target_pairs={{1,0},{0,1},{3,2},{2,3},{5,4},{4,5},{7,6},{6,7},{9,8},{8,9},{11,10... | collective-permute-start | bytes 393224 | tf_op jit(solution)/shard_map/ppermute | solution.py:30
  46.7 2.3 %collective-permute-start.14 = (bf16[256,256]{1,0:T(8,128)(2,1)S(1)}, bf16[256,256]{1,0:T(8,128)(2,1)S(1)}, u32[]{:S(2)}, u32[]{:S(2)}) collective-permute-start(bf16[256,256]{1,0:T(8,128)(2,1)S(1)} %get-tuple-element.88), channel_id=1, source_target_pairs={{1,0},{0,1},{3,2},{2,3},{5,4},{4,5},{7,6},{6,7},{9,8},{8,9},{11,10... | collective-permute-start | bytes 393224 | tf_op jit(solution)/shard_map/ppermute | solution.py:30

commit v12 on v11

--- a/solution.py
+++ b/solution.py
@@ -92,11 +92,15 @@
             place += size
 
 
-def slice_kernel(descriptors, out, sem):
+def slice_kernel(descriptors, out, sems):
     half = pl.multiple_of((lax.axis_index("sp") % 2) * 1024, 1024)
-    copy = pltpu.make_async_copy(descriptors.at[pl.ds(half, 1024), :], out, sem)
-    copy.start()
-    copy.wait()
+    copies = []
+    for i in range(4):
+        rows = descriptors.at[pl.ds(half + 256 * i, 256), :]
+        copies.append(pltpu.make_async_copy(rows, out.at[pl.ds(256 * i, 256), :], sems.at[i]))
+        copies[i].start()
+    for copy in copies:
+        copy.wait()
 
 
 def split_kernel(near, *outs):
@@ -212,8 +216,8 @@
         slice_kernel,
         out_shape=shape(1024, 512),
         in_specs=[pl.BlockSpec(memory_space=pl.ANY)],
-        out_specs=vmem_spec(),
-        scratch_shapes=(pltpu.SemaphoreType.DMA,),
+        out_specs=pl.BlockSpec(memory_space=pl.ANY),
+        scratch_shapes=(pltpu.SemaphoreType.DMA((4,)),),
         compiler_params=pltpu.CompilerParams(vmem_limit_bytes=61 * 1024 * 1024),
         cost_estimate=pl.CostEstimate(flops=0, bytes_accessed=1 << 21, transcendentals=0),
     )(descriptors)

time: 72.9 us -> 103 us (1.41)
  Pallas kernels: 17.6 us -> 48.1 us
    pallas_call x1, Pallas kernels: 2.38 us -> 32.9 us  [on_device(): pl.pallas_call(slice_kernel, out_shape=shape(1024, 512), in_specs=[pl.Blo...]
  transfers between devices with their start and end apart: 15 -> 15, of which waited for: 7 -> 7; matrix products, arithmetic and copies ran while one was open for 0% -> 0% of each run, Pallas kernels for 16% -> 11%
where the time goes in v12:
time: 103 us
  Pallas kernels  48.1 us (47%)
  starting transfers between devices  23.7 us (23%)
  blocking collectives  22.4 us (22%)
  waiting for transfers between devices  8.76 us (9%)
    pallas_call x1, Pallas kernels, on_device(): pl.pallas_call(slice_kernel, out_shape=shape(1024, 512), in_specs=[pl.Blo...  32.9 us
    ppermute x15, starting transfers between devices, fetch(): return lax.ppermute(value, ('env', 'sp'), pairs)  23.7 us
    all_to_all x1, blocking collectives, on_device(): pieces = lax.all_to_all(packed, 'env', 0, 0, tiled=True)  22.4 us
    pallas_call x4, Pallas kernels, take(): call(column_kernel, pair, 5, 2 * 1073741824, 1 << 23, (pltpu.VMEM((256, 4...  9.62 us
    ppermute x15, waiting for transfers between devices, fetch(): return lax.ppermute(value, ('env', 'sp'), pairs)  8.76 us
    pallas_call x2, Pallas kernels, rows(): call(body, (shape(envs, 512), shape(512, envs)) + sums, n_in, envs * 7864...  4.41 us
  transfers between devices with their start and end apart: 15, of which 7 were waited for; matrix products, arithmetic and copies ran while one was open for 0% of the time, Pallas kernels for 11%

profile of v12, /device:TPU:1, one launch (start us, length us, event | category | flops | bytes accessed | tf_op | source)
XLA Modules:
  0.0 103.1 jit_solution(8877132500655237222)
XLA Ops:
  0.0 0.0 copy-start
  0.0 0.0 copy-start.1
  0.0 32.9 %shard_map.29 = bf16[1024,512]{1,0:T(8,128)(2,1)} custom-call(bf16[2048,512]{1,0:T(8,128)(2,1)} %descriptors.1), custom_call_target="tpu_custom_call" | custom-call | bytes 2097152 | tf_op jit(solution)/shard_map/pallas_call | solution.py:215
  32.9 2.1 %collective-permute-start.4 = (bf16[1024,512]{1,0:T(8,128)(2,1)}, bf16[1024,512]{1,0:T(8,128)(2,1)S(1)}, u32[]{:S(2)}, u32[]{:S(2)}) collective-permute-start(bf16[1024,512]{1,0:T(8,128)(2,1)} %shard_map.29), channel_id=1, source_target_pairs={{32,0},{97,1},{34,2},{99,3},{36,4},{101,5},{38,6},{103,7},{40,8},{... | collective-permute-start | bytes 3145736 | tf_op jit(solution)/shard_map/ppermute | solution.py:30
  35.0 0.0 copy-done.1
  35.0 2.2 %collective-permute-start.1 = (bf16[256,512]{1,0:T(8,128)(2,1)S(1)}, bf16[256,512]{1,0:T(8,128)(2,1)S(1)}, u32[]{:S(2)}, u32[]{:S(2)}) collective-permute-start(bf16[256,512]{1,0:T(8,128)(2,1)S(1)} %copy-done.1), channel_id=1, source_target_pairs={{1,0},{0,1},{3,2},{2,3},{5,4},{4,5},{7,6},{6,7},{9,8},{8,9},{11,10... | collective-permute-start | bytes 786440 | tf_op jit(solution)/shard_map/ppermute | solution.py:30
  37.3 5.6 %collective-permute-start = (bf16[256,512]{1,0:T(8,128)(2,1)S(1)}, bf16[256,512]{1,0:T(8,128)(2,1)S(1)}, u32[]{:S(2)}, u32[]{:S(2)}) collective-permute-start(bf16[256,512]{1,0:T(8,128)(2,1)S(1)} %copy-done.1), channel_id=1, source_target_pairs={{4,0},{5,1},{6,2},{7,3},{8,4},{9,5},{10,6},{11,7},{12,8},{13,9},{1... | collective-permute-start | bytes 786440 | tf_op jit(solution)/shard_map/ppermute | solution.py:30
  42.8 0.0 collective-permute-done.1.sib_points
  42.8 0.0 copy-done
  42.8 2.2 %shard_map.28 = (bf16[2048,512]{1,0:T(8,128)(2,1)S(1)}, bf16[512,2048]{1,0:T(8,128)(2,1)S(1)}, f32[512,256]{1,0:T(8,128)S(1)}, bf16[512,512]{1,0:T(8,128)(2,1)S(1)}) custom-call(bf16[2048,512]{1,0:T(8,128)(2,1)S(1)} %copy-done, bf16[256,512]{1,0:T(8,128)(2,1)S(1)} %copy-done.1, bf16[256,512]{1,0:T(8,128)(2,1)S(1)} %collective-permute-done.1.sib_points), custom_call_target="tpu_custom_call" | custom-call | flops 1610612736 | bytes 8388608 | tf_op jit(solution)/shard_map/pallas_call | solution.py:208
  45.1 3.5 %collective-permute-done.points = bf16[256,512]{1,0:T(8,128)(2,1)S(1)} collective-permute-done((bf16[256,512]{1,0:T(8,128)(2,1)S(1)}, bf16[256,512]{1,0:T(8,128)(2,1)S(1)}, u32[]{:S(2)}, u32[]{:S(2)}) %collective-permute-start) | collective-permute-done | bytes 262176 | tf_op jit(solution)/shard_map/ppermute | solution.py:30
  48.6 3.4 %collective-permute-start.2 = (bf16[256,512]{1,0:T(8,128)(2,1)S(1)}, bf16[256,512]{1,0:T(8,128)(2,1)S(1)}, u32[]{:S(2)}, u32[]{:S(2)}) collective-permute-start(bf16[256,512]{1,0:T(8,128)(2,1)S(1)} %collective-permute-done.points), channel_id=1, source_target_pairs={{4,0},{5,1},{6,2},{7,3},{8,4},{9,5},{10,6},{11,7},{12,8},{13,9},{1... | collective-permute-start | bytes 786440 | tf_op jit(solution)/shard_map/ppermute | solution.py:30
  52.0 0.0 collective-permute-done.4.near
  52.0 0.1 shard_map.30
  52.1 1.2 %collective-permute-start.5 = (bf16[256,512]{1,0:T(8,128)(2,1)S(1)}, bf16[256,512]{1,0:T(8,128)(2,1)S(1)}, u32[]{:S(2)}, u32[]{:S(2)}) collective-permute-start(bf16[256,512]{1,0:T(8,128)(2,1)S(1)} %get-tuple-element.53.refs_0_), channel_id=1, source_target_pairs={{1,0},{0,1},{3,2},{2,3},{5,4},{4,5},{7,6},{6,7},{9,8},{8,9},{11,10... | collective-permute-start | bytes 786440 | tf_op jit(solution)/shard_map/ppermute | solution.py:30
  53.2 0.1 collective-permute-start.6
  53.3 0.4 collective-permute-start.7
  53.7 0.1 collective-permute-start.8
  53.8 3.0 %collective-permute-done.2.points = bf16[256,512]{1,0:T(8,128)(2,1)S(1)} collective-permute-done((bf16[256,512]{1,0:T(8,128)(2,1)S(1)}, bf16[256,512]{1,0:T(8,128)(2,1)S(1)}, u32[]{:S(2)}, u32[]{:S(2)}) %collective-permute-start.2) | collective-permute-done | bytes 262176 | tf_op jit(solution)/shard_map/ppermute | solution.py:30
  56.8 3.4 %collective-permute-start.3 = (bf16[256,512]{1,0:T(8,128)(2,1)S(1)}, bf16[256,512]{1,0:T(8,128)(2,1)S(1)}, u32[]{:S(2)}, u32[]{:S(2)}) collective-permute-start(bf16[256,512]{1,0:T(8,128)(2,1)S(1)} %collective-permute-done.2.points), channel_id=1, source_target_pairs={{4,0},{5,1},{6,2},{7,3},{8,4},{9,5},{10,6},{11,7},{12,8},{13,9},{1... | collective-permute-start | bytes 786440 | tf_op jit(solution)/shard_map/ppermute | solution.py:30
  60.2 0.0 collective-permute-done.5.refs_4_
  60.2 0.0 collective-permute-done.6.refs_5_
  60.2 0.0 collective-permute-done.7.refs_6_
  60.3 0.0 collective-permute-done.8.refs_7_
  60.3 2.2 %shard_map.31 = (bf16[2048,512]{1,0:T(8,128)(2,1)S(1)}, bf16[512,2048]{1,0:T(8,128)(2,1)S(1)}, bf16[256,256]{1,0:T(8,128)(2,1)S(1)}, bf16[256,256]{1,0:T(8,128)(2,1)S(1)}) custom-call(bf16[256,512]{1,0:T(8,128)(2,1)S(1)} %get-tuple-element.53.refs_0_, bf16[256,512]{1,0:T(8,128)(2,1)S(1)} %get-tuple-element.54.refs_1_, ...), custom_call_target="tpu_custom_call" | custom-call | flops 1610612736 | bytes 8388608 | tf_op jit(solution)/shard_map/pallas_call | solution.py:208
  62.4 2.4 %shard_map.33 = (bf16[256,256]{1,0:T(8,128)(2,1)S(1)}, bf16[256,256]{1,0:T(8,128)(2,1)S(1)}) custom-call(bf16[256,512]{1,0:T(8,128)(2,1)S(1)} %collective-permute-done.2.points, bf16[2048,512]{1,0:T(8,128)(2,1)S(1)} %get-tuple-element.61.refs_0_, bf16[2048,512]{1,0:T(8,128)(2,1)S(1)} %get-tuple-element.62.refs_1_, ...), custom_call_target="tpu_custom_call" | custom-call | flops 2147483648 | bytes 8388608 | tf_op jit(solution)/shard_map/pallas_call | solution.py:237
  64.9 2.4 %shard_map.32 = (bf16[256,256]{1,0:T(8,128)(2,1)S(1)}, bf16[256,256]{1,0:T(8,128)(2,1)S(1)}) custom-call(bf16[256,512]{1,0:T(8,128)(2,1)S(1)} %collective-permute-done.points, bf16[2048,512]{1,0:T(8,128)(2,1)S(1)} %get-tuple-element.61.refs_0_, bf16[2048,512]{1,0:T(8,128)(2,1)S(1)} %get-tuple-element.62.refs_1_, ...), custom_call_target="tpu_custom_call" | custom-call | flops 2147483648 | bytes 8388608 | tf_op jit(solution)/shard_map/pallas_call | solution.py:237
  67.3 0.0 collective-permute-done.3.points
  67.3 0.3 collective-permute-start.9
  67.6 2.4 %shard_map.34 = (bf16[256,256]{1,0:T(8,128)(2,1)S(1)}, bf16[256,256]{1,0:T(8,128)(2,1)S(1)}) custom-call(bf16[256,512]{1,0:T(8,128)(2,1)S(1)} %collective-permute-done.3.points, bf16[2048,512]{1,0:T(8,128)(2,1)S(1)} %get-tuple-element.61.refs_0_, bf16[2048,512]{1,0:T(8,128)(2,1)S(1)} %get-tuple-element.62.refs_1_, ...), custom_call_target="tpu_custom_call" | custom-call | flops 2147483648 | bytes 8388608 | tf_op jit(solution)/shard_map/pallas_call | solution.py:237
  70.0 3.0 %collective-permute-start.13 = (bf16[256,256]{1,0:T(8,128)(2,1)S(1)}, bf16[256,256]{1,0:T(8,128)(2,1)S(1)}, u32[]{:S(2)}, u32[]{:S(2)}) collective-permute-start(bf16[256,256]{1,0:T(8,128)(2,1)S(1)} %get-tuple-element.77), channel_id=1, source_target_pairs={{1,0},{0,1},{3,2},{2,3},{5,4},{4,5},{7,6},{6,7},{9,8},{8,9},{11,10... | collective-permute-start | bytes 393224 | tf_op jit(solution)/shard_map/ppermute | solution.py:30
  72.9 0.1 collective-permute-start.10
  73.0 0.4 collective-permute-start.11
  73.5 0.1 collective-permute-start.12
  73.6 0.4 collective-permute-done.13.refs_8_
  73.9 0.4 collective-permute-done.10.refs_5_
  74.3 0.2 collective-permute-done.11.refs_6_
  74.5 0.3 collective-permute-done.12.refs_7_
  74.8 0.0 collective-permute-done.9.points
  74.8 2.4 %shard_map.35 = (bf16[256,256]{1,0:T(8,128)(2,1)S(1)}, bf16[256,256]{1,0:T(8,128)(2,1)S(1)}) custom-call(bf16[256,512]{1,0:T(8,128)(2,1)S(1)} %collective-permute-done.9.points, bf16[2048,512]{1,0:T(8,128)(2,1)S(1)} %get-tuple-element.61.refs_0_, bf16[2048,512]{1,0:T(8,128)(2,1)S(1)} %get-tuple-element.62.refs_1_, ...), custom_call_target="tpu_custom_call" | custom-call | flops 2147483648 | bytes 8388608 | tf_op jit(solution)/shard_map/pallas_call | solution.py:237
  77.2 1.4 %collective-permute-start.14 = (bf16[256,256]{1,0:T(8,128)(2,1)S(1)}, bf16[256,256]{1,0:T(8,128)(2,1)S(1)}, u32[]{:S(2)}, u32[]{:S(2)}) collective-permute-start(bf16[256,256]{1,0:T(8,128)(2,1)S(1)} %get-tuple-element.88), channel_id=1, source_target_pairs={{1,0},{0,1},{3,2},{2,3},{5,4},{4,5},{7,6},{6,7},{9,8},{8,9},{11,10... | collective-permute-start | bytes 393224 | tf_op jit(solution)/shard_map/ppermute | solution.py:30
  78.6 1.0 collective-permute-done.14.refs_9_
  79.6 0.1 shard_map.36
  79.7 22.4 %all_to_all.5.pieces = bf16[8,9,32,256]{3,2,1,0:T(8,128)(2,1)S(1)} all-to-all(bf16[8,9,32,256]{3,2,1,0:T(8,128)(2,1)S(1)} %shard_map.36), channel_id=1, replica_groups=mesh['env'=8,'sp'=32] {'env'}, dimensions={0} | all-to-all | bytes 2359296 | tf_op jit(solution)/shard_map/all_to_all | solution.py:253
  102.1 1.0 shard_map.37
Async XLA Ops:
  0.0 42.8 %copy-start = (bf16[2048,512]{1,0:T(8,128)(2,1)S(1)}, bf16[2048,512]{1,0:T(8,128)(2,1)}, u32[]{:S(2)}) copy-start(bf16[2048,512]{1,0:T(8,128)(2,1)} %descriptors.1) | copy-start | bytes 6291460
  0.0 35.0 %copy-start.1 = (bf16[256,512]{1,0:T(8,128)(2,1)S(1)}, bf16[256,512]{1,0:T(8,128)(2,1)}, u32[]{:S(2)}) copy-start(bf16[256,512]{1,0:T(8,128)(2,1)} %own_points.1) | copy-start | bytes 786436
  32.9 19.1 %collective-permute-start.4 = (bf16[1024,512]{1,0:T(8,128)(2,1)}, bf16[1024,512]{1,0:T(8,128)(2,1)S(1)}, u32[]{:S(2)}, u32[]{:S(2)}) collective-permute-start(bf16[1024,512]{1,0:T(8,128)(2,1)} %shard_map.29), channel_id=1, source_target_pairs={{32,0},{97,1},{34,2},{99,3},{36,4},{101,5},{38,6},{103,7},{40,8},{... | collective-permute-start | bytes 3145736 | tf_op jit(solution)/shard_map/ppermute | solution.py:30
  35.0 7.8 %collective-permute-start.1 = (bf16[256,512]{1,0:T(8,128)(2,1)S(1)}, bf16[256,512]{1,0:T(8,128)(2,1)S(1)}, u32[]{:S(2)}, u32[]{:S(2)}) collective-permute-start(bf16[256,512]{1,0:T(8,128)(2,1)S(1)} %copy-done.1), channel_id=1, source_target_pairs={{1,0},{0,1},{3,2},{2,3},{5,4},{4,5},{7,6},{6,7},{9,8},{8,9},{11,10... | collective-permute-start | bytes 786440 | tf_op jit(solution)/shard_map/ppermute | solution.py:30
  37.3 11.3 %collective-permute-start = (bf16[256,512]{1,0:T(8,128)(2,1)S(1)}, bf16[256,512]{1,0:T(8,128)(2,1)S(1)}, u32[]{:S(2)}, u32[]{:S(2)}) collective-permute-start(bf16[256,512]{1,0:T(8,128)(2,1)S(1)} %copy-done.1), channel_id=1, source_target_pairs={{4,0},{5,1},{6,2},{7,3},{8,4},{9,5},{10,6},{11,7},{12,8},{13,9},{1... | collective-permute-start | bytes 786440 | tf_op jit(solution)/shard_map/ppermute | solution.py:30
  48.6 8.3 %collective-permute-start.2 = (bf16[256,512]{1,0:T(8,128)(2,1)S(1)}, bf16[256,512]{1,0:T(8,128)(2,1)S(1)}, u32[]{:S(2)}, u32[]{:S(2)}) collective-permute-start(bf16[256,512]{1,0:T(8,128)(2,1)S(1)} %collective-permute-done.points), channel_id=1, source_target_pairs={{4,0},{5,1},{6,2},{7,3},{8,4},{9,5},{10,6},{11,7},{12,8},{13,9},{1... | collective-permute-start | bytes 786440 | tf_op jit(solution)/shard_map/ppermute | solution.py:30
  52.1 8.2 %collective-permute-start.5 = (bf16[256,512]{1,0:T(8,128)(2,1)S(1)}, bf16[256,512]{1,0:T(8,128)(2,1)S(1)}, u32[]{:S(2)}, u32[]{:S(2)}) collective-permute-start(bf16[256,512]{1,0:T(8,128)(2,1)S(1)} %get-tuple-element.53.refs_0_), channel_id=1, source_target_pairs={{1,0},{0,1},{3,2},{2,3},{5,4},{4,5},{7,6},{6,7},{9,8},{8,9},{11,10... | collective-permute-start | bytes 786440 | tf_op jit(solution)/shard_map/ppermute | solution.py:30
  53.2 7.0 %collective-permute-start.6 = (bf16[256,512]{1,0:T(8,128)(2,1)S(1)}, bf16[256,512]{1,0:T(8,128)(2,1)S(1)}, u32[]{:S(2)}, u32[]{:S(2)}) collective-permute-start(bf16[256,512]{1,0:T(8,128)(2,1)S(1)} %get-tuple-element.54.refs_1_), channel_id=1, source_target_pairs={{1,0},{0,1},{3,2},{2,3},{5,4},{4,5},{7,6},{6,7},{9,8},{8,9},{11,10... | collective-permute-start | bytes 786440 | tf_op jit(solution)/shard_map/ppermute | solution.py:30
  53.3 6.9 %collective-permute-start.7 = (bf16[256,512]{1,0:T(8,128)(2,1)S(1)}, bf16[256,512]{1,0:T(8,128)(2,1)S(1)}, u32[]{:S(2)}, u32[]{:S(2)}) collective-permute-start(bf16[256,512]{1,0:T(8,128)(2,1)S(1)} %get-tuple-element.55.refs_2_), channel_id=1, source_target_pairs={{1,0},{0,1},{3,2},{2,3},{5,4},{4,5},{7,6},{6,7},{9,8},{8,9},{11,10... | collective-permute-start | bytes 786440 | tf_op jit(solution)/shard_map/ppermute | solution.py:30
  53.7 6.5 %collective-permute-start.8 = (bf16[256,512]{1,0:T(8,128)(2,1)S(1)}, bf16[256,512]{1,0:T(8,128)(2,1)S(1)}, u32[]{:S(2)}, u32[]{:S(2)}) collective-permute-start(bf16[256,512]{1,0:T(8,128)(2,1)S(1)} %get-tuple-element.56.refs_3_), channel_id=1, source_target_pairs={{1,0},{0,1},{3,2},{2,3},{5,4},{4,5},{7,6},{6,7},{9,8},{8,9},{11,10... | collective-permute-start | bytes 786440 | tf_op jit(solution)/shard_map/ppermute | solution.py:30
  56.8 10.5 %collective-permute-start.3 = (bf16[256,512]{1,0:T(8,128)(2,1)S(1)}, bf16[256,512]{1,0:T(8,128)(2,1)S(1)}, u32[]{:S(2)}, u32[]{:S(2)}) collective-permute-start(bf16[256,512]{1,0:T(8,128)(2,1)S(1)} %collective-permute-done.2.points), channel_id=1, source_target_pairs={{4,0},{5,1},{6,2},{7,3},{8,4},{9,5},{10,6},{11,7},{12,8},{13,9},{1... | collective-permute-start | bytes 786440 | tf_op jit(solution)/shard_map/ppermute | solution.py:30
  67.3 7.5 %collective-permute-start.9 = (bf16[256,512]{1,0:T(8,128)(2,1)S(1)}, bf16[256,512]{1,0:T(8,128)(2,1)S(1)}, u32[]{:S(2)}, u32[]{:S(2)}) collective-permute-start(bf16[256,512]{1,0:T(8,128)(2,1)S(1)} %collective-permute-done.3.points), channel_id=1, source_target_pairs={{4,0},{5,1},{6,2},{7,3},{8,4},{9,5},{10,6},{11,7},{12,8},{13,9},{1... | collective-permute-start | bytes 786440 | tf_op jit(solution)/shard_map/ppermute | solution.py:30
  70.0 3.9 %collective-permute-start.13 = (bf16[256,256]{1,0:T(8,128)(2,1)S(1)}, bf16[256,256]{1,0:T(8,128)(2,1)S(1)}, u32[]{:S(2)}, u32[]{:S(2)}) collective-permute-start(bf16[256,256]{1,0:T(8,128)(2,1)S(1)} %get-tuple-element.77), channel_id=1, source_target_pairs={{1,0},{0,1},{3,2},{2,3},{5,4},{4,5},{7,6},{6,7},{9,8},{8,9},{11,10... | collective-permute-start | bytes 393224 | tf_op jit(solution)/shard_map/ppermute | solution.py:30
  72.9 1.3 %collective-permute-start.10 = (bf16[256,256]{1,0:T(8,128)(2,1)S(1)}, bf16[256,256]{1,0:T(8,128)(2,1)S(1)}, u32[]{:S(2)}, u32[]{:S(2)}) collective-permute-start(bf16[256,256]{1,0:T(8,128)(2,1)S(1)} %get-tuple-element.74), channel_id=1, source_target_pairs={{1,0},{0,1},{3,2},{2,3},{5,4},{4,5},{7,6},{6,7},{9,8},{8,9},{11,10... | collective-permute-start | bytes 393224 | tf_op jit(solution)/shard_map/ppermute | solution.py:30
  73.0 1.4 %collective-permute-start.11 = (bf16[256,256]{1,0:T(8,128)(2,1)S(1)}, bf16[256,256]{1,0:T(8,128)(2,1)S(1)}, u32[]{:S(2)}, u32[]{:S(2)}) collective-permute-start(bf16[256,256]{1,0:T(8,128)(2,1)S(1)} %get-tuple-element.75), channel_id=1, source_target_pairs={{1,0},{0,1},{3,2},{2,3},{5,4},{4,5},{7,6},{6,7},{9,8},{8,9},{11,10... | collective-permute-start | bytes 393224 | tf_op jit(solution)/shard_map/ppermute | solution.py:30
  73.5 1.3 %collective-permute-start.12 = (bf16[256,256]{1,0:T(8,128)(2,1)S(1)}, bf16[256,256]{1,0:T(8,128)(2,1)S(1)}, u32[]{:S(2)}, u32[]{:S(2)}) collective-permute-start(bf16[256,256]{1,0:T(8,128)(2,1)S(1)} %get-tuple-element.76), channel_id=1, source_target_pairs={{1,0},{0,1},{3,2},{2,3},{5,4},{4,5},{7,6},{6,7},{9,8},{8,9},{11,10... | collective-permute-start | bytes 393224 | tf_op jit(solution)/shard_map/ppermute | solution.py:30
  77.2 2.3 %collective-permute-start.14 = (bf16[256,256]{1,0:T(8,128)(2,1)S(1)}, bf16[256,256]{1,0:T(8,128)(2,1)S(1)}, u32[]{:S(2)}, u32[]{:S(2)}) collective-permute-start(bf16[256,256]{1,0:T(8,128)(2,1)S(1)} %get-tuple-element.88), channel_id=1, source_target_pairs={{1,0},{0,1},{3,2},{2,3},{5,4},{4,5},{7,6},{6,7},{9,8},{8,9},{11,10... | collective-permute-start | bytes 393224 | tf_op jit(solution)/shard_map/ppermute | solution.py:30

commit v13 on v12

--- a/solution.py
+++ b/solution.py
@@ -92,14 +92,19 @@
             place += size
 
 
-def slice_kernel(descriptors, out, sems):
+def slice_kernel(descriptors, out, held, arrived, left):
     half = pl.multiple_of((lax.axis_index("sp") % 2) * 1024, 1024)
-    copies = []
+    inward, outward = [], []
     for i in range(4):
-        rows = descriptors.at[pl.ds(half + 256 * i, 256), :]
-        copies.append(pltpu.make_async_copy(rows, out.at[pl.ds(256 * i, 256), :], sems.at[i]))
-        copies[i].start()
-    for copy in copies:
+        part = pl.ds(256 * i, 256)
+        source = descriptors.at[pl.ds(half + 256 * i, 256), :]
+        inward.append(pltpu.make_async_copy(source, held.at[part, :], arrived.at[i]))
+        outward.append(pltpu.make_async_copy(held.at[part, :], out.at[part, :], left.at[i]))
+        inward[i].start()
+    for i in range(4):
+        inward[i].wait()
+        outward[i].start()
+    for copy in outward:
         copy.wait()
 
 
@@ -217,7 +222,11 @@
         out_shape=shape(1024, 512),
         in_specs=[pl.BlockSpec(memory_space=pl.ANY)],
         out_specs=pl.BlockSpec(memory_space=pl.ANY),
-        scratch_shapes=(pltpu.SemaphoreType.DMA((4,)),),
+        scratch_shapes=(
+            pltpu.VMEM((1024, 512), BF16),
+            pltpu.SemaphoreType.DMA((4,)),
+            pltpu.SemaphoreType.DMA((4,)),
+        ),
         compiler_params=pltpu.CompilerParams(vmem_limit_bytes=61 * 1024 * 1024),
         cost_estimate=pl.CostEstimate(flops=0, bytes_accessed=1 << 21, transcendentals=0),
     )(descriptors)

time: 103 us -> 72.7 us (0.71)
  Pallas kernels: 48.1 us -> 17.4 us
    pallas_call x1, Pallas kernels: 32.9 us -> 2.17 us  [on_device(): pl.pallas_call(slice_kernel, out_shape=shape(1024, 512), in_specs=[pl.Blo...]
  transfers between devices with their start and end apart: 15 -> 15, of which waited for: 7 -> 7; matrix products, arithmetic and copies ran while one was open for 0% -> 0% of each run, Pallas kernels for 11% -> 16%
where the time goes in v13:
time: 72.7 us; the launch traced here: 72.3 us
  starting transfers between devices  23.7 us (33%)
  blocking collectives  22.4 us (31%)
  Pallas kernels  17.4 us (24%)
  waiting for transfers between devices  8.76 us (12%)
    ppermute x15, starting transfers between devices, fetch(): return lax.ppermute(value, ('env', 'sp'), pairs)  23.7 us
    all_to_all x1, blocking collectives, on_device(): pieces = lax.all_to_all(packed, 'env', 0, 0, tiled=True)  22.4 us
    pallas_call x4, Pallas kernels, take(): call(column_kernel, pair, 5, 2 * 1073741824, 1 << 23, (pltpu.VMEM((256, 4...  9.62 us
    ppermute x15, waiting for transfers between devices, fetch(): return lax.ppermute(value, ('env', 'sp'), pairs)  8.76 us
    pallas_call x2, Pallas kernels, rows(): call(body, (shape(envs, 512), shape(512, envs)) + sums, n_in, envs * 7864...  4.41 us
    pallas_call x1, Pallas kernels, on_device(): pl.pallas_call(slice_kernel, out_shape=shape(1024, 512), in_specs=[pl.Blo...  2.17 us
  transfers between devices with their start and end apart: 15, of which 7 were waited for; matrix products, arithmetic and copies ran while one was open for 0% of the time, Pallas kernels for 16%

profile of v13, /device:TPU:1, one launch (start us, length us, event | category | flops | bytes accessed | tf_op | source)
XLA Modules:
  0.0 72.3 jit_solution(11156180698091896986)
XLA Ops:
  0.0 0.0 copy-start
  0.0 0.0 copy-start.1
  0.0 2.2 %shard_map.29 = bf16[1024,512]{1,0:T(8,128)(2,1)} custom-call(bf16[2048,512]{1,0:T(8,128)(2,1)} %descriptors.1), custom_call_target="tpu_custom_call" | custom-call | bytes 2097152 | tf_op jit(solution)/shard_map/pallas_call | solution.py:220
  2.2 2.1 %collective-permute-start.4 = (bf16[1024,512]{1,0:T(8,128)(2,1)}, bf16[1024,512]{1,0:T(8,128)(2,1)S(1)}, u32[]{:S(2)}, u32[]{:S(2)}) collective-permute-start(bf16[1024,512]{1,0:T(8,128)(2,1)} %shard_map.29), channel_id=1, source_target_pairs={{32,0},{97,1},{34,2},{99,3},{36,4},{101,5},{38,6},{103,7},{40,8},{... | collective-permute-start | bytes 3145736 | tf_op jit(solution)/shard_map/ppermute | solution.py:30
  4.3 0.0 copy-done.1
  4.3 2.2 %collective-permute-start.1 = (bf16[256,512]{1,0:T(8,128)(2,1)S(1)}, bf16[256,512]{1,0:T(8,128)(2,1)S(1)}, u32[]{:S(2)}, u32[]{:S(2)}) collective-permute-start(bf16[256,512]{1,0:T(8,128)(2,1)S(1)} %copy-done.1), channel_id=1, source_target_pairs={{1,0},{0,1},{3,2},{2,3},{5,4},{4,5},{7,6},{6,7},{9,8},{8,9},{11,10... | collective-permute-start | bytes 786440 | tf_op jit(solution)/shard_map/ppermute | solution.py:30
  6.5 5.6 %collective-permute-start = (bf16[256,512]{1,0:T(8,128)(2,1)S(1)}, bf16[256,512]{1,0:T(8,128)(2,1)S(1)}, u32[]{:S(2)}, u32[]{:S(2)}) collective-permute-start(bf16[256,512]{1,0:T(8,128)(2,1)S(1)} %copy-done.1), channel_id=1, source_target_pairs={{4,0},{5,1},{6,2},{7,3},{8,4},{9,5},{10,6},{11,7},{12,8},{13,9},{1... | collective-permute-start | bytes 786440 | tf_op jit(solution)/shard_map/ppermute | solution.py:30
  12.1 0.0 collective-permute-done.1.sib_points
  12.1 0.0 copy-done
  12.1 2.2 %shard_map.28 = (bf16[2048,512]{1,0:T(8,128)(2,1)S(1)}, bf16[512,2048]{1,0:T(8,128)(2,1)S(1)}, f32[512,256]{1,0:T(8,128)S(1)}, bf16[512,512]{1,0:T(8,128)(2,1)S(1)}) custom-call(bf16[2048,512]{1,0:T(8,128)(2,1)S(1)} %copy-done, bf16[256,512]{1,0:T(8,128)(2,1)S(1)} %copy-done.1, bf16[256,512]{1,0:T(8,128)(2,1)S(1)} %collective-permute-done.1.sib_points), custom_call_target="tpu_custom_call" | custom-call | flops 1610612736 | bytes 8388608 | tf_op jit(solution)/shard_map/pallas_call | solution.py:213
  14.3 3.5 %collective-permute-done.points = bf16[256,512]{1,0:T(8,128)(2,1)S(1)} collective-permute-done((bf16[256,512]{1,0:T(8,128)(2,1)S(1)}, bf16[256,512]{1,0:T(8,128)(2,1)S(1)}, u32[]{:S(2)}, u32[]{:S(2)}) %collective-permute-start) | collective-permute-done | bytes 262176 | tf_op jit(solution)/shard_map/ppermute | solution.py:30
  17.8 3.4 %collective-permute-start.2 = (bf16[256,512]{1,0:T(8,128)(2,1)S(1)}, bf16[256,512]{1,0:T(8,128)(2,1)S(1)}, u32[]{:S(2)}, u32[]{:S(2)}) collective-permute-start(bf16[256,512]{1,0:T(8,128)(2,1)S(1)} %collective-permute-done.points), channel_id=1, source_target_pairs={{4,0},{5,1},{6,2},{7,3},{8,4},{9,5},{10,6},{11,7},{12,8},{13,9},{1... | collective-permute-start | bytes 786440 | tf_op jit(solution)/shard_map/ppermute | solution.py:30
  21.3 0.0 collective-permute-done.4.near
  21.3 0.1 shard_map.30
  21.3 1.2 %collective-permute-start.5 = (bf16[256,512]{1,0:T(8,128)(2,1)S(1)}, bf16[256,512]{1,0:T(8,128)(2,1)S(1)}, u32[]{:S(2)}, u32[]{:S(2)}) collective-permute-start(bf16[256,512]{1,0:T(8,128)(2,1)S(1)} %get-tuple-element.53.refs_0_), channel_id=1, source_target_pairs={{1,0},{0,1},{3,2},{2,3},{5,4},{4,5},{7,6},{6,7},{9,8},{8,9},{11,10... | collective-permute-start | bytes 786440 | tf_op jit(solution)/shard_map/ppermute | solution.py:30
  22.5 0.1 collective-permute-start.6
  22.6 0.4 collective-permute-start.7
  23.0 0.1 collective-permute-start.8
  23.1 3.0 %collective-permute-done.2.points = bf16[256,512]{1,0:T(8,128)(2,1)S(1)} collective-permute-done((bf16[256,512]{1,0:T(8,128)(2,1)S(1)}, bf16[256,512]{1,0:T(8,128)(2,1)S(1)}, u32[]{:S(2)}, u32[]{:S(2)}) %collective-permute-start.2) | collective-permute-done | bytes 262176 | tf_op jit(solution)/shard_map/ppermute | solution.py:30
  26.1 3.4 %collective-permute-start.3 = (bf16[256,512]{1,0:T(8,128)(2,1)S(1)}, bf16[256,512]{1,0:T(8,128)(2,1)S(1)}, u32[]{:S(2)}, u32[]{:S(2)}) collective-permute-start(bf16[256,512]{1,0:T(8,128)(2,1)S(1)} %collective-permute-done.2.points), channel_id=1, source_target_pairs={{4,0},{5,1},{6,2},{7,3},{8,4},{9,5},{10,6},{11,7},{12,8},{13,9},{1... | collective-permute-start | bytes 786440 | tf_op jit(solution)/shard_map/ppermute | solution.py:30
  29.5 0.0 collective-permute-done.5.refs_4_
  29.5 0.0 collective-permute-done.6.refs_5_
  29.5 0.0 collective-permute-done.7.refs_6_
  29.5 0.0 collective-permute-done.8.refs_7_
  29.5 2.2 %shard_map.31 = (bf16[2048,512]{1,0:T(8,128)(2,1)S(1)}, bf16[512,2048]{1,0:T(8,128)(2,1)S(1)}, bf16[256,256]{1,0:T(8,128)(2,1)S(1)}, bf16[256,256]{1,0:T(8,128)(2,1)S(1)}) custom-call(bf16[256,512]{1,0:T(8,128)(2,1)S(1)} %get-tuple-element.53.refs_0_, bf16[256,512]{1,0:T(8,128)(2,1)S(1)} %get-tuple-element.54.refs_1_, ...), custom_call_target="tpu_custom_call" | custom-call | flops 1610612736 | bytes 8388608 | tf_op jit(solution)/shard_map/pallas_call | solution.py:213
  31.7 2.4 %shard_map.33 = (bf16[256,256]{1,0:T(8,128)(2,1)S(1)}, bf16[256,256]{1,0:T(8,128)(2,1)S(1)}) custom-call(bf16[256,512]{1,0:T(8,128)(2,1)S(1)} %collective-permute-done.2.points, bf16[2048,512]{1,0:T(8,128)(2,1)S(1)} %get-tuple-element.61.refs_0_, bf16[2048,512]{1,0:T(8,128)(2,1)S(1)} %get-tuple-element.62.refs_1_, ...), custom_call_target="tpu_custom_call" | custom-call | flops 2147483648 | bytes 8388608 | tf_op jit(solution)/shard_map/pallas_call | solution.py:246
  34.1 2.4 %shard_map.32 = (bf16[256,256]{1,0:T(8,128)(2,1)S(1)}, bf16[256,256]{1,0:T(8,128)(2,1)S(1)}) custom-call(bf16[256,512]{1,0:T(8,128)(2,1)S(1)} %collective-permute-done.points, bf16[2048,512]{1,0:T(8,128)(2,1)S(1)} %get-tuple-element.61.refs_0_, bf16[2048,512]{1,0:T(8,128)(2,1)S(1)} %get-tuple-element.62.refs_1_, ...), custom_call_target="tpu_custom_call" | custom-call | flops 2147483648 | bytes 8388608 | tf_op jit(solution)/shard_map/pallas_call | solution.py:246
  36.5 0.0 collective-permute-done.3.points
  36.6 0.3 collective-permute-start.9
  36.8 2.4 %shard_map.34 = (bf16[256,256]{1,0:T(8,128)(2,1)S(1)}, bf16[256,256]{1,0:T(8,128)(2,1)S(1)}) custom-call(bf16[256,512]{1,0:T(8,128)(2,1)S(1)} %collective-permute-done.3.points, bf16[2048,512]{1,0:T(8,128)(2,1)S(1)} %get-tuple-element.61.refs_0_, bf16[2048,512]{1,0:T(8,128)(2,1)S(1)} %get-tuple-element.62.refs_1_, ...), custom_call_target="tpu_custom_call" | custom-call | flops 2147483648 | bytes 8388608 | tf_op jit(solution)/shard_map/pallas_call | solution.py:246
  39.3 3.0 %collective-permute-start.13 = (bf16[256,256]{1,0:T(8,128)(2,1)S(1)}, bf16[256,256]{1,0:T(8,128)(2,1)S(1)}, u32[]{:S(2)}, u32[]{:S(2)}) collective-permute-start(bf16[256,256]{1,0:T(8,128)(2,1)S(1)} %get-tuple-element.77), channel_id=1, source_target_pairs={{1,0},{0,1},{3,2},{2,3},{5,4},{4,5},{7,6},{6,7},{9,8},{8,9},{11,10... | collective-permute-start | bytes 393224 | tf_op jit(solution)/shard_map/ppermute | solution.py:30
  42.2 0.1 collective-permute-start.10
  42.3 0.4 collective-permute-start.11
  42.7 0.1 collective-permute-start.12
  42.8 0.4 collective-permute-done.13.refs_8_
  43.2 0.4 collective-permute-done.10.refs_5_
  43.6 0.2 collective-permute-done.11.refs_6_
  43.8 0.3 collective-permute-done.12.refs_7_
  44.1 0.0 collective-permute-done.9.points
  44.1 2.4 %shard_map.35 = (bf16[256,256]{1,0:T(8,128)(2,1)S(1)}, bf16[256,256]{1,0:T(8,128)(2,1)S(1)}) custom-call(bf16[256,512]{1,0:T(8,128)(2,1)S(1)} %collective-permute-done.9.points, bf16[2048,512]{1,0:T(8,128)(2,1)S(1)} %get-tuple-element.61.refs_0_, bf16[2048,512]{1,0:T(8,128)(2,1)S(1)} %get-tuple-element.62.refs_1_, ...), custom_call_target="tpu_custom_call" | custom-call | flops 2147483648 | bytes 8388608 | tf_op jit(solution)/shard_map/pallas_call | solution.py:246
  46.5 1.4 %collective-permute-start.14 = (bf16[256,256]{1,0:T(8,128)(2,1)S(1)}, bf16[256,256]{1,0:T(8,128)(2,1)S(1)}, u32[]{:S(2)}, u32[]{:S(2)}) collective-permute-start(bf16[256,256]{1,0:T(8,128)(2,1)S(1)} %get-tuple-element.88), channel_id=1, source_target_pairs={{1,0},{0,1},{3,2},{2,3},{5,4},{4,5},{7,6},{6,7},{9,8},{8,9},{11,10... | collective-permute-start | bytes 393224 | tf_op jit(solution)/shard_map/ppermute | solution.py:30
  47.9 1.0 %collective-permute-done.14.refs_9_ = bf16[256,256]{1,0:T(8,128)(2,1)S(1)} collective-permute-done((bf16[256,256]{1,0:T(8,128)(2,1)S(1)}, bf16[256,256]{1,0:T(8,128)(2,1)S(1)}, u32[]{:S(2)}, u32[]{:S(2)}) %collective-permute-start.14) | collective-permute-done | bytes 131104 | tf_op jit(solution)/shard_map/ppermute | solution.py:30
  48.8 0.1 shard_map.36
  48.9 22.4 %all_to_all.5.pieces = bf16[8,9,32,256]{3,2,1,0:T(8,128)(2,1)S(1)} all-to-all(bf16[8,9,32,256]{3,2,1,0:T(8,128)(2,1)S(1)} %shard_map.36), channel_id=1, replica_groups=mesh['env'=8,'sp'=32] {'env'}, dimensions={0} | all-to-all | bytes 2359296 | tf_op jit(solution)/shard_map/all_to_all | solution.py:262
  71.3 1.0 %shard_map.37 = f32[17,32,256]{2,1,0:T(8,128)} custom-call(bf16[8,9,32,256]{3,2,1,0:T(8,128)(2,1)S(1)} %all_to_all.5.pieces), custom_call_target="tpu_custom_call" | custom-call | bytes 2097152 | tf_op jit(solution)/shard_map/pallas_call | solution.py:263
Async XLA Ops:
  0.0 12.1 %copy-start = (bf16[2048,512]{1,0:T(8,128)(2,1)S(1)}, bf16[2048,512]{1,0:T(8,128)(2,1)}, u32[]{:S(2)}) copy-start(bf16[2048,512]{1,0:T(8,128)(2,1)} %descriptors.1) | copy-start | bytes 6291460
  0.0 4.3 %copy-start.1 = (bf16[256,512]{1,0:T(8,128)(2,1)S(1)}, bf16[256,512]{1,0:T(8,128)(2,1)}, u32[]{:S(2)}) copy-start(bf16[256,512]{1,0:T(8,128)(2,1)} %own_points.1) | copy-start | bytes 786436
  2.2 19.1 %collective-permute-start.4 = (bf16[1024,512]{1,0:T(8,128)(2,1)}, bf16[1024,512]{1,0:T(8,128)(2,1)S(1)}, u32[]{:S(2)}, u32[]{:S(2)}) collective-permute-start(bf16[1024,512]{1,0:T(8,128)(2,1)} %shard_map.29), channel_id=1, source_target_pairs={{32,0},{97,1},{34,2},{99,3},{36,4},{101,5},{38,6},{103,7},{40,8},{... | collective-permute-start | bytes 3145736 | tf_op jit(solution)/shard_map/ppermute | solution.py:30
  4.3 7.8 %collective-permute-start.1 = (bf16[256,512]{1,0:T(8,128)(2,1)S(1)}, bf16[256,512]{1,0:T(8,128)(2,1)S(1)}, u32[]{:S(2)}, u32[]{:S(2)}) collective-permute-start(bf16[256,512]{1,0:T(8,128)(2,1)S(1)} %copy-done.1), channel_id=1, source_target_pairs={{1,0},{0,1},{3,2},{2,3},{5,4},{4,5},{7,6},{6,7},{9,8},{8,9},{11,10... | collective-permute-start | bytes 786440 | tf_op jit(solution)/shard_map/ppermute | solution.py:30
  6.5 11.3 %collective-permute-start = (bf16[256,512]{1,0:T(8,128)(2,1)S(1)}, bf16[256,512]{1,0:T(8,128)(2,1)S(1)}, u32[]{:S(2)}, u32[]{:S(2)}) collective-permute-start(bf16[256,512]{1,0:T(8,128)(2,1)S(1)} %copy-done.1), channel_id=1, source_target_pairs={{4,0},{5,1},{6,2},{7,3},{8,4},{9,5},{10,6},{11,7},{12,8},{13,9},{1... | collective-permute-start | bytes 786440 | tf_op jit(solution)/shard_map/ppermute | solution.py:30
  17.8 8.3 %collective-permute-start.2 = (bf16[256,512]{1,0:T(8,128)(2,1)S(1)}, bf16[256,512]{1,0:T(8,128)(2,1)S(1)}, u32[]{:S(2)}, u32[]{:S(2)}) collective-permute-start(bf16[256,512]{1,0:T(8,128)(2,1)S(1)} %collective-permute-done.points), channel_id=1, source_target_pairs={{4,0},{5,1},{6,2},{7,3},{8,4},{9,5},{10,6},{11,7},{12,8},{13,9},{1... | collective-permute-start | bytes 786440 | tf_op jit(solution)/shard_map/ppermute | solution.py:30
  21.3 8.2 %collective-permute-start.5 = (bf16[256,512]{1,0:T(8,128)(2,1)S(1)}, bf16[256,512]{1,0:T(8,128)(2,1)S(1)}, u32[]{:S(2)}, u32[]{:S(2)}) collective-permute-start(bf16[256,512]{1,0:T(8,128)(2,1)S(1)} %get-tuple-element.53.refs_0_), channel_id=1, source_target_pairs={{1,0},{0,1},{3,2},{2,3},{5,4},{4,5},{7,6},{6,7},{9,8},{8,9},{11,10... | collective-permute-start | bytes 786440 | tf_op jit(solution)/shard_map/ppermute | solution.py:30
  22.5 7.0 %collective-permute-start.6 = (bf16[256,512]{1,0:T(8,128)(2,1)S(1)}, bf16[256,512]{1,0:T(8,128)(2,1)S(1)}, u32[]{:S(2)}, u32[]{:S(2)}) collective-permute-start(bf16[256,512]{1,0:T(8,128)(2,1)S(1)} %get-tuple-element.54.refs_1_), channel_id=1, source_target_pairs={{1,0},{0,1},{3,2},{2,3},{5,4},{4,5},{7,6},{6,7},{9,8},{8,9},{11,10... | collective-permute-start | bytes 786440 | tf_op jit(solution)/shard_map/ppermute | solution.py:30
  22.6 6.9 %collective-permute-start.7 = (bf16[256,512]{1,0:T(8,128)(2,1)S(1)}, bf16[256,512]{1,0:T(8,128)(2,1)S(1)}, u32[]{:S(2)}, u32[]{:S(2)}) collective-permute-start(bf16[256,512]{1,0:T(8,128)(2,1)S(1)} %get-tuple-element.55.refs_2_), channel_id=1, source_target_pairs={{1,0},{0,1},{3,2},{2,3},{5,4},{4,5},{7,6},{6,7},{9,8},{8,9},{11,10... | collective-permute-start | bytes 786440 | tf_op jit(solution)/shard_map/ppermute | solution.py:30
  23.0 6.5 %collective-permute-start.8 = (bf16[256,512]{1,0:T(8,128)(2,1)S(1)}, bf16[256,512]{1,0:T(8,128)(2,1)S(1)}, u32[]{:S(2)}, u32[]{:S(2)}) collective-permute-start(bf16[256,512]{1,0:T(8,128)(2,1)S(1)} %get-tuple-element.56.refs_3_), channel_id=1, source_target_pairs={{1,0},{0,1},{3,2},{2,3},{5,4},{4,5},{7,6},{6,7},{9,8},{8,9},{11,10... | collective-permute-start | bytes 786440 | tf_op jit(solution)/shard_map/ppermute | solution.py:30
  26.1 10.5 %collective-permute-start.3 = (bf16[256,512]{1,0:T(8,128)(2,1)S(1)}, bf16[256,512]{1,0:T(8,128)(2,1)S(1)}, u32[]{:S(2)}, u32[]{:S(2)}) collective-permute-start(bf16[256,512]{1,0:T(8,128)(2,1)S(1)} %collective-permute-done.2.points), channel_id=1, source_target_pairs={{4,0},{5,1},{6,2},{7,3},{8,4},{9,5},{10,6},{11,7},{12,8},{13,9},{1... | collective-permute-start | bytes 786440 | tf_op jit(solution)/shard_map/ppermute | solution.py:30
  36.6 7.5 %collective-permute-start.9 = (bf16[256,512]{1,0:T(8,128)(2,1)S(1)}, bf16[256,512]{1,0:T(8,128)(2,1)S(1)}, u32[]{:S(2)}, u32[]{:S(2)}) collective-permute-start(bf16[256,512]{1,0:T(8,128)(2,1)S(1)} %collective-permute-done.3.points), channel_id=1, source_target_pairs={{4,0},{5,1},{6,2},{7,3},{8,4},{9,5},{10,6},{11,7},{12,8},{13,9},{1... | collective-permute-start | bytes 786440 | tf_op jit(solution)/shard_map/ppermute | solution.py:30
  39.3 3.9 %collective-permute-start.13 = (bf16[256,256]{1,0:T(8,128)(2,1)S(1)}, bf16[256,256]{1,0:T(8,128)(2,1)S(1)}, u32[]{:S(2)}, u32[]{:S(2)}) collective-permute-start(bf16[256,256]{1,0:T(8,128)(2,1)S(1)} %get-tuple-element.77), channel_id=1, source_target_pairs={{1,0},{0,1},{3,2},{2,3},{5,4},{4,5},{7,6},{6,7},{9,8},{8,9},{11,10... | collective-permute-start | bytes 393224 | tf_op jit(solution)/shard_map/ppermute | solution.py:30
  42.2 1.3 %collective-permute-start.10 = (bf16[256,256]{1,0:T(8,128)(2,1)S(1)}, bf16[256,256]{1,0:T(8,128)(2,1)S(1)}, u32[]{:S(2)}, u32[]{:S(2)}) collective-permute-start(bf16[256,256]{1,0:T(8,128)(2,1)S(1)} %get-tuple-element.74), channel_id=1, source_target_pairs={{1,0},{0,1},{3,2},{2,3},{5,4},{4,5},{7,6},{6,7},{9,8},{8,9},{11,10... | collective-permute-start | bytes 393224 | tf_op jit(solution)/shard_map/ppermute | solution.py:30
  42.3 1.4 %collective-permute-start.11 = (bf16[256,256]{1,0:T(8,128)(2,1)S(1)}, bf16[256,256]{1,0:T(8,128)(2,1)S(1)}, u32[]{:S(2)}, u32[]{:S(2)}) collective-permute-start(bf16[256,256]{1,0:T(8,128)(2,1)S(1)} %get-tuple-element.75), channel_id=1, source_target_pairs={{1,0},{0,1},{3,2},{2,3},{5,4},{4,5},{7,6},{6,7},{9,8},{8,9},{11,10... | collective-permute-start | bytes 393224 | tf_op jit(solution)/shard_map/ppermute | solution.py:30
  42.7 1.3 %collective-permute-start.12 = (bf16[256,256]{1,0:T(8,128)(2,1)S(1)}, bf16[256,256]{1,0:T(8,128)(2,1)S(1)}, u32[]{:S(2)}, u32[]{:S(2)}) collective-permute-start(bf16[256,256]{1,0:T(8,128)(2,1)S(1)} %get-tuple-element.76), channel_id=1, source_target_pairs={{1,0},{0,1},{3,2},{2,3},{5,4},{4,5},{7,6},{6,7},{9,8},{8,9},{11,10... | collective-permute-start | bytes 393224 | tf_op jit(solution)/shard_map/ppermute | solution.py:30
  46.5 2.3 %collective-permute-start.14 = (bf16[256,256]{1,0:T(8,128)(2,1)S(1)}, bf16[256,256]{1,0:T(8,128)(2,1)S(1)}, u32[]{:S(2)}, u32[]{:S(2)}) collective-permute-start(bf16[256,256]{1,0:T(8,128)(2,1)S(1)} %get-tuple-element.88), channel_id=1, source_target_pairs={{1,0},{0,1},{3,2},{2,3},{5,4},{4,5},{7,6},{6,7},{9,8},{8,9},{11,10... | collective-permute-start | bytes 393224 | tf_op jit(solution)/shard_map/ppermute | solution.py:30

commit v14 on v13

--- a/solution.py
+++ b/solution.py
@@ -227,7 +227,7 @@
             pltpu.SemaphoreType.DMA((4,)),
             pltpu.SemaphoreType.DMA((4,)),
         ),
-        compiler_params=pltpu.CompilerParams(vmem_limit_bytes=61 * 1024 * 1024),
+        compiler_params=pltpu.CompilerParams(vmem_limit_bytes=62 * 1024 * 1024),
         cost_estimate=pl.CostEstimate(flops=0, bytes_accessed=1 << 21, transcendentals=0),
     )(descriptors)
     near = fetch(near, near_x)

time: 72.7 us -> 72.6 us (level)
  local copies, waits for them, and re-layouts: 0.01 us -> 1.6 us
  waiting for transfers between devices: 8.76 us -> 7.17 us
    ppermute x15, waiting for transfers between devices: 8.76 us -> 7.17 us  [fetch(): return lax.ppermute(value, ('env', 'sp'), pairs)]
    unnamed x4, local copies, waits for them, and re-layouts: 0.01 us -> 1.6 us
where the time goes in v14:
time: 72.6 us; the launch traced here: 72.2 us
  starting transfers between devices  23.7 us (33%)
  blocking collectives  22.4 us (31%)
  Pallas kernels  17.3 us (24%)
  waiting for transfers between devices  7.17 us (10%)
  local copies, waits for them, and re-layouts  1.6 us (2%)
    ppermute x15, starting transfers between devices, fetch(): return lax.ppermute(value, ('env', 'sp'), pairs)  23.7 us
    all_to_all x1, blocking collectives, on_device(): pieces = lax.all_to_all(packed, 'env', 0, 0, tiled=True)  22.4 us
    pallas_call x4, Pallas kernels, take(): call(column_kernel, pair, 5, 2 * 1073741824, 1 << 23, (pltpu.VMEM((256, 4...  9.63 us
    ppermute x15, waiting for transfers between devices, fetch(): return lax.ppermute(value, ('env', 'sp'), pairs)  7.17 us
    pallas_call x2, Pallas kernels, rows(): call(body, (shape(envs, 512), shape(512, envs)) + sums, n_in, envs * 7864...  4.41 us
    pallas_call x1, Pallas kernels, on_device(): pl.pallas_call(slice_kernel, out_shape=shape(1024, 512), in_specs=[pl.Blo...  2.06 us
    unnamed x4, local copies, waits for them, and re-layouts  1.6 us
  transfers between devices with their start and end apart: 15, of which 7 were waited for; matrix products, arithmetic and copies ran while one was open for 0% of the time, Pallas kernels for 16%

profile of v14, /device:TPU:1, one launch (start us, length us, event | category | flops | bytes accessed | tf_op | source)
XLA Modules:
  0.0 72.2 jit_solution(10453772269095993435)
XLA Ops:
  0.0 0.0 copy-start.1
  0.0 2.1 %shard_map.29 = bf16[1024,512]{1,0:T(8,128)(2,1)} custom-call(bf16[2048,512]{1,0:T(8,128)(2,1)} %descriptors.1), custom_call_target="tpu_custom_call" | custom-call | bytes 2097152 | tf_op jit(solution)/shard_map/pallas_call | solution.py:220
  2.1 2.1 %collective-permute-start.4 = (bf16[1024,512]{1,0:T(8,128)(2,1)}, bf16[1024,512]{1,0:T(8,128)(2,1)S(1)}, u32[]{:S(2)}, u32[]{:S(2)}) collective-permute-start(bf16[1024,512]{1,0:T(8,128)(2,1)} %shard_map.29), channel_id=1, source_target_pairs={{32,0},{97,1},{34,2},{99,3},{36,4},{101,5},{38,6},{103,7},{40,8},{... | collective-permute-start | bytes 3145736 | tf_op jit(solution)/shard_map/ppermute | solution.py:30
  4.2 0.0 copy-done.1
  4.2 2.2 %collective-permute-start.1 = (bf16[256,512]{1,0:T(8,128)(2,1)S(1)}, bf16[256,512]{1,0:T(8,128)(2,1)S(1)}, u32[]{:S(2)}, u32[]{:S(2)}) collective-permute-start(bf16[256,512]{1,0:T(8,128)(2,1)S(1)} %copy-done.1), channel_id=1, source_target_pairs={{1,0},{0,1},{3,2},{2,3},{5,4},{4,5},{7,6},{6,7},{9,8},{8,9},{11,10... | collective-permute-start | bytes 786440 | tf_op jit(solution)/shard_map/ppermute | solution.py:30
  6.4 5.6 %collective-permute-start = (bf16[256,512]{1,0:T(8,128)(2,1)S(1)}, bf16[256,512]{1,0:T(8,128)(2,1)S(1)}, u32[]{:S(2)}, u32[]{:S(2)}) collective-permute-start(bf16[256,512]{1,0:T(8,128)(2,1)S(1)} %copy-done.1), channel_id=1, source_target_pairs={{4,0},{5,1},{6,2},{7,3},{8,4},{9,5},{10,6},{11,7},{12,8},{13,9},{1... | collective-permute-start | bytes 786440 | tf_op jit(solution)/shard_map/ppermute | solution.py:30
  12.0 0.0 collective-permute-done.1.sib_points
  12.0 0.0 copy-start
  12.0 1.6 %copy-done = bf16[2048,512]{1,0:T(8,128)(2,1)S(1)} copy-done((bf16[2048,512]{1,0:T(8,128)(2,1)S(1)}, bf16[2048,512]{1,0:T(8,128)(2,1)}, u32[]{:S(2)}) %copy-start) | copy-done | bytes 2097176
  13.6 2.2 %shard_map.28 = (bf16[2048,512]{1,0:T(8,128)(2,1)S(1)}, bf16[512,2048]{1,0:T(8,128)(2,1)S(1)}, f32[512,256]{1,0:T(8,128)S(1)}, bf16[512,512]{1,0:T(8,128)(2,1)S(1)}) custom-call(bf16[2048,512]{1,0:T(8,128)(2,1)S(1)} %copy-done, bf16[256,512]{1,0:T(8,128)(2,1)S(1)} %copy-done.1, bf16[256,512]{1,0:T(8,128)(2,1)S(1)} %collective-permute-done.1.sib_points), custom_call_target="tpu_custom_call" | custom-call | flops 1610612736 | bytes 8388608 | tf_op jit(solution)/shard_map/pallas_call | solution.py:213
  15.8 1.9 %collective-permute-done.points = bf16[256,512]{1,0:T(8,128)(2,1)S(1)} collective-permute-done((bf16[256,512]{1,0:T(8,128)(2,1)S(1)}, bf16[256,512]{1,0:T(8,128)(2,1)S(1)}, u32[]{:S(2)}, u32[]{:S(2)}) %collective-permute-start) | collective-permute-done | bytes 262176 | tf_op jit(solution)/shard_map/ppermute | solution.py:30
  17.7 3.4 %collective-permute-start.2 = (bf16[256,512]{1,0:T(8,128)(2,1)S(1)}, bf16[256,512]{1,0:T(8,128)(2,1)S(1)}, u32[]{:S(2)}, u32[]{:S(2)}) collective-permute-start(bf16[256,512]{1,0:T(8,128)(2,1)S(1)} %collective-permute-done.points), channel_id=1, source_target_pairs={{4,0},{5,1},{6,2},{7,3},{8,4},{9,5},{10,6},{11,7},{12,8},{13,9},{1... | collective-permute-start | bytes 786440 | tf_op jit(solution)/shard_map/ppermute | solution.py:30
  21.1 0.0 collective-permute-done.4.near
  21.1 0.1 shard_map.30
  21.2 1.2 %collective-permute-start.5 = (bf16[256,512]{1,0:T(8,128)(2,1)S(1)}, bf16[256,512]{1,0:T(8,128)(2,1)S(1)}, u32[]{:S(2)}, u32[]{:S(2)}) collective-permute-start(bf16[256,512]{1,0:T(8,128)(2,1)S(1)} %get-tuple-element.53.refs_0_), channel_id=1, source_target_pairs={{1,0},{0,1},{3,2},{2,3},{5,4},{4,5},{7,6},{6,7},{9,8},{8,9},{11,10... | collective-permute-start | bytes 786440 | tf_op jit(solution)/shard_map/ppermute | solution.py:30
  22.4 0.1 collective-permute-start.6
  22.5 0.4 collective-permute-start.7
  22.9 0.1 collective-permute-start.8
  23.0 3.0 %collective-permute-done.2.points = bf16[256,512]{1,0:T(8,128)(2,1)S(1)} collective-permute-done((bf16[256,512]{1,0:T(8,128)(2,1)S(1)}, bf16[256,512]{1,0:T(8,128)(2,1)S(1)}, u32[]{:S(2)}, u32[]{:S(2)}) %collective-permute-start.2) | collective-permute-done | bytes 262176 | tf_op jit(solution)/shard_map/ppermute | solution.py:30
  26.0 3.4 %collective-permute-start.3 = (bf16[256,512]{1,0:T(8,128)(2,1)S(1)}, bf16[256,512]{1,0:T(8,128)(2,1)S(1)}, u32[]{:S(2)}, u32[]{:S(2)}) collective-permute-start(bf16[256,512]{1,0:T(8,128)(2,1)S(1)} %collective-permute-done.2.points), channel_id=1, source_target_pairs={{4,0},{5,1},{6,2},{7,3},{8,4},{9,5},{10,6},{11,7},{12,8},{13,9},{1... | collective-permute-start | bytes 786440 | tf_op jit(solution)/shard_map/ppermute | solution.py:30
  29.4 0.0 collective-permute-done.5.refs_4_
  29.4 0.0 collective-permute-done.6.refs_5_
  29.4 0.0 collective-permute-done.7.refs_6_
  29.4 0.0 collective-permute-done.8.refs_7_
  29.4 2.2 %shard_map.31 = (bf16[2048,512]{1,0:T(8,128)(2,1)S(1)}, bf16[512,2048]{1,0:T(8,128)(2,1)S(1)}, bf16[256,256]{1,0:T(8,128)(2,1)S(1)}, bf16[256,256]{1,0:T(8,128)(2,1)S(1)}) custom-call(bf16[256,512]{1,0:T(8,128)(2,1)S(1)} %get-tuple-element.53.refs_0_, bf16[256,512]{1,0:T(8,128)(2,1)S(1)} %get-tuple-element.54.refs_1_, ...), custom_call_target="tpu_custom_call" | custom-call | flops 1610612736 | bytes 8388608 | tf_op jit(solution)/shard_map/pallas_call | solution.py:213
  31.6 2.4 %shard_map.33 = (bf16[256,256]{1,0:T(8,128)(2,1)S(1)}, bf16[256,256]{1,0:T(8,128)(2,1)S(1)}) custom-call(bf16[256,512]{1,0:T(8,128)(2,1)S(1)} %collective-permute-done.2.points, bf16[2048,512]{1,0:T(8,128)(2,1)S(1)} %get-tuple-element.61.refs_0_, bf16[2048,512]{1,0:T(8,128)(2,1)S(1)} %get-tuple-element.62.refs_1_, ...), custom_call_target="tpu_custom_call" | custom-call | flops 2147483648 | bytes 8388608 | tf_op jit(solution)/shard_map/pallas_call | solution.py:246
  34.0 2.4 %shard_map.32 = (bf16[256,256]{1,0:T(8,128)(2,1)S(1)}, bf16[256,256]{1,0:T(8,128)(2,1)S(1)}) custom-call(bf16[256,512]{1,0:T(8,128)(2,1)S(1)} %collective-permute-done.points, bf16[2048,512]{1,0:T(8,128)(2,1)S(1)} %get-tuple-element.61.refs_0_, bf16[2048,512]{1,0:T(8,128)(2,1)S(1)} %get-tuple-element.62.refs_1_, ...), custom_call_target="tpu_custom_call" | custom-call | flops 2147483648 | bytes 8388608 | tf_op jit(solution)/shard_map/pallas_call | solution.py:246
  36.4 0.0 collective-permute-done.3.points
  36.4 0.3 collective-permute-start.9
  36.7 2.4 %shard_map.34 = (bf16[256,256]{1,0:T(8,128)(2,1)S(1)}, bf16[256,256]{1,0:T(8,128)(2,1)S(1)}) custom-call(bf16[256,512]{1,0:T(8,128)(2,1)S(1)} %collective-permute-done.3.points, bf16[2048,512]{1,0:T(8,128)(2,1)S(1)} %get-tuple-element.61.refs_0_, bf16[2048,512]{1,0:T(8,128)(2,1)S(1)} %get-tuple-element.62.refs_1_, ...), custom_call_target="tpu_custom_call" | custom-call | flops 2147483648 | bytes 8388608 | tf_op jit(solution)/shard_map/pallas_call | solution.py:246
  39.1 3.0 %collective-permute-start.13 = (bf16[256,256]{1,0:T(8,128)(2,1)S(1)}, bf16[256,256]{1,0:T(8,128)(2,1)S(1)}, u32[]{:S(2)}, u32[]{:S(2)}) collective-permute-start(bf16[256,256]{1,0:T(8,128)(2,1)S(1)} %get-tuple-element.77), channel_id=1, source_target_pairs={{1,0},{0,1},{3,2},{2,3},{5,4},{4,5},{7,6},{6,7},{9,8},{8,9},{11,10... | collective-permute-start | bytes 393224 | tf_op jit(solution)/shard_map/ppermute | solution.py:30
  42.1 0.1 collective-permute-start.10
  42.2 0.4 collective-permute-start.11
  42.6 0.1 collective-permute-start.12
  42.7 0.4 collective-permute-done.13.refs_8_
  43.1 0.4 collective-permute-done.10.refs_5_
  43.5 0.2 collective-permute-done.11.refs_6_
  43.6 0.3 collective-permute-done.12.refs_7_
  44.0 0.0 collective-permute-done.9.points
  44.0 2.4 %shard_map.35 = (bf16[256,256]{1,0:T(8,128)(2,1)S(1)}, bf16[256,256]{1,0:T(8,128)(2,1)S(1)}) custom-call(bf16[256,512]{1,0:T(8,128)(2,1)S(1)} %collective-permute-done.9.points, bf16[2048,512]{1,0:T(8,128)(2,1)S(1)} %get-tuple-element.61.refs_0_, bf16[2048,512]{1,0:T(8,128)(2,1)S(1)} %get-tuple-element.62.refs_1_, ...), custom_call_target="tpu_custom_call" | custom-call | flops 2147483648 | bytes 8388608 | tf_op jit(solution)/shard_map/pallas_call | solution.py:246
  46.4 1.4 %collective-permute-start.14 = (bf16[256,256]{1,0:T(8,128)(2,1)S(1)}, bf16[256,256]{1,0:T(8,128)(2,1)S(1)}, u32[]{:S(2)}, u32[]{:S(2)}) collective-permute-start(bf16[256,256]{1,0:T(8,128)(2,1)S(1)} %get-tuple-element.88), channel_id=1, source_target_pairs={{1,0},{0,1},{3,2},{2,3},{5,4},{4,5},{7,6},{6,7},{9,8},{8,9},{11,10... | collective-permute-start | bytes 393224 | tf_op jit(solution)/shard_map/ppermute | solution.py:30
  47.7 1.0 %collective-permute-done.14.refs_9_ = bf16[256,256]{1,0:T(8,128)(2,1)S(1)} collective-permute-done((bf16[256,256]{1,0:T(8,128)(2,1)S(1)}, bf16[256,256]{1,0:T(8,128)(2,1)S(1)}, u32[]{:S(2)}, u32[]{:S(2)}) %collective-permute-start.14) | collective-permute-done | bytes 131104 | tf_op jit(solution)/shard_map/ppermute | solution.py:30
  48.7 0.1 shard_map.36
  48.8 22.4 %all_to_all.5.pieces = bf16[8,9,32,256]{3,2,1,0:T(8,128)(2,1)S(1)} all-to-all(bf16[8,9,32,256]{3,2,1,0:T(8,128)(2,1)S(1)} %shard_map.36), channel_id=1, replica_groups=mesh['env'=8,'sp'=32] {'env'}, dimensions={0} | all-to-all | bytes 2359296 | tf_op jit(solution)/shard_map/all_to_all | solution.py:262
  71.2 1.0 %shard_map.37 = f32[17,32,256]{2,1,0:T(8,128)} custom-call(bf16[8,9,32,256]{3,2,1,0:T(8,128)(2,1)S(1)} %all_to_all.5.pieces), custom_call_target="tpu_custom_call" | custom-call | bytes 2097152 | tf_op jit(solution)/shard_map/pallas_call | solution.py:263
Async XLA Ops:
  0.0 4.2 %copy-start.1 = (bf16[256,512]{1,0:T(8,128)(2,1)S(1)}, bf16[256,512]{1,0:T(8,128)(2,1)}, u32[]{:S(2)}) copy-start(bf16[256,512]{1,0:T(8,128)(2,1)} %own_points.1) | copy-start | bytes 786436
  2.1 19.1 %collective-permute-start.4 = (bf16[1024,512]{1,0:T(8,128)(2,1)}, bf16[1024,512]{1,0:T(8,128)(2,1)S(1)}, u32[]{:S(2)}, u32[]{:S(2)}) collective-permute-start(bf16[1024,512]{1,0:T(8,128)(2,1)} %shard_map.29), channel_id=1, source_target_pairs={{32,0},{97,1},{34,2},{99,3},{36,4},{101,5},{38,6},{103,7},{40,8},{... | collective-permute-start | bytes 3145736 | tf_op jit(solution)/shard_map/ppermute | solution.py:30
  4.2 7.8 %collective-permute-start.1 = (bf16[256,512]{1,0:T(8,128)(2,1)S(1)}, bf16[256,512]{1,0:T(8,128)(2,1)S(1)}, u32[]{:S(2)}, u32[]{:S(2)}) collective-permute-start(bf16[256,512]{1,0:T(8,128)(2,1)S(1)} %copy-done.1), channel_id=1, source_target_pairs={{1,0},{0,1},{3,2},{2,3},{5,4},{4,5},{7,6},{6,7},{9,8},{8,9},{11,10... | collective-permute-start | bytes 786440 | tf_op jit(solution)/shard_map/ppermute | solution.py:30
  6.4 11.3 %collective-permute-start = (bf16[256,512]{1,0:T(8,128)(2,1)S(1)}, bf16[256,512]{1,0:T(8,128)(2,1)S(1)}, u32[]{:S(2)}, u32[]{:S(2)}) collective-permute-start(bf16[256,512]{1,0:T(8,128)(2,1)S(1)} %copy-done.1), channel_id=1, source_target_pairs={{4,0},{5,1},{6,2},{7,3},{8,4},{9,5},{10,6},{11,7},{12,8},{13,9},{1... | collective-permute-start | bytes 786440 | tf_op jit(solution)/shard_map/ppermute | solution.py:30
  12.0 1.6 %copy-start = (bf16[2048,512]{1,0:T(8,128)(2,1)S(1)}, bf16[2048,512]{1,0:T(8,128)(2,1)}, u32[]{:S(2)}) copy-start(bf16[2048,512]{1,0:T(8,128)(2,1)} %descriptors.1) | copy-start | bytes 6291460
  17.7 8.3 %collective-permute-start.2 = (bf16[256,512]{1,0:T(8,128)(2,1)S(1)}, bf16[256,512]{1,0:T(8,128)(2,1)S(1)}, u32[]{:S(2)}, u32[]{:S(2)}) collective-permute-start(bf16[256,512]{1,0:T(8,128)(2,1)S(1)} %collective-permute-done.points), channel_id=1, source_target_pairs={{4,0},{5,1},{6,2},{7,3},{8,4},{9,5},{10,6},{11,7},{12,8},{13,9},{1... | collective-permute-start | bytes 786440 | tf_op jit(solution)/shard_map/ppermute | solution.py:30
  21.2 8.2 %collective-permute-start.5 = (bf16[256,512]{1,0:T(8,128)(2,1)S(1)}, bf16[256,512]{1,0:T(8,128)(2,1)S(1)}, u32[]{:S(2)}, u32[]{:S(2)}) collective-permute-start(bf16[256,512]{1,0:T(8,128)(2,1)S(1)} %get-tuple-element.53.refs_0_), channel_id=1, source_target_pairs={{1,0},{0,1},{3,2},{2,3},{5,4},{4,5},{7,6},{6,7},{9,8},{8,9},{11,10... | collective-permute-start | bytes 786440 | tf_op jit(solution)/shard_map/ppermute | solution.py:30
  22.4 7.0 %collective-permute-start.6 = (bf16[256,512]{1,0:T(8,128)(2,1)S(1)}, bf16[256,512]{1,0:T(8,128)(2,1)S(1)}, u32[]{:S(2)}, u32[]{:S(2)}) collective-permute-start(bf16[256,512]{1,0:T(8,128)(2,1)S(1)} %get-tuple-element.54.refs_1_), channel_id=1, source_target_pairs={{1,0},{0,1},{3,2},{2,3},{5,4},{4,5},{7,6},{6,7},{9,8},{8,9},{11,10... | collective-permute-start | bytes 786440 | tf_op jit(solution)/shard_map/ppermute | solution.py:30
  22.5 6.9 %collective-permute-start.7 = (bf16[256,512]{1,0:T(8,128)(2,1)S(1)}, bf16[256,512]{1,0:T(8,128)(2,1)S(1)}, u32[]{:S(2)}, u32[]{:S(2)}) collective-permute-start(bf16[256,512]{1,0:T(8,128)(2,1)S(1)} %get-tuple-element.55.refs_2_), channel_id=1, source_target_pairs={{1,0},{0,1},{3,2},{2,3},{5,4},{4,5},{7,6},{6,7},{9,8},{8,9},{11,10... | collective-permute-start | bytes 786440 | tf_op jit(solution)/shard_map/ppermute | solution.py:30
  22.9 6.5 %collective-permute-start.8 = (bf16[256,512]{1,0:T(8,128)(2,1)S(1)}, bf16[256,512]{1,0:T(8,128)(2,1)S(1)}, u32[]{:S(2)}, u32[]{:S(2)}) collective-permute-start(bf16[256,512]{1,0:T(8,128)(2,1)S(1)} %get-tuple-element.56.refs_3_), channel_id=1, source_target_pairs={{1,0},{0,1},{3,2},{2,3},{5,4},{4,5},{7,6},{6,7},{9,8},{8,9},{11,10... | collective-permute-start | bytes 786440 | tf_op jit(solution)/shard_map/ppermute | solution.py:30
  26.0 10.4 %collective-permute-start.3 = (bf16[256,512]{1,0:T(8,128)(2,1)S(1)}, bf16[256,512]{1,0:T(8,128)(2,1)S(1)}, u32[]{:S(2)}, u32[]{:S(2)}) collective-permute-start(bf16[256,512]{1,0:T(8,128)(2,1)S(1)} %collective-permute-done.2.points), channel_id=1, source_target_pairs={{4,0},{5,1},{6,2},{7,3},{8,4},{9,5},{10,6},{11,7},{12,8},{13,9},{1... | collective-permute-start | bytes 786440 | tf_op jit(solution)/shard_map/ppermute | solution.py:30
  36.4 7.5 %collective-permute-start.9 = (bf16[256,512]{1,0:T(8,128)(2,1)S(1)}, bf16[256,512]{1,0:T(8,128)(2,1)S(1)}, u32[]{:S(2)}, u32[]{:S(2)}) collective-permute-start(bf16[256,512]{1,0:T(8,128)(2,1)S(1)} %collective-permute-done.3.points), channel_id=1, source_target_pairs={{4,0},{5,1},{6,2},{7,3},{8,4},{9,5},{10,6},{11,7},{12,8},{13,9},{1... | collective-permute-start | bytes 786440 | tf_op jit(solution)/shard_map/ppermute | solution.py:30
  39.1 3.9 %collective-permute-start.13 = (bf16[256,256]{1,0:T(8,128)(2,1)S(1)}, bf16[256,256]{1,0:T(8,128)(2,1)S(1)}, u32[]{:S(2)}, u32[]{:S(2)}) collective-permute-start(bf16[256,256]{1,0:T(8,128)(2,1)S(1)} %get-tuple-element.77), channel_id=1, source_target_pairs={{1,0},{0,1},{3,2},{2,3},{5,4},{4,5},{7,6},{6,7},{9,8},{8,9},{11,10... | collective-permute-start | bytes 393224 | tf_op jit(solution)/shard_map/ppermute | solution.py:30
  42.1 1.3 %collective-permute-start.10 = (bf16[256,256]{1,0:T(8,128)(2,1)S(1)}, bf16[256,256]{1,0:T(8,128)(2,1)S(1)}, u32[]{:S(2)}, u32[]{:S(2)}) collective-permute-start(bf16[256,256]{1,0:T(8,128)(2,1)S(1)} %get-tuple-element.74), channel_id=1, source_target_pairs={{1,0},{0,1},{3,2},{2,3},{5,4},{4,5},{7,6},{6,7},{9,8},{8,9},{11,10... | collective-permute-start | bytes 393224 | tf_op jit(solution)/shard_map/ppermute | solution.py:30
  42.2 1.4 %collective-permute-start.11 = (bf16[256,256]{1,0:T(8,128)(2,1)S(1)}, bf16[256,256]{1,0:T(8,128)(2,1)S(1)}, u32[]{:S(2)}, u32[]{:S(2)}) collective-permute-start(bf16[256,256]{1,0:T(8,128)(2,1)S(1)} %get-tuple-element.75), channel_id=1, source_target_pairs={{1,0},{0,1},{3,2},{2,3},{5,4},{4,5},{7,6},{6,7},{9,8},{8,9},{11,10... | collective-permute-start | bytes 393224 | tf_op jit(solution)/shard_map/ppermute | solution.py:30
  42.6 1.3 %collective-permute-start.12 = (bf16[256,256]{1,0:T(8,128)(2,1)S(1)}, bf16[256,256]{1,0:T(8,128)(2,1)S(1)}, u32[]{:S(2)}, u32[]{:S(2)}) collective-permute-start(bf16[256,256]{1,0:T(8,128)(2,1)S(1)} %get-tuple-element.76), channel_id=1, source_target_pairs={{1,0},{0,1},{3,2},{2,3},{5,4},{4,5},{7,6},{6,7},{9,8},{8,9},{11,10... | collective-permute-start | bytes 393224 | tf_op jit(solution)/shard_map/ppermute | solution.py:30
  46.4 2.3 %collective-permute-start.14 = (bf16[256,256]{1,0:T(8,128)(2,1)S(1)}, bf16[256,256]{1,0:T(8,128)(2,1)S(1)}, u32[]{:S(2)}, u32[]{:S(2)}) collective-permute-start(bf16[256,256]{1,0:T(8,128)(2,1)S(1)} %get-tuple-element.88), channel_id=1, source_target_pairs={{1,0},{0,1},{3,2},{2,3},{5,4},{4,5},{7,6},{6,7},{9,8},{8,9},{11,10... | collective-permute-start | bytes 393224 | tf_op jit(solution)/shard_map/ppermute | solution.py:30
